TPU v7x, 32 devices: a whole 2x2x4 slice. The times are simulated.
32 devices in a mesh: tm: 2 (over x), ulysses: 4 (over z), dp: 4 (over y, core).
Axes of the slice: x: 2, y: 2, z: 4, core: 2. Of those that a mesh axis runs over, the one named last changes fastest.
Arguments:
- queries: bfloat16 [4, 1536, 1536], P('dp', ('tm', 'ulysses')), may hold values from -16 to 16
- keys: bfloat16 [4, 1536, 1536], P('dp', ('tm', 'ulysses')), may hold values from -16 to 16
- values: bfloat16 [4, 1536, 1536], P('dp', ('tm', 'ulysses')), may hold values from -6 to 6
- attn_out: bfloat16 [4, 1536, 1536], P('dp', ('tm', 'ulysses')), may hold values from -4 to 4
- out_grad: bfloat16 [4, 1536, 1536], P('dp', ('tm', 'ulysses')), may hold values from -6 to 6
- out_gain: float32 [1536], replicated, may hold values from 0.5 to 2
Outputs:
- query_grad: bfloat16 [4, 1536, 1536], P('dp', ('tm', 'ulysses'))
- key_grad: bfloat16 [4, 1536, 1536], P('dp', ('tm', 'ulysses'))
- value_grad: bfloat16 [4, 1536, 1536], P('dp', ('tm', 'ulysses'))
- gain_grad: float32 [1536], replicated
All inputs are finite; a program needn't handle non-finite values.
Results may differ from a plain program's by a relative error of at most 0.0058.
Values may be sent and summed in bfloat16 or wider, within the bound.
No kernel may reach another device: no remote copies, remote signals or barrier semaphores. Data moves between devices by JAX's collectives and lax.ppermute only.
A program may use at most 128 MiB of HBM per device.

v0:
```python
import jax
import jax.numpy as jnp
from jax import lax
from jax.sharding import PartitionSpec as P

HD = 128
TILE = 384
TILES_W = 2


def with_halo(value, sides, width):
    for axis, dim in sides:
        size, length = (lax.axis_size(axis), value.shape[dim])
        up = [(i, (i + 1) % size) for i in range(size - 1)]
        down = [(j, i) for i, j in up]
        last = lax.slice_in_dim(value, length - width, length, axis=dim)
        initial = lax.slice_in_dim(value, 0, width, axis=dim)
        before = lax.ppermute(last, axis, up)
        after = lax.ppermute(initial, axis, down)
        value = jnp.concatenate([before, value, after], axis=dim)
    return value


def from_behind(value, axis, steps):
    count = lax.axis_size(axis)
    initial, last = (max(0, -steps), min(count, count - steps))
    return lax.ppermute(value, axis, [(source, source + steps) for source in range(initial, last)])


def row_spans(slab_rows, column):
    lowest = max(column - 1, 0)
    highest = min(column + 1, TILES_W - 1)
    return [
        (source * slab_rows + lowest * TILE, source * slab_rows + (highest + 1) * TILE)
        for source in range(3)
    ]


def take_rows(matrix, windows):
    return jnp.concatenate([matrix[first_row:end_row] for first_row, end_row in windows], axis=0)


def tile_scores(query_tile, key_rows):
    return jnp.einsum("qhd,khd->hqk", query_tile, key_rows, preferred_element_type=jnp.float32) * (
        1.0 / HD**0.5
    )


def log_totals(scores):
    row_max = jnp.max(scores, axis=2, keepdims=True)
    sum_exp = jnp.sum(jnp.exp(scores - row_max), axis=2, keepdims=True)
    return row_max + jnp.log(sum_exp)


def tile_grads(scores, log_total, grad_tile, dots_tile, value_rows):
    weights = jnp.exp(scores - log_total)
    grad_weights = jnp.einsum(
        "qhd,khd->hqk", grad_tile, value_rows, preferred_element_type=jnp.float32
    )
    grad_scores = (weights * (grad_weights - dots_tile[:, :, None]) * (1.0 / HD**0.5)).astype(
        jnp.bfloat16
    )
    return (weights.astype(jnp.bfloat16), grad_scores)


def masked_scores(query_tile, key_ext, windows, flags):
    usable = jnp.concatenate(
        [
            jnp.broadcast_to(flags[source], (end_row - first_row,))
            for source, (first_row, end_row) in enumerate(windows)
        ]
    )
    key_rows = take_rows(key_ext, windows)
    scores = jnp.where(usable[None, None, :], tile_scores(query_tile, key_rows), -jnp.inf)
    return (scores, key_rows)


def local(queries, keys, values, attn_out, out_grad, out_gain):
    grad_out = (out_grad[0].astype(jnp.float32) * out_gain).astype(jnp.bfloat16)
    gain_part = jnp.sum(out_grad[0].astype(jnp.float32) * attn_out[0].astype(jnp.float32), axis=0)
    gain_total = lax.psum(gain_part, ("tm", "ulysses", "dp"))
    token_count = (
        queries.shape[1] * lax.axis_size("tm") * lax.axis_size("ulysses") * lax.axis_size("dp")
    )
    gain_grad = gain_total / token_count
    query_h, key_h, value_h, output_h, grad_h = (
        lax.all_to_all(queries[0], "ulysses", split_axis=1, concat_axis=0, tiled=True),
        lax.all_to_all(keys[0], "ulysses", split_axis=1, concat_axis=0, tiled=True),
        lax.all_to_all(values[0], "ulysses", split_axis=1, concat_axis=0, tiled=True),
        lax.all_to_all(attn_out[0], "ulysses", split_axis=1, concat_axis=0, tiled=True),
        lax.all_to_all(grad_out, "ulysses", split_axis=1, concat_axis=0, tiled=True),
    )
    slab_rows = query_h.shape[0]
    head_count = query_h.shape[1] // HD
    shape_heads = (slab_rows, head_count, HD)
    query_heads = query_h.reshape(shape_heads)
    grad_heads = grad_h.reshape(shape_heads)
    dots_rows = jnp.transpose(
        jnp.sum(
            grad_h.astype(jnp.float32).reshape(shape_heads)
            * output_h.astype(jnp.float32).reshape(shape_heads),
            axis=2,
        )
    )
    position = lax.axis_index("tm")
    flags = (position > 0, position >= 0, position < lax.axis_size("tm") - 1)
    wide_shape = (3 * slab_rows, head_count, HD)
    query_grads = []
    extended = with_halo(jnp.stack([key_h, value_h]), (("tm", 1),), slab_rows)
    key_ext = extended[0].reshape(wide_shape)
    value_ext = extended[1].reshape(wide_shape)
    key_grad = jnp.zeros(wide_shape, jnp.float32)
    value_grad = jnp.zeros(wide_shape, jnp.float32)
    for column in range(TILES_W):
        windows = row_spans(slab_rows, column)
        tile_rows = slice(column * TILE, (column + 1) * TILE)
        scores, key_rows = masked_scores(query_heads[tile_rows], key_ext, windows, flags)
        weights_low, grad_scores = tile_grads(
            scores,
            log_totals(scores),
            grad_heads[tile_rows],
            dots_rows[:, tile_rows],
            take_rows(value_ext, windows),
        )
        query_grads.append(
            jnp.einsum("hqk,khd->qhd", grad_scores, key_rows, preferred_element_type=jnp.float32)
        )
        key_part = jnp.einsum(
            "hqk,qhd->khd", grad_scores, query_heads[tile_rows], preferred_element_type=jnp.float32
        )
        value_part = jnp.einsum(
            "hqk,qhd->khd", weights_low, grad_heads[tile_rows], preferred_element_type=jnp.float32
        )
        offset = 0
        for first_row, end_row in windows:
            length = end_row - first_row
            key_grad = key_grad.at[first_row:end_row].add(key_part[offset : offset + length])
            value_grad = value_grad.at[first_row:end_row].add(value_part[offset : offset + length])
            offset += length
    lower = from_behind(jnp.stack([key_grad[:slab_rows], value_grad[:slab_rows]]), "tm", -1)
    upper = from_behind(
        jnp.stack([key_grad[2 * slab_rows :], value_grad[2 * slab_rows :]]), "tm", 1
    )
    key_total = key_grad[slab_rows : 2 * slab_rows] + lower[0] + upper[0]
    value_total = value_grad[slab_rows : 2 * slab_rows] + lower[1] + upper[1]
    flat_shape = (slab_rows, head_count * HD)
    grad_query = jnp.concatenate(query_grads, axis=0).astype(jnp.bfloat16).reshape(flat_shape)
    grad_key = key_total.astype(jnp.bfloat16).reshape(flat_shape)
    grad_value = value_total.astype(jnp.bfloat16).reshape(flat_shape)
    token_query, token_key, token_value = (
        lax.all_to_all(grad_query, "ulysses", split_axis=0, concat_axis=1, tiled=True),
        lax.all_to_all(grad_key, "ulysses", split_axis=0, concat_axis=1, tiled=True),
        lax.all_to_all(grad_value, "ulysses", split_axis=0, concat_axis=1, tiled=True),
    )
    return (token_query[None], token_key[None], token_value[None], gain_grad)


def solution(mesh):
    return jax.shard_map(
        local,
        mesh=mesh,
        in_specs=(
            P("dp", ("tm", "ulysses"), None),
            P("dp", ("tm", "ulysses"), None),
            P("dp", ("tm", "ulysses"), None),
            P("dp", ("tm", "ulysses"), None),
            P("dp", ("tm", "ulysses"), None),
            P(),
        ),
        out_specs=(
            P("dp", ("tm", "ulysses"), None),
            P("dp", ("tm", "ulysses"), None),
            P("dp", ("tm", "ulysses"), None),
            P(),
        ),
        check_vma=False,
    )
```

profile of v0, /device:TPU:0, one launch (start us, length us, event | category | flops | bytes accessed | tf_op | source)
XLA Modules:
  0.0 298.9 jit_solution(2678267301156928809)
XLA Ops:
  3.2 6.3 %all-to-all-start.2 = ((bf16[192,4,384]{2,0,1:T(8,128)(2,1)}), bf16[192,4,384]{2,0,1:T(8,128)(2,1)S(1)}, u32[]{:S(2)}, u32[]{:S(2)}) async-start(bf16[192,4,384]{2,0,1:T(8,128)(2,1)} %copy.107), calls=%async_computation.2 | async-start | bytes 1179648 | tf_op jit(solution)/shard_map/all_to_all | solution.py:87
  10.5 14.9 %all-to-all-done.2 = bf16[192,4,384]{2,0,1:T(8,128)(2,1)S(1)} async-done(((bf16[192,4,384]{2,0,1:T(8,128)(2,1)}), bf16[192,4,384]{2,0,1:T(8,128)(2,1)S(1)}, u32[]{:S(2)}, u32[]{:S(2)}) %all-to-all-start.2) | async-done | bytes 589856 | tf_op jit(solution)/shard_map/all_to_all | solution.py:87
  25.4 3.5 %all-to-all-start = ((bf16[192,4,384]{2,0,1:T(8,128)(2,1)}), bf16[192,4,384]{2,0,1:T(8,128)(2,1)S(1)}, u32[]{:S(2)}, u32[]{:S(2)}) async-start(bf16[192,4,384]{2,0,1:T(8,128)(2,1)} %copy.100), calls=%async_computation | async-start | bytes 1179648 | tf_op jit(solution)/shard_map/all_to_all | solution.py:88
  31.5 12.8 %all-to-all-done = bf16[192,4,384]{2,0,1:T(8,128)(2,1)S(1)} async-done(((bf16[192,4,384]{2,0,1:T(8,128)(2,1)}), bf16[192,4,384]{2,0,1:T(8,128)(2,1)S(1)}, u32[]{:S(2)}, u32[]{:S(2)}) %all-to-all-start) | async-done | bytes 589856 | tf_op jit(solution)/shard_map/all_to_all | solution.py:88
  44.3 3.5 %all-to-all-start.1 = ((bf16[192,4,384]{2,0,1:T(8,128)(2,1)}), bf16[192,4,384]{2,0,1:T(8,128)(2,1)S(1)}, u32[]{:S(2)}, u32[]{:S(2)}) async-start(bf16[192,4,384]{2,0,1:T(8,128)(2,1)} %copy.101), calls=%async_computation.1 | async-start | bytes 1179648 | tf_op jit(solution)/shard_map/all_to_all | solution.py:89
  48.8 14.3 %all-to-all-done.1 = bf16[192,4,384]{2,0,1:T(8,128)(2,1)S(1)} async-done(((bf16[192,4,384]{2,0,1:T(8,128)(2,1)}), bf16[192,4,384]{2,0,1:T(8,128)(2,1)S(1)}, u32[]{:S(2)}, u32[]{:S(2)}) %all-to-all-start.1) | async-done | bytes 589856 | tf_op jit(solution)/shard_map/all_to_all | solution.py:89
  63.1 4.1 %all-to-all-start.4 = ((bf16[192,4,384]{2,0,1:T(8,128)(2,1)}), bf16[192,4,384]{2,0,1:T(8,128)(2,1)}, u32[]{:S(2)}, u32[]{:S(2)}) async-start(bf16[192,4,384]{2,0,1:T(8,128)(2,1)} %copy.116), calls=%async_computation.4 | async-start | bytes 1179648 | tf_op jit(solution)/shard_map/all_to_all | solution.py:90
  68.6 14.1 %all-to-all-done.4 = bf16[192,4,384]{2,0,1:T(8,128)(2,1)} async-done(((bf16[192,4,384]{2,0,1:T(8,128)(2,1)}), bf16[192,4,384]{2,0,1:T(8,128)(2,1)}, u32[]{:S(2)}, u32[]{:S(2)}) %all-to-all-start.4) | async-done | bytes 589856 | tf_op jit(solution)/shard_map/all_to_all | solution.py:90
  88.7 7.1 %collective-permute-start = (bf16[2,768,384]{2,1,0:T(8,128)(2,1)}, bf16[2,768,384]{2,1,0:T(8,128)(2,1)}, u32[]{:S(2)}, u32[]{:S(2)}) collective-permute-start(bf16[2,768,384]{2,1,0:T(8,128)(2,1)} %pad_maximum_fusion.4), channel_id=1, source_target_pairs={{0,16},{1,17},{2,18},{3,19},{4,20},{5,21},{6,22},{7,23},{8,24},{9,... | collective-permute-start | bytes 3538952 | tf_op jit(solution)/shard_map/ppermute | solution.py:18
  105.9 10.6 %collective-permute-done.1 = bf16[2,768,384]{2,1,0:T(8,128)(2,1)} collective-permute-done((bf16[2,768,384]{2,1,0:T(8,128)(2,1)}, bf16[2,768,384]{2,1,0:T(8,128)(2,1)}, u32[]{:S(2)}, u32[]{:S(2)}) %collective-permute-start.1) | collective-permute-done | bytes 1179680 | tf_op jit(solution)/shard_map/ppermute | solution.py:19
  126.9 3.7 %fusion.17 = f32[2304,3,128]{2,0,1:T(8,128)} fusion(bf16[384,3,128]{0,2,1:T(8,128)(2,1)S(1)} %copy.135, f32[3,2304,384]{2,1,0:T(8,128)S(1)} %get-tuple-element.167, f32[3,384]{1,0:T(4,128)S(1)} %log_add_fusion), kind=kOutput, calls=%fused_computation.25 | convolution fusion | flops 684785664 | bytes 14455296 | tf_op jit(solution)/shard_map/hqk,qhd->khd/dot_general | solution.py:131
  130.7 6.0 %multiply_convert_fusion = bf16[3,384,2304]{1,2,0:T(8,128)(2,1)S(1)} fusion(f32[3,2304,384]{2,1,0:T(8,128)S(1)} %get-tuple-element.167, bf16[384,3,128]{0,2,1:T(8,128)(2,1)S(1)} %copy.135, f32[3,384]{1,0:T(4,128)S(1)} %copy.123, f32[3,384]{1,0:T(4,128)S(1)} %log_add_fusion, bf16[768,3,128]{2,0,1:T(8,128)(2,1)S(1)} %copy-done.20, ...), kind=kOutput, calls=%fused_computation.12 | convolution fusion | flops 698056704 | bytes 17998848 | tf_op jit(solution)/shard_map/qhd,khd->hqk/dot_general | solution.py:57
  145.8 7.6 %multiply_convert_fusion.1 = bf16[3,384,2304]{1,2,0:T(8,128)(2,1)} fusion(f32[3,2304,384]{2,1,0:T(8,128)S(1)} %get-tuple-element.169, bf16[384,3,128]{0,2,1:T(8,128)(2,1)S(1)} %copy-done.12, f32[3,384]{1,0:T(4,128)S(1)} %copy.117, f32[3,384]{1,0:T(4,128)S(1)} %log_add_fusion.1, bf16[768,3,128]{2,0,1:T(8,128)(2,1)S(1)} %copy-done.21, ...), kind=kOutput, calls=%fused_computation.14 | convolution fusion | flops 698056704 | bytes 17998848 | tf_op jit(solution)/shard_map/qhd,khd->hqk/dot_general | solution.py:57
  153.4 4.0 %broadcast_select_fusion.1 = (f32[2304,3,128]{2,0,1:T(8,128)S(1)}, f32[2304,3,128]{2,0,1:T(8,128)S(1)}, f32[2304,3,128]{2,0,1:T(8,128)S(1)}) fusion(pred[2304]{0:T(1024)(128)(4,1)S(1)} %copy-done.29, f32[2304,3,128]{2,0,1:T(8,128)S(1)} %fusion.14, bf16[3,384,2304]{1,2,0:T(8,128)(2,1)} %multiply_convert_fusion.1, bf16[384,3,128]{2,1,0:T(4,128)(2,1)S(1)} %copy-done.11), kind=kOutput, calls=%fused_computation.31 | convolution fusion | flops 681246720 | bytes 19761408 | tf_op jit(solution)/shard_map/hqk,qhd->khd/dot_general | solution.py:128
  168.3 7.5 %collective-permute-start.3 = (f32[2,768,3,128]{3,1,2,0:T(8,128)}, f32[2,768,3,128]{3,1,2,0:T(8,128)}, u32[]{:S(2)}, u32[]{:S(2)}) collective-permute-start(f32[2,768,3,128]{3,1,2,0:T(8,128)} %pad_maximum_fusion.1), channel_id=1, source_target_pairs={{0,16},{1,17},{2,18},{3,19},{4,20},{5,21},{6,22},{7,23},{8,24},{9,... | collective-permute-start | bytes 7077896 | tf_op jit(solution)/shard_map/ppermute | solution.py:27
  179.4 4.9 %convolution_convert_fusion.1 = bf16[3,128,384]{2,1,0:T(8,128)(2,1)} fusion(bf16[3,384,2304]{1,2,0:T(8,128)(2,1)} %multiply_convert_fusion.1, bf16[768,3,128]{2,0,1:T(8,128)(2,1)} %copy-done.14, bf16[768,3,128]{2,0,1:T(8,128)(2,1)} %copy.105, bf16[768,3,128]{2,0,1:T(8,128)(2,1)} %copy-done.17), kind=kOutput, calls=%fused_computation.33 | convolution fusion | flops 684933120 | bytes 7372800 | tf_op jit(solution)/shard_map/hqk,khd->qhd/dot_general | solution.py:126
  188.2 4.8 %all-to-all-start.5 = ((bf16[4,192,384]{2,1,0:T(8,128)(2,1)}), bf16[4,192,384]{2,1,0:T(8,128)(2,1)}, u32[]{:S(2)}, u32[]{:S(2)}) async-start(bf16[4,192,384]{2,1,0:T(8,128)(2,1)} %bitcast.117), calls=%async_computation.5 | async-start | bytes 1179648 | tf_op jit(solution)/shard_map/all_to_all | solution.py:151
  192.9 25.9 %collective-permute-done.2 = f32[2,768,3,128]{3,1,2,0:T(8,128)} collective-permute-done((f32[2,768,3,128]{3,1,2,0:T(8,128)}, f32[2,768,3,128]{3,1,2,0:T(8,128)}, u32[]{:S(2)}, u32[]{:S(2)}) %collective-permute-start.2) | collective-permute-done | bytes 2359328 | tf_op jit(solution)/shard_map/ppermute | solution.py:27
  218.8 4.2 %collective-permute-done.3 = f32[2,768,3,128]{3,1,2,0:T(8,128)} collective-permute-done((f32[2,768,3,128]{3,1,2,0:T(8,128)}, f32[2,768,3,128]{3,1,2,0:T(8,128)}, u32[]{:S(2)}, u32[]{:S(2)}) %collective-permute-start.3) | collective-permute-done | bytes 2359328 | tf_op jit(solution)/shard_map/ppermute | solution.py:27
  223.0 4.6 %fusion.21 = (bf16[768,3,128]{2,0,1:T(8,128)(2,1)S(1)}, bf16[768,3,128]{2,0,1:T(8,128)(2,1)}) fusion(f32[2,768,3,128]{3,1,2,0:T(8,128)} %collective-permute-done.3, f32[2,768,3,128]{3,1,2,0:T(8,128)} %collective-permute-done.2, f32[2304,3,128]{2,0,1:T(8,128)} %fusion.17, f32[2304,3,128]{2,0,1:T(8,128)} %copy-done.1, ...), kind=kLoop, calls=%fused_computation.36 | loop fusion | flops 2359296 | bytes 10616832 | tf_op jit(solution)/shard_map/convert_element_type | solution.py:149
  229.5 4.5 %all-to-all-start.7 = ((bf16[4,192,384]{2,1,0:T(8,128)(2,1)}), bf16[4,192,384]{2,1,0:T(8,128)(2,1)S(1)}, u32[]{:S(2)}, u32[]{:S(2)}) async-start(bf16[4,192,384]{2,1,0:T(8,128)(2,1)} %all_to_all.108), calls=%async_computation.7 | async-start | bytes 1179648 | tf_op jit(solution)/shard_map/all_to_all | solution.py:153
  235.7 10.9 %all-to-all-done.7 = bf16[4,192,384]{2,1,0:T(8,128)(2,1)S(1)} async-done(((bf16[4,192,384]{2,1,0:T(8,128)(2,1)}), bf16[4,192,384]{2,1,0:T(8,128)(2,1)S(1)}, u32[]{:S(2)}, u32[]{:S(2)}) %all-to-all-start.7) | async-done | bytes 589856 | tf_op jit(solution)/shard_map/all_to_all | solution.py:153
  246.6 3.7 %all-to-all-start.6 = ((bf16[4,192,384]{2,1,0:T(8,128)(2,1)}), bf16[4,192,384]{2,1,0:T(8,128)(2,1)S(1)}, u32[]{:S(2)}, u32[]{:S(2)}) async-start(bf16[4,192,384]{2,1,0:T(8,128)(2,1)} %all_to_all.105), calls=%async_computation.6 | async-start | bytes 1179648 | tf_op jit(solution)/shard_map/all_to_all | solution.py:152
  250.6 41.9 %psum.7 = f32[1536]{0:T(1024)S(1)} all-reduce(f32[1536]{0:T(1024)S(1)} %multiply_reduce_fusion), channel_id=1, replica_groups=mesh['tm'=2,'ulysses'=4,'dp'=4] {'tm','ulysses','dp'}, use_global_device_ids=true, to_apply=%region_6.7 | all-reduce | flops 1536 | bytes 12288 | tf_op jit(solution)/shard_map/psum | solution.py:81
  (147 shorter events, 71.9 us)
Async XLA Ops:
  0.6 8.9 %copy-start.13 = (bf16[1,192,1536]{2,1,0:T(8,128)(2,1)S(1)}, bf16[1,192,1536]{2,1,0:T(8,128)(2,1)}, u32[]{:S(2)}) copy-start(bf16[1,192,1536]{2,1,0:T(8,128)(2,1)} %param.31) | copy-start | bytes 1769476
  3.2 22.2 %all-to-all-start.2 = ((bf16[192,4,384]{2,0,1:T(8,128)(2,1)}), bf16[192,4,384]{2,0,1:T(8,128)(2,1)S(1)}, u32[]{:S(2)}, u32[]{:S(2)}) async-start(bf16[192,4,384]{2,0,1:T(8,128)(2,1)} %copy.107), calls=%async_computation.2 | async-start | bytes 1179648 | tf_op jit(solution)/shard_map/all_to_all | solution.py:87
  9.5 38.2 %copy-start.6 = (bf16[1,192,1536]{2,1,0:T(8,128)(2,1)S(1)}, bf16[1,192,1536]{2,1,0:T(8,128)(2,1)}, u32[]{:S(2)}) copy-start(bf16[1,192,1536]{2,1,0:T(8,128)(2,1)} %param.33) | copy-start | bytes 1769476
  25.4 18.9 %all-to-all-start = ((bf16[192,4,384]{2,0,1:T(8,128)(2,1)}), bf16[192,4,384]{2,0,1:T(8,128)(2,1)S(1)}, u32[]{:S(2)}, u32[]{:S(2)}) async-start(bf16[192,4,384]{2,0,1:T(8,128)(2,1)} %copy.100), calls=%async_computation | async-start | bytes 1179648 | tf_op jit(solution)/shard_map/all_to_all | solution.py:88
  28.9 38.4 %copy-start.28 = (f32[1536]{0:T(1024)S(1)}, f32[1536]{0:T(1024)}, u32[]{:S(2)}) copy-start(f32[1536]{0:T(1024)} %param.35) | copy-start | bytes 18436
  28.9 38.4 %copy-start.4 = (bf16[1,192,1536]{2,1,0:T(8,128)(2,1)S(1)}, bf16[1,192,1536]{2,1,0:T(8,128)(2,1)}, u32[]{:S(2)}) copy-start(bf16[1,192,1536]{2,1,0:T(8,128)(2,1)} %param.34) | copy-start | bytes 1769476
  44.3 18.8 %all-to-all-start.1 = ((bf16[192,4,384]{2,0,1:T(8,128)(2,1)}), bf16[192,4,384]{2,0,1:T(8,128)(2,1)S(1)}, u32[]{:S(2)}, u32[]{:S(2)}) async-start(bf16[192,4,384]{2,0,1:T(8,128)(2,1)} %copy.101), calls=%async_computation.1 | async-start | bytes 1179648 | tf_op jit(solution)/shard_map/all_to_all | solution.py:89
  63.1 19.6 %all-to-all-start.4 = ((bf16[192,4,384]{2,0,1:T(8,128)(2,1)}), bf16[192,4,384]{2,0,1:T(8,128)(2,1)}, u32[]{:S(2)}, u32[]{:S(2)}) async-start(bf16[192,4,384]{2,0,1:T(8,128)(2,1)} %copy.116), calls=%async_computation.4 | async-start | bytes 1179648 | tf_op jit(solution)/shard_map/all_to_all | solution.py:90
  82.7 18.8 %all-to-all-start.3 = ((bf16[192,4,384]{2,0,1:T(8,128)(2,1)}), bf16[192,4,384]{2,0,1:T(8,128)(2,1)S(1)}, u32[]{:S(2)}, u32[]{:S(2)}) async-start(bf16[192,4,384]{2,0,1:T(8,128)(2,1)} %fusion.32), calls=%async_computation.3 | async-start | bytes 1179648 | tf_op jit(solution)/shard_map/all_to_all | solution.py:91
  87.3 29.1 %collective-permute-start.1 = (bf16[2,768,384]{2,1,0:T(8,128)(2,1)}, bf16[2,768,384]{2,1,0:T(8,128)(2,1)}, u32[]{:S(2)}, u32[]{:S(2)}) collective-permute-start(bf16[2,768,384]{2,1,0:T(8,128)(2,1)} %pad_maximum_fusion.4), channel_id=1, source_target_pairs={{16,0},{17,1},{18,2},{19,3},{20,4},{21,5},{22,6},{23,7},{24,8},{25... | collective-permute-start | bytes 3538952 | tf_op jit(solution)/shard_map/ppermute | solution.py:19
  88.7 31.0 %collective-permute-start = (bf16[2,768,384]{2,1,0:T(8,128)(2,1)}, bf16[2,768,384]{2,1,0:T(8,128)(2,1)}, u32[]{:S(2)}, u32[]{:S(2)}) collective-permute-start(bf16[2,768,384]{2,1,0:T(8,128)(2,1)} %pad_maximum_fusion.4), channel_id=1, source_target_pairs={{0,16},{1,17},{2,18},{3,19},{4,20},{5,21},{6,22},{7,23},{8,24},{9,... | collective-permute-start | bytes 3538952 | tf_op jit(solution)/shard_map/ppermute | solution.py:18
  121.9 8.8 %copy-start.22 = (bf16[768,3,128]{2,0,1:T(8,128)(2,1)}, bf16[768,3,128]{2,0,1:T(8,128)(2,1)S(1)}, u32[]{:S(2)}) copy-start(bf16[768,3,128]{2,0,1:T(8,128)(2,1)S(1)} %copy.112) | copy-start | bytes 1769476
  162.1 13.6 %slice-start = ((s8[5308416]{0:T(1024)(128)(4,1)}), s8[4194304]{0:T(1024)(128)(4,1)S(1)}, s32[]{:S(2)}) async-start(s8[5308416]{0:T(1024)(128)(4,1)} %bitcast.108), calls=%async_computation.8 | async-start | bytes 8388608
  162.2 13.5 %slice-start.1 = ((s8[5308416]{0:T(1024)(128)(4,1)}), s8[1114112]{0:T(1024)(128)(4,1)S(1)}, s32[]{:S(2)}) async-start(s8[5308416]{0:T(1024)(128)(4,1)} %bitcast.108), calls=%async_computation.9 | async-start | bytes 2228224
  165.1 10.6 %copy-start.16 = (bf16[768,3,128]{2,0,1:T(8,128)(2,1)S(1)}, bf16[768,3,128]{2,0,1:T(8,128)(2,1)}, u32[]{:S(2)}) copy-start(bf16[768,3,128]{2,0,1:T(8,128)(2,1)} %copy-done.14) | copy-start | bytes 1769476
  165.1 10.6 %copy-start.19 = (bf16[768,3,128]{2,0,1:T(8,128)(2,1)S(1)}, bf16[768,3,128]{2,0,1:T(8,128)(2,1)}, u32[]{:S(2)}) copy-start(bf16[768,3,128]{2,0,1:T(8,128)(2,1)} %copy-done.17) | copy-start | bytes 1769476
  165.1 10.6 %copy-start.25 = (bf16[768,3,128]{2,0,1:T(8,128)(2,1)S(1)}, bf16[768,3,128]{2,0,1:T(8,128)(2,1)}, u32[]{:S(2)}) copy-start(bf16[768,3,128]{2,0,1:T(8,128)(2,1)} %copy.105) | copy-start | bytes 1769476
  165.1 53.7 %collective-permute-start.2 = (f32[2,768,3,128]{3,1,2,0:T(8,128)}, f32[2,768,3,128]{3,1,2,0:T(8,128)}, u32[]{:S(2)}, u32[]{:S(2)}) collective-permute-start(f32[2,768,3,128]{3,1,2,0:T(8,128)} %pad_maximum_fusion), channel_id=1, source_target_pairs={{16,0},{17,1},{18,2},{19,3},{20,4},{21,5},{22,6},{23,7},{24,8},{25... | collective-permute-start | bytes 7077896 | tf_op jit(solution)/shard_map/ppermute | solution.py:27
  168.3 54.8 %collective-permute-start.3 = (f32[2,768,3,128]{3,1,2,0:T(8,128)}, f32[2,768,3,128]{3,1,2,0:T(8,128)}, u32[]{:S(2)}, u32[]{:S(2)}) collective-permute-start(f32[2,768,3,128]{3,1,2,0:T(8,128)} %pad_maximum_fusion.1), channel_id=1, source_target_pairs={{0,16},{1,17},{2,18},{3,19},{4,20},{5,21},{6,22},{7,23},{8,24},{9,... | collective-permute-start | bytes 7077896 | tf_op jit(solution)/shard_map/ppermute | solution.py:27
  188.2 41.3 %all-to-all-start.5 = ((bf16[4,192,384]{2,1,0:T(8,128)(2,1)}), bf16[4,192,384]{2,1,0:T(8,128)(2,1)}, u32[]{:S(2)}, u32[]{:S(2)}) async-start(bf16[4,192,384]{2,1,0:T(8,128)(2,1)} %bitcast.117), calls=%async_computation.5 | async-start | bytes 1179648 | tf_op jit(solution)/shard_map/all_to_all | solution.py:151
  228.2 22.2 %copy-start.5 = (bf16[1,192,1536]{2,1,0:T(8,128)(2,1)S(1)}, bf16[1,192,1536]{2,1,0:T(8,128)(2,1)}, u32[]{:S(2)}) copy-start(bf16[1,192,1536]{2,1,0:T(8,128)(2,1)} %param.34) | copy-start | bytes 1769476
  228.2 22.2 %copy-start.7 = (bf16[1,192,1536]{2,1,0:T(8,128)(2,1)S(1)}, bf16[1,192,1536]{2,1,0:T(8,128)(2,1)}, u32[]{:S(2)}) copy-start(bf16[1,192,1536]{2,1,0:T(8,128)(2,1)} %param.33) | copy-start | bytes 1769476
  229.5 17.2 %all-to-all-start.7 = ((bf16[4,192,384]{2,1,0:T(8,128)(2,1)}), bf16[4,192,384]{2,1,0:T(8,128)(2,1)S(1)}, u32[]{:S(2)}, u32[]{:S(2)}) async-start(bf16[4,192,384]{2,1,0:T(8,128)(2,1)} %all_to_all.108), calls=%async_computation.7 | async-start | bytes 1179648 | tf_op jit(solution)/shard_map/all_to_all | solution.py:153
  246.6 50.5 %all-to-all-start.6 = ((bf16[4,192,384]{2,1,0:T(8,128)(2,1)}), bf16[4,192,384]{2,1,0:T(8,128)(2,1)S(1)}, u32[]{:S(2)}, u32[]{:S(2)}) async-start(bf16[4,192,384]{2,1,0:T(8,128)(2,1)} %all_to_all.105), calls=%async_computation.6 | async-start | bytes 1179648 | tf_op jit(solution)/shard_map/all_to_all | solution.py:152
  (20 other events, 61.0 us)
where the time goes:
time: 303 us; the launch traced here: 299 us
  waiting for transfers between devices  110 us (36%)
  starting transfers between devices  51.2 us (17%)
  blocking collectives  41.9 us (14%)
  local copies, waits for them, and re-layouts  38.3 us (13%)
  matrix products  36.3 us (12%)
  other arithmetic  20.1 us (7%)
    psum x1, blocking collectives, local(): gain_total = lax.psum(gain_part, ('tm', 'ulysses', 'dp'))  41.9 us
    ppermute x2, waiting for transfers between devices, from_behind(): lax.ppermute(value, axis, [(source, source + steps) for source in range(i...  30.1 us
    all_to_all x1, waiting for transfers between devices, local(): lax.all_to_all(queries[0], 'ulysses', split_axis=1, concat_axis=0, tiled=...  14.9 us
    all_to_all x1, waiting for transfers between devices, local(): lax.all_to_all(values[0], 'ulysses', split_axis=1, concat_axis=0, tiled=T...  14.3 us
    all_to_all x1, waiting for transfers between devices, local(): lax.all_to_all(attn_out[0], 'ulysses', split_axis=1, concat_axis=0, tiled...  14.1 us
    dot_general x2, matrix products, tile_grads(): jnp.einsum('qhd,khd->hqk', grad_tile, value_rows, preferred_element_type=...  13.5 us
    all_to_all x1, waiting for transfers between devices, local(): lax.all_to_all(keys[0], 'ulysses', split_axis=1, concat_axis=0, tiled=True)  12.8 us
    all_to_all x1, waiting for transfers between devices, local(): lax.all_to_all(grad_value, 'ulysses', split_axis=0, concat_axis=1, tiled=...  10.9 us
  transfers between devices with their start and end apart: 12, of which 9 were waited for; matrix products, arithmetic and copies ran while one was open for 14% of the time, Pallas kernels for 0%

commit v1 on v0

v1 whole, which is shorter than its diff:
```python
import functools
import math

import jax
import jax.numpy as jnp
from jax import lax
from jax.experimental import pallas as pl
from jax.experimental.pallas import tpu as pltpu
from jax.sharding import PartitionSpec as P

HD = 128
LANES = 128
TILE_ROWS = 16
QUERY_BLOCK = 256
KEY_BLOCK = 256
VMEM_LIMIT = 48 * 1024 * 1024
SCALE = 1.0 / math.sqrt(HD)
SCALE_LOG2 = SCALE / math.log(2.0)


def params():
    return pltpu.CompilerParams(vmem_limit_bytes=VMEM_LIMIT)


def head_columns(head):
    return slice(head * HD, (head + 1) * HD)


def pack_pairs_kernel(first_ref, second_ref, out_ref):
    rows, width = first_ref.shape
    for head in range(width // HD):
        start = 2 * head * rows
        out_ref[0, start : start + rows] = first_ref[:, head_columns(head)]
        out_ref[0, start + rows : start + 2 * rows] = second_ref[:, head_columns(head)]


def pack_pairs(first, second, parts):
    rows, channels = first.shape
    width = channels // parts
    depth = 2 * rows * (width // HD)
    piece = pl.BlockSpec((rows, width), lambda part: (0, part))
    return pl.pallas_call(
        pack_pairs_kernel,
        grid=(parts,),
        in_specs=[piece, piece],
        out_specs=pl.BlockSpec((1, depth, HD), lambda part: (part, 0, 0)),
        out_shape=jax.ShapeDtypeStruct((parts, depth, HD), first.dtype),
        compiler_params=params(),
        cost_estimate=pl.CostEstimate(flops=0, bytes_accessed=8 * rows * channels, transcendentals=0),
    )(first, second)


def dot_groups(rows):
    return -(-rows // LANES)


def dots_rows(rows, heads):
    group = -(-2 * heads // TILE_ROWS) * TILE_ROWS
    return group, group * dot_groups(rows)


def pack_queries_kernel(query_ref, out_grad_ref, attn_ref, gain_ref, out_ref, gain_part_ref):
    rows, width = query_ref.shape
    heads = width // HD
    out_grad = out_grad_ref[...].astype(jnp.float32)
    attn = attn_ref[...].astype(jnp.float32)
    grad = (out_grad * gain_ref[...]).astype(jnp.bfloat16)
    gain_part_ref[...] = jnp.sum(out_grad * attn, axis=0, keepdims=True)
    product = grad.astype(jnp.float32) * attn
    group, _ = dots_rows(rows, heads)
    base = 2 * heads * rows
    dots = []
    for head in range(heads):
        start = 2 * head * rows
        out_ref[0, start : start + rows] = query_ref[:, head_columns(head)]
        out_ref[0, start + rows : start + 2 * rows] = grad[:, head_columns(head)]
        dots.append(jnp.sum(jnp.transpose(product[:, head_columns(head)]), axis=0, keepdims=True))
    for index in range(dot_groups(rows)):
        first, last = index * LANES, min(rows, (index + 1) * LANES)
        terms = []
        for head in range(heads):
            value = dots[head][:, first:last]
            if last - first < LANES:
                value = jnp.concatenate([value, jnp.zeros((1, LANES - last + first), jnp.float32)], axis=1)
            high = value.astype(jnp.bfloat16).astype(jnp.float32)
            terms += [high, value - high]
        terms.append(jnp.zeros((group - 2 * heads, LANES), jnp.float32))
        out_ref[0, base + index * group : base + (index + 1) * group] = jnp.concatenate(terms, axis=0).astype(
            jnp.bfloat16
        )


def pack_queries(queries, out_grad, attn_out, out_gain, parts):
    rows, channels = queries.shape
    width = channels // parts
    heads = width // HD
    depth = 2 * rows * heads + dots_rows(rows, heads)[1]
    piece = pl.BlockSpec((rows, width), lambda part: (0, part))
    line = pl.BlockSpec((1, width), lambda part: (0, part))
    return pl.pallas_call(
        pack_queries_kernel,
        grid=(parts,),
        in_specs=[piece, piece, piece, line],
        out_specs=[pl.BlockSpec((1, depth, HD), lambda part: (part, 0, 0)), line],
        out_shape=[
            jax.ShapeDtypeStruct((parts, depth, HD), jnp.bfloat16),
            jax.ShapeDtypeStruct((1, channels), jnp.float32),
        ],
        compiler_params=params(),
        cost_estimate=pl.CostEstimate(
            flops=8 * rows * channels, bytes_accessed=10 * rows * channels, transcendentals=0
        ),
    )(queries, out_grad, attn_out, out_gain.reshape(1, channels))


def attention_kernel(sources, masked, head, *refs):
    flags_ref = None
    if masked:
        flags_ref, refs = refs[0], refs[1:]
    query_ref, grad_ref, dots_ref = refs[:3]
    key_refs = refs[3 : 3 + 2 * sources : 2]
    value_refs = refs[4 : 4 + 2 * sources : 2]
    outs = refs[3 + 2 * sources :]
    query_grad_ref, own_ref = outs[0], outs[1]
    side_refs = outs[2 : 1 + sources]
    score_ref, key_acc, value_acc = outs[1 + sources :]
    parts, rows, _ = query_ref.shape
    slab = parts * rows
    queries = query_ref[...].reshape(slab, HD)
    grads = grad_ref[...].reshape(slab, HD)
    groups = dot_groups(rows)
    group = dots_ref.shape[1] // groups
    pieces = []
    for part in range(parts):
        for index in range(groups):
            count = min(LANES, rows - index * LANES)
            pair = dots_ref[part, index * group : (index + 1) * group].astype(jnp.float32)
            line = 2 * head
            pieces.append((pair[line : line + 1] + pair[line + 1 : line + 2])[:, :count])
    dots = jnp.concatenate(pieces, axis=1)
    keys = [ref[...].reshape(slab, HD) for ref in key_refs]
    values = [ref[...].reshape(slab, HD) for ref in value_refs]
    blocks = [(source, first) for source in range(sources) for first in range(0, slab, KEY_BLOCK)]
    query_grads = []
    for query_first in range(0, slab, QUERY_BLOCK):
        span = slice(query_first, query_first + QUERY_BLOCK)
        query_block, grad_block = queries[span], grads[span]
        query_flip, grad_flip = jnp.transpose(query_block), jnp.transpose(grad_block)
        dots_block = dots[:, span]
        top = None
        for source, first in blocks:
            scores = jnp.dot(
                keys[source][first : first + KEY_BLOCK], query_flip, preferred_element_type=jnp.float32
            )
            if masked and source > 0:
                scores = jnp.where(flags_ref[source - 1] > 0, scores, -jnp.inf)
            place = source * slab + first
            score_ref[place : place + KEY_BLOCK] = scores
            part_top = jnp.max(scores.reshape(-1, 8, QUERY_BLOCK), axis=0)
            top = part_top if top is None else jnp.maximum(top, part_top)
        top = jnp.max(top, axis=0, keepdims=True) * SCALE_LOG2
        total = None
        for source, first in blocks:
            place = source * slab + first
            powers = jnp.exp2(score_ref[place : place + KEY_BLOCK] * SCALE_LOG2 - top)
            score_ref[place : place + KEY_BLOCK] = powers
            part_total = jnp.sum(powers.reshape(-1, 8, QUERY_BLOCK), axis=0)
            total = part_total if total is None else total + part_total
        inverse = 1.0 / jnp.sum(total, axis=0, keepdims=True)
        query_acc = None
        for source, first in blocks:
            place = source * slab + first
            stretch = slice(first, first + KEY_BLOCK)
            weights = score_ref[place : place + KEY_BLOCK] * inverse
            grad_weights = jnp.dot(values[source][stretch], grad_flip, preferred_element_type=jnp.float32)
            grad_scores = (weights * (grad_weights - dots_block)).astype(jnp.bfloat16)
            value_part = jnp.dot(weights.astype(jnp.bfloat16), grad_block, preferred_element_type=jnp.float32)
            key_part = jnp.dot(grad_scores, query_block, preferred_element_type=jnp.float32)
            query_part = lax.dot_general(
                grad_scores,
                keys[source][stretch],
                (((0,), (0,)), ((), ())),
                preferred_element_type=jnp.float32,
            )
            query_acc = query_part if query_acc is None else query_acc + query_part
            if query_first == 0:
                key_acc[place : place + KEY_BLOCK] = key_part
                value_acc[place : place + KEY_BLOCK] = value_part
            else:
                key_acc[place : place + KEY_BLOCK] += key_part
                value_acc[place : place + KEY_BLOCK] += value_part
        query_grads.append((query_acc * SCALE).astype(jnp.bfloat16))
    query_grad_ref[...] = jnp.concatenate(query_grads, axis=0).reshape(parts, rows, HD)
    for source in range(sources):
        out_ref = own_ref if source == 0 else side_refs[source - 1]
        span = slice(source * slab, (source + 1) * slab)
        out_ref[:, :rows] = (key_acc[span] * SCALE).astype(out_ref.dtype).reshape(parts, rows, HD)
        out_ref[:, rows:] = value_acc[span].astype(out_ref.dtype).reshape(parts, rows, HD)


def attention(head, heads, packed_queries, packed_pairs, flags):
    parts, depth, _ = packed_pairs[0].shape
    sources = len(packed_pairs)
    masked = flags is not None
    packed_depth = packed_queries.shape[1]
    dots_depth = packed_depth - depth
    rows = depth // (2 * heads)
    slab = parts * rows

    def block(index):
        return pl.BlockSpec((parts, rows, HD), lambda step: (0, index, 0))

    in_specs = [block(2 * head), block(2 * head + 1)]
    in_specs.append(pl.BlockSpec((parts, dots_depth, HD), lambda step: (0, depth // dots_depth, 0)))
    operands = [packed_queries, packed_queries, packed_queries]
    for pairs in packed_pairs:
        in_specs += [block(2 * head), block(2 * head + 1)]
        operands += [pairs, pairs]
    if masked:
        in_specs = [pl.BlockSpec(memory_space=pltpu.SMEM)] + in_specs
        operands = [flags] + operands
    whole = pl.BlockSpec((parts, rows, HD), lambda step: (0, 0, 0))
    double = pl.BlockSpec((parts, 2 * rows, HD), lambda step: (0, 0, 0))
    shape = (parts, 2 * rows, HD)
    pairs_of = slab * sources * slab
    return pl.pallas_call(
        functools.partial(attention_kernel, sources, masked, head),
        grid=(1,),
        in_specs=in_specs,
        out_specs=[whole] + [double] * sources,
        out_shape=[
            jax.ShapeDtypeStruct((parts, rows, HD), jnp.bfloat16),
            jax.ShapeDtypeStruct(shape, jnp.float32),
        ]
        + [jax.ShapeDtypeStruct(shape, jnp.bfloat16)] * (sources - 1),
        scratch_shapes=[
            pltpu.VMEM((sources * slab, QUERY_BLOCK), jnp.float32),
            pltpu.VMEM((sources * slab, HD), jnp.float32),
            pltpu.VMEM((sources * slab, HD), jnp.float32),
        ],
        compiler_params=params(),
        cost_estimate=pl.CostEstimate(
            flops=10 * pairs_of * HD, bytes_accessed=slab * HD * 2 * (4 + 6 * sources), transcendentals=pairs_of
        ),
    )(*operands)


def exchange(value):
    return lax.all_to_all(value, "ulysses", split_axis=0, concat_axis=0, tiled=True)


def neighbours(size):
    if size == 1:
        return []
    if size == 2:
        swap = [(0, 1), (1, 0)]
        return [(swap, swap)]
    up = [(index, index + 1) for index in range(size - 1)]
    down = [(index + 1, index) for index in range(size - 1)]
    return [(up, down), (down, up)]


def unpack(received, heads):
    parts, depth, _ = received.shape
    rows = depth // heads
    laid = received.reshape(parts, heads, rows, HD)
    return jnp.transpose(laid, (2, 0, 1, 3)).reshape(1, rows, parts * heads * HD)


def local(queries, keys, values, attn_out, out_grad, out_gain):
    parts = lax.axis_size("ulysses")
    span = lax.axis_size("tm")
    rows, channels = queries.shape[1:]
    heads = channels // (parts * HD)
    sides = neighbours(span)
    pairs_sent = pack_pairs(keys[0], values[0], parts)
    queries_sent, gain_part = pack_queries(queries[0], out_grad[0], attn_out[0], out_gain, parts)
    pairs = exchange(pairs_sent)
    packed_queries = exchange(queries_sent)
    side_pairs = [lax.ppermute(pairs, "tm", there) for there, _ in sides]
    gain_all = lax.all_gather(gain_part, ("tm", "ulysses", "dp"), axis=0, tiled=True)
    token_count = rows * span * parts * lax.axis_size("dp")
    gain_grad = jnp.sum(gain_all, axis=0) / token_count
    flags = None
    if len(sides) > 1:
        position = lax.axis_index("tm")
        flags = jnp.stack([position > 0, position < span - 1]).astype(jnp.int32)
    query_grads, pair_grads = [], []
    for head in range(heads):
        query_grad, own, *others = attention(head, heads, packed_queries, [pairs] + side_pairs, flags)
        query_grads.append(query_grad)
        total = own
        for other, (_, back) in zip(others, sides):
            total = total + lax.ppermute(other, "tm", back).astype(jnp.float32)
        pair_grads.append(total.astype(jnp.bfloat16))
    token_query = unpack(exchange(jnp.concatenate(query_grads, axis=1)), heads)
    received = exchange(jnp.concatenate(pair_grads, axis=1)).reshape(parts, heads, 2, rows, HD)
    token_key = unpack(received[:, :, 0].reshape(parts, heads * rows, HD), heads)
    token_value = unpack(received[:, :, 1].reshape(parts, heads * rows, HD), heads)
    return (token_query, token_key, token_value, gain_grad)


def solution(mesh):
    split = P("dp", ("tm", "ulysses"), None)
    return jax.shard_map(
        local,
        mesh=mesh,
        in_specs=(split,) * 5 + (P(),),
        out_specs=(split,) * 3 + (P(),),
        check_vma=False,
    )
```

time: 303 us -> 184 us (0.61); the launches traced: 299 us -> 183 us
  waiting for transfers between devices: 110 us -> 64.5 us
  matrix products: 36.3 us -> 0 us
  starting transfers between devices: 51.2 us -> 22.2 us
  local copies, waits for them, and re-layouts: 38.3 us -> 10.3 us
  Pallas kernels: 0 us -> 25.9 us
  other arithmetic: 20.1 us -> 5.04 us
  blocking collectives: 41.9 us -> 54.8 us
    all_gather x0 -> x1, blocking collectives: none -> 54.8 us  [local(): lax.all_gather(gain_part, ('tm', 'ulysses', 'dp'), axis=0, tiled=True)]
    psum x1 -> x0, blocking collectives: 41.9 us -> none  [local(): gain_total = lax.psum(gain_part, ('tm', 'ulysses', 'dp'))]
    ppermute x4, waiting for transfers between devices: 40.7 us -> 1.49 us  [the longest x3 1.49 us: local(): total = total + lax.ppermute(other, 'tm', back).astype(jnp.float32)]
    dot_general x10 -> x0, matrix products: 36.3 us -> none  [the longest x2 13.5 us: tile_grads(): jnp.einsum('qhd,khd->hqk', grad_tile, value_rows, preferred_element_type=...]
    pallas_call x0 -> x5, Pallas kernels: none -> 25.9 us  [the longest x3 23 us: attention(): pl.pallas_call(functools.partial(attention_kernel, sources, masked, head)...]
    all_to_all x8 -> x4, starting transfers between devices: 33.9 us -> 17.1 us  [exchange(): lax.all_to_all(value, 'ulysses', split_axis=0, concat_axis=0, tiled=True)]
    ppermute x4, starting transfers between devices: 17.4 us -> 5.05 us  [the longest x3 3.5 us: local(): total = total + lax.ppermute(other, 'tm', back).astype(jnp.float32)]
    all_to_all x13 -> x0, local copies, waits for them, and re-layouts: 12.1 us -> none  [the longest x2 2.55 us: local(): lax.all_to_all(values[0], 'ulysses', split_axis=1, concat_axis=0, tiled=T...]
  transfers between devices with their start and end apart: 12 -> 8, of which waited for: 9 -> 4; matrix products, arithmetic and copies ran while one was open for 14% -> 4% of each run, Pallas kernels for 0% -> 9%
where the time goes in v1:
time: 184 us; the launch traced here: 183 us
  waiting for transfers between devices  64.5 us (35%)
  blocking collectives  54.8 us (30%)
  Pallas kernels  25.9 us (14%)
  starting transfers between devices  22.2 us (12%)
  local copies, waits for them, and re-layouts  10.3 us (6%)
  other arithmetic  5.04 us (3%)
    all_to_all x4, waiting for transfers between devices, exchange(): lax.all_to_all(value, 'ulysses', split_axis=0, concat_axis=0, tiled=True)  63 us
    all_gather x1, blocking collectives, local(): lax.all_gather(gain_part, ('tm', 'ulysses', 'dp'), axis=0, tiled=True)  54.8 us
    pallas_call x3, Pallas kernels, attention(): pl.pallas_call(functools.partial(attention_kernel, sources, masked, head)...  23 us
    all_to_all x4, starting transfers between devices, exchange(): lax.all_to_all(value, 'ulysses', split_axis=0, concat_axis=0, tiled=True)  17.1 us
    unnamed x22, local copies, waits for them, and re-layouts  4.95 us
    reshape x3, local copies, waits for them, and re-layouts, unpack(): jnp.transpose(laid, (2, 0, 1, 3)).reshape(1, rows, parts * heads * HD)  3.74 us
  transfers between devices with their start and end apart: 8, of which 4 were waited for; matrix products, arithmetic and copies ran while one was open for 4% of the time, Pallas kernels for 9%

profile of v1, /device:TPU:0, one launch (start us, length us, event | category | flops | bytes accessed | tf_op | source)
XLA Modules:
  0.0 183.5 jit_solution(5072642980840052385)
XLA Ops:
  1.7 1.1 copy-done.6
  2.8 1.8 shard_map.94
  4.5 6.5 %all-to-all-start.1 = ((bf16[4,1152,128]{2,1,0:T(8,128)(2,1)}), bf16[4,1152,128]{2,1,0:T(8,128)(2,1)S(1)}, u32[]{:S(2)}, u32[]{:S(2)}) async-start(bf16[4,1152,128]{2,1,0:T(8,128)(2,1)} %shard_map.94), calls=%async_computation.1 | async-start | bytes 2359296 | tf_op jit(solution)/shard_map/all_to_all | solution.py:249
  11.0 1.1 shard_map.93
  13.2 26.3 %all-to-all-done.1.refs_3_.refs_4_ = bf16[4,1152,128]{2,1,0:T(8,128)(2,1)S(1)} async-done(((bf16[4,1152,128]{2,1,0:T(8,128)(2,1)}), bf16[4,1152,128]{2,1,0:T(8,128)(2,1)S(1)}, u32[]{:S(2)}, u32[]{:S(2)}) %all-to-all-start.1) | async-done | bytes 1179680 | tf_op jit(solution)/shard_map/all_to_all | solution.py:249
  39.5 3.5 %all-to-all-start = ((bf16[4,1184,128]{2,1,0:T(8,128)(2,1)}), bf16[4,1184,128]{2,1,0:T(8,128)(2,1)S(1)}, u32[]{:S(2)}, u32[]{:S(2)}) async-start(bf16[4,1184,128]{2,1,0:T(8,128)(2,1)} %copy-done), calls=%async_computation | async-start | bytes 2424832 | tf_op jit(solution)/shard_map/all_to_all | solution.py:249
  43.1 1.6 collective-permute-start
  44.6 27.2 %all-to-all-done.refs_0_.refs_1_.refs_2_ = bf16[4,1184,128]{2,1,0:T(8,128)(2,1)S(1)} async-done(((bf16[4,1184,128]{2,1,0:T(8,128)(2,1)}), bf16[4,1184,128]{2,1,0:T(8,128)(2,1)S(1)}, u32[]{:S(2)}, u32[]{:S(2)}) %all-to-all-start) | async-done | bytes 1212448 | tf_op jit(solution)/shard_map/all_to_all | solution.py:249
  71.8 7.6 %shard_map.95 = (bf16[4,192,128]{2,1,0:T(8,128)(2,1)S(1)}, f32[4,384,128]{2,1,0:T(8,128)S(1)}, bf16[4,384,128]{2,1,0:T(8,128)(2,1)}) custom-call(bf16[4,1184,128]{2,1,0:T(8,128)(2,1)S(1)} %all-to-all-done.refs_0_.refs_1_.refs_2_, bf16[4,1184,128]{2,1,0:T(8,128)(2,1)S(1)} %all-to-all-done.refs_0_.refs_1_.refs_2_, ...), custom_call_target="tpu_custom_call" | custom-call | flops 1509949440 | bytes 3145728 | tf_op jit(solution)/shard_map/pallas_call | solution.py:226
  79.4 1.5 collective-permute-start.1
  80.9 7.6 %shard_map.96 = (bf16[4,192,128]{2,1,0:T(8,128)(2,1)S(1)}, f32[4,384,128]{2,1,0:T(8,128)S(1)}, bf16[4,384,128]{2,1,0:T(8,128)(2,1)}) custom-call(bf16[4,1184,128]{2,1,0:T(8,128)(2,1)S(1)} %all-to-all-done.refs_0_.refs_1_.refs_2_, bf16[4,1184,128]{2,1,0:T(8,128)(2,1)S(1)} %all-to-all-done.refs_0_.refs_1_.refs_2_, ...), custom_call_target="tpu_custom_call" | custom-call | flops 1509949440 | bytes 3145728 | tf_op jit(solution)/shard_map/pallas_call | solution.py:226
  89.9 7.8 %shard_map.97 = (bf16[4,192,128]{2,1,0:T(8,128)(2,1)S(1)}, f32[4,384,128]{2,1,0:T(8,128)S(1)}, bf16[4,384,128]{2,1,0:T(8,128)(2,1)}) custom-call(bf16[4,1184,128]{2,1,0:T(8,128)(2,1)S(1)} %all-to-all-done.refs_0_.refs_1_.refs_2_, bf16[4,1184,128]{2,1,0:T(8,128)(2,1)S(1)} %all-to-all-done.refs_0_.refs_1_.refs_2_, ...), custom_call_target="tpu_custom_call" | custom-call | flops 1509949440 | bytes 3145728 | tf_op jit(solution)/shard_map/pallas_call | solution.py:226
  98.6 1.5 collective-permute-start.3
  100.9 3.6 %all-to-all-start.2 = ((bf16[4,576,128]{2,1,0:T(8,128)(2,1)}), bf16[4,576,128]{2,1,0:T(8,128)(2,1)S(1)}, u32[]{:S(2)}, u32[]{:S(2)}) async-start(bf16[4,576,128]{2,1,0:T(8,128)(2,1)} %pad_maximum_fusion.1), calls=%async_computation.2 | async-start | bytes 1179648 | tf_op jit(solution)/shard_map/all_to_all | solution.py:249
  104.6 1.1 add_convert_fusion.2
  105.7 1.2 add_convert_fusion.1
  106.9 1.5 collective-permute-done.3
  108.4 1.1 pad_maximum_fusion
  109.6 9.5 %all-to-all-done.2 = bf16[4,576,128]{2,1,0:T(8,128)(2,1)S(1)} async-done(((bf16[4,576,128]{2,1,0:T(8,128)(2,1)}), bf16[4,576,128]{2,1,0:T(8,128)(2,1)S(1)}, u32[]{:S(2)}, u32[]{:S(2)}) %all-to-all-start.2) | async-done | bytes 589856 | tf_op jit(solution)/shard_map/all_to_all | solution.py:249
  119.1 3.5 %all-to-all-start.3 = ((bf16[4,1152,128]{2,1,0:T(8,128)(2,1)}), bf16[4,1152,128]{2,1,0:T(8,128)(2,1)S(1)}, u32[]{:S(2)}, u32[]{:S(2)}) async-start(bf16[4,1152,128]{2,1,0:T(8,128)(2,1)} %pad_maximum_fusion), calls=%async_computation.3 | async-start | bytes 2359296 | tf_op jit(solution)/shard_map/all_to_all | solution.py:249
  122.6 54.8 %all-gather = f32[32,1,1536]{2,1,0:T(1,128)S(1)} all-gather(f32[1,1,1536]{2,1,0:T(1,128)S(1)} %bitcast.24), channel_id=1, replica_groups=mesh['tm'=2,'ulysses'=4,'dp'=4] {'tm','ulysses','dp'}, dimensions={0}, use_global_device_ids=true | all-gather | bytes 202752 | tf_op jit(solution)/shard_map/all_gather | solution.py:281
  178.6 1.3 reshape.28
  181.0 1.3 reshape.30
  182.2 1.2 reshape.31
  (34 shorter events, 7.7 us)
Async XLA Ops:
  0.6 1.1 copy-start.5
  1.7 1.1 copy-start.6
  4.5 6.5 %copy-start.10 = (f32[1536]{0:T(1024)S(1)}, f32[1536]{0:T(1024)}, u32[]{:S(2)}) copy-start(f32[1536]{0:T(1024)} %param.11) | copy-start | bytes 18436
  4.5 6.5 %copy-start.7 = (bf16[1,192,1536]{2,1,0:T(8,128)(2,1)S(1)}, bf16[1,192,1536]{2,1,0:T(8,128)(2,1)}, u32[]{:S(2)}) copy-start(bf16[1,192,1536]{2,1,0:T(8,128)(2,1)} %param.6) | copy-start | bytes 1769476
  4.5 6.5 %copy-start.8 = (bf16[1,192,1536]{2,1,0:T(8,128)(2,1)S(1)}, bf16[1,192,1536]{2,1,0:T(8,128)(2,1)}, u32[]{:S(2)}) copy-start(bf16[1,192,1536]{2,1,0:T(8,128)(2,1)} %param.10) | copy-start | bytes 1769476
  4.5 6.5 %copy-start.9 = (bf16[1,192,1536]{2,1,0:T(8,128)(2,1)S(1)}, bf16[1,192,1536]{2,1,0:T(8,128)(2,1)}, u32[]{:S(2)}) copy-start(bf16[1,192,1536]{2,1,0:T(8,128)(2,1)} %param.9) | copy-start | bytes 1769476
  4.5 35.0 %all-to-all-start.1 = ((bf16[4,1152,128]{2,1,0:T(8,128)(2,1)}), bf16[4,1152,128]{2,1,0:T(8,128)(2,1)S(1)}, u32[]{:S(2)}, u32[]{:S(2)}) async-start(bf16[4,1152,128]{2,1,0:T(8,128)(2,1)} %shard_map.94), calls=%async_computation.1 | async-start | bytes 2359296 | tf_op jit(solution)/shard_map/all_to_all | solution.py:249
  12.2 1.0 copy-start
  39.5 32.2 %all-to-all-start = ((bf16[4,1184,128]{2,1,0:T(8,128)(2,1)}), bf16[4,1184,128]{2,1,0:T(8,128)(2,1)S(1)}, u32[]{:S(2)}, u32[]{:S(2)}) async-start(bf16[4,1184,128]{2,1,0:T(8,128)(2,1)} %copy-done), calls=%async_computation | async-start | bytes 2424832 | tf_op jit(solution)/shard_map/all_to_all | solution.py:249
  43.1 28.7 %collective-permute-start = (bf16[4,1152,128]{2,1,0:T(8,128)(2,1)S(1)}, bf16[4,1152,128]{2,1,0:T(8,128)(2,1)}, u32[]{:S(2)}, u32[]{:S(2)}) collective-permute-start(bf16[4,1152,128]{2,1,0:T(8,128)(2,1)S(1)} %all-to-all-done.1.refs_3_.refs_4_), channel_id=1, source_target_pairs={{0,16},{16,0},{1,17},{17,1},{2,18},{18,2},{3,19},{19,3},{4,20},{20... | collective-permute-start | bytes 3538952 | tf_op jit(solution)/shard_map/ppermute | solution.py:280
  79.4 25.2 %collective-permute-start.1 = (bf16[4,384,128]{2,1,0:T(8,128)(2,1)}, bf16[4,384,128]{2,1,0:T(8,128)(2,1)}, u32[]{:S(2)}, u32[]{:S(2)}) collective-permute-start(bf16[4,384,128]{2,1,0:T(8,128)(2,1)} %get-tuple-element.20), channel_id=1, source_target_pairs={{0,16},{16,0},{1,17},{17,1},{2,18},{18,2},{3,19},{19,3},{4,20},{20... | collective-permute-start | bytes 1179656 | tf_op jit(solution)/shard_map/ppermute | solution.py:294
  88.5 0.9 copy-start.1
  89.4 16.3 %collective-permute-start.2 = (bf16[4,384,128]{2,1,0:T(8,128)(2,1)}, bf16[4,384,128]{2,1,0:T(8,128)(2,1)}, u32[]{:S(2)}, u32[]{:S(2)}) collective-permute-start(bf16[4,384,128]{2,1,0:T(8,128)(2,1)} %get-tuple-element.22), channel_id=1, source_target_pairs={{0,16},{16,0},{1,17},{17,1},{2,18},{18,2},{3,19},{19,3},{4,20},{20... | collective-permute-start | bytes 1179656 | tf_op jit(solution)/shard_map/ppermute | solution.py:294
  97.7 0.9 copy-start.3
  98.6 9.7 %collective-permute-start.3 = (bf16[4,384,128]{2,1,0:T(8,128)(2,1)}, bf16[4,384,128]{2,1,0:T(8,128)(2,1)S(1)}, u32[]{:S(2)}, u32[]{:S(2)}) collective-permute-start(bf16[4,384,128]{2,1,0:T(8,128)(2,1)} %get-tuple-element.24), channel_id=1, source_target_pairs={{0,16},{16,0},{1,17},{17,1},{2,18},{18,2},{3,19},{19,3},{4,20},{20... | collective-permute-start | bytes 1179656 | tf_op jit(solution)/shard_map/ppermute | solution.py:294
  100.9 4.7 %copy-start.2 = (f32[4,384,128]{2,1,0:T(8,128)S(1)}, f32[4,384,128]{2,1,0:T(8,128)}, u32[]{:S(2)}) copy-start(f32[4,384,128]{2,1,0:T(8,128)} %copy-done.1) | copy-start | bytes 2359300
  100.9 18.1 %all-to-all-start.2 = ((bf16[4,576,128]{2,1,0:T(8,128)(2,1)}), bf16[4,576,128]{2,1,0:T(8,128)(2,1)S(1)}, u32[]{:S(2)}, u32[]{:S(2)}) async-start(bf16[4,576,128]{2,1,0:T(8,128)(2,1)} %pad_maximum_fusion.1), calls=%async_computation.2 | async-start | bytes 1179648 | tf_op jit(solution)/shard_map/all_to_all | solution.py:249
  105.7 2.7 %copy-start.4 = (f32[4,384,128]{2,1,0:T(8,128)S(1)}, f32[4,384,128]{2,1,0:T(8,128)}, u32[]{:S(2)}) copy-start(f32[4,384,128]{2,1,0:T(8,128)} %copy-done.3) | copy-start | bytes 2359300
  119.1 60.8 %all-to-all-start.3 = ((bf16[4,1152,128]{2,1,0:T(8,128)(2,1)}), bf16[4,1152,128]{2,1,0:T(8,128)(2,1)S(1)}, u32[]{:S(2)}, u32[]{:S(2)}) async-start(bf16[4,1152,128]{2,1,0:T(8,128)(2,1)} %pad_maximum_fusion), calls=%async_computation.3 | async-start | bytes 2359296 | tf_op jit(solution)/shard_map/all_to_all | solution.py:249

commit v2 on v1

v2 whole, which is shorter than its diff:
```python
import functools
import math

import jax
import jax.numpy as jnp
from jax import lax
from jax.experimental import pallas as pl
from jax.experimental.pallas import tpu as pltpu
from jax.sharding import PartitionSpec as P

HD = 128
LANES = 128
TILE_ROWS = 16
QUERY_BLOCK = 256
KEY_BLOCK = 256
VMEM_LIMIT = 48 * 1024 * 1024
SCALE = 1.0 / math.sqrt(HD)
SCALE_LOG2 = SCALE / math.log(2.0)


def params():
    return pltpu.CompilerParams(vmem_limit_bytes=VMEM_LIMIT)


def partner(distance):
    return lax.axis_index("ulysses") ^ distance


def column_of(distance, heads, head):
    return pl.multiple_of((partner(distance) * heads + head) * HD, HD)


def run_copies(pairs, semaphores):
    copies = [
        pltpu.make_async_copy(source, target, semaphores.at[index]) for index, (source, target) in enumerate(pairs)
    ]
    for copy in copies:
        copy.start()
    for copy in copies:
        copy.wait()


def pack_pairs_kernel(parts, key_ref, value_ref, *refs):
    pieces, semaphores = refs[:parts], refs[parts]
    rows, channels = key_ref.shape
    heads = channels // (parts * HD)
    pairs = []
    for distance in range(parts):
        for head in range(heads):
            columns = pl.ds(column_of(distance, heads, head), HD)
            for half, ref in enumerate((key_ref, value_ref)):
                start = (2 * head + half) * rows
                pairs.append((ref.at[:, columns], pieces[distance].at[start : start + rows]))
    run_copies(pairs, semaphores)


def pack_pairs(keys, values, parts):
    rows, channels = keys.shape
    heads = channels // (parts * HD)
    whole = pl.BlockSpec(memory_space=pl.ANY)
    return pl.pallas_call(
        functools.partial(pack_pairs_kernel, parts),
        in_specs=[whole, whole],
        out_specs=[whole] * parts,
        out_shape=[jax.ShapeDtypeStruct((2 * heads * rows, HD), keys.dtype)] * parts,
        scratch_shapes=[pltpu.SemaphoreType.DMA((2 * heads * parts,))],
        compiler_params=params(),
        cost_estimate=pl.CostEstimate(flops=0, bytes_accessed=8 * rows * channels, transcendentals=0),
    )(keys, values)


def dot_groups(rows):
    return -(-rows // LANES)


def dots_depth(rows):
    return -(-2 * dot_groups(rows) // TILE_ROWS) * TILE_ROWS


def pack_queries_kernel(parts, groups, query_ref, out_grad_ref, attn_ref, gain_ref, *refs):
    gain_part_ref = refs[-1]
    rows, channels = query_ref.shape
    heads = channels // (parts * HD)
    depth = 2 * rows + dots_depth(rows)
    for number, group in enumerate(groups):
        for distance in range(parts):
            piece = refs[number * parts + distance]
            for place, head in enumerate(group):
                columns = pl.ds(column_of(distance, heads, head), HD)
                out_grad = out_grad_ref[:, columns].astype(jnp.float32)
                attn = attn_ref[:, columns].astype(jnp.float32)
                grad = (out_grad * gain_ref[:, columns]).astype(jnp.bfloat16)
                gain_part_ref[:, columns] = jnp.sum(out_grad * attn, axis=0, keepdims=True)
                base = place * depth
                piece[base : base + rows] = query_ref[:, columns]
                piece[base + rows : base + 2 * rows] = grad
                dots = jnp.sum(jnp.transpose(grad.astype(jnp.float32) * attn), axis=0, keepdims=True)
                terms = []
                for first in range(0, rows, LANES):
                    value = dots[:, first : first + LANES]
                    if value.shape[1] < LANES:
                        rest = jnp.zeros((1, LANES - value.shape[1]), jnp.float32)
                        value = jnp.concatenate([value, rest], axis=1)
                    high = value.astype(jnp.bfloat16).astype(jnp.float32)
                    terms += [high, value - high]
                terms.append(jnp.zeros((dots_depth(rows) - len(terms), LANES), jnp.float32))
                piece[base + 2 * rows : base + depth] = jnp.concatenate(terms, axis=0).astype(jnp.bfloat16)


def pack_queries(queries, out_grad, attn_out, out_gain, parts, groups):
    rows, channels = queries.shape
    depth = 2 * rows + dots_depth(rows)
    out_shape = [
        jax.ShapeDtypeStruct((depth * len(group), HD), jnp.bfloat16) for group in groups for _ in range(parts)
    ]
    *pieces, gain_part = pl.pallas_call(
        functools.partial(pack_queries_kernel, parts, groups),
        out_shape=out_shape + [jax.ShapeDtypeStruct((1, channels), jnp.float32)],
        compiler_params=params(),
        cost_estimate=pl.CostEstimate(
            flops=8 * rows * channels, bytes_accessed=10 * rows * channels, transcendentals=0
        ),
    )(queries, out_grad, attn_out, out_gain.reshape(1, channels))
    return [pieces[number * parts : (number + 1) * parts] for number in range(len(groups))], gain_part


def attention_kernel(parts, sources, masked, rows, *refs):
    flags_ref = None
    if masked:
        flags_ref, refs = refs[0], refs[1:]
    query_refs, refs = refs[:parts], refs[parts:]
    pair_refs, refs = refs[: parts * sources], refs[parts * sources :]
    query_grad_refs, own_ref = refs[:parts], refs[parts]
    side_refs = refs[parts + 1 : parts + sources]
    score_ref, key_acc, value_acc = refs[parts + sources :]
    slab = parts * rows
    queries = jnp.concatenate([ref[:rows] for ref in query_refs], axis=0)
    grads = jnp.concatenate([ref[rows : 2 * rows] for ref in query_refs], axis=0)
    lines = []
    for ref in query_refs:
        terms = ref[2 * rows : 2 * rows + dots_depth(rows)].astype(jnp.float32)
        for index in range(dot_groups(rows)):
            count = min(LANES, rows - index * LANES)
            lines.append((terms[2 * index : 2 * index + 1] + terms[2 * index + 1 : 2 * index + 2])[:, :count])
    dots = jnp.concatenate(lines, axis=1)
    keys, values = [], []
    for source in range(sources):
        held = pair_refs[source * parts : (source + 1) * parts]
        keys.append(jnp.concatenate([ref[:rows] for ref in held], axis=0))
        values.append(jnp.concatenate([ref[rows:] for ref in held], axis=0))
    blocks = [(source, first) for source in range(sources) for first in range(0, slab, KEY_BLOCK)]
    query_grads = []
    for query_first in range(0, slab, QUERY_BLOCK):
        span = slice(query_first, query_first + QUERY_BLOCK)
        query_block, grad_block = queries[span], grads[span]
        query_flip, grad_flip = jnp.transpose(query_block), jnp.transpose(grad_block)
        dots_block = dots[:, span]
        top = None
        for source, first in blocks:
            scores = jnp.dot(
                keys[source][first : first + KEY_BLOCK], query_flip, preferred_element_type=jnp.float32
            )
            if masked and source > 0:
                scores = jnp.where(flags_ref[source - 1] > 0, scores, -jnp.inf)
            place = source * slab + first
            score_ref[place : place + KEY_BLOCK] = scores
            part_top = jnp.max(scores.reshape(-1, 8, QUERY_BLOCK), axis=0)
            top = part_top if top is None else jnp.maximum(top, part_top)
        top = jnp.max(top, axis=0, keepdims=True) * SCALE_LOG2
        total = None
        for source, first in blocks:
            place = source * slab + first
            powers = jnp.exp2(score_ref[place : place + KEY_BLOCK] * SCALE_LOG2 - top)
            score_ref[place : place + KEY_BLOCK] = powers
            part_total = jnp.sum(powers.reshape(-1, 8, QUERY_BLOCK), axis=0)
            total = part_total if total is None else total + part_total
        inverse = 1.0 / jnp.sum(total, axis=0, keepdims=True)
        query_acc = None
        for source, first in blocks:
            place = source * slab + first
            stretch = slice(first, first + KEY_BLOCK)
            weights = score_ref[place : place + KEY_BLOCK] * inverse
            grad_weights = jnp.dot(values[source][stretch], grad_flip, preferred_element_type=jnp.float32)
            grad_scores = (weights * (grad_weights - dots_block)).astype(jnp.bfloat16)
            value_part = jnp.dot(weights.astype(jnp.bfloat16), grad_block, preferred_element_type=jnp.float32)
            key_part = jnp.dot(grad_scores, query_block, preferred_element_type=jnp.float32)
            query_part = lax.dot_general(
                grad_scores,
                keys[source][stretch],
                (((0,), (0,)), ((), ())),
                preferred_element_type=jnp.float32,
            )
            query_acc = query_part if query_acc is None else query_acc + query_part
            if query_first == 0:
                key_acc[place : place + KEY_BLOCK] = key_part
                value_acc[place : place + KEY_BLOCK] = value_part
            else:
                key_acc[place : place + KEY_BLOCK] += key_part
                value_acc[place : place + KEY_BLOCK] += value_part
        query_grads.append((query_acc * SCALE).astype(jnp.bfloat16))
    query_grad = jnp.concatenate(query_grads, axis=0)
    for part in range(parts):
        query_grad_refs[part][...] = query_grad[part * rows : (part + 1) * rows]
    for source in range(sources):
        out_ref = own_ref if source == 0 else side_refs[source - 1]
        for part in range(parts):
            span = slice(source * slab + part * rows, source * slab + (part + 1) * rows)
            start = 2 * part * rows
            out_ref[start : start + rows] = (key_acc[span] * SCALE).astype(out_ref.dtype)
            out_ref[start + rows : start + 2 * rows] = value_acc[span].astype(out_ref.dtype)


def attention(head, place, query_pieces, pair_pieces, rows, flags):
    parts = len(query_pieces)
    sources = len(pair_pieces)
    masked = flags is not None
    slab = parts * rows
    query_depth = 2 * rows + dots_depth(rows)

    def block(depth, index):
        return pl.BlockSpec((depth, HD), lambda step: (index, 0))

    in_specs = [block(query_depth, place)] * parts + [block(2 * rows, head)] * (parts * sources)
    operands = list(query_pieces) + [piece for held in pair_pieces for piece in held]
    if masked:
        in_specs = [pl.BlockSpec(memory_space=pltpu.SMEM)] + in_specs
        operands = [flags] + operands
    pairs_of = slab * sources * slab
    outs = pl.pallas_call(
        functools.partial(attention_kernel, parts, sources, masked, rows),
        grid=(1,),
        in_specs=in_specs,
        out_specs=[block(rows, 0)] * parts + [block(2 * slab, 0)] * sources,
        out_shape=[jax.ShapeDtypeStruct((rows, HD), jnp.bfloat16)] * parts
        + [jax.ShapeDtypeStruct((2 * slab, HD), jnp.float32)]
        + [jax.ShapeDtypeStruct((2 * slab, HD), jnp.bfloat16)] * (sources - 1),
        scratch_shapes=[
            pltpu.VMEM((sources * slab, QUERY_BLOCK), jnp.float32),
            pltpu.VMEM((sources * slab, HD), jnp.float32),
            pltpu.VMEM((sources * slab, HD), jnp.float32),
        ],
        compiler_params=params(),
        cost_estimate=pl.CostEstimate(
            flops=10 * pairs_of * HD, bytes_accessed=slab * HD * 2 * (4 + 6 * sources), transcendentals=pairs_of
        ),
    )(*operands)
    return outs[:parts], outs[parts], outs[parts + 1 :]


def close_kernel(parts, rows, sides, lead, *refs):
    leads, refs = refs[: parts * lead], refs[parts * lead :]
    own_ref, side_refs, pieces = refs[0], refs[1 : 1 + sides], refs[1 + sides :]
    for part in range(parts):
        base = 0
        if lead:
            pieces[part][:rows] = leads[part][...]
            base = rows
        span = slice(2 * part * rows, 2 * (part + 1) * rows)
        total = own_ref[span]
        for ref in side_refs:
            total = total + ref[span].astype(jnp.float32)
        pieces[part][base : base + 2 * rows] = total.astype(jnp.bfloat16)


def close(query_grads, own, sides):
    lead = int(query_grads is not None)
    leads = list(query_grads) if lead else []
    parts = len(leads) if lead else lax.axis_size("ulysses")
    rows = own.shape[0] // (2 * parts)
    depth = (2 + lead) * rows
    return pl.pallas_call(
        functools.partial(close_kernel, parts, rows, len(sides), lead),
        out_shape=[jax.ShapeDtypeStruct((depth, HD), jnp.bfloat16)] * parts,
        compiler_params=params(),
        cost_estimate=pl.CostEstimate(
            flops=own.size * (1 + len(sides)), bytes_accessed=own.size * 8, transcendentals=0
        ),
    )(*leads, own, *sides)


def unpack_kernel(parts, rows, heads, stages, *refs):
    count = parts * len(stages)
    pieces, outs, semaphores = refs[:count], refs[count:-1], refs[-1]
    pairs = []
    for number, blocks in enumerate(stages):
        for distance in range(parts):
            piece = pieces[number * parts + distance]
            for index, (output, head) in enumerate(blocks):
                columns = pl.ds(column_of(distance, heads, head), HD)
                pairs.append((piece.at[index * rows : (index + 1) * rows], outs[output].at[:, columns]))
    run_copies(pairs, semaphores)


def unpack(stages, pieces, rows, heads):
    parts = len(pieces[0])
    whole = pl.BlockSpec(memory_space=pl.ANY)
    channels = parts * heads * HD
    return pl.pallas_call(
        functools.partial(unpack_kernel, parts, rows, heads, stages),
        in_specs=[whole] * (parts * len(stages)),
        out_specs=[whole] * 3,
        out_shape=[jax.ShapeDtypeStruct((rows, channels), jnp.bfloat16)] * 3,
        scratch_shapes=[pltpu.SemaphoreType.DMA((3 * heads * parts,))],
        compiler_params=params(),
        cost_estimate=pl.CostEstimate(flops=0, bytes_accessed=12 * rows * channels, transcendentals=0),
    )(*[piece for stage in pieces for piece in stage])


def swap(value, axis, distance):
    return lax.ppermute(value, axis, [(index, index ^ distance) for index in range(lax.axis_size(axis))])


def swap_pieces(pieces):
    return [pieces[0]] + [swap(piece, "ulysses", distance) for distance, piece in enumerate(pieces) if distance]


def total_of(value, axes):
    for axis in axes:
        size = lax.axis_size(axis)
        if size & (size - 1):
            value = lax.psum(value, axis)
            continue
        distance = 1
        while distance < size:
            value = value + swap(value, axis, distance)
            distance *= 2
    return value


def after(values, *earlier):
    return lax.optimization_barrier((list(values), earlier))[0]


def neighbours(size):
    if size == 1:
        return []
    if size == 2:
        swapped = [(0, 1), (1, 0)]
        return [(swapped, swapped)]
    up = [(index, index + 1) for index in range(size - 1)]
    down = [(index + 1, index) for index in range(size - 1)]
    return [(up, down), (down, up)]


def local(queries, keys, values, attn_out, out_grad, out_gain):
    parts = lax.axis_size("ulysses")
    span = lax.axis_size("tm")
    rows, channels = queries.shape[1:]
    heads = channels // (parts * HD)
    sides = neighbours(span)
    groups = [[head] for head in range(heads)]
    pairs = swap_pieces(pack_pairs(keys[0], values[0], parts))
    side_pairs = [[lax.ppermute(piece, "tm", there) for piece in pairs] for there, _ in sides]
    sent, gain_part = pack_queries(queries[0], out_grad[0], attn_out[0], out_gain, parts, groups)
    token_count = rows * span * parts * lax.axis_size("dp")
    gain_grad = total_of(gain_part.reshape(-1, LANES), ("tm", "dp", "ulysses")).reshape(channels) / token_count
    flags = None
    if len(sides) > 1:
        position = lax.axis_index("tm")
        flags = jnp.stack([position > 0, position < span - 1]).astype(jnp.int32)
    gates = [pairs[1 % parts], pairs[2 % parts]]
    held = []
    for number in range(len(groups)):
        held.append(swap_pieces(after(sent[number], gates[number])))
        gates.append(held[-1][2 % parts])
    stages, pieces = [], []
    own = others = None
    for head in range(heads):
        query_grads, next_own, next_others = attention(head, 0, held[head], [pairs] + side_pairs, rows, flags)
        if head == 0:
            stages.append([(0, 0)])
            pieces.append(swap_pieces(query_grads))
        else:
            stages.append([(0, head), (1, head - 1), (2, head - 1)])
            pieces.append(swap_pieces(close(query_grads, own, others)))
        own = next_own
        others = [lax.ppermute(other, "tm", back) for other, (_, back) in zip(next_others, sides)]
    stages.append([(1, heads - 1), (2, heads - 1)])
    pieces.append(swap_pieces(close(None, own, others)))
    grads = unpack(stages, pieces, rows, heads)
    return tuple(grad[None] for grad in grads) + (gain_grad,)


def solution(mesh):
    split = P("dp", ("tm", "ulysses"), None)
    return jax.shard_map(
        local,
        mesh=mesh,
        in_specs=(split,) * 5 + (P(),),
        out_specs=(split,) * 3 + (P(),),
        check_vma=False,
    )
```

time: 184 us -> 136 us (0.74)
  blocking collectives: 54.8 us -> 0 us
  starting transfers between devices: 22.2 us -> 52.3 us
  waiting for transfers between devices: 64.5 us -> 54.3 us
  local copies, waits for them, and re-layouts: 10.3 us -> 5.42 us
  other arithmetic: 5.04 us -> 0.64 us
  Pallas kernels: 25.9 us -> 21.7 us
    all_to_all x4 -> x0, waiting for transfers between devices: 63 us -> none  [exchange(): lax.all_to_all(value, 'ulysses', split_axis=0, concat_axis=0, tiled=True)]
    all_gather x1 -> x0, blocking collectives: 54.8 us -> none  [local(): lax.all_gather(gain_part, ('tm', 'ulysses', 'dp'), axis=0, tiled=True)]
    ppermute x4 -> x36, waiting for transfers between devices: 1.49 us -> 54.3 us  [the longest x29 54.2 us: swap(): lax.ppermute(value, axis, [(index, index ^ distance) for index in range(l...]
    ppermute x4 -> x36, starting transfers between devices: 5.05 us -> 52.3 us  [the longest x29 43.3 us: swap(): lax.ppermute(value, axis, [(index, index ^ distance) for index in range(l...]
    all_to_all x4 -> x0, starting transfers between devices: 17.1 us -> none  [exchange(): lax.all_to_all(value, 'ulysses', split_axis=0, concat_axis=0, tiled=True)]
    reshape x4 -> x0, local copies, waits for them, and re-layouts: 4.25 us -> none  [the longest x3 3.74 us: unpack(): jnp.transpose(laid, (2, 0, 1, 3)).reshape(1, rows, parts * heads * HD)]
    pallas_call x5 -> x9, Pallas kernels: 25.9 us -> 21.7 us  [the longest x3 19 us: attention(): pl.pallas_call(functools.partial(attention_kernel, parts, sources, masked...]
    convert_element_type x3 -> x0, other arithmetic: 2.33 us -> none  [local(): pair_grads.append(total.astype(jnp.bfloat16))]
  transfers between devices with their start and end apart: 8 -> 36, of which waited for: 4 -> 13; matrix products, arithmetic and copies ran while one was open for 4% -> 1% of each run, Pallas kernels for 9% -> 15%
where the time goes in v2:
time: 136 us; the launch traced here: 135 us
  waiting for transfers between devices  54.3 us (40%)
  starting transfers between devices  52.3 us (38%)
  Pallas kernels  21.7 us (16%)
  local copies, waits for them, and re-layouts  5.42 us (4%)
    ppermute x29, waiting for transfers between devices, swap(): lax.ppermute(value, axis, [(index, index ^ distance) for index in range(l...  54.2 us
    ppermute x29, starting transfers between devices, swap(): lax.ppermute(value, axis, [(index, index ^ distance) for index in range(l...  43.3 us
    pallas_call x3, Pallas kernels, attention(): pl.pallas_call(functools.partial(attention_kernel, parts, sources, masked...  19 us
    ppermute x4, starting transfers between devices, local(): lax.ppermute(piece, 'tm', there)  5.23 us
    unnamed x14, local copies, waits for them, and re-layouts  4.72 us
    ppermute x3, starting transfers between devices, local(): lax.ppermute(other, 'tm', back)  3.77 us
  transfers between devices with their start and end apart: 36, of which 13 were waited for; matrix products, arithmetic and copies ran while one was open for 1% of the time, Pallas kernels for 15%

profile of v2, /device:TPU:0, one launch (start us, length us, event | category | flops | bytes accessed | tf_op | source)
XLA Modules:
  0.0 135.3 jit_solution(5583507599055778874)
XLA Ops:
  3.3 3.1 %collective-permute-start = (bf16[1152,128]{1,0:T(8,128)(2,1)S(1)}, bf16[1152,128]{1,0:T(8,128)(2,1)S(1)}, u32[]{:S(2)}, u32[]{:S(2)}) collective-permute-start(bf16[1152,128]{1,0:T(8,128)(2,1)S(1)} %get-tuple-element.70), channel_id=1, source_target_pairs={{0,4},{4,0},{8,12},{12,8},{1,5},{5,1},{9,13},{13,9},{2,6},{6,2},{1... | collective-permute-start | bytes 884744 | tf_op jit(solution)/shard_map/ppermute | solution.py:310
  6.4 2.6 %collective-permute-start.4 = (bf16[1152,128]{1,0:T(8,128)(2,1)S(1)}, bf16[1152,128]{1,0:T(8,128)(2,1)S(1)}, u32[]{:S(2)}, u32[]{:S(2)}) collective-permute-start(bf16[1152,128]{1,0:T(8,128)(2,1)S(1)} %get-tuple-element.76), channel_id=1, source_target_pairs={{0,8},{4,12},{8,0},{12,4},{1,9},{5,13},{9,1},{13,5},{2,10},{6,14},... | collective-permute-start | bytes 884744 | tf_op jit(solution)/shard_map/ppermute | solution.py:310
  8.9 1.7 %collective-permute-start.6 = (bf16[1152,128]{1,0:T(8,128)(2,1)S(1)}, bf16[1152,128]{1,0:T(8,128)(2,1)S(1)}, u32[]{:S(2)}, u32[]{:S(2)}) collective-permute-start(bf16[1152,128]{1,0:T(8,128)(2,1)S(1)} %get-tuple-element.75.refs_4_), channel_id=1, source_target_pairs={{0,16},{16,0},{1,17},{17,1},{2,18},{18,2},{3,19},{19,3},{4,20},{20... | collective-permute-start | bytes 884744 | tf_op jit(solution)/shard_map/ppermute | solution.py:353
  13.0 5.9 %collective-permute-done.refs_5_ = bf16[1152,128]{1,0:T(8,128)(2,1)S(1)} collective-permute-done((bf16[1152,128]{1,0:T(8,128)(2,1)S(1)}, bf16[1152,128]{1,0:T(8,128)(2,1)S(1)}, u32[]{:S(2)}, u32[]{:S(2)}) %collective-permute-start) | collective-permute-done | bytes 294944 | tf_op jit(solution)/shard_map/ppermute | solution.py:310
  21.7 10.3 %collective-permute-done.4.refs_6_ = bf16[1152,128]{1,0:T(8,128)(2,1)S(1)} collective-permute-done((bf16[1152,128]{1,0:T(8,128)(2,1)S(1)}, bf16[1152,128]{1,0:T(8,128)(2,1)S(1)}, u32[]{:S(2)}, u32[]{:S(2)}) %collective-permute-start.4) | collective-permute-done | bytes 294944 | tf_op jit(solution)/shard_map/ppermute | solution.py:310
  34.1 5.1 %collective-permute-done.2.refs_2_ = bf16[400,128]{1,0:T(8,128)(2,1)S(1)} collective-permute-done((bf16[400,128]{1,0:T(8,128)(2,1)S(1)}, bf16[400,128]{1,0:T(8,128)(2,1)S(1)}, u32[]{:S(2)}, u32[]{:S(2)}) %collective-permute-start.2) | collective-permute-done | bytes 102432 | tf_op jit(solution)/shard_map/ppermute | solution.py:310
  40.1 2.1 %collective-permute-start.21 = (bf16[400,128]{1,0:T(8,128)(2,1)S(1)}, bf16[400,128]{1,0:T(8,128)(2,1)}, u32[]{:S(2)}, u32[]{:S(2)}) collective-permute-start(bf16[400,128]{1,0:T(8,128)(2,1)S(1)} %get-tuple-element.106), channel_id=1, source_target_pairs={{0,8},{4,12},{8,0},{12,4},{1,9},{5,13},{9,1},{13,5},{2,10},{6,14},... | collective-permute-start | bytes 307208 | tf_op jit(solution)/shard_map/ppermute | solution.py:310
  44.4 2.5 %collective-permute-start.22 = (bf16[400,128]{1,0:T(8,128)(2,1)S(1)}, bf16[400,128]{1,0:T(8,128)(2,1)}, u32[]{:S(2)}, u32[]{:S(2)}) collective-permute-start(bf16[400,128]{1,0:T(8,128)(2,1)S(1)} %get-tuple-element.107), channel_id=1, source_target_pairs={{0,12},{4,8},{8,4},{12,0},{1,13},{5,9},{9,5},{13,1},{2,14},{6,10},... | collective-permute-start | bytes 307208 | tf_op jit(solution)/shard_map/ppermute | solution.py:310
  49.4 1.7 %collective-permute-done.22.refs_3_ = bf16[400,128]{1,0:T(8,128)(2,1)} collective-permute-done((bf16[400,128]{1,0:T(8,128)(2,1)S(1)}, bf16[400,128]{1,0:T(8,128)(2,1)}, u32[]{:S(2)}, u32[]{:S(2)}) %collective-permute-start.22) | collective-permute-done | bytes 102432 | tf_op jit(solution)/shard_map/ppermute | solution.py:310
  51.1 3.6 %collective-permute-start.14 = (bf16[400,128]{1,0:T(8,128)(2,1)S(1)}, bf16[400,128]{1,0:T(8,128)(2,1)S(1)}, u32[]{:S(2)}, u32[]{:S(2)}) collective-permute-start(bf16[400,128]{1,0:T(8,128)(2,1)S(1)} %get-tuple-element.88), channel_id=1, source_target_pairs={{0,8},{4,12},{8,0},{12,4},{1,9},{5,13},{9,1},{13,5},{2,10},{6,14},... | collective-permute-start | bytes 307208 | tf_op jit(solution)/shard_map/ppermute | solution.py:310
  56.4 6.9 %shard_map.98 = (bf16[192,128]{1,0:T(8,128)(2,1)S(1)}, bf16[192,128]{1,0:T(8,128)(2,1)S(1)}, bf16[192,128]{1,0:T(8,128)(2,1)S(1)}, bf16[192,128]{1,0:T(8,128)(2,...) custom-call(bf16[400,128]{1,0:T(8,128)(2,1)S(1)} %get-tuple-element.104.refs_0_, ...), custom_call_target="tpu_custom_call" | custom-call | flops 1509949440 | bytes 3145728 | tf_op jit(solution)/shard_map/pallas_call | solution.py:229
  63.3 3.1 %collective-permute-start.3 = (bf16[400,128]{1,0:T(8,128)(2,1)S(1)}, bf16[400,128]{1,0:T(8,128)(2,1)S(1)}, u32[]{:S(2)}, u32[]{:S(2)}) collective-permute-start(bf16[400,128]{1,0:T(8,128)(2,1)S(1)} %get-tuple-element.74), channel_id=1, source_target_pairs={{0,12},{4,8},{8,4},{12,0},{1,13},{5,9},{9,5},{13,1},{2,14},{6,10},... | collective-permute-start | bytes 307208 | tf_op jit(solution)/shard_map/ppermute | solution.py:310
  68.0 6.1 %shard_map.96 = (bf16[192,128]{1,0:T(8,128)(2,1)S(1)}, bf16[192,128]{1,0:T(8,128)(2,1)S(1)}, bf16[192,128]{1,0:T(8,128)(2,1)S(1)}, bf16[192,128]{1,0:T(8,128)(2,...) custom-call(bf16[400,128]{1,0:T(8,128)(2,1)S(1)} %get-tuple-element.86.refs_0_, ...), custom_call_target="tpu_custom_call" | custom-call | flops 1509949440 | bytes 3145728 | tf_op jit(solution)/shard_map/pallas_call | solution.py:229
  74.6 5.9 %shard_map.95 = (bf16[192,128]{1,0:T(8,128)(2,1)S(1)}, bf16[192,128]{1,0:T(8,128)(2,1)S(1)}, bf16[192,128]{1,0:T(8,128)(2,1)S(1)}, bf16[192,128]{1,0:T(8,128)(2,...) custom-call(bf16[400,128]{1,0:T(8,128)(2,1)S(1)} %get-tuple-element.71.refs_0_, ...), custom_call_target="tpu_custom_call" | custom-call | flops 1509949440 | bytes 3145728 | tf_op jit(solution)/shard_map/pallas_call | solution.py:229
  80.6 1.7 %collective-permute-start.16 = (bf16[1536,128]{1,0:T(8,128)(2,1)S(1)}, bf16[1536,128]{1,0:T(8,128)(2,1)S(1)}, u32[]{:S(2)}, u32[]{:S(2)}) collective-permute-start(bf16[1536,128]{1,0:T(8,128)(2,1)S(1)} %get-tuple-element.95), channel_id=1, source_target_pairs={{0,16},{16,0},{1,17},{17,1},{2,18},{18,2},{3,19},{19,3},{4,20},{20... | collective-permute-start | bytes 1179656 | tf_op jit(solution)/shard_map/ppermute | solution.py:377
  85.0 2.1 %collective-permute-done.33 = f32[12,128]{1,0:T(8,128)S(1)} collective-permute-done((f32[12,128]{1,0:T(8,128)S(1)}, f32[12,128]{1,0:T(8,128)S(1)}, u32[]{:S(2)}, u32[]{:S(2)}) %collective-permute-start.33) | collective-permute-done | bytes 6176 | tf_op jit(solution)/shard_map/ppermute | solution.py:310
  93.4 3.0 %collective-permute-done.35 = f32[12,128]{1,0:T(8,128)S(1)} collective-permute-done((f32[12,128]{1,0:T(8,128)S(1)}, f32[12,128]{1,0:T(8,128)S(1)}, u32[]{:S(2)}, u32[]{:S(2)}) %collective-permute-start.35) | collective-permute-done | bytes 6176 | tf_op jit(solution)/shard_map/ppermute | solution.py:310
  98.8 2.0 %collective-permute-start.30 = (bf16[384,128]{1,0:T(8,128)(2,1)S(1)}, bf16[384,128]{1,0:T(8,128)(2,1)S(1)}, u32[]{:S(2)}, u32[]{:S(2)}) collective-permute-start(bf16[384,128]{1,0:T(8,128)(2,1)S(1)} %get-tuple-element.123), channel_id=1, source_target_pairs={{0,12},{4,8},{8,4},{12,0},{1,13},{5,9},{9,5},{13,1},{2,14},{6,10},... | collective-permute-start | bytes 294920 | tf_op jit(solution)/shard_map/ppermute | solution.py:310
  100.9 1.8 %collective-permute-start.12 = (bf16[192,128]{1,0:T(8,128)(2,1)S(1)}, bf16[192,128]{1,0:T(8,128)(2,1)S(1)}, u32[]{:S(2)}, u32[]{:S(2)}) collective-permute-start(bf16[192,128]{1,0:T(8,128)(2,1)S(1)} %get-tuple-element.81), channel_id=1, source_target_pairs={{0,12},{4,8},{8,4},{12,0},{1,13},{5,9},{9,5},{13,1},{2,14},{6,10},... | collective-permute-start | bytes 147464 | tf_op jit(solution)/shard_map/ppermute | solution.py:310
  102.7 4.1 %collective-permute-done.12.refs_3_ = bf16[192,128]{1,0:T(8,128)(2,1)S(1)} collective-permute-done((bf16[192,128]{1,0:T(8,128)(2,1)S(1)}, bf16[192,128]{1,0:T(8,128)(2,1)S(1)}, u32[]{:S(2)}, u32[]{:S(2)}) %collective-permute-start.12) | collective-permute-done | bytes 49184 | tf_op jit(solution)/shard_map/ppermute | solution.py:310
  106.8 3.5 %collective-permute-start.25 = (bf16[576,128]{1,0:T(8,128)(2,1)S(1)}, bf16[576,128]{1,0:T(8,128)(2,1)S(1)}, u32[]{:S(2)}, u32[]{:S(2)}) collective-permute-start(bf16[576,128]{1,0:T(8,128)(2,1)S(1)} %get-tuple-element.116), channel_id=1, source_target_pairs={{0,8},{4,12},{8,0},{12,4},{1,9},{5,13},{9,1},{13,5},{2,10},{6,14},... | collective-permute-start | bytes 442376 | tf_op jit(solution)/shard_map/ppermute | solution.py:310
  112.0 2.8 %collective-permute-start.18 = (bf16[576,128]{1,0:T(8,128)(2,1)S(1)}, bf16[576,128]{1,0:T(8,128)(2,1)S(1)}, u32[]{:S(2)}, u32[]{:S(2)}) collective-permute-start(bf16[576,128]{1,0:T(8,128)(2,1)S(1)} %get-tuple-element.98), channel_id=1, source_target_pairs={{0,8},{4,12},{8,0},{12,4},{1,9},{5,13},{9,1},{13,5},{2,10},{6,14},... | collective-permute-start | bytes 442376 | tf_op jit(solution)/shard_map/ppermute | solution.py:310
  116.9 5.3 %collective-permute-done.25.refs_10_ = bf16[576,128]{1,0:T(8,128)(2,1)S(1)} collective-permute-done((bf16[576,128]{1,0:T(8,128)(2,1)S(1)}, bf16[576,128]{1,0:T(8,128)(2,1)S(1)}, u32[]{:S(2)}, u32[]{:S(2)}) %collective-permute-start.25) | collective-permute-done | bytes 147488 | tf_op jit(solution)/shard_map/ppermute | solution.py:310
  122.2 11.4 %collective-permute-done.18.refs_6_ = bf16[576,128]{1,0:T(8,128)(2,1)S(1)} collective-permute-done((bf16[576,128]{1,0:T(8,128)(2,1)S(1)}, bf16[576,128]{1,0:T(8,128)(2,1)S(1)}, u32[]{:S(2)}, u32[]{:S(2)}) %collective-permute-start.18) | collective-permute-done | bytes 147488 | tf_op jit(solution)/shard_map/ppermute | solution.py:310
  (78 shorter events, 36.0 us)
Async XLA Ops:
  3.3 15.6 %collective-permute-start = (bf16[1152,128]{1,0:T(8,128)(2,1)S(1)}, bf16[1152,128]{1,0:T(8,128)(2,1)S(1)}, u32[]{:S(2)}, u32[]{:S(2)}) collective-permute-start(bf16[1152,128]{1,0:T(8,128)(2,1)S(1)} %get-tuple-element.70), channel_id=1, source_target_pairs={{0,4},{4,0},{8,12},{12,8},{1,5},{5,1},{9,13},{13,9},{2,6},{6,2},{1... | collective-permute-start | bytes 884744 | tf_op jit(solution)/shard_map/ppermute | solution.py:310
  6.4 25.7 %collective-permute-start.4 = (bf16[1152,128]{1,0:T(8,128)(2,1)S(1)}, bf16[1152,128]{1,0:T(8,128)(2,1)S(1)}, u32[]{:S(2)}, u32[]{:S(2)}) collective-permute-start(bf16[1152,128]{1,0:T(8,128)(2,1)S(1)} %get-tuple-element.76), channel_id=1, source_target_pairs={{0,8},{4,12},{8,0},{12,4},{1,9},{5,13},{9,1},{13,5},{2,10},{6,14},... | collective-permute-start | bytes 884744 | tf_op jit(solution)/shard_map/ppermute | solution.py:310
  8.9 24.6 %collective-permute-start.5 = (bf16[1152,128]{1,0:T(8,128)(2,1)S(1)}, bf16[1152,128]{1,0:T(8,128)(2,1)S(1)}, u32[]{:S(2)}, u32[]{:S(2)}) collective-permute-start(bf16[1152,128]{1,0:T(8,128)(2,1)S(1)} %get-tuple-element.77), channel_id=1, source_target_pairs={{0,12},{4,8},{8,4},{12,0},{1,13},{5,9},{9,5},{13,1},{2,14},{6,10},... | collective-permute-start | bytes 884744 | tf_op jit(solution)/shard_map/ppermute | solution.py:310
  8.9 31.1 %collective-permute-start.6 = (bf16[1152,128]{1,0:T(8,128)(2,1)S(1)}, bf16[1152,128]{1,0:T(8,128)(2,1)S(1)}, u32[]{:S(2)}, u32[]{:S(2)}) collective-permute-start(bf16[1152,128]{1,0:T(8,128)(2,1)S(1)} %get-tuple-element.75.refs_4_), channel_id=1, source_target_pairs={{0,16},{16,0},{1,17},{17,1},{2,18},{18,2},{3,19},{19,3},{4,20},{20... | collective-permute-start | bytes 884744 | tf_op jit(solution)/shard_map/ppermute | solution.py:353
  18.9 20.2 %collective-permute-start.2 = (bf16[400,128]{1,0:T(8,128)(2,1)S(1)}, bf16[400,128]{1,0:T(8,128)(2,1)S(1)}, u32[]{:S(2)}, u32[]{:S(2)}) collective-permute-start(bf16[400,128]{1,0:T(8,128)(2,1)S(1)} %get-tuple-element.73), channel_id=1, source_target_pairs={{0,8},{4,12},{8,0},{12,4},{1,9},{5,13},{9,1},{13,5},{2,10},{6,14},... | collective-permute-start | bytes 307208 | tf_op jit(solution)/shard_map/ppermute | solution.py:310
  20.2 30.9 %collective-permute-start.7 = (bf16[1152,128]{1,0:T(8,128)(2,1)S(1)}, bf16[1152,128]{1,0:T(8,128)(2,1)S(1)}, u32[]{:S(2)}, u32[]{:S(2)}) collective-permute-start(bf16[1152,128]{1,0:T(8,128)(2,1)S(1)} %collective-permute-done.refs_5_), channel_id=1, source_target_pairs={{0,16},{16,0},{1,17},{17,1},{2,18},{18,2},{3,19},{19,3},{4,20},{20... | collective-permute-start | bytes 884744 | tf_op jit(solution)/shard_map/ppermute | solution.py:353
  32.0 22.7 %collective-permute-start.8 = (bf16[1152,128]{1,0:T(8,128)(2,1)S(1)}, bf16[1152,128]{1,0:T(8,128)(2,1)S(1)}, u32[]{:S(2)}, u32[]{:S(2)}) collective-permute-start(bf16[1152,128]{1,0:T(8,128)(2,1)S(1)} %collective-permute-done.4.refs_6_), channel_id=1, source_target_pairs={{0,16},{16,0},{1,17},{17,1},{2,18},{18,2},{3,19},{19,3},{4,20},{20... | collective-permute-start | bytes 884744 | tf_op jit(solution)/shard_map/ppermute | solution.py:353
  33.5 22.0 %collective-permute-start.9 = (bf16[1152,128]{1,0:T(8,128)(2,1)S(1)}, bf16[1152,128]{1,0:T(8,128)(2,1)S(1)}, u32[]{:S(2)}, u32[]{:S(2)}) collective-permute-start(bf16[1152,128]{1,0:T(8,128)(2,1)S(1)} %collective-permute-done.5.refs_7_), channel_id=1, source_target_pairs={{0,16},{16,0},{1,17},{17,1},{2,18},{18,2},{3,19},{19,3},{4,20},{20... | collective-permute-start | bytes 884744 | tf_op jit(solution)/shard_map/ppermute | solution.py:353
  48.5 33.8 %collective-permute-start.31 = (f32[12,128]{1,0:T(8,128)S(1)}, f32[12,128]{1,0:T(8,128)S(1)}, u32[]{:S(2)}, u32[]{:S(2)}) collective-permute-start(f32[12,128]{1,0:T(8,128)S(1)} %bitcast.19), channel_id=1, source_target_pairs={{0,16},{16,0},{1,17},{17,1},{2,18},{18,2},{3,19},{19,3},{4,20},{20... | collective-permute-start | bytes 18440 | tf_op jit(solution)/shard_map/ppermute | solution.py:310
  51.1 12.2 %collective-permute-start.13 = (bf16[400,128]{1,0:T(8,128)(2,1)S(1)}, bf16[400,128]{1,0:T(8,128)(2,1)S(1)}, u32[]{:S(2)}, u32[]{:S(2)}) collective-permute-start(bf16[400,128]{1,0:T(8,128)(2,1)S(1)} %get-tuple-element.87), channel_id=1, source_target_pairs={{0,4},{4,0},{8,12},{12,8},{1,5},{5,1},{9,13},{13,9},{2,6},{6,2},{1... | collective-permute-start | bytes 307208 | tf_op jit(solution)/shard_map/ppermute | solution.py:310
  51.1 15.3 %collective-permute-start.14 = (bf16[400,128]{1,0:T(8,128)(2,1)S(1)}, bf16[400,128]{1,0:T(8,128)(2,1)S(1)}, u32[]{:S(2)}, u32[]{:S(2)}) collective-permute-start(bf16[400,128]{1,0:T(8,128)(2,1)S(1)} %get-tuple-element.88), channel_id=1, source_target_pairs={{0,8},{4,12},{8,0},{12,4},{1,9},{5,13},{9,1},{13,5},{2,10},{6,14},... | collective-permute-start | bytes 307208 | tf_op jit(solution)/shard_map/ppermute | solution.py:310
  54.7 13.3 %collective-permute-start.15 = (bf16[400,128]{1,0:T(8,128)(2,1)S(1)}, bf16[400,128]{1,0:T(8,128)(2,1)S(1)}, u32[]{:S(2)}, u32[]{:S(2)}) collective-permute-start(bf16[400,128]{1,0:T(8,128)(2,1)S(1)} %get-tuple-element.89), channel_id=1, source_target_pairs={{0,12},{4,8},{8,4},{12,0},{1,13},{5,9},{9,5},{13,1},{2,14},{6,10},... | collective-permute-start | bytes 307208 | tf_op jit(solution)/shard_map/ppermute | solution.py:310
  55.5 19.1 %collective-permute-start.1 = (bf16[400,128]{1,0:T(8,128)(2,1)S(1)}, bf16[400,128]{1,0:T(8,128)(2,1)S(1)}, u32[]{:S(2)}, u32[]{:S(2)}) collective-permute-start(bf16[400,128]{1,0:T(8,128)(2,1)S(1)} %get-tuple-element.72), channel_id=1, source_target_pairs={{0,4},{4,0},{8,12},{12,8},{1,5},{5,1},{9,13},{13,9},{2,6},{6,2},{1... | collective-permute-start | bytes 307208 | tf_op jit(solution)/shard_map/ppermute | solution.py:310
  66.4 25.5 %collective-permute-start.27 = (bf16[1536,128]{1,0:T(8,128)(2,1)S(1)}, bf16[1536,128]{1,0:T(8,128)(2,1)S(1)}, u32[]{:S(2)}, u32[]{:S(2)}) collective-permute-start(bf16[1536,128]{1,0:T(8,128)(2,1)S(1)} %get-tuple-element.119), channel_id=1, source_target_pairs={{0,16},{16,0},{1,17},{17,1},{2,18},{18,2},{3,19},{19,3},{4,20},{20... | collective-permute-start | bytes 1179656 | tf_op jit(solution)/shard_map/ppermute | solution.py:377
  74.2 15.0 %collective-permute-start.23 = (bf16[1536,128]{1,0:T(8,128)(2,1)S(1)}, bf16[1536,128]{1,0:T(8,128)(2,1)S(1)}, u32[]{:S(2)}, u32[]{:S(2)}) collective-permute-start(bf16[1536,128]{1,0:T(8,128)(2,1)S(1)} %get-tuple-element.113), channel_id=1, source_target_pairs={{0,16},{16,0},{1,17},{17,1},{2,18},{18,2},{3,19},{19,3},{4,20},{20... | collective-permute-start | bytes 1179656 | tf_op jit(solution)/shard_map/ppermute | solution.py:377
  80.6 20.3 %collective-permute-start.16 = (bf16[1536,128]{1,0:T(8,128)(2,1)S(1)}, bf16[1536,128]{1,0:T(8,128)(2,1)S(1)}, u32[]{:S(2)}, u32[]{:S(2)}) collective-permute-start(bf16[1536,128]{1,0:T(8,128)(2,1)S(1)} %get-tuple-element.95), channel_id=1, source_target_pairs={{0,16},{16,0},{1,17},{17,1},{2,18},{18,2},{3,19},{19,3},{4,20},{20... | collective-permute-start | bytes 1179656 | tf_op jit(solution)/shard_map/ppermute | solution.py:377
  90.8 24.0 %collective-permute-start.24 = (bf16[576,128]{1,0:T(8,128)(2,1)S(1)}, bf16[576,128]{1,0:T(8,128)(2,1)S(1)}, u32[]{:S(2)}, u32[]{:S(2)}) collective-permute-start(bf16[576,128]{1,0:T(8,128)(2,1)S(1)} %get-tuple-element.115), channel_id=1, source_target_pairs={{0,4},{4,0},{8,12},{12,8},{1,5},{5,1},{9,13},{13,9},{2,6},{6,2},{1... | collective-permute-start | bytes 442376 | tf_op jit(solution)/shard_map/ppermute | solution.py:310
  96.5 13.9 %collective-permute-start.28 = (bf16[384,128]{1,0:T(8,128)(2,1)S(1)}, bf16[384,128]{1,0:T(8,128)(2,1)S(1)}, u32[]{:S(2)}, u32[]{:S(2)}) collective-permute-start(bf16[384,128]{1,0:T(8,128)(2,1)S(1)} %get-tuple-element.121), channel_id=1, source_target_pairs={{0,4},{4,0},{8,12},{12,8},{1,5},{5,1},{9,13},{13,9},{2,6},{6,2},{1... | collective-permute-start | bytes 294920 | tf_op jit(solution)/shard_map/ppermute | solution.py:310
  97.4 14.5 %collective-permute-start.29 = (bf16[384,128]{1,0:T(8,128)(2,1)S(1)}, bf16[384,128]{1,0:T(8,128)(2,1)S(1)}, u32[]{:S(2)}, u32[]{:S(2)}) collective-permute-start(bf16[384,128]{1,0:T(8,128)(2,1)S(1)} %get-tuple-element.122), channel_id=1, source_target_pairs={{0,8},{4,12},{8,0},{12,4},{1,9},{5,13},{9,1},{13,5},{2,10},{6,14},... | collective-permute-start | bytes 294920 | tf_op jit(solution)/shard_map/ppermute | solution.py:310
  98.8 13.1 %collective-permute-start.30 = (bf16[384,128]{1,0:T(8,128)(2,1)S(1)}, bf16[384,128]{1,0:T(8,128)(2,1)S(1)}, u32[]{:S(2)}, u32[]{:S(2)}) collective-permute-start(bf16[384,128]{1,0:T(8,128)(2,1)S(1)} %get-tuple-element.123), channel_id=1, source_target_pairs={{0,12},{4,8},{8,4},{12,0},{1,13},{5,9},{9,5},{13,1},{2,14},{6,10},... | collective-permute-start | bytes 294920 | tf_op jit(solution)/shard_map/ppermute | solution.py:310
  106.8 15.4 %collective-permute-start.25 = (bf16[576,128]{1,0:T(8,128)(2,1)S(1)}, bf16[576,128]{1,0:T(8,128)(2,1)S(1)}, u32[]{:S(2)}, u32[]{:S(2)}) collective-permute-start(bf16[576,128]{1,0:T(8,128)(2,1)S(1)} %get-tuple-element.116), channel_id=1, source_target_pairs={{0,8},{4,12},{8,0},{12,4},{1,9},{5,13},{9,1},{13,5},{2,10},{6,14},... | collective-permute-start | bytes 442376 | tf_op jit(solution)/shard_map/ppermute | solution.py:310
  110.3 11.9 %collective-permute-start.26 = (bf16[576,128]{1,0:T(8,128)(2,1)S(1)}, bf16[576,128]{1,0:T(8,128)(2,1)S(1)}, u32[]{:S(2)}, u32[]{:S(2)}) collective-permute-start(bf16[576,128]{1,0:T(8,128)(2,1)S(1)} %get-tuple-element.117), channel_id=1, source_target_pairs={{0,12},{4,8},{8,4},{12,0},{1,13},{5,9},{9,5},{13,1},{2,14},{6,10},... | collective-permute-start | bytes 442376 | tf_op jit(solution)/shard_map/ppermute | solution.py:310
  112.0 21.6 %collective-permute-start.18 = (bf16[576,128]{1,0:T(8,128)(2,1)S(1)}, bf16[576,128]{1,0:T(8,128)(2,1)S(1)}, u32[]{:S(2)}, u32[]{:S(2)}) collective-permute-start(bf16[576,128]{1,0:T(8,128)(2,1)S(1)} %get-tuple-element.98), channel_id=1, source_target_pairs={{0,8},{4,12},{8,0},{12,4},{1,9},{5,13},{9,1},{13,5},{2,10},{6,14},... | collective-permute-start | bytes 442376 | tf_op jit(solution)/shard_map/ppermute | solution.py:310
  114.7 18.9 %collective-permute-start.19 = (bf16[576,128]{1,0:T(8,128)(2,1)S(1)}, bf16[576,128]{1,0:T(8,128)(2,1)S(1)}, u32[]{:S(2)}, u32[]{:S(2)}) collective-permute-start(bf16[576,128]{1,0:T(8,128)(2,1)S(1)} %get-tuple-element.99), channel_id=1, source_target_pairs={{0,12},{4,8},{8,4},{12,0},{1,13},{5,9},{9,5},{13,1},{2,14},{6,10},... | collective-permute-start | bytes 442376 | tf_op jit(solution)/shard_map/ppermute | solution.py:310
  (19 other events, 101.2 us)

commit v3 on v2

v3 whole, which is shorter than its diff:
```python
import functools
import math

import jax
import jax.numpy as jnp
from jax import lax
from jax.experimental import pallas as pl
from jax.experimental.pallas import tpu as pltpu
from jax.sharding import PartitionSpec as P

HD = 128
LANES = 128
TILE_ROWS = 16
KEY_BLOCK = 256
QUERY_BLOCK = 256
VMEM_LIMIT = 48 * 1024 * 1024
SCALE = 1.0 / math.sqrt(HD)
SCALE_LOG2 = SCALE / math.log(2.0)
COST = pl.CostEstimate(flops=1, bytes_accessed=1, transcendentals=0)


def params():
    return pltpu.CompilerParams(vmem_limit_bytes=VMEM_LIMIT)


def partner(distance):
    return lax.axis_index("ulysses") ^ distance


def column_of(distance, heads, head):
    return pl.multiple_of((partner(distance) * heads + head) * HD, HD)


def run_copies(pairs, semaphores):
    copies = [
        pltpu.make_async_copy(source, target, semaphores.at[index]) for index, (source, target) in enumerate(pairs)
    ]
    for copy in copies:
        copy.start()
    for copy in copies:
        copy.wait()


def pack_kernel(parts, *refs):
    sources, pieces, semaphores = refs[: -parts - 1], refs[-parts - 1 : -1], refs[-1]
    rows, channels = sources[0].shape
    heads = channels // (parts * HD)
    pairs = []
    for distance in range(parts):
        for half, ref in enumerate(sources):
            for head in range(heads):
                columns = pl.ds(column_of(distance, heads, head), HD)
                start = (half * heads + head) * rows
                pairs.append((ref.at[:, columns], pieces[distance].at[start : start + rows]))
    run_copies(pairs, semaphores)


def pack(sources, parts):
    rows, channels = sources[0].shape
    heads = channels // (parts * HD)
    depth = len(sources) * heads * rows
    whole = pl.BlockSpec(memory_space=pl.ANY)
    return pl.pallas_call(
        functools.partial(pack_kernel, parts),
        in_specs=[whole] * len(sources),
        out_specs=[whole] * parts,
        out_shape=[jax.ShapeDtypeStruct((depth, HD), sources[0].dtype)] * parts,
        scratch_shapes=[pltpu.SemaphoreType.DMA((len(sources) * heads * parts,))],
        compiler_params=params(),
        cost_estimate=COST,
    )(*sources)


def dot_groups(rows):
    return -(-rows // LANES)


def dots_depth(rows, heads):
    return -(-2 * heads * dot_groups(rows) // TILE_ROWS) * TILE_ROWS


def pack_grads_kernel(parts, out_grad_ref, attn_ref, gain_ref, *refs):
    pieces, gain_part_ref = refs[:-1], refs[-1]
    rows, channels = out_grad_ref.shape
    heads = channels // (parts * HD)
    for distance, piece in enumerate(pieces):
        terms = []
        for head in range(heads):
            columns = pl.ds(column_of(distance, heads, head), HD)
            out_grad = out_grad_ref[:, columns].astype(jnp.float32)
            attn = attn_ref[:, columns].astype(jnp.float32)
            grad = (out_grad * gain_ref[:, columns]).astype(jnp.bfloat16)
            gain_part_ref[:, columns] = jnp.sum(out_grad * attn, axis=0, keepdims=True)
            piece[head * rows : (head + 1) * rows] = grad
            dots = jnp.sum(jnp.transpose(grad.astype(jnp.float32) * attn), axis=0, keepdims=True)
            for first in range(0, rows, LANES):
                value = dots[:, first : first + LANES]
                if value.shape[1] < LANES:
                    rest = jnp.zeros((1, LANES - value.shape[1]), jnp.float32)
                    value = jnp.concatenate([value, rest], axis=1)
                high = value.astype(jnp.bfloat16).astype(jnp.float32)
                terms += [high, value - high]
        rest = dots_depth(rows, heads) - len(terms)
        if rest:
            terms.append(jnp.zeros((rest, LANES), jnp.float32))
        piece[heads * rows :] = jnp.concatenate(terms, axis=0).astype(jnp.bfloat16)


def pack_grads(out_grad, attn_out, out_gain, parts):
    rows, channels = out_grad.shape
    heads = channels // (parts * HD)
    depth = heads * rows + dots_depth(rows, heads)
    outs = pl.pallas_call(
        functools.partial(pack_grads_kernel, parts),
        out_shape=[jax.ShapeDtypeStruct((depth, HD), jnp.bfloat16)] * parts
        + [jax.ShapeDtypeStruct((1, channels), jnp.float32)],
        compiler_params=params(),
        cost_estimate=COST,
    )(out_grad, attn_out, out_gain.reshape(1, channels))
    return outs[:parts], outs[parts]


def rows_of(refs, first, count):
    return jnp.concatenate([ref[first : first + count] for ref in refs], axis=0)


def totals_kernel(parts, sources, heads, rows, *refs):
    held, refs = refs[:parts], refs[parts:]
    sides, refs = refs[: parts * (sources - 1)], refs[parts * (sources - 1) :]
    outs, score_ref = refs[:sources], refs[sources]
    slab = parts * rows
    for head in range(heads):
        keys = rows_of(held, head * rows, rows)
        for source in range(sources):
            if source == 0:
                queries = rows_of(held, (heads + head) * rows, rows)
            else:
                queries = rows_of(sides[(source - 1) * parts : source * parts], head * rows, rows)
            flip = jnp.transpose(queries)
            top = None
            for first in range(0, slab, KEY_BLOCK):
                scores = jnp.dot(keys[first : first + KEY_BLOCK], flip, preferred_element_type=jnp.float32)
                score_ref[first : first + KEY_BLOCK] = scores
                part_top = jnp.max(scores.reshape(-1, 8, slab), axis=0)
                top = part_top if top is None else jnp.maximum(top, part_top)
            top = jnp.max(top, axis=0, keepdims=True) * SCALE_LOG2
            total = None
            for first in range(0, slab, KEY_BLOCK):
                powers = jnp.exp2(score_ref[first : first + KEY_BLOCK] * SCALE_LOG2 - top)
                part_total = jnp.sum(powers.reshape(-1, 8, slab), axis=0)
                total = part_total if total is None else total + part_total
            total = jnp.sum(total, axis=0, keepdims=True)
            outs[source][head : head + 1] = top + jnp.log(total) * (1.0 / math.log(2.0))


def partial_totals(pairs, side_queries, heads, rows):
    parts = len(pairs)
    sources = 1 + len(side_queries)
    slab = parts * rows
    return pl.pallas_call(
        functools.partial(totals_kernel, parts, sources, heads, rows),
        out_shape=[jax.ShapeDtypeStruct((heads, slab), jnp.float32)] * sources,
        scratch_shapes=[pltpu.VMEM((slab, slab), jnp.float32)],
        compiler_params=params(),
        cost_estimate=pl.CostEstimate(
            flops=2 * heads * sources * slab * slab * HD,
            bytes_accessed=heads * sources * slab * HD * 4,
            transcendentals=heads * sources * slab * slab,
        ),
    )(*pairs, *[piece for held in side_queries for piece in held])


def join_totals(values):
    top = functools.reduce(jnp.maximum, values)
    return top + jnp.log2(functools.reduce(jnp.add, [jnp.exp2(value - top) for value in values]))


def attention_kernel(parts, sources, head, rows, before, *refs):
    slab = parts * rows

    def take(count):
        nonlocal refs
        taken, refs = refs[:count], refs[count:]
        return taken

    key_refs, value_refs = take(parts), take(parts)
    query_refs, grad_refs, dots_refs = take(parts * sources), take(parts * sources), take(parts * sources)
    total_refs = take(sources)
    before_refs = take(sources) if before else ()
    piece_refs, query_grad_refs = take(parts), take(sources)
    weight_ref, score_ref = refs
    if before:
        closed = before_refs[0][...]
        for ref in before_refs[1:]:
            closed = closed + ref[...].astype(jnp.float32)
        closed = closed.astype(jnp.bfloat16)
        for part in range(parts):
            piece_refs[part][2 * rows :] = closed[part * rows : (part + 1) * rows]
    keys, values = rows_of(key_refs, 0, rows), rows_of(value_refs, 0, rows)
    queries, grads = rows_of(query_refs, 0, rows), rows_of(grad_refs, 0, rows)
    query_flip, grad_flip = jnp.transpose(queries), jnp.transpose(grads)
    lines = []
    for ref in dots_refs:
        terms = ref[...].astype(jnp.float32)
        for index in range(dot_groups(rows)):
            line = 2 * (head * dot_groups(rows) + index)
            count = min(LANES, rows - index * LANES)
            lines.append((terms[line : line + 1] + terms[line + 1 : line + 2])[:, :count])
    dots = jnp.concatenate(lines, axis=1)
    totals = jnp.concatenate([ref[head : head + 1] for ref in total_refs], axis=1)
    width = sources * slab
    for first in range(0, slab, KEY_BLOCK):
        stretch = slice(first, first + KEY_BLOCK)
        for start in range(0, width, QUERY_BLOCK):
            span = slice(start, start + QUERY_BLOCK)
            scores = jnp.dot(keys[stretch], query_flip[:, span], preferred_element_type=jnp.float32)
            weights = jnp.exp2(scores * SCALE_LOG2 - totals[:, span])
            grad_weights = jnp.dot(values[stretch], grad_flip[:, span], preferred_element_type=jnp.float32)
            weight_ref[stretch, span] = weights.astype(jnp.bfloat16)
            score_ref[stretch, span] = (weights * (grad_weights - dots[:, span])).astype(jnp.bfloat16)
        value_grad = jnp.dot(weight_ref[stretch], grads, preferred_element_type=jnp.float32)
        key_grad = jnp.dot(score_ref[stretch], queries, preferred_element_type=jnp.float32) * SCALE
        key_grad, value_grad = key_grad.astype(jnp.bfloat16), value_grad.astype(jnp.bfloat16)
        for part in range(parts):
            low, high = max(first, part * rows), min(first + KEY_BLOCK, (part + 1) * rows)
            if low < high:
                place = low - part * rows
                piece_refs[part][place : place + high - low] = key_grad[low - first : high - first]
                piece_refs[part][rows + place : rows + place + high - low] = value_grad[low - first : high - first]
    for source in range(sources):
        query_grad = lax.dot_general(
            score_ref[:, source * slab : (source + 1) * slab],
            keys,
            (((0,), (0,)), ((), ())),
            preferred_element_type=jnp.float32,
        )
        query_grad_refs[source][...] = (query_grad * SCALE).astype(query_grad_refs[source].dtype)


def attention(head, heads, rows, pairs, values, queries, grads, totals, before):
    parts = len(pairs)
    sources = len(queries)
    slab = parts * rows
    dots = dots_depth(rows, heads)

    def block(depth, index):
        return pl.BlockSpec((depth, HD), lambda step: (index, 0))

    flat_queries = [piece for held in queries for piece in held]
    flat_grads = [piece for held in grads for piece in held]
    operands = list(pairs) + list(values) + flat_queries + flat_grads + flat_grads + list(totals) + list(before)
    in_specs = [block(rows, head)] * (2 * parts)
    in_specs += [block(rows, heads + head)] * parts + [block(rows, head)] * (parts * (sources - 1))
    in_specs += [block(rows, head)] * (parts * sources) + [block(dots, heads * rows // dots)] * (parts * sources)
    in_specs += [pl.BlockSpec((heads, slab), lambda step: (0, 0))] * sources + [block(slab, 0)] * len(before)
    depth = (3 if before else 2) * rows
    outs = pl.pallas_call(
        functools.partial(attention_kernel, parts, sources, head, rows, bool(before)),
        grid=(1,),
        in_specs=in_specs,
        out_specs=[block(depth, 0)] * parts + [block(slab, 0)] * sources,
        out_shape=[jax.ShapeDtypeStruct((depth, HD), jnp.bfloat16)] * parts
        + [jax.ShapeDtypeStruct((slab, HD), jnp.float32)]
        + [jax.ShapeDtypeStruct((slab, HD), jnp.bfloat16)] * (sources - 1),
        scratch_shapes=[pltpu.VMEM((slab, sources * slab), jnp.bfloat16)] * 2,
        compiler_params=params(),
        cost_estimate=pl.CostEstimate(
            flops=10 * slab * sources * slab * HD,
            bytes_accessed=32 * slab * HD,
            transcendentals=slab * sources * slab,
        ),
    )(*operands)
    return outs[:parts], outs[parts:]


def close_kernel(parts, *refs):
    own_ref, side_refs, pieces = refs[0], refs[1:-parts], refs[-parts:]
    rows = pieces[0].shape[0]
    for part in range(parts):
        span = slice(part * rows, (part + 1) * rows)
        total = own_ref[span]
        for ref in side_refs:
            total = total + ref[span].astype(jnp.float32)
        pieces[part][...] = total.astype(jnp.bfloat16)


def close(query_grads, parts):
    rows = query_grads[0].shape[0] // parts
    return pl.pallas_call(
        functools.partial(close_kernel, parts),
        out_shape=[jax.ShapeDtypeStruct((rows, HD), jnp.bfloat16)] * parts,
        compiler_params=params(),
        cost_estimate=COST,
    )(*query_grads)


def unpack_kernel(parts, rows, heads, stages, *refs):
    count = parts * len(stages)
    pieces, outs, semaphores = refs[:count], refs[count:-1], refs[-1]
    pairs = []
    for number, blocks in enumerate(stages):
        for distance in range(parts):
            piece = pieces[number * parts + distance]
            for index, (output, head) in enumerate(blocks):
                columns = pl.ds(column_of(distance, heads, head), HD)
                pairs.append((piece.at[index * rows : (index + 1) * rows], outs[output].at[:, columns]))
    run_copies(pairs, semaphores)


def unpack(stages, pieces, rows, heads):
    parts = len(pieces[0])
    whole = pl.BlockSpec(memory_space=pl.ANY)
    channels = parts * heads * HD
    return pl.pallas_call(
        functools.partial(unpack_kernel, parts, rows, heads, stages),
        in_specs=[whole] * (parts * len(stages)),
        out_specs=[whole] * 3,
        out_shape=[jax.ShapeDtypeStruct((rows, channels), jnp.bfloat16)] * 3,
        scratch_shapes=[pltpu.SemaphoreType.DMA((3 * heads * parts,))],
        compiler_params=params(),
        cost_estimate=COST,
    )(*[piece for stage in pieces for piece in stage])


def swap(value, axis, distance):
    return lax.ppermute(value, axis, [(index, index ^ distance) for index in range(lax.axis_size(axis))])


def swap_pieces(pieces):
    return [pieces[0]] + [swap(piece, "ulysses", distance) for distance, piece in enumerate(pieces) if distance]


def total_of(value, axes):
    for axis in axes:
        size = lax.axis_size(axis)
        if size & (size - 1):
            value = lax.psum(value, axis)
            continue
        distance = 1
        while distance < size:
            value = value + swap(value, axis, distance)
            distance *= 2
    return value


def after(values, *earlier):
    return lax.optimization_barrier((list(values), earlier))[0]


def neighbours(size):
    if size == 1:
        return []
    if size == 2:
        swapped = [(0, 1), (1, 0)]
        return [(swapped, swapped)]
    up = [(index, index + 1) for index in range(size - 1)]
    down = [(index + 1, index) for index in range(size - 1)]
    return [(up, down), (down, up)]


def exchange_totals(partial, sides):
    if not sides:
        return partial
    if len(sides) == 1:
        other = lax.ppermute(jnp.concatenate(partial), "tm", sides[0][0])
        heads = partial[0].shape[0]
        return [join_totals([partial[0], other[heads:]]), join_totals([partial[1], other[:heads]])]
    position = lax.axis_index("tm")
    present = [position < lax.axis_size("tm") - 1, position > 0]
    values = [partial[0]]
    for value, (_, back), flag in zip(partial[1:], sides, present):
        values.append(jnp.where(flag, lax.ppermute(value, "tm", back), -jnp.inf))
    own = join_totals(values)
    return [own] + [lax.ppermute(own, "tm", there) for there, _ in sides]


def local(queries, keys, values, attn_out, out_grad, out_gain):
    parts = lax.axis_size("ulysses")
    span = lax.axis_size("tm")
    rows, channels = queries.shape[1:]
    heads = channels // (parts * HD)
    sides = neighbours(span)
    with jax.named_scope("keys_queries"):
        pairs = swap_pieces(pack([keys[0], queries[0]], parts))
    with jax.named_scope("halo_queries"):
        side_queries = [[lax.ppermute(piece[heads * rows :], "tm", there) for piece in pairs] for there, _ in sides]
    with jax.named_scope("grads"):
        sent, gain_part = pack_grads(out_grad[0], attn_out[0], out_gain, parts)
        held_grads = swap_pieces(after(sent, pairs))
    with jax.named_scope("halo_grads"):
        side_grads = [[lax.ppermute(piece, "tm", there) for piece in held_grads] for there, _ in sides]
    with jax.named_scope("values"):
        held_values = swap_pieces(after(pack([values[0]], parts), held_grads))
    token_count = rows * span * parts * lax.axis_size("dp")
    with jax.named_scope("gain"):
        gain_total = total_of(gain_part.reshape(-1, LANES), ("tm", "dp", "ulysses"))
        gain_grad = gain_total.reshape(channels) / token_count
    with jax.named_scope("totals"):
        part_totals = partial_totals(pairs, side_queries, heads, rows)
        totals = exchange_totals(after(part_totals, held_grads), sides)
    held_values = after(held_values, gain_total)
    stages, pieces = [], []
    before = ()
    for head in range(heads):
        with jax.named_scope("attention_%d" % head):
            leaving, query_grads = attention(
                head,
                heads,
                rows,
                pairs,
                held_values,
                [pairs] + side_queries,
                [held_grads] + side_grads,
                totals,
                before,
            )
        stages.append([(1, head), (2, head)] + ([(0, head - 1)] if head else []))
        if head:
            leaving, query_grads = lax.optimization_barrier((leaving, query_grads, pieces[-1][1:]))[:2]
        with jax.named_scope("halo_query_grads_%d" % head):
            before = list(query_grads[:1]) + [
                lax.ppermute(other, "tm", back) for other, (_, back) in zip(query_grads[1:], sides)
            ]
        with jax.named_scope("returns_%d" % head):
            pieces.append(swap_pieces(leaving))
    with jax.named_scope("returns_last"):
        stages.append([(0, heads - 1)])
        pieces.append(swap_pieces(close(before, parts)))
    result = unpack(stages, pieces, rows, heads)
    return tuple(grad[None] for grad in result) + (gain_grad,)


def solution(mesh):
    split = P("dp", ("tm", "ulysses"), None)
    return jax.shard_map(
        local,
        mesh=mesh,
        in_specs=(split,) * 5 + (P(),),
        out_specs=(split,) * 3 + (P(),),
        check_vma=False,
    )
```

time: 136 us -> 123 us (0.904)
  waiting for transfers between devices: 54.3 us -> 39.8 us
  starting transfers between devices: 52.3 us -> 62.3 us
  Pallas kernels: 21.7 us -> 16.6 us
  local copies, waits for them, and re-layouts: 5.42 us -> 2.88 us
    ppermute x29 -> x26, waiting for transfers between devices: 54.2 us -> 35.5 us  [swap(): lax.ppermute(value, axis, [(index, index ^ distance) for index in range(l...]
    ppermute x0 -> x5, starting transfers between devices: none -> 6.25 us  [the longest x4 5.65 us: local(): lax.ppermute(piece[heads * rows:], 'tm', there)]
    pallas_call x8, Pallas kernels: 20.2 us -> 15.1 us  [the longest x3 10.2 us: attention(): pl.pallas_call(functools.partial(attention_kernel, parts, sources, head,...]
    ppermute x29 -> x26, starting transfers between devices: 43.3 us -> 47.4 us  [swap(): lax.ppermute(value, axis, [(index, index ^ distance) for index in range(l...]
    ppermute x4, waiting for transfers between devices: 0.01 us -> 3.78 us  [local(): lax.ppermute(piece, 'tm', there)]
    unnamed x14 -> x10, local copies, waits for them, and re-layouts: 4.72 us -> 2.13 us
  transfers between devices with their start and end apart: 36 -> 38, of which waited for: 13 -> 15; matrix products, arithmetic and copies ran while one was open for 1% -> 1% of each run, Pallas kernels for 15% -> 9%
where the time goes in v3:
time: 123 us
  starting transfers between devices  62.3 us (51%)
  waiting for transfers between devices  39.8 us (32%)
  Pallas kernels  16.6 us (13%)
  local copies, waits for them, and re-layouts  2.88 us (2%)
    ppermute x26, starting transfers between devices, swap(): lax.ppermute(value, axis, [(index, index ^ distance) for index in range(l...  47.4 us
    ppermute x26, waiting for transfers between devices, swap(): lax.ppermute(value, axis, [(index, index ^ distance) for index in range(l...  35.5 us
    pallas_call x3, Pallas kernels, attention(): pl.pallas_call(functools.partial(attention_kernel, parts, sources, head,...  10.2 us
    ppermute x4, starting transfers between devices, local(): lax.ppermute(piece[heads * rows:], 'tm', there)  5.65 us
    ppermute x4, starting transfers between devices, local(): lax.ppermute(piece, 'tm', there)  4.86 us
    ppermute x4, waiting for transfers between devices, local(): lax.ppermute(piece, 'tm', there)  3.78 us
    ppermute x3, starting transfers between devices, local(): lax.ppermute(other, 'tm', back)  3.77 us
    pallas_call x1, Pallas kernels, partial_totals(): pl.pallas_call(functools.partial(totals_kernel, parts, sources, heads, ro...  3.6 us
  transfers between devices with their start and end apart: 38, of which 15 were waited for; matrix products, arithmetic and copies ran while one was open for 1% of the time, Pallas kernels for 9%

profile of v3, /device:TPU:0, one launch (start us, length us, event | category | flops | bytes accessed | tf_op | source)
XLA Modules:
  0.0 123.2 jit_solution(12251918839109048138)
XLA Ops:
  3.3 3.1 %collective-permute-start = (bf16[1152,128]{1,0:T(8,128)(2,1)S(1)}, bf16[1152,128]{1,0:T(8,128)(2,1)S(1)}, u32[]{:S(2)}, u32[]{:S(2)}) collective-permute-start(bf16[1152,128]{1,0:T(8,128)(2,1)S(1)} %get-tuple-element.71), channel_id=1, source_target_pairs={{0,4},{4,0},{8,12},{12,8},{1,5},{5,1},{9,13},{13,9},{2,6},{6,2},{1... | collective-permute-start | bytes 884744 | tf_op jit(solution)/shard_map/keys_queries/ppermute | solution.py:326
  6.4 2.6 %collective-permute-start.1 = (bf16[1152,128]{1,0:T(8,128)(2,1)S(1)}, bf16[1152,128]{1,0:T(8,128)(2,1)S(1)}, u32[]{:S(2)}, u32[]{:S(2)}) collective-permute-start(bf16[1152,128]{1,0:T(8,128)(2,1)S(1)} %get-tuple-element.72), channel_id=1, source_target_pairs={{0,8},{4,12},{8,0},{12,4},{1,9},{5,13},{9,1},{13,5},{2,10},{6,14},... | collective-permute-start | bytes 884744 | tf_op jit(solution)/shard_map/keys_queries/ppermute | solution.py:326
  15.7 3.2 %collective-permute-done.refs_1_.refs_9_ = bf16[1152,128]{1,0:T(8,128)(2,1)S(1)} collective-permute-done((bf16[1152,128]{1,0:T(8,128)(2,1)S(1)}, bf16[1152,128]{1,0:T(8,128)(2,1)S(1)}, u32[]{:S(2)}, u32[]{:S(2)}) %collective-permute-start) | collective-permute-done | bytes 294944 | tf_op jit(solution)/shard_map/keys_queries/ppermute | solution.py:326
  20.6 9.2 %collective-permute-done.1.refs_2_.refs_10_ = bf16[1152,128]{1,0:T(8,128)(2,1)S(1)} collective-permute-done((bf16[1152,128]{1,0:T(8,128)(2,1)S(1)}, bf16[1152,128]{1,0:T(8,128)(2,1)S(1)}, u32[]{:S(2)}, u32[]{:S(2)}) %collective-permute-start.1) | collective-permute-done | bytes 294944 | tf_op jit(solution)/shard_map/keys_queries/ppermute | solution.py:326
  33.5 2.1 %collective-permute-done.11 = f32[12,128]{1,0:T(8,128)S(1)} collective-permute-done((f32[12,128]{1,0:T(8,128)S(1)}, f32[12,128]{1,0:T(8,128)S(1)}, u32[]{:S(2)}, u32[]{:S(2)}) %collective-permute-start.11) | collective-permute-done | bytes 6176 | tf_op jit(solution)/shard_map/gain/ppermute | solution.py:326
  35.7 4.8 %collective-permute-start.12 = (f32[12,128]{1,0:T(8,128)S(1)}, f32[12,128]{1,0:T(8,128)S(1)}, u32[]{:S(2)}, u32[]{:S(2)}) collective-permute-start(f32[12,128]{1,0:T(8,128)S(1)} %add.29), channel_id=1, source_target_pairs={{0,4},{4,0},{8,12},{12,8},{1,5},{5,1},{9,13},{13,9},{2,6},{6,2},{1... | collective-permute-start | bytes 18440 | tf_op jit(solution)/shard_map/gain/ppermute | solution.py:326
  42.2 2.1 %collective-permute-start.3 = (bf16[592,128]{1,0:T(8,128)(2,1)S(1)}, bf16[592,128]{1,0:T(8,128)(2,1)S(1)}, u32[]{:S(2)}, u32[]{:S(2)}) collective-permute-start(bf16[592,128]{1,0:T(8,128)(2,1)S(1)} %get-tuple-element.83), channel_id=1, source_target_pairs={{0,4},{4,0},{8,12},{12,8},{1,5},{5,1},{9,13},{13,9},{2,6},{6,2},{1... | collective-permute-start | bytes 454664 | tf_op jit(solution)/shard_map/grads/ppermute | solution.py:326
  47.1 2.0 %collective-permute-start.13 = (f32[12,128]{1,0:T(8,128)S(1)}, f32[12,128]{1,0:T(8,128)S(1)}, u32[]{:S(2)}, u32[]{:S(2)}) collective-permute-start(f32[12,128]{1,0:T(8,128)S(1)} %add.30), channel_id=1, source_target_pairs={{0,8},{4,12},{8,0},{12,4},{1,9},{5,13},{9,1},{13,5},{2,10},{6,14},... | collective-permute-start | bytes 18440 | tf_op jit(solution)/shard_map/gain/ppermute | solution.py:326
  49.1 3.6 %totals.1 = (f32[3,768]{1,0:T(4,128)S(1)}, f32[3,768]{1,0:T(4,128)S(1)}) custom-call(bf16[1152,128]{1,0:T(8,128)(2,1)S(1)} %get-tuple-element.70.refs_0_.refs_8_, bf16[1152,128]{1,0:T(8,128)(2,1)S(1)} %collective-permute-done.refs_1_.refs_9_, bf16[1152,128]{1,0:T(8,128)(2,1)S(1)} %collective-permute-done.1.refs_2_.refs_10_, ...), custom_call_target="tpu_custom_call" | custom-call | flops 905969664 | bytes 2359296 | tf_op jit(solution)/shard_map/totals/pallas_call | solution.py:160
  52.7 2.7 %collective-permute-done.4.refs_18_.refs_26_ = bf16[592,128]{1,0:T(8,128)(2,1)S(1)} collective-permute-done((bf16[592,128]{1,0:T(8,128)(2,1)S(1)}, bf16[592,128]{1,0:T(8,128)(2,1)S(1)}, u32[]{:S(2)}, u32[]{:S(2)}) %collective-permute-start.4) | collective-permute-done | bytes 151584 | tf_op jit(solution)/shard_map/grads/ppermute | solution.py:326
  56.0 2.2 %collective-permute-start.6 = (bf16[576,128]{1,0:T(8,128)(2,1)S(1)}, bf16[576,128]{1,0:T(8,128)(2,1)S(1)}, u32[]{:S(2)}, u32[]{:S(2)}) collective-permute-start(bf16[576,128]{1,0:T(8,128)(2,1)S(1)} %get-tuple-element.87), channel_id=1, source_target_pairs={{0,4},{4,0},{8,12},{12,8},{1,5},{5,1},{9,13},{13,9},{2,6},{6,2},{1... | collective-permute-start | bytes 442376 | tf_op jit(solution)/shard_map/values/ppermute | solution.py:326
  64.9 5.8 %collective-permute-done.7.refs_6_ = bf16[576,128]{1,0:T(8,128)(2,1)S(1)} collective-permute-done((bf16[576,128]{1,0:T(8,128)(2,1)S(1)}, bf16[576,128]{1,0:T(8,128)(2,1)S(1)}, u32[]{:S(2)}, u32[]{:S(2)}) %collective-permute-start.7) | collective-permute-done | bytes 147488 | tf_op jit(solution)/shard_map/values/ppermute | solution.py:326
  72.5 3.4 %collective-permute-done.21.refs_23_.refs_31_ = bf16[592,128]{1,0:T(8,128)(2,1)S(1)} collective-permute-done((bf16[592,128]{1,0:T(8,128)(2,1)S(1)}, bf16[592,128]{1,0:T(8,128)(2,1)S(1)}, u32[]{:S(2)}, u32[]{:S(2)}) %collective-permute-start.21) | collective-permute-done | bytes 151584 | tf_op jit(solution)/shard_map/halo_grads/ppermute | solution.py:391
  75.9 3.3 %attention_0.1 = (bf16[384,128]{1,0:T(8,128)(2,1)S(1)}, bf16[384,128]{1,0:T(8,128)(2,1)S(1)}, bf16[384,128]{1,0:T(8,128)(2,1)S(1)}, bf16[384,128]{1,0:T(8,128)(2...) custom-call(bf16[1152,128]{1,0:T(8,128)(2,1)S(1)} %get-tuple-element.70.refs_0_.refs_8_, ...), custom_call_target="tpu_custom_call" | custom-call | flops 1509949440 | bytes 3145728 | tf_op jit(solution)/shard_map/attention_0/pallas_call | solution.py:257
  80.6 2.5 %collective-permute-start.24 = (bf16[384,128]{1,0:T(8,128)(2,1)S(1)}, bf16[384,128]{1,0:T(8,128)(2,1)S(1)}, u32[]{:S(2)}, u32[]{:S(2)}) collective-permute-start(bf16[384,128]{1,0:T(8,128)(2,1)S(1)} %get-tuple-element.101), channel_id=1, source_target_pairs={{0,8},{4,12},{8,0},{12,4},{1,9},{5,13},{9,1},{13,5},{2,10},{6,14},... | collective-permute-start | bytes 294920 | tf_op jit(solution)/shard_map/returns_0/ppermute | solution.py:326
  85.0 3.5 %attention_1.1 = (bf16[576,128]{1,0:T(8,128)(2,1)S(1)}, bf16[576,128]{1,0:T(8,128)(2,1)S(1)}, bf16[576,128]{1,0:T(8,128)(2,1)S(1)}, bf16[576,128]{1,0:T(8,128)(2...) custom-call(bf16[1152,128]{1,0:T(8,128)(2,1)S(1)} %get-tuple-element.70.refs_0_.refs_8_, ...), custom_call_target="tpu_custom_call" | custom-call | flops 1509949440 | bytes 3145728 | tf_op jit(solution)/shard_map/attention_1/pallas_call | solution.py:257
  88.6 2.1 %collective-permute-done.25.refs_3_ = bf16[384,128]{1,0:T(8,128)(2,1)S(1)} collective-permute-done((bf16[384,128]{1,0:T(8,128)(2,1)S(1)}, bf16[384,128]{1,0:T(8,128)(2,1)S(1)}, u32[]{:S(2)}, u32[]{:S(2)}) %collective-permute-start.25) | collective-permute-done | bytes 98336 | tf_op jit(solution)/shard_map/returns_0/ppermute | solution.py:326
  91.4 2.3 %collective-permute-start.28 = (bf16[576,128]{1,0:T(8,128)(2,1)S(1)}, bf16[576,128]{1,0:T(8,128)(2,1)S(1)}, u32[]{:S(2)}, u32[]{:S(2)}) collective-permute-start(bf16[576,128]{1,0:T(8,128)(2,1)S(1)} %get-tuple-element.113), channel_id=1, source_target_pairs={{0,8},{4,12},{8,0},{12,4},{1,9},{5,13},{9,1},{13,5},{2,10},{6,14},... | collective-permute-start | bytes 442376 | tf_op jit(solution)/shard_map/returns_1/ppermute | solution.py:326
  93.8 2.0 %collective-permute-start.29 = (bf16[576,128]{1,0:T(8,128)(2,1)S(1)}, bf16[576,128]{1,0:T(8,128)(2,1)S(1)}, u32[]{:S(2)}, u32[]{:S(2)}) collective-permute-start(bf16[576,128]{1,0:T(8,128)(2,1)S(1)} %get-tuple-element.114), channel_id=1, source_target_pairs={{0,12},{4,8},{8,4},{12,0},{1,13},{5,9},{9,5},{13,1},{2,14},{6,10},... | collective-permute-start | bytes 442376 | tf_op jit(solution)/shard_map/returns_1/ppermute | solution.py:326
  96.3 3.3 %attention_2.1 = (bf16[576,128]{1,0:T(8,128)(2,1)S(1)}, bf16[576,128]{1,0:T(8,128)(2,1)S(1)}, bf16[576,128]{1,0:T(8,128)(2,1)S(1)}, bf16[576,128]{1,0:T(8,128)(2...) custom-call(bf16[1152,128]{1,0:T(8,128)(2,1)S(1)} %get-tuple-element.70.refs_0_.refs_8_, ...), custom_call_target="tpu_custom_call" | custom-call | flops 1509949440 | bytes 3145728 | tf_op jit(solution)/shard_map/attention_2/pallas_call | solution.py:257
  103.0 6.6 %collective-permute-start.31 = (bf16[576,128]{1,0:T(8,128)(2,1)S(1)}, bf16[576,128]{1,0:T(8,128)(2,1)S(1)}, u32[]{:S(2)}, u32[]{:S(2)}) collective-permute-start(bf16[576,128]{1,0:T(8,128)(2,1)S(1)} %get-tuple-element.124), channel_id=1, source_target_pairs={{0,4},{4,0},{8,12},{12,8},{1,5},{5,1},{9,13},{13,9},{2,6},{6,2},{1... | collective-permute-start | bytes 442376 | tf_op jit(solution)/shard_map/returns_2/ppermute | solution.py:326
  109.5 2.4 %collective-permute-start.33 = (bf16[576,128]{1,0:T(8,128)(2,1)S(1)}, bf16[576,128]{1,0:T(8,128)(2,1)S(1)}, u32[]{:S(2)}, u32[]{:S(2)}) collective-permute-start(bf16[576,128]{1,0:T(8,128)(2,1)S(1)} %get-tuple-element.126), channel_id=1, source_target_pairs={{0,12},{4,8},{8,4},{12,0},{1,13},{5,9},{9,5},{13,1},{2,14},{6,10},... | collective-permute-start | bytes 442376 | tf_op jit(solution)/shard_map/returns_2/ppermute | solution.py:326
  112.0 2.1 %collective-permute-start.35 = (bf16[192,128]{1,0:T(8,128)(2,1)S(1)}, bf16[192,128]{1,0:T(8,128)(2,1)S(1)}, u32[]{:S(2)}, u32[]{:S(2)}) collective-permute-start(bf16[192,128]{1,0:T(8,128)(2,1)S(1)} %get-tuple-element.130), channel_id=1, source_target_pairs={{0,4},{4,0},{8,12},{12,8},{1,5},{5,1},{9,13},{13,9},{2,6},{6,2},{1... | collective-permute-start | bytes 147464 | tf_op jit(solution)/shard_map/returns_last/ppermute | solution.py:326
  118.9 2.7 %collective-permute-done.36.refs_14_ = bf16[192,128]{1,0:T(8,128)(2,1)S(1)} collective-permute-done((bf16[192,128]{1,0:T(8,128)(2,1)S(1)}, bf16[192,128]{1,0:T(8,128)(2,1)S(1)}, u32[]{:S(2)}, u32[]{:S(2)}) %collective-permute-start.36) | collective-permute-done | bytes 49184 | tf_op jit(solution)/shard_map/returns_last/ppermute | solution.py:326
  (84 shorter events, 42.6 us)
Async XLA Ops:
  3.3 15.6 %collective-permute-start = (bf16[1152,128]{1,0:T(8,128)(2,1)S(1)}, bf16[1152,128]{1,0:T(8,128)(2,1)S(1)}, u32[]{:S(2)}, u32[]{:S(2)}) collective-permute-start(bf16[1152,128]{1,0:T(8,128)(2,1)S(1)} %get-tuple-element.71), channel_id=1, source_target_pairs={{0,4},{4,0},{8,12},{12,8},{1,5},{5,1},{9,13},{13,9},{2,6},{6,2},{1... | collective-permute-start | bytes 884744 | tf_op jit(solution)/shard_map/keys_queries/ppermute | solution.py:326
  6.4 23.5 %collective-permute-start.1 = (bf16[1152,128]{1,0:T(8,128)(2,1)S(1)}, bf16[1152,128]{1,0:T(8,128)(2,1)S(1)}, u32[]{:S(2)}, u32[]{:S(2)}) collective-permute-start(bf16[1152,128]{1,0:T(8,128)(2,1)S(1)} %get-tuple-element.72), channel_id=1, source_target_pairs={{0,8},{4,12},{8,0},{12,4},{1,9},{5,13},{9,1},{13,5},{2,10},{6,14},... | collective-permute-start | bytes 884744 | tf_op jit(solution)/shard_map/keys_queries/ppermute | solution.py:326
  8.9 22.5 %collective-permute-start.2 = (bf16[1152,128]{1,0:T(8,128)(2,1)S(1)}, bf16[1152,128]{1,0:T(8,128)(2,1)S(1)}, u32[]{:S(2)}, u32[]{:S(2)}) collective-permute-start(bf16[1152,128]{1,0:T(8,128)(2,1)S(1)} %get-tuple-element.73), channel_id=1, source_target_pairs={{0,12},{4,8},{8,4},{12,0},{1,13},{5,9},{9,5},{13,1},{2,14},{6,10},... | collective-permute-start | bytes 884744 | tf_op jit(solution)/shard_map/keys_queries/ppermute | solution.py:326
  13.9 18.1 %collective-permute-start.10 = (f32[12,128]{1,0:T(8,128)S(1)}, f32[12,128]{1,0:T(8,128)S(1)}, u32[]{:S(2)}, u32[]{:S(2)}) collective-permute-start(f32[12,128]{1,0:T(8,128)S(1)} %bitcast_add_fusion), channel_id=1, source_target_pairs={{0,1},{1,0},{2,3},{3,2},{4,5},{5,4},{6,7},{7,6},{8,9},{9,8},{10,11... | collective-permute-start | bytes 18440 | tf_op jit(solution)/shard_map/gain/ppermute | solution.py:326
  13.9 30.3 %collective-permute-start.14 = (bf16[576,128]{1,0:T(8,128)(2,1)S(1)}, bf16[576,128]{1,0:T(8,128)(2,1)S(1)}, u32[]{:S(2)}, u32[]{:S(2)}) collective-permute-start(bf16[576,128]{1,0:T(8,128)(2,1)S(1)} %slice.18), channel_id=1, source_target_pairs={{0,16},{16,0},{1,17},{17,1},{2,18},{18,2},{3,19},{19,3},{4,20},{20... | collective-permute-start | bytes 442376 | tf_op jit(solution)/shard_map/halo_queries/ppermute | solution.py:386
  18.9 26.3 %collective-permute-start.15 = (bf16[576,128]{1,0:T(8,128)(2,1)S(1)}, bf16[576,128]{1,0:T(8,128)(2,1)S(1)}, u32[]{:S(2)}, u32[]{:S(2)}) collective-permute-start(bf16[576,128]{1,0:T(8,128)(2,1)S(1)} %slice.24), channel_id=1, source_target_pairs={{0,16},{16,0},{1,17},{17,1},{2,18},{18,2},{3,19},{19,3},{4,20},{20... | collective-permute-start | bytes 442376 | tf_op jit(solution)/shard_map/halo_queries/ppermute | solution.py:386
  29.8 17.2 %collective-permute-start.16 = (bf16[576,128]{1,0:T(8,128)(2,1)S(1)}, bf16[576,128]{1,0:T(8,128)(2,1)S(1)}, u32[]{:S(2)}, u32[]{:S(2)}) collective-permute-start(bf16[576,128]{1,0:T(8,128)(2,1)S(1)} %slice.25), channel_id=1, source_target_pairs={{0,16},{16,0},{1,17},{17,1},{2,18},{18,2},{3,19},{19,3},{4,20},{20... | collective-permute-start | bytes 442376 | tf_op jit(solution)/shard_map/halo_queries/ppermute | solution.py:386
  31.4 17.7 %collective-permute-start.17 = (bf16[576,128]{1,0:T(8,128)(2,1)S(1)}, bf16[576,128]{1,0:T(8,128)(2,1)S(1)}, u32[]{:S(2)}, u32[]{:S(2)}) collective-permute-start(bf16[576,128]{1,0:T(8,128)(2,1)S(1)} %slice.26), channel_id=1, source_target_pairs={{0,16},{16,0},{1,17},{17,1},{2,18},{18,2},{3,19},{19,3},{4,20},{20... | collective-permute-start | bytes 442376 | tf_op jit(solution)/shard_map/halo_queries/ppermute | solution.py:386
  42.2 10.5 %collective-permute-start.3 = (bf16[592,128]{1,0:T(8,128)(2,1)S(1)}, bf16[592,128]{1,0:T(8,128)(2,1)S(1)}, u32[]{:S(2)}, u32[]{:S(2)}) collective-permute-start(bf16[592,128]{1,0:T(8,128)(2,1)S(1)} %get-tuple-element.83), channel_id=1, source_target_pairs={{0,4},{4,0},{8,12},{12,8},{1,5},{5,1},{9,13},{13,9},{2,6},{6,2},{1... | collective-permute-start | bytes 454664 | tf_op jit(solution)/shard_map/grads/ppermute | solution.py:326
  44.2 11.2 %collective-permute-start.4 = (bf16[592,128]{1,0:T(8,128)(2,1)S(1)}, bf16[592,128]{1,0:T(8,128)(2,1)S(1)}, u32[]{:S(2)}, u32[]{:S(2)}) collective-permute-start(bf16[592,128]{1,0:T(8,128)(2,1)S(1)} %get-tuple-element.84), channel_id=1, source_target_pairs={{0,8},{4,12},{8,0},{12,4},{1,9},{5,13},{9,1},{13,5},{2,10},{6,14},... | collective-permute-start | bytes 454664 | tf_op jit(solution)/shard_map/grads/ppermute | solution.py:326
  45.3 10.2 %collective-permute-start.5 = (bf16[592,128]{1,0:T(8,128)(2,1)S(1)}, bf16[592,128]{1,0:T(8,128)(2,1)S(1)}, u32[]{:S(2)}, u32[]{:S(2)}) collective-permute-start(bf16[592,128]{1,0:T(8,128)(2,1)S(1)} %get-tuple-element.85), channel_id=1, source_target_pairs={{0,12},{4,8},{8,4},{12,0},{1,13},{5,9},{9,5},{13,1},{2,14},{6,10},... | collective-permute-start | bytes 454664 | tf_op jit(solution)/shard_map/grads/ppermute | solution.py:326
  47.1 12.2 %collective-permute-start.13 = (f32[12,128]{1,0:T(8,128)S(1)}, f32[12,128]{1,0:T(8,128)S(1)}, u32[]{:S(2)}, u32[]{:S(2)}) collective-permute-start(f32[12,128]{1,0:T(8,128)S(1)} %add.30), channel_id=1, source_target_pairs={{0,8},{4,12},{8,0},{12,4},{1,9},{5,13},{9,1},{13,5},{2,10},{6,14},... | collective-permute-start | bytes 18440 | tf_op jit(solution)/shard_map/gain/ppermute | solution.py:326
  58.2 12.4 %collective-permute-start.7 = (bf16[576,128]{1,0:T(8,128)(2,1)S(1)}, bf16[576,128]{1,0:T(8,128)(2,1)S(1)}, u32[]{:S(2)}, u32[]{:S(2)}) collective-permute-start(bf16[576,128]{1,0:T(8,128)(2,1)S(1)} %get-tuple-element.88), channel_id=1, source_target_pairs={{0,8},{4,12},{8,0},{12,4},{1,9},{5,13},{9,1},{13,5},{2,10},{6,14},... | collective-permute-start | bytes 442376 | tf_op jit(solution)/shard_map/values/ppermute | solution.py:326
  59.9 12.2 %collective-permute-start.18 = (bf16[592,128]{1,0:T(8,128)(2,1)S(1)}, bf16[592,128]{1,0:T(8,128)(2,1)S(1)}, u32[]{:S(2)}, u32[]{:S(2)}) collective-permute-start(bf16[592,128]{1,0:T(8,128)(2,1)S(1)} %get-tuple-element.82.refs_16_.refs_24_), channel_id=1, source_target_pairs={{0,16},{16,0},{1,17},{17,1},{2,18},{18,2},{3,19},{19,3},{4,20},{20... | collective-permute-start | bytes 454664 | tf_op jit(solution)/shard_map/halo_grads/ppermute | solution.py:391
  61.4 10.7 %collective-permute-start.8 = (bf16[576,128]{1,0:T(8,128)(2,1)S(1)}, bf16[576,128]{1,0:T(8,128)(2,1)S(1)}, u32[]{:S(2)}, u32[]{:S(2)}) collective-permute-start(bf16[576,128]{1,0:T(8,128)(2,1)S(1)} %get-tuple-element.89), channel_id=1, source_target_pairs={{0,12},{4,8},{8,4},{12,0},{1,13},{5,9},{9,5},{13,1},{2,14},{6,10},... | collective-permute-start | bytes 442376 | tf_op jit(solution)/shard_map/values/ppermute | solution.py:326
  62.8 9.2 %collective-permute-start.19 = (bf16[592,128]{1,0:T(8,128)(2,1)S(1)}, bf16[592,128]{1,0:T(8,128)(2,1)S(1)}, u32[]{:S(2)}, u32[]{:S(2)}) collective-permute-start(bf16[592,128]{1,0:T(8,128)(2,1)S(1)} %collective-permute-done.3.refs_17_.refs_25_), channel_id=1, source_target_pairs={{0,16},{16,0},{1,17},{17,1},{2,18},{18,2},{3,19},{19,3},{4,20},{20... | collective-permute-start | bytes 454664 | tf_op jit(solution)/shard_map/halo_grads/ppermute | solution.py:391
  63.4 9.1 %collective-permute-start.20 = (bf16[592,128]{1,0:T(8,128)(2,1)S(1)}, bf16[592,128]{1,0:T(8,128)(2,1)S(1)}, u32[]{:S(2)}, u32[]{:S(2)}) collective-permute-start(bf16[592,128]{1,0:T(8,128)(2,1)S(1)} %collective-permute-done.4.refs_18_.refs_26_), channel_id=1, source_target_pairs={{0,16},{16,0},{1,17},{17,1},{2,18},{18,2},{3,19},{19,3},{4,20},{20... | collective-permute-start | bytes 454664 | tf_op jit(solution)/shard_map/halo_grads/ppermute | solution.py:391
  80.6 8.0 %collective-permute-start.24 = (bf16[384,128]{1,0:T(8,128)(2,1)S(1)}, bf16[384,128]{1,0:T(8,128)(2,1)S(1)}, u32[]{:S(2)}, u32[]{:S(2)}) collective-permute-start(bf16[384,128]{1,0:T(8,128)(2,1)S(1)} %get-tuple-element.101), channel_id=1, source_target_pairs={{0,8},{4,12},{8,0},{12,4},{1,9},{5,13},{9,1},{13,5},{2,10},{6,14},... | collective-permute-start | bytes 294920 | tf_op jit(solution)/shard_map/returns_0/ppermute | solution.py:326
  91.4 8.2 %collective-permute-start.27 = (bf16[576,128]{1,0:T(8,128)(2,1)S(1)}, bf16[576,128]{1,0:T(8,128)(2,1)S(1)}, u32[]{:S(2)}, u32[]{:S(2)}) collective-permute-start(bf16[576,128]{1,0:T(8,128)(2,1)S(1)} %get-tuple-element.112), channel_id=1, source_target_pairs={{0,4},{4,0},{8,12},{12,8},{1,5},{5,1},{9,13},{13,9},{2,6},{6,2},{1... | collective-permute-start | bytes 442376 | tf_op jit(solution)/shard_map/returns_1/ppermute | solution.py:326
  91.4 8.2 %collective-permute-start.28 = (bf16[576,128]{1,0:T(8,128)(2,1)S(1)}, bf16[576,128]{1,0:T(8,128)(2,1)S(1)}, u32[]{:S(2)}, u32[]{:S(2)}) collective-permute-start(bf16[576,128]{1,0:T(8,128)(2,1)S(1)} %get-tuple-element.113), channel_id=1, source_target_pairs={{0,8},{4,12},{8,0},{12,4},{1,9},{5,13},{9,1},{13,5},{2,10},{6,14},... | collective-permute-start | bytes 442376 | tf_op jit(solution)/shard_map/returns_1/ppermute | solution.py:326
  101.4 10.5 %collective-permute-start.34 = (bf16[768,128]{1,0:T(8,128)(2,1)S(1)}, bf16[768,128]{1,0:T(8,128)(2,1)S(1)}, u32[]{:S(2)}, u32[]{:S(2)}) collective-permute-start(bf16[768,128]{1,0:T(8,128)(2,1)S(1)} %get-tuple-element.128), channel_id=1, source_target_pairs={{0,16},{16,0},{1,17},{17,1},{2,18},{18,2},{3,19},{19,3},{4,20},{20... | collective-permute-start | bytes 589832 | tf_op jit(solution)/shard_map/halo_query_grads_2/ppermute | solution.py:422
  103.0 11.9 %collective-permute-start.31 = (bf16[576,128]{1,0:T(8,128)(2,1)S(1)}, bf16[576,128]{1,0:T(8,128)(2,1)S(1)}, u32[]{:S(2)}, u32[]{:S(2)}) collective-permute-start(bf16[576,128]{1,0:T(8,128)(2,1)S(1)} %get-tuple-element.124), channel_id=1, source_target_pairs={{0,4},{4,0},{8,12},{12,8},{1,5},{5,1},{9,13},{13,9},{2,6},{6,2},{1... | collective-permute-start | bytes 442376 | tf_op jit(solution)/shard_map/returns_2/ppermute | solution.py:326
  109.5 8.9 %collective-permute-start.32 = (bf16[576,128]{1,0:T(8,128)(2,1)S(1)}, bf16[576,128]{1,0:T(8,128)(2,1)S(1)}, u32[]{:S(2)}, u32[]{:S(2)}) collective-permute-start(bf16[576,128]{1,0:T(8,128)(2,1)S(1)} %get-tuple-element.125), channel_id=1, source_target_pairs={{0,8},{4,12},{8,0},{12,4},{1,9},{5,13},{9,1},{13,5},{2,10},{6,14},... | collective-permute-start | bytes 442376 | tf_op jit(solution)/shard_map/returns_2/ppermute | solution.py:326
  109.5 8.9 %collective-permute-start.33 = (bf16[576,128]{1,0:T(8,128)(2,1)S(1)}, bf16[576,128]{1,0:T(8,128)(2,1)S(1)}, u32[]{:S(2)}, u32[]{:S(2)}) collective-permute-start(bf16[576,128]{1,0:T(8,128)(2,1)S(1)} %get-tuple-element.126), channel_id=1, source_target_pairs={{0,12},{4,8},{8,4},{12,0},{1,13},{5,9},{9,5},{13,1},{2,14},{6,10},... | collective-permute-start | bytes 442376 | tf_op jit(solution)/shard_map/returns_2/ppermute | solution.py:326
  (19 other events, 138.2 us)

commit v4 on v3

--- a/solution.py
+++ b/solution.py
@@ -41,36 +41,59 @@
         copy.wait()
 
 
-def pack_kernel(parts, *refs):
+def pack_kernel(parts, chosen, *refs):
     sources, pieces, semaphores = refs[: -parts - 1], refs[-parts - 1 : -1], refs[-1]
     rows, channels = sources[0].shape
     heads = channels // (parts * HD)
     pairs = []
     for distance in range(parts):
         for half, ref in enumerate(sources):
-            for head in range(heads):
+            for place, head in enumerate(chosen):
                 columns = pl.ds(column_of(distance, heads, head), HD)
-                start = (half * heads + head) * rows
+                start = (half * len(chosen) + place) * rows
                 pairs.append((ref.at[:, columns], pieces[distance].at[start : start + rows]))
     run_copies(pairs, semaphores)
 
 
-def pack(sources, parts):
-    rows, channels = sources[0].shape
-    heads = channels // (parts * HD)
-    depth = len(sources) * heads * rows
+def pack(sources, parts, chosen):
+    rows = sources[0].shape[0]
+    depth = len(sources) * len(chosen) * rows
     whole = pl.BlockSpec(memory_space=pl.ANY)
     return pl.pallas_call(
-        functools.partial(pack_kernel, parts),
+        functools.partial(pack_kernel, parts, chosen),
         in_specs=[whole] * len(sources),
         out_specs=[whole] * parts,
         out_shape=[jax.ShapeDtypeStruct((depth, HD), sources[0].dtype)] * parts,
-        scratch_shapes=[pltpu.SemaphoreType.DMA((len(sources) * heads * parts,))],
+        scratch_shapes=[pltpu.SemaphoreType.DMA((len(sources) * len(chosen) * parts,))],
         compiler_params=params(),
         cost_estimate=COST,
     )(*sources)
 
 
+def gather_kernel(ranges, *refs):
+    arrays, out_ref, semaphores = refs[:-2], refs[-2], refs[-1]
+    pairs = []
+    place = 0
+    for number, first, count in ranges:
+        pairs.append((arrays[number].at[first : first + count], out_ref.at[place : place + count]))
+        place += count
+    run_copies(pairs, semaphores)
+
+
+def gather_rows(arrays, ranges):
+    whole = pl.BlockSpec(memory_space=pl.ANY)
+    depth = sum(count for _, _, count in ranges)
+    return pl.pallas_call(
+        functools.partial(gather_kernel, ranges),
+        in_specs=[whole] * len(arrays),
+        out_specs=whole,
+        out_shape=jax.ShapeDtypeStruct((depth, HD), arrays[0].dtype),
+        scratch_shapes=[pltpu.SemaphoreType.DMA((len(ranges),))],
+        compiler_params=params(),
+        cost_estimate=COST,
+    )(*arrays)
+
+
 def dot_groups(rows):
     return -(-rows // LANES)
 
@@ -79,11 +102,11 @@
     return -(-2 * heads * dot_groups(rows) // TILE_ROWS) * TILE_ROWS
 
 
-def pack_grads_kernel(parts, out_grad_ref, attn_ref, gain_ref, *refs):
-    pieces, gain_part_ref = refs[:-1], refs[-1]
+def pack_grads_kernel(parts, out_grad_ref, attn_ref, value_ref, gain_ref, *refs):
+    leads, rests, gain_part_ref = refs[:parts], refs[parts:-1], refs[-1]
     rows, channels = out_grad_ref.shape
     heads = channels // (parts * HD)
-    for distance, piece in enumerate(pieces):
+    for distance in range(parts):
         terms = []
         for head in range(heads):
             columns = pl.ds(column_of(distance, heads, head), HD)
@@ -91,7 +114,11 @@
             attn = attn_ref[:, columns].astype(jnp.float32)
             grad = (out_grad * gain_ref[:, columns]).astype(jnp.bfloat16)
             gain_part_ref[:, columns] = jnp.sum(out_grad * attn, axis=0, keepdims=True)
-            piece[head * rows : (head + 1) * rows] = grad
+            if head:
+                rests[distance][(head - 1) * rows : head * rows] = grad
+            else:
+                leads[distance][:rows] = grad
+                leads[distance][rows : 2 * rows] = value_ref[:, columns]
             dots = jnp.sum(jnp.transpose(grad.astype(jnp.float32) * attn), axis=0, keepdims=True)
             for first in range(0, rows, LANES):
                 value = dots[:, first : first + LANES]
@@ -103,40 +130,44 @@
         rest = dots_depth(rows, heads) - len(terms)
         if rest:
             terms.append(jnp.zeros((rest, LANES), jnp.float32))
-        piece[heads * rows :] = jnp.concatenate(terms, axis=0).astype(jnp.bfloat16)
-
-
-def pack_grads(out_grad, attn_out, out_gain, parts):
+        leads[distance][2 * rows :] = jnp.concatenate(terms, axis=0).astype(jnp.bfloat16)
+
+
+def pack_grads(out_grad, attn_out, values, out_gain, parts):
     rows, channels = out_grad.shape
     heads = channels // (parts * HD)
-    depth = heads * rows + dots_depth(rows, heads)
+    lead = jax.ShapeDtypeStruct((2 * rows + dots_depth(rows, heads), HD), jnp.bfloat16)
+    rest = jax.ShapeDtypeStruct(((heads - 1) * rows, HD), jnp.bfloat16)
     outs = pl.pallas_call(
         functools.partial(pack_grads_kernel, parts),
-        out_shape=[jax.ShapeDtypeStruct((depth, HD), jnp.bfloat16)] * parts
-        + [jax.ShapeDtypeStruct((1, channels), jnp.float32)],
+        out_shape=[lead] * parts + [rest] * parts + [jax.ShapeDtypeStruct((1, channels), jnp.float32)],
         compiler_params=params(),
         cost_estimate=COST,
-    )(out_grad, attn_out, out_gain.reshape(1, channels))
-    return outs[:parts], outs[parts]
-
-
-def rows_of(refs, first, count):
-    return jnp.concatenate([ref[first : first + count] for ref in refs], axis=0)
-
-
-def totals_kernel(parts, sources, heads, rows, *refs):
-    held, refs = refs[:parts], refs[parts:]
-    sides, refs = refs[: parts * (sources - 1)], refs[parts * (sources - 1) :]
+    )(out_grad, attn_out, values, out_gain.reshape(1, channels))
+    return outs[:parts], outs[parts : 2 * parts], outs[2 * parts]
+
+
+def stacked(refs):
+    return jnp.concatenate([ref[...] for ref in refs], axis=0)
+
+
+def block_specs(depth, places):
+    def block(index):
+        return pl.BlockSpec((depth, HD), lambda step: (index, 0))
+
+    return [block(index) for _, index in places], [array for array, _ in places]
+
+
+def totals_kernel(parts, sources, heads, *refs):
+    key_refs, refs = refs[: parts * heads], refs[parts * heads :]
+    query_refs, refs = refs[: parts * heads * sources], refs[parts * heads * sources :]
     outs, score_ref = refs[:sources], refs[sources]
-    slab = parts * rows
+    slab = score_ref.shape[0]
     for head in range(heads):
-        keys = rows_of(held, head * rows, rows)
+        keys = stacked(key_refs[head * parts : (head + 1) * parts])
         for source in range(sources):
-            if source == 0:
-                queries = rows_of(held, (heads + head) * rows, rows)
-            else:
-                queries = rows_of(sides[(source - 1) * parts : source * parts], head * rows, rows)
-            flip = jnp.transpose(queries)
+            start = (source * heads + head) * parts
+            flip = jnp.transpose(stacked(query_refs[start : start + parts]))
             top = None
             for first in range(0, slab, KEY_BLOCK):
                 scores = jnp.dot(keys[first : first + KEY_BLOCK], flip, preferred_element_type=jnp.float32)
@@ -153,12 +184,18 @@
             outs[source][head : head + 1] = top + jnp.log(total) * (1.0 / math.log(2.0))
 
 
-def partial_totals(pairs, side_queries, heads, rows):
-    parts = len(pairs)
-    sources = 1 + len(side_queries)
+def partial_totals(keys, queries, rows):
+    heads, parts, sources = len(keys), len(keys[0]), len(queries)
     slab = parts * rows
+    places = [place for head in keys for place in head]
+    places += [place for source in queries for head in source for place in head]
+    in_specs, operands = block_specs(rows, places)
+    line = pl.BlockSpec((heads, slab), lambda step: (0, 0))
     return pl.pallas_call(
-        functools.partial(totals_kernel, parts, sources, heads, rows),
+        functools.partial(totals_kernel, parts, sources, heads),
+        grid=(1,),
+        in_specs=in_specs,
+        out_specs=[line] * sources,
         out_shape=[jax.ShapeDtypeStruct((heads, slab), jnp.float32)] * sources,
         scratch_shapes=[pltpu.VMEM((slab, slab), jnp.float32)],
         compiler_params=params(),
@@ -167,7 +204,7 @@
             bytes_accessed=heads * sources * slab * HD * 4,
             transcendentals=heads * sources * slab * slab,
         ),
-    )(*pairs, *[piece for held in side_queries for piece in held])
+    )(*operands)
 
 
 def join_totals(values):
@@ -196,8 +233,7 @@
         closed = closed.astype(jnp.bfloat16)
         for part in range(parts):
             piece_refs[part][2 * rows :] = closed[part * rows : (part + 1) * rows]
-    keys, values = rows_of(key_refs, 0, rows), rows_of(value_refs, 0, rows)
-    queries, grads = rows_of(query_refs, 0, rows), rows_of(grad_refs, 0, rows)
+    keys, values, queries, grads = stacked(key_refs), stacked(value_refs), stacked(query_refs), stacked(grad_refs)
     query_flip, grad_flip = jnp.transpose(queries), jnp.transpose(grads)
     lines = []
     for ref in dots_refs:
@@ -237,28 +273,22 @@
         query_grad_refs[source][...] = (query_grad * SCALE).astype(query_grad_refs[source].dtype)
 
 
-def attention(head, heads, rows, pairs, values, queries, grads, totals, before):
-    parts = len(pairs)
-    sources = len(queries)
+def attention(head, heads, rows, keys, values, queries, grads, dots, totals, before):
+    parts = len(keys)
+    sources = len(totals)
     slab = parts * rows
-    dots = dots_depth(rows, heads)
-
-    def block(depth, index):
-        return pl.BlockSpec((depth, HD), lambda step: (index, 0))
-
-    flat_queries = [piece for held in queries for piece in held]
-    flat_grads = [piece for held in grads for piece in held]
-    operands = list(pairs) + list(values) + flat_queries + flat_grads + flat_grads + list(totals) + list(before)
-    in_specs = [block(rows, head)] * (2 * parts)
-    in_specs += [block(rows, heads + head)] * parts + [block(rows, head)] * (parts * (sources - 1))
-    in_specs += [block(rows, head)] * (parts * sources) + [block(dots, heads * rows // dots)] * (parts * sources)
-    in_specs += [pl.BlockSpec((heads, slab), lambda step: (0, 0))] * sources + [block(slab, 0)] * len(before)
+    in_specs, operands = block_specs(rows, keys + values + queries + grads)
+    dot_specs, dot_arrays = block_specs(dots_depth(rows, heads), dots)
+    before_specs, before_arrays = block_specs(slab, [(array, 0) for array in before])
+    line = pl.BlockSpec((heads, slab), lambda step: (0, 0))
     depth = (3 if before else 2) * rows
+    out_specs, _ = block_specs(depth, [(None, 0)] * parts)
+    query_specs, _ = block_specs(slab, [(None, 0)] * sources)
     outs = pl.pallas_call(
         functools.partial(attention_kernel, parts, sources, head, rows, bool(before)),
         grid=(1,),
-        in_specs=in_specs,
-        out_specs=[block(depth, 0)] * parts + [block(slab, 0)] * sources,
+        in_specs=in_specs + dot_specs + [line] * sources + before_specs,
+        out_specs=out_specs + query_specs,
         out_shape=[jax.ShapeDtypeStruct((depth, HD), jnp.bfloat16)] * parts
         + [jax.ShapeDtypeStruct((slab, HD), jnp.float32)]
         + [jax.ShapeDtypeStruct((slab, HD), jnp.bfloat16)] * (sources - 1),
@@ -269,7 +299,7 @@
             bytes_accessed=32 * slab * HD,
             transcendentals=slab * sources * slab,
         ),
-    )(*operands)
+    )(*operands, *dot_arrays, *totals, *before_arrays)
     return outs[:parts], outs[parts:]
 
 
@@ -330,17 +360,18 @@
     return [pieces[0]] + [swap(piece, "ulysses", distance) for distance, piece in enumerate(pieces) if distance]
 
 
-def total_of(value, axes):
+def sum_steps(axes):
+    steps = []
     for axis in axes:
         size = lax.axis_size(axis)
         if size & (size - 1):
-            value = lax.psum(value, axis)
+            steps.append(functools.partial(lax.psum, axis_name=axis))
             continue
         distance = 1
         while distance < size:
-            value = value + swap(value, axis, distance)
+            steps.append(lambda value, axis=axis, distance=distance: value + swap(value, axis, distance))
             distance *= 2
-    return value
+    return steps
 
 
 def after(values, *earlier):
@@ -379,55 +410,108 @@
     span = lax.axis_size("tm")
     rows, channels = queries.shape[1:]
     heads = channels // (parts * HD)
+    rest = list(range(1, heads))
+    dots = dots_depth(rows, heads)
+    every = list(range(parts))
     sides = neighbours(span)
+
+    def forward(array):
+        return [lax.ppermute(array, "tm", there) for there, _ in sides]
+
     with jax.named_scope("keys_queries"):
-        pairs = swap_pieces(pack([keys[0], queries[0]], parts))
+        packed = pack([keys[0], queries[0]], parts, list(range(heads)))
+        pairs = swap_pieces(packed)
+    with jax.named_scope("grads"):
+        out_grad = after([out_grad], packed[0])[0]
+        sent_lead, sent_rest, gain_part = pack_grads(out_grad[0], attn_out[0], values[0], out_gain, parts)
+    token_count = rows * span * parts * lax.axis_size("dp")
+    gain = gain_part.reshape(-1, LANES)
+    steps = sum_steps(("tm", "dp", "ulysses"))
+
+    def advance(value, count=1):
+        with jax.named_scope("gain"):
+            for step in steps[:count]:
+                value = step(value)
+        del steps[:count]
+        return value
+
+    gain = advance(gain, max(1, len(steps) - 4))
     with jax.named_scope("halo_queries"):
-        side_queries = [[lax.ppermute(piece[heads * rows :], "tm", there) for piece in pairs] for there, _ in sides]
-    with jax.named_scope("grads"):
-        sent, gain_part = pack_grads(out_grad[0], attn_out[0], out_gain, parts)
-        held_grads = swap_pieces(after(sent, pairs))
-    with jax.named_scope("halo_grads"):
-        side_grads = [[lax.ppermute(piece, "tm", there) for piece in held_grads] for there, _ in sides]
-    with jax.named_scope("values"):
-        held_values = swap_pieces(after(pack([values[0]], parts), held_grads))
-    token_count = rows * span * parts * lax.axis_size("dp")
-    with jax.named_scope("gain"):
-        gain_total = total_of(gain_part.reshape(-1, LANES), ("tm", "dp", "ulysses"))
-        gain_grad = gain_total.reshape(channels) / token_count
+        width = heads * rows
+        first_side = forward(pairs[0][width:])
+        late = after(pairs[1:], gain, first_side)
+        late_side = forward(gather_rows(late, [(number, width, width) for number in range(parts - 1)]))
+    with jax.named_scope("first_grads"):
+        lead = swap_pieces(after(sent_lead, late))
+    with jax.named_scope("halo_first_grads"):
+        ranges = [(part, 0, rows) for part in every] + [(part, 2 * rows, dots) for part in every]
+        lead_side = forward(gather_rows(lead, ranges))
     with jax.named_scope("totals"):
-        part_totals = partial_totals(pairs, side_queries, heads, rows)
-        totals = exchange_totals(after(part_totals, held_grads), sides)
-    held_values = after(held_values, gain_total)
-    stages, pieces = [], []
-    before = ()
+        key_places = [[(piece, head) for piece in pairs] for head in range(heads)]
+        query_places = [[[(piece, heads + head) for piece in pairs] for head in range(heads)]]
+        for first, others in zip(first_side, late_side):
+            query_places.append(
+                [
+                    [(first, head)] + [(others, (part - 1) * heads + head) for part in every[1:]]
+                    for head in range(heads)
+                ]
+            )
+        part_totals = partial_totals(key_places, query_places, rows)
+        totals = exchange_totals(part_totals, sides)
+    gain = advance(after([gain], late)[0], 2)
+    with jax.named_scope("rest_grads"):
+        rest_grads = swap_pieces(after(sent_rest, lead, gain))
+    with jax.named_scope("halo_rest_grads"):
+        ranges = [(part, place * rows, rows) for place in range(heads - 1) for part in every]
+        rest_side = forward(gather_rows(rest_grads, ranges))
+    with jax.named_scope("rest_values"):
+        rest_values = swap_pieces(after(pack([values[0]], parts, rest), rest_grads, part_totals))
+    dot_places = [(piece, 2 * rows // dots) for piece in lead]
+    dot_places += [(array, parts * rows // dots + part) for array in lead_side for part in every]
+    stages, pieces, open_grads = [], [], []
+    gate = rest_values[1:]
     for head in range(heads):
+        if head == 0:
+            value_places = [(piece, 1) for piece in lead]
+            grad_places = [(piece, 0) for piece in lead] + [(array, part) for array in lead_side for part in every]
+        else:
+            value_places = [(piece, head - 1) for piece in rest_values]
+            grad_places = [(piece, head - 1) for piece in rest_grads]
+            grad_places += [(array, (head - 1) * parts + part) for array in rest_side for part in every]
+        final = head == heads - 1
+        before = open_grads if head else ()
         with jax.named_scope("attention_%d" % head):
             leaving, query_grads = attention(
                 head,
                 heads,
                 rows,
-                pairs,
-                held_values,
-                [pairs] + side_queries,
-                [held_grads] + side_grads,
+                key_places[head],
+                value_places,
+                [place for source in query_places for place in source[head]],
+                grad_places,
+                dot_places,
                 totals,
                 before,
             )
-        stages.append([(1, head), (2, head)] + ([(0, head - 1)] if head else []))
-        if head:
-            leaving, query_grads = lax.optimization_barrier((leaving, query_grads, pieces[-1][1:]))[:2]
+        stages.append([(1, head), (2, head)] + ([(0, head - 1)] if before else []))
+        leaving, query_grads = lax.optimization_barrier((leaving, query_grads, gate))[:2]
         with jax.named_scope("halo_query_grads_%d" % head):
-            before = list(query_grads[:1]) + [
-                lax.ppermute(other, "tm", back) for other, (_, back) in zip(query_grads[1:], sides)
-            ]
+            back_grads = [lax.ppermute(other, "tm", back) for other, (_, back) in zip(query_grads[1:], sides)]
+            open_grads = list(query_grads[:1]) + back_grads
         with jax.named_scope("returns_%d" % head):
             pieces.append(swap_pieces(leaving))
+        gate = pieces[-1][1:]
+        if not final:
+            ready = after([gain], gate)[0]
+            if head:
+                gate = gate + [gain]
+            gain = advance(ready)
     with jax.named_scope("returns_last"):
         stages.append([(0, heads - 1)])
-        pieces.append(swap_pieces(close(before, parts)))
+        pieces.append(swap_pieces(close(open_grads, parts)))
     result = unpack(stages, pieces, rows, heads)
-    return tuple(grad[None] for grad in result) + (gain_grad,)
+    gain = advance(gain, len(steps)).reshape(channels) / token_count
+    return tuple(grad[None] for grad in result) + (gain,)
 
 
 def solution(mesh):

time: 123 us -> 122 us (level)
  starting transfers between devices: 62.3 us -> 56.6 us
  waiting for transfers between devices: 39.8 us -> 41.6 us
  Pallas kernels: 16.6 us -> 18.1 us
    ppermute x8 -> x4, starting transfers between devices: 10.5 us -> 4.09 us  [forward(): return [lax.ppermute(array, 'tm', there) for there, _ in sides]]
    ppermute x26 -> x29, waiting for transfers between devices: 35.5 us -> 37.9 us  [swap(): lax.ppermute(value, axis, [(index, index ^ distance) for index in range(l...]
    pallas_call x4 -> x7, Pallas kernels: 4.84 us -> 6.46 us  [the longest x1 3.6 us: partial_totals(): pl.pallas_call(functools.partial(totals_kernel, parts, sources, heads), g...]
    ppermute x26 -> x29, starting transfers between devices: 47.4 us -> 48.3 us  [swap(): lax.ppermute(value, axis, [(index, index ^ distance) for index in range(l...]
    ppermute x8 -> x4, waiting for transfers between devices: 3.79 us -> 3.72 us  [forward(): return [lax.ppermute(array, 'tm', there) for there, _ in sides]]
  transfers between devices with their start and end apart: 38 -> 37, of which waited for: 15 -> 14; matrix products, arithmetic and copies ran while one was open for 1% -> 1% of each run, Pallas kernels for 9% -> 13%
where the time goes in v4:
time: 122 us
  starting transfers between devices  56.6 us (46%)
  waiting for transfers between devices  41.6 us (34%)
  Pallas kernels  18.1 us (15%)
  local copies, waits for them, and re-layouts  3.9 us (3%)
    ppermute x29, starting transfers between devices, swap(): lax.ppermute(value, axis, [(index, index ^ distance) for index in range(l...  48.3 us
    ppermute x29, waiting for transfers between devices, swap(): lax.ppermute(value, axis, [(index, index ^ distance) for index in range(l...  37.9 us
    pallas_call x3, Pallas kernels, attention(): pl.pallas_call(functools.partial(attention_kernel, parts, sources, head,...  10.1 us
    ppermute x4, starting transfers between devices, forward(): return [lax.ppermute(array, 'tm', there) for there, _ in sides]  4.09 us
    ppermute x4, waiting for transfers between devices, forward(): return [lax.ppermute(array, 'tm', there) for there, _ in sides]  3.72 us
    pallas_call x1, Pallas kernels, partial_totals(): pl.pallas_call(functools.partial(totals_kernel, parts, sources, heads), g...  3.6 us
    ppermute x3, starting transfers between devices, local(): lax.ppermute(other, 'tm', back)  3.52 us
    unnamed x10, local copies, waits for them, and re-layouts  3.19 us
  transfers between devices with their start and end apart: 37, of which 14 were waited for; matrix products, arithmetic and copies ran while one was open for 1% of the time, Pallas kernels for 13%

profile of v4, /device:TPU:0, one launch (start us, length us, event | category | flops | bytes accessed | tf_op | source)
XLA Modules:
  0.0 121.8 jit_solution(7501705785107645691)
XLA Ops:
  3.3 3.1 %collective-permute-start = (bf16[1152,128]{1,0:T(8,128)(2,1)S(1)}, bf16[1152,128]{1,0:T(8,128)(2,1)S(1)}, u32[]{:S(2)}, u32[]{:S(2)}) collective-permute-start(bf16[1152,128]{1,0:T(8,128)(2,1)S(1)} %get-tuple-element.86), channel_id=1, source_target_pairs={{0,4},{4,0},{8,12},{12,8},{1,5},{5,1},{9,13},{13,9},{2,6},{6,2},{1... | collective-permute-start | bytes 884744 | tf_op jit(solution)/shard_map/keys_queries/ppermute | solution.py:356
  6.4 2.6 %collective-permute-start.1 = (bf16[1152,128]{1,0:T(8,128)(2,1)S(1)}, bf16[1152,128]{1,0:T(8,128)(2,1)S(1)}, u32[]{:S(2)}, u32[]{:S(2)}) collective-permute-start(bf16[1152,128]{1,0:T(8,128)(2,1)S(1)} %get-tuple-element.87), channel_id=1, source_target_pairs={{0,8},{4,12},{8,0},{12,4},{1,9},{5,13},{9,1},{13,5},{2,10},{6,14},... | collective-permute-start | bytes 884744 | tf_op jit(solution)/shard_map/keys_queries/ppermute | solution.py:356
  11.3 1.8 %collective-permute-start.3 = (f32[12,128]{1,0:T(8,128)S(1)}, f32[12,128]{1,0:T(8,128)S(1)}, u32[]{:S(2)}, u32[]{:S(2)}) collective-permute-start(f32[12,128]{1,0:T(8,128)S(1)} %bitcast.18), channel_id=1, source_target_pairs={{0,16},{16,0},{1,17},{17,1},{2,18},{18,2},{3,19},{19,3},{4,20},{20... | collective-permute-start | bytes 18440 | tf_op jit(solution)/shard_map/gain/ppermute | solution.py:356
  15.0 3.3 %collective-permute-done.4.refs_24_.refs_28_.refs_32_.refs_12_ = bf16[576,128]{1,0:T(8,128)(2,1)S(1)} collective-permute-done((bf16[576,128]{1,0:T(8,128)(2,1)S(1)}, bf16[576,128]{1,0:T(8,128)(2,1)S(1)}, u32[]{:S(2)}, u32[]{:S(2)}) %collective-permute-start.4) | collective-permute-done | bytes 147488 | tf_op jit(solution)/shard_map/halo_queries/ppermute | solution.py:419
  18.9 10.9 %collective-permute-done.1.refs_1_.refs_2_.refs_6_.refs_10_.refs_14_.refs_18_.refs_22_ = bf16[1152,128]{1,0:T(8,128)(2,1)S(1)} collective-permute-done((bf16[1152,128]{1,0:T(8,128)(2,1)S(1)}, bf16[1152,128]{1,0:T(8,128)(2,1)S(1)}, u32[]{:S(2)}, u32[]{:S(2)}) %collective-permute-start.1) | collective-permute-done | bytes 294944 | tf_op jit(solution)/shard_map/keys_queries/ppermute | solution.py:356
  32.0 5.4 %collective-permute-start.5 = (bf16[400,128]{1,0:T(8,128)(2,1)S(1)}, bf16[400,128]{1,0:T(8,128)(2,1)S(1)}, u32[]{:S(2)}, u32[]{:S(2)}) collective-permute-start(bf16[400,128]{1,0:T(8,128)(2,1)S(1)} %get-tuple-element.99), channel_id=1, source_target_pairs={{0,4},{4,0},{8,12},{12,8},{1,5},{5,1},{9,13},{13,9},{2,6},{6,2},{1... | collective-permute-start | bytes 307208 | tf_op jit(solution)/shard_map/first_grads/ppermute | solution.py:356
  42.6 2.1 %collective-permute-done.12 = f32[12,128]{1,0:T(8,128)S(1)} collective-permute-done((f32[12,128]{1,0:T(8,128)S(1)}, f32[12,128]{1,0:T(8,128)S(1)}, u32[]{:S(2)}, u32[]{:S(2)}) %collective-permute-start.12) | collective-permute-done | bytes 6176 | tf_op jit(solution)/shard_map/gain/ppermute | solution.py:356
  44.7 2.0 %collective-permute-done.6.refs_2_.refs_6_.refs_18_.refs_26_ = bf16[400,128]{1,0:T(8,128)(2,1)S(1)} collective-permute-done((bf16[400,128]{1,0:T(8,128)(2,1)S(1)}, bf16[400,128]{1,0:T(8,128)(2,1)S(1)}, u32[]{:S(2)}, u32[]{:S(2)}) %collective-permute-start.6) | collective-permute-done | bytes 102432 | tf_op jit(solution)/shard_map/first_grads/ppermute | solution.py:356
  49.4 1.7 %collective-permute-start.15 = (bf16[384,128]{1,0:T(8,128)(2,1)S(1)}, bf16[384,128]{1,0:T(8,128)(2,1)S(1)}, u32[]{:S(2)}, u32[]{:S(2)}) collective-permute-start(bf16[384,128]{1,0:T(8,128)(2,1)S(1)} %get-tuple-element.122), channel_id=1, source_target_pairs={{0,12},{4,8},{8,4},{12,0},{1,13},{5,9},{9,5},{13,1},{2,14},{6,10},... | collective-permute-start | bytes 294920 | tf_op jit(solution)/shard_map/rest_grads/ppermute | solution.py:356
  51.1 3.6 %totals.1 = (f32[3,768]{1,0:T(4,128)S(1)}, f32[3,768]{1,0:T(4,128)S(1)}) custom-call(bf16[1152,128]{1,0:T(8,128)(2,1)S(1)} %get-tuple-element.85.refs_0_.refs_4_.refs_8_.refs_12_.refs_16_.refs_20_, bf16[1152,128]{1,0:T(8,128)(2,1)S(1)} %collective-permute-done.refs_0_.refs_1_.refs_5_.refs_9_.refs_13_.refs_17_.refs_21_, ...), custom_call_target="tpu_custom_call" | custom-call | flops 905969664 | bytes 2359296 | tf_op jit(solution)/shard_map/totals/pallas_call | solution.py:194
  64.2 3.3 %attention_0.1 = (bf16[384,128]{1,0:T(8,128)(2,1)S(1)}, bf16[384,128]{1,0:T(8,128)(2,1)S(1)}, bf16[384,128]{1,0:T(8,128)(2,1)S(1)}, bf16[384,128]{1,0:T(8,128)(2...) custom-call(bf16[1152,128]{1,0:T(8,128)(2,1)S(1)} %get-tuple-element.85.refs_0_.refs_4_.refs_8_.refs_12_.refs_16_.refs_20_, ...), custom_call_target="tpu_custom_call" | custom-call | flops 1509949440 | bytes 3145728 | tf_op jit(solution)/shard_map/attention_0/pallas_call | solution.py:287
  67.5 2.7 %collective-permute-done.17.refs_6_ = bf16[384,128]{1,0:T(8,128)(2,1)S(1)} collective-permute-done((bf16[384,128]{1,0:T(8,128)(2,1)S(1)}, bf16[384,128]{1,0:T(8,128)(2,1)S(1)}, u32[]{:S(2)}, u32[]{:S(2)}) %collective-permute-start.17) | collective-permute-done | bytes 98336 | tf_op jit(solution)/shard_map/rest_values/ppermute | solution.py:356
  76.1 3.4 %attention_1.1 = (bf16[576,128]{1,0:T(8,128)(2,1)S(1)}, bf16[576,128]{1,0:T(8,128)(2,1)S(1)}, bf16[576,128]{1,0:T(8,128)(2,1)S(1)}, bf16[576,128]{1,0:T(8,128)(2...) custom-call(bf16[1152,128]{1,0:T(8,128)(2,1)S(1)} %get-tuple-element.85.refs_0_.refs_4_.refs_8_.refs_12_.refs_16_.refs_20_, ...), custom_call_target="tpu_custom_call" | custom-call | flops 1509949440 | bytes 3145728 | tf_op jit(solution)/shard_map/attention_1/pallas_call | solution.py:287
  79.5 3.1 %collective-permute-done.20.refs_2_ = bf16[384,128]{1,0:T(8,128)(2,1)S(1)} collective-permute-done((bf16[384,128]{1,0:T(8,128)(2,1)S(1)}, bf16[384,128]{1,0:T(8,128)(2,1)S(1)}, u32[]{:S(2)}, u32[]{:S(2)}) %collective-permute-start.20) | collective-permute-done | bytes 98336 | tf_op jit(solution)/shard_map/returns_0/ppermute | solution.py:356
  85.2 2.5 %collective-permute-start.25 = (bf16[576,128]{1,0:T(8,128)(2,1)S(1)}, bf16[576,128]{1,0:T(8,128)(2,1)S(1)}, u32[]{:S(2)}, u32[]{:S(2)}) collective-permute-start(bf16[576,128]{1,0:T(8,128)(2,1)S(1)} %get-tuple-element.141), channel_id=1, source_target_pairs={{0,8},{4,12},{8,0},{12,4},{1,9},{5,13},{9,1},{13,5},{2,10},{6,14},... | collective-permute-start | bytes 442376 | tf_op jit(solution)/shard_map/returns_1/ppermute | solution.py:356
  89.2 3.4 %attention_2.1 = (bf16[576,128]{1,0:T(8,128)(2,1)S(1)}, bf16[576,128]{1,0:T(8,128)(2,1)S(1)}, bf16[576,128]{1,0:T(8,128)(2,1)S(1)}, bf16[576,128]{1,0:T(8,128)(2...) custom-call(bf16[1152,128]{1,0:T(8,128)(2,1)S(1)} %get-tuple-element.85.refs_0_.refs_4_.refs_8_.refs_12_.refs_16_.refs_20_, ...), custom_call_target="tpu_custom_call" | custom-call | flops 1509949440 | bytes 3145728 | tf_op jit(solution)/shard_map/attention_2/pallas_call | solution.py:287
  92.6 5.4 %collective-permute-done.25.refs_6_ = bf16[576,128]{1,0:T(8,128)(2,1)S(1)} collective-permute-done((bf16[576,128]{1,0:T(8,128)(2,1)S(1)}, bf16[576,128]{1,0:T(8,128)(2,1)S(1)}, u32[]{:S(2)}, u32[]{:S(2)}) %collective-permute-start.25) | collective-permute-done | bytes 147488 | tf_op jit(solution)/shard_map/returns_1/ppermute | solution.py:356
  99.5 2.1 %collective-permute-start.29 = (bf16[576,128]{1,0:T(8,128)(2,1)S(1)}, bf16[576,128]{1,0:T(8,128)(2,1)S(1)}, u32[]{:S(2)}, u32[]{:S(2)}) collective-permute-start(bf16[576,128]{1,0:T(8,128)(2,1)S(1)} %get-tuple-element.153), channel_id=1, source_target_pairs={{0,4},{4,0},{8,12},{12,8},{1,5},{5,1},{9,13},{13,9},{2,6},{6,2},{1... | collective-permute-start | bytes 442376 | tf_op jit(solution)/shard_map/returns_2/ppermute | solution.py:356
  102.6 1.9 %collective-permute-start.30 = (bf16[576,128]{1,0:T(8,128)(2,1)S(1)}, bf16[576,128]{1,0:T(8,128)(2,1)S(1)}, u32[]{:S(2)}, u32[]{:S(2)}) collective-permute-start(bf16[576,128]{1,0:T(8,128)(2,1)S(1)} %get-tuple-element.154), channel_id=1, source_target_pairs={{0,8},{4,12},{8,0},{12,4},{1,9},{5,13},{9,1},{13,5},{2,10},{6,14},... | collective-permute-start | bytes 442376 | tf_op jit(solution)/shard_map/returns_2/ppermute | solution.py:356
  104.6 2.4 %collective-permute-start.31 = (bf16[576,128]{1,0:T(8,128)(2,1)S(1)}, bf16[576,128]{1,0:T(8,128)(2,1)S(1)}, u32[]{:S(2)}, u32[]{:S(2)}) collective-permute-start(bf16[576,128]{1,0:T(8,128)(2,1)S(1)} %get-tuple-element.155), channel_id=1, source_target_pairs={{0,12},{4,8},{8,4},{12,0},{1,13},{5,9},{9,5},{13,1},{2,14},{6,10},... | collective-permute-start | bytes 442376 | tf_op jit(solution)/shard_map/returns_2/ppermute | solution.py:356
  107.2 2.3 %collective-permute-start.34 = (bf16[192,128]{1,0:T(8,128)(2,1)S(1)}, bf16[192,128]{1,0:T(8,128)(2,1)S(1)}, u32[]{:S(2)}, u32[]{:S(2)}) collective-permute-start(bf16[192,128]{1,0:T(8,128)(2,1)S(1)} %get-tuple-element.160), channel_id=1, source_target_pairs={{0,8},{4,12},{8,0},{12,4},{1,9},{5,13},{9,1},{13,5},{2,10},{6,14},... | collective-permute-start | bytes 147464 | tf_op jit(solution)/shard_map/returns_last/ppermute | solution.py:356
  109.4 2.4 %collective-permute-start.35 = (bf16[192,128]{1,0:T(8,128)(2,1)S(1)}, bf16[192,128]{1,0:T(8,128)(2,1)S(1)}, u32[]{:S(2)}, u32[]{:S(2)}) collective-permute-start(bf16[192,128]{1,0:T(8,128)(2,1)S(1)} %get-tuple-element.161), channel_id=1, source_target_pairs={{0,12},{4,8},{8,4},{12,0},{1,13},{5,9},{9,5},{13,1},{2,14},{6,10},... | collective-permute-start | bytes 147464 | tf_op jit(solution)/shard_map/returns_last/ppermute | solution.py:356
  112.5 4.8 %collective-permute-done.30.refs_10_ = bf16[576,128]{1,0:T(8,128)(2,1)S(1)} collective-permute-done((bf16[576,128]{1,0:T(8,128)(2,1)S(1)}, bf16[576,128]{1,0:T(8,128)(2,1)S(1)}, u32[]{:S(2)}, u32[]{:S(2)}) %collective-permute-start.30) | collective-permute-done | bytes 147488 | tf_op jit(solution)/shard_map/returns_2/ppermute | solution.py:356
  117.2 2.9 %collective-permute-done.34.refs_14_ = bf16[192,128]{1,0:T(8,128)(2,1)S(1)} collective-permute-done((bf16[192,128]{1,0:T(8,128)(2,1)S(1)}, bf16[192,128]{1,0:T(8,128)(2,1)S(1)}, u32[]{:S(2)}, u32[]{:S(2)}) %collective-permute-start.34) | collective-permute-done | bytes 49184 | tf_op jit(solution)/shard_map/returns_last/ppermute | solution.py:356
  (82 shorter events, 41.5 us)
Async XLA Ops:
  3.3 15.6 %collective-permute-start = (bf16[1152,128]{1,0:T(8,128)(2,1)S(1)}, bf16[1152,128]{1,0:T(8,128)(2,1)S(1)}, u32[]{:S(2)}, u32[]{:S(2)}) collective-permute-start(bf16[1152,128]{1,0:T(8,128)(2,1)S(1)} %get-tuple-element.86), channel_id=1, source_target_pairs={{0,4},{4,0},{8,12},{12,8},{1,5},{5,1},{9,13},{13,9},{2,6},{6,2},{1... | collective-permute-start | bytes 884744 | tf_op jit(solution)/shard_map/keys_queries/ppermute | solution.py:356
  6.4 23.5 %collective-permute-start.1 = (bf16[1152,128]{1,0:T(8,128)(2,1)S(1)}, bf16[1152,128]{1,0:T(8,128)(2,1)S(1)}, u32[]{:S(2)}, u32[]{:S(2)}) collective-permute-start(bf16[1152,128]{1,0:T(8,128)(2,1)S(1)} %get-tuple-element.87), channel_id=1, source_target_pairs={{0,8},{4,12},{8,0},{12,4},{1,9},{5,13},{9,1},{13,5},{2,10},{6,14},... | collective-permute-start | bytes 884744 | tf_op jit(solution)/shard_map/keys_queries/ppermute | solution.py:356
  8.9 20.9 %collective-permute-start.2 = (bf16[1152,128]{1,0:T(8,128)(2,1)S(1)}, bf16[1152,128]{1,0:T(8,128)(2,1)S(1)}, u32[]{:S(2)}, u32[]{:S(2)}) collective-permute-start(bf16[1152,128]{1,0:T(8,128)(2,1)S(1)} %get-tuple-element.88), channel_id=1, source_target_pairs={{0,12},{4,8},{8,4},{12,0},{1,13},{5,9},{9,5},{13,1},{2,14},{6,10},... | collective-permute-start | bytes 884744 | tf_op jit(solution)/shard_map/keys_queries/ppermute | solution.py:356
  30.4 20.7 %collective-permute-start.8 = (bf16[1728,128]{1,0:T(8,128)(2,1)S(1)}, bf16[1728,128]{1,0:T(8,128)(2,1)S(1)}, u32[]{:S(2)}, u32[]{:S(2)}) collective-permute-start(bf16[1728,128]{1,0:T(8,128)(2,1)S(1)} %halo_queries.1), channel_id=1, source_target_pairs={{0,16},{16,0},{1,17},{17,1},{2,18},{18,2},{3,19},{19,3},{4,20},{20... | collective-permute-start | bytes 1327112 | tf_op jit(solution)/shard_map/halo_queries/ppermute | solution.py:419
  32.0 12.8 %collective-permute-start.5 = (bf16[400,128]{1,0:T(8,128)(2,1)S(1)}, bf16[400,128]{1,0:T(8,128)(2,1)S(1)}, u32[]{:S(2)}, u32[]{:S(2)}) collective-permute-start(bf16[400,128]{1,0:T(8,128)(2,1)S(1)} %get-tuple-element.99), channel_id=1, source_target_pairs={{0,4},{4,0},{8,12},{12,8},{1,5},{5,1},{9,13},{13,9},{2,6},{6,2},{1... | collective-permute-start | bytes 307208 | tf_op jit(solution)/shard_map/first_grads/ppermute | solution.py:356
  37.4 9.3 %collective-permute-start.6 = (bf16[400,128]{1,0:T(8,128)(2,1)S(1)}, bf16[400,128]{1,0:T(8,128)(2,1)S(1)}, u32[]{:S(2)}, u32[]{:S(2)}) collective-permute-start(bf16[400,128]{1,0:T(8,128)(2,1)S(1)} %get-tuple-element.100), channel_id=1, source_target_pairs={{0,8},{4,12},{8,0},{12,4},{1,9},{5,13},{9,1},{13,5},{2,10},{6,14},... | collective-permute-start | bytes 307208 | tf_op jit(solution)/shard_map/first_grads/ppermute | solution.py:356
  38.4 8.3 %collective-permute-start.7 = (bf16[400,128]{1,0:T(8,128)(2,1)S(1)}, bf16[400,128]{1,0:T(8,128)(2,1)S(1)}, u32[]{:S(2)}, u32[]{:S(2)}) collective-permute-start(bf16[400,128]{1,0:T(8,128)(2,1)S(1)} %get-tuple-element.101), channel_id=1, source_target_pairs={{0,12},{4,8},{8,4},{12,0},{1,13},{5,9},{9,5},{13,1},{2,14},{6,10},... | collective-permute-start | bytes 307208 | tf_op jit(solution)/shard_map/first_grads/ppermute | solution.py:356
  46.7 10.7 %collective-permute-start.13 = (bf16[384,128]{1,0:T(8,128)(2,1)S(1)}, bf16[384,128]{1,0:T(8,128)(2,1)S(1)}, u32[]{:S(2)}, u32[]{:S(2)}) collective-permute-start(bf16[384,128]{1,0:T(8,128)(2,1)S(1)} %get-tuple-element.120), channel_id=1, source_target_pairs={{0,4},{4,0},{8,12},{12,8},{1,5},{5,1},{9,13},{13,9},{2,6},{6,2},{1... | collective-permute-start | bytes 294920 | tf_op jit(solution)/shard_map/rest_grads/ppermute | solution.py:356
  48.4 9.5 %collective-permute-start.14 = (bf16[384,128]{1,0:T(8,128)(2,1)S(1)}, bf16[384,128]{1,0:T(8,128)(2,1)S(1)}, u32[]{:S(2)}, u32[]{:S(2)}) collective-permute-start(bf16[384,128]{1,0:T(8,128)(2,1)S(1)} %get-tuple-element.121), channel_id=1, source_target_pairs={{0,8},{4,12},{8,0},{12,4},{1,9},{5,13},{9,1},{13,5},{2,10},{6,14},... | collective-permute-start | bytes 294920 | tf_op jit(solution)/shard_map/rest_grads/ppermute | solution.py:356
  49.4 8.5 %collective-permute-start.15 = (bf16[384,128]{1,0:T(8,128)(2,1)S(1)}, bf16[384,128]{1,0:T(8,128)(2,1)S(1)}, u32[]{:S(2)}, u32[]{:S(2)}) collective-permute-start(bf16[384,128]{1,0:T(8,128)(2,1)S(1)} %get-tuple-element.122), channel_id=1, source_target_pairs={{0,12},{4,8},{8,4},{12,0},{1,13},{5,9},{9,5},{13,1},{2,14},{6,10},... | collective-permute-start | bytes 294920 | tf_op jit(solution)/shard_map/rest_grads/ppermute | solution.py:356
  55.9 8.3 %collective-permute-start.9 = (bf16[832,128]{1,0:T(8,128)(2,1)S(1)}, bf16[832,128]{1,0:T(8,128)(2,1)S(1)}, u32[]{:S(2)}, u32[]{:S(2)}) collective-permute-start(bf16[832,128]{1,0:T(8,128)(2,1)S(1)} %halo_first_grads.1), channel_id=1, source_target_pairs={{0,16},{16,0},{1,17},{17,1},{2,18},{18,2},{3,19},{19,3},{4,20},{20... | collective-permute-start | bytes 638984 | tf_op jit(solution)/shard_map/halo_first_grads/ppermute | solution.py:419
  58.7 17.4 %collective-permute-start.22 = (bf16[1536,128]{1,0:T(8,128)(2,1)S(1)}, bf16[1536,128]{1,0:T(8,128)(2,1)S(1)}, u32[]{:S(2)}, u32[]{:S(2)}) collective-permute-start(bf16[1536,128]{1,0:T(8,128)(2,1)S(1)} %halo_rest_grads.1), channel_id=1, source_target_pairs={{0,16},{16,0},{1,17},{17,1},{2,18},{18,2},{3,19},{19,3},{4,20},{20... | collective-permute-start | bytes 1179656 | tf_op jit(solution)/shard_map/halo_rest_grads/ppermute | solution.py:419
  60.9 9.3 %collective-permute-start.17 = (bf16[384,128]{1,0:T(8,128)(2,1)S(1)}, bf16[384,128]{1,0:T(8,128)(2,1)S(1)}, u32[]{:S(2)}, u32[]{:S(2)}) collective-permute-start(bf16[384,128]{1,0:T(8,128)(2,1)S(1)} %get-tuple-element.124), channel_id=1, source_target_pairs={{0,8},{4,12},{8,0},{12,4},{1,9},{5,13},{9,1},{13,5},{2,10},{6,14},... | collective-permute-start | bytes 294920 | tf_op jit(solution)/shard_map/rest_values/ppermute | solution.py:356
  61.9 8.3 %collective-permute-start.18 = (bf16[384,128]{1,0:T(8,128)(2,1)S(1)}, bf16[384,128]{1,0:T(8,128)(2,1)S(1)}, u32[]{:S(2)}, u32[]{:S(2)}) collective-permute-start(bf16[384,128]{1,0:T(8,128)(2,1)S(1)} %get-tuple-element.125), channel_id=1, source_target_pairs={{0,12},{4,8},{8,4},{12,0},{1,13},{5,9},{9,5},{13,1},{2,14},{6,10},... | collective-permute-start | bytes 294920 | tf_op jit(solution)/shard_map/rest_values/ppermute | solution.py:356
  73.3 9.3 %collective-permute-start.20 = (bf16[384,128]{1,0:T(8,128)(2,1)S(1)}, bf16[384,128]{1,0:T(8,128)(2,1)S(1)}, u32[]{:S(2)}, u32[]{:S(2)}) collective-permute-start(bf16[384,128]{1,0:T(8,128)(2,1)S(1)} %get-tuple-element.128), channel_id=1, source_target_pairs={{0,8},{4,12},{8,0},{12,4},{1,9},{5,13},{9,1},{13,5},{2,10},{6,14},... | collective-permute-start | bytes 294920 | tf_op jit(solution)/shard_map/returns_0/ppermute | solution.py:356
  85.2 12.8 %collective-permute-start.25 = (bf16[576,128]{1,0:T(8,128)(2,1)S(1)}, bf16[576,128]{1,0:T(8,128)(2,1)S(1)}, u32[]{:S(2)}, u32[]{:S(2)}) collective-permute-start(bf16[576,128]{1,0:T(8,128)(2,1)S(1)} %get-tuple-element.141), channel_id=1, source_target_pairs={{0,8},{4,12},{8,0},{12,4},{1,9},{5,13},{9,1},{13,5},{2,10},{6,14},... | collective-permute-start | bytes 442376 | tf_op jit(solution)/shard_map/returns_1/ppermute | solution.py:356
  87.7 10.3 %collective-permute-start.26 = (bf16[576,128]{1,0:T(8,128)(2,1)S(1)}, bf16[576,128]{1,0:T(8,128)(2,1)S(1)}, u32[]{:S(2)}, u32[]{:S(2)}) collective-permute-start(bf16[576,128]{1,0:T(8,128)(2,1)S(1)} %get-tuple-element.142), channel_id=1, source_target_pairs={{0,12},{4,8},{8,4},{12,0},{1,13},{5,9},{9,5},{13,1},{2,14},{6,10},... | collective-permute-start | bytes 442376 | tf_op jit(solution)/shard_map/returns_1/ppermute | solution.py:356
  98.0 9.0 %collective-permute-start.32 = (bf16[768,128]{1,0:T(8,128)(2,1)S(1)}, bf16[768,128]{1,0:T(8,128)(2,1)S(1)}, u32[]{:S(2)}, u32[]{:S(2)}) collective-permute-start(bf16[768,128]{1,0:T(8,128)(2,1)S(1)} %get-tuple-element.157), channel_id=1, source_target_pairs={{0,16},{16,0},{1,17},{17,1},{2,18},{18,2},{3,19},{19,3},{4,20},{20... | collective-permute-start | bytes 589832 | tf_op jit(solution)/shard_map/halo_query_grads_2/ppermute | solution.py:499
  99.5 9.9 %collective-permute-start.29 = (bf16[576,128]{1,0:T(8,128)(2,1)S(1)}, bf16[576,128]{1,0:T(8,128)(2,1)S(1)}, u32[]{:S(2)}, u32[]{:S(2)}) collective-permute-start(bf16[576,128]{1,0:T(8,128)(2,1)S(1)} %get-tuple-element.153), channel_id=1, source_target_pairs={{0,4},{4,0},{8,12},{12,8},{1,5},{5,1},{9,13},{13,9},{2,6},{6,2},{1... | collective-permute-start | bytes 442376 | tf_op jit(solution)/shard_map/returns_2/ppermute | solution.py:356
  102.6 14.6 %collective-permute-start.30 = (bf16[576,128]{1,0:T(8,128)(2,1)S(1)}, bf16[576,128]{1,0:T(8,128)(2,1)S(1)}, u32[]{:S(2)}, u32[]{:S(2)}) collective-permute-start(bf16[576,128]{1,0:T(8,128)(2,1)S(1)} %get-tuple-element.154), channel_id=1, source_target_pairs={{0,8},{4,12},{8,0},{12,4},{1,9},{5,13},{9,1},{13,5},{2,10},{6,14},... | collective-permute-start | bytes 442376 | tf_op jit(solution)/shard_map/returns_2/ppermute | solution.py:356
  104.6 12.7 %collective-permute-start.31 = (bf16[576,128]{1,0:T(8,128)(2,1)S(1)}, bf16[576,128]{1,0:T(8,128)(2,1)S(1)}, u32[]{:S(2)}, u32[]{:S(2)}) collective-permute-start(bf16[576,128]{1,0:T(8,128)(2,1)S(1)} %get-tuple-element.155), channel_id=1, source_target_pairs={{0,12},{4,8},{8,4},{12,0},{1,13},{5,9},{9,5},{13,1},{2,14},{6,10},... | collective-permute-start | bytes 442376 | tf_op jit(solution)/shard_map/returns_2/ppermute | solution.py:356
  107.1 10.2 %collective-permute-start.33 = (bf16[192,128]{1,0:T(8,128)(2,1)S(1)}, bf16[192,128]{1,0:T(8,128)(2,1)S(1)}, u32[]{:S(2)}, u32[]{:S(2)}) collective-permute-start(bf16[192,128]{1,0:T(8,128)(2,1)S(1)} %get-tuple-element.159), channel_id=1, source_target_pairs={{0,4},{4,0},{8,12},{12,8},{1,5},{5,1},{9,13},{13,9},{2,6},{6,2},{1... | collective-permute-start | bytes 147464 | tf_op jit(solution)/shard_map/returns_last/ppermute | solution.py:356
  107.2 13.0 %collective-permute-start.34 = (bf16[192,128]{1,0:T(8,128)(2,1)S(1)}, bf16[192,128]{1,0:T(8,128)(2,1)S(1)}, u32[]{:S(2)}, u32[]{:S(2)}) collective-permute-start(bf16[192,128]{1,0:T(8,128)(2,1)S(1)} %get-tuple-element.160), channel_id=1, source_target_pairs={{0,8},{4,12},{8,0},{12,4},{1,9},{5,13},{9,1},{13,5},{2,10},{6,14},... | collective-permute-start | bytes 147464 | tf_op jit(solution)/shard_map/returns_last/ppermute | solution.py:356
  109.4 10.7 %collective-permute-start.35 = (bf16[192,128]{1,0:T(8,128)(2,1)S(1)}, bf16[192,128]{1,0:T(8,128)(2,1)S(1)}, u32[]{:S(2)}, u32[]{:S(2)}) collective-permute-start(bf16[192,128]{1,0:T(8,128)(2,1)S(1)} %get-tuple-element.161), channel_id=1, source_target_pairs={{0,12},{4,8},{8,4},{12,0},{1,13},{5,9},{9,5},{13,1},{2,14},{6,10},... | collective-permute-start | bytes 147464 | tf_op jit(solution)/shard_map/returns_last/ppermute | solution.py:356
  (18 other events, 93.8 us)

commit v5 on v4

--- a/solution.py
+++ b/solution.py
@@ -356,8 +356,14 @@
     return lax.ppermute(value, axis, [(index, index ^ distance) for index in range(lax.axis_size(axis))])
 
 
-def swap_pieces(pieces):
-    return [pieces[0]] + [swap(piece, "ulysses", distance) for distance, piece in enumerate(pieces) if distance]
+def swap_pieces(pieces, earlier=None):
+    held = [pieces[0]]
+    for distance in range(1, len(pieces)):
+        piece = pieces[distance]
+        if earlier is not None:
+            piece = after([piece], earlier[distance])[0]
+        held.append(swap(piece, "ulysses", distance))
+    return held
 
 
 def sum_steps(axes):
@@ -442,7 +448,7 @@
         late = after(pairs[1:], gain, first_side)
         late_side = forward(gather_rows(late, [(number, width, width) for number in range(parts - 1)]))
     with jax.named_scope("first_grads"):
-        lead = swap_pieces(after(sent_lead, late))
+        lead = swap_pieces(sent_lead, pairs)
     with jax.named_scope("halo_first_grads"):
         ranges = [(part, 0, rows) for part in every] + [(part, 2 * rows, dots) for part in every]
         lead_side = forward(gather_rows(lead, ranges))
@@ -460,16 +466,16 @@
         totals = exchange_totals(part_totals, sides)
     gain = advance(after([gain], late)[0], 2)
     with jax.named_scope("rest_grads"):
-        rest_grads = swap_pieces(after(sent_rest, lead, gain))
+        rest_grads = swap_pieces(after(sent_rest, gain), lead)
     with jax.named_scope("halo_rest_grads"):
         ranges = [(part, place * rows, rows) for place in range(heads - 1) for part in every]
         rest_side = forward(gather_rows(rest_grads, ranges))
     with jax.named_scope("rest_values"):
-        rest_values = swap_pieces(after(pack([values[0]], parts, rest), rest_grads, part_totals))
+        rest_values = swap_pieces(after(pack([values[0]], parts, rest), part_totals), rest_grads)
     dot_places = [(piece, 2 * rows // dots) for piece in lead]
     dot_places += [(array, parts * rows // dots + part) for array in lead_side for part in every]
     stages, pieces, open_grads = [], [], []
-    gate = rest_values[1:]
+    gate = rest_values
     for head in range(heads):
         if head == 0:
             value_places = [(piece, 1) for piece in lead]
@@ -494,18 +500,15 @@
                 before,
             )
         stages.append([(1, head), (2, head)] + ([(0, head - 1)] if before else []))
-        leaving, query_grads = lax.optimization_barrier((leaving, query_grads, gate))[:2]
+        query_grads = after(query_grads, gate[-1])
         with jax.named_scope("halo_query_grads_%d" % head):
             back_grads = [lax.ppermute(other, "tm", back) for other, (_, back) in zip(query_grads[1:], sides)]
             open_grads = list(query_grads[:1]) + back_grads
         with jax.named_scope("returns_%d" % head):
-            pieces.append(swap_pieces(leaving))
-        gate = pieces[-1][1:]
+            pieces.append(swap_pieces(leaving, gate))
+        gate = pieces[-1]
         if not final:
-            ready = after([gain], gate)[0]
-            if head:
-                gate = gate + [gain]
-            gain = advance(ready)
+            gain = advance(after([gain], gate[-1])[0])
     with jax.named_scope("returns_last"):
         stages.append([(0, heads - 1)])
         pieces.append(swap_pieces(close(open_grads, parts)))

time: 122 us -> 117 us (0.959)
  waiting for transfers between devices: 41.6 us -> 35.7 us
    ppermute x29, waiting for transfers between devices: 37.9 us -> 32.3 us  [swap(): lax.ppermute(value, axis, [(index, index ^ distance) for index in range(l...]
    ppermute x3, starting transfers between devices: 3.52 us -> 5.28 us  [local(): lax.ppermute(other, 'tm', back)]
    ppermute x29, starting transfers between devices: 48.3 us -> 47.1 us  [swap(): lax.ppermute(value, axis, [(index, index ^ distance) for index in range(l...]
  transfers between devices with their start and end apart: 37 -> 37, of which waited for: 14 -> 16; matrix products, arithmetic and copies ran while one was open for 1% -> 1% of each run, Pallas kernels for 13% -> 13%
where the time goes in v5:
time: 117 us; the launch traced here: 116 us
  starting transfers between devices  57.1 us (49%)
  waiting for transfers between devices  35.7 us (31%)
  Pallas kernels  18.1 us (15%)
  local copies, waits for them, and re-layouts  3.9 us (3%)
    ppermute x29, starting transfers between devices, swap(): lax.ppermute(value, axis, [(index, index ^ distance) for index in range(l...  47.1 us
    ppermute x29, waiting for transfers between devices, swap(): lax.ppermute(value, axis, [(index, index ^ distance) for index in range(l...  32.3 us
    pallas_call x3, Pallas kernels, attention(): pl.pallas_call(functools.partial(attention_kernel, parts, sources, head,...  10 us
    ppermute x3, starting transfers between devices, local(): lax.ppermute(other, 'tm', back)  5.28 us
    ppermute x4, starting transfers between devices, forward(): return [lax.ppermute(array, 'tm', there) for there, _ in sides]  4.09 us
    pallas_call x1, Pallas kernels, partial_totals(): pl.pallas_call(functools.partial(totals_kernel, parts, sources, heads), g...  3.61 us
    ppermute x4, waiting for transfers between devices, forward(): return [lax.ppermute(array, 'tm', there) for there, _ in sides]  3.33 us
    unnamed x10, local copies, waits for them, and re-layouts  3.19 us
  transfers between devices with their start and end apart: 37, of which 16 were waited for; matrix products, arithmetic and copies ran while one was open for 1% of the time, Pallas kernels for 13%

profile of v5, /device:TPU:0, one launch (start us, length us, event | category | flops | bytes accessed | tf_op | source)
XLA Modules:
  0.0 116.3 jit_solution(4993323684086963071)
XLA Ops:
  3.3 3.1 %collective-permute-start = (bf16[1152,128]{1,0:T(8,128)(2,1)S(1)}, bf16[1152,128]{1,0:T(8,128)(2,1)S(1)}, u32[]{:S(2)}, u32[]{:S(2)}) collective-permute-start(bf16[1152,128]{1,0:T(8,128)(2,1)S(1)} %get-tuple-element.88), channel_id=1, source_target_pairs={{0,4},{4,0},{8,12},{12,8},{1,5},{5,1},{9,13},{13,9},{2,6},{6,2},{1... | collective-permute-start | bytes 884744 | tf_op jit(solution)/shard_map/keys_queries/ppermute | solution.py:356
  6.4 2.6 %collective-permute-start.1 = (bf16[1152,128]{1,0:T(8,128)(2,1)S(1)}, bf16[1152,128]{1,0:T(8,128)(2,1)S(1)}, u32[]{:S(2)}, u32[]{:S(2)}) collective-permute-start(bf16[1152,128]{1,0:T(8,128)(2,1)S(1)} %get-tuple-element.89), channel_id=1, source_target_pairs={{0,8},{4,12},{8,0},{12,4},{1,9},{5,13},{9,1},{13,5},{2,10},{6,14},... | collective-permute-start | bytes 884744 | tf_op jit(solution)/shard_map/keys_queries/ppermute | solution.py:356
  15.0 3.3 %collective-permute-done.6.refs_24_.refs_28_.refs_32_.refs_12_ = bf16[576,128]{1,0:T(8,128)(2,1)S(1)} collective-permute-done((bf16[576,128]{1,0:T(8,128)(2,1)S(1)}, bf16[576,128]{1,0:T(8,128)(2,1)S(1)}, u32[]{:S(2)}, u32[]{:S(2)}) %collective-permute-start.6) | collective-permute-done | bytes 147488 | tf_op jit(solution)/shard_map/halo_queries/ppermute | solution.py:425
  18.9 10.9 %collective-permute-done.1.refs_1_.refs_2_.refs_6_.refs_10_.refs_14_.refs_18_.refs_22_ = bf16[1152,128]{1,0:T(8,128)(2,1)S(1)} collective-permute-done((bf16[1152,128]{1,0:T(8,128)(2,1)S(1)}, bf16[1152,128]{1,0:T(8,128)(2,1)S(1)}, u32[]{:S(2)}, u32[]{:S(2)}) %collective-permute-start.1) | collective-permute-done | bytes 294944 | tf_op jit(solution)/shard_map/keys_queries/ppermute | solution.py:356
  32.0 2.5 %collective-permute-start.5 = (bf16[400,128]{1,0:T(8,128)(2,1)S(1)}, bf16[400,128]{1,0:T(8,128)(2,1)S(1)}, u32[]{:S(2)}, u32[]{:S(2)}) collective-permute-start(bf16[400,128]{1,0:T(8,128)(2,1)S(1)} %get-tuple-element.98), channel_id=1, source_target_pairs={{0,12},{4,8},{8,4},{12,0},{1,13},{5,9},{9,5},{13,1},{2,14},{6,10},... | collective-permute-start | bytes 307208 | tf_op jit(solution)/shard_map/first_grads/ppermute | solution.py:356
  34.4 5.5 %collective-permute-start.4 = (bf16[400,128]{1,0:T(8,128)(2,1)S(1)}, bf16[400,128]{1,0:T(8,128)(2,1)S(1)}, u32[]{:S(2)}, u32[]{:S(2)}) collective-permute-start(bf16[400,128]{1,0:T(8,128)(2,1)S(1)} %get-tuple-element.96), channel_id=1, source_target_pairs={{0,8},{4,12},{8,0},{12,4},{1,9},{5,13},{9,1},{13,5},{2,10},{6,14},... | collective-permute-start | bytes 307208 | tf_op jit(solution)/shard_map/first_grads/ppermute | solution.py:356
  42.8 2.1 %collective-permute-done.12 = f32[12,128]{1,0:T(8,128)S(1)} collective-permute-done((f32[12,128]{1,0:T(8,128)S(1)}, f32[12,128]{1,0:T(8,128)S(1)}, u32[]{:S(2)}, u32[]{:S(2)}) %collective-permute-start.12) | collective-permute-done | bytes 6176 | tf_op jit(solution)/shard_map/gain/ppermute | solution.py:356
  44.9 2.4 %collective-permute-start.19 = (bf16[384,128]{1,0:T(8,128)(2,1)S(1)}, bf16[384,128]{1,0:T(8,128)(2,1)S(1)}, u32[]{:S(2)}, u32[]{:S(2)}) collective-permute-start(bf16[384,128]{1,0:T(8,128)(2,1)S(1)} %get-tuple-element.130), channel_id=1, source_target_pairs={{0,12},{4,8},{8,4},{12,0},{1,13},{5,9},{9,5},{13,1},{2,14},{6,10},... | collective-permute-start | bytes 294920 | tf_op jit(solution)/shard_map/rest_grads/ppermute | solution.py:356
  49.3 3.6 %totals.1 = (f32[3,768]{1,0:T(4,128)S(1)}, f32[3,768]{1,0:T(4,128)S(1)}) custom-call(bf16[1152,128]{1,0:T(8,128)(2,1)S(1)} %get-tuple-element.87.refs_0_.refs_4_.refs_8_.refs_12_.refs_16_.refs_20_, bf16[1152,128]{1,0:T(8,128)(2,1)S(1)} %collective-permute-done.refs_0_.refs_1_.refs_5_.refs_9_.refs_13_.refs_17_.refs_21_, ...), custom_call_target="tpu_custom_call" | custom-call | flops 905969664 | bytes 2359296 | tf_op jit(solution)/shard_map/totals/pallas_call | solution.py:194
  58.0 2.5 %collective-permute-start.20 = (bf16[384,128]{1,0:T(8,128)(2,1)S(1)}, bf16[384,128]{1,0:T(8,128)(2,1)S(1)}, u32[]{:S(2)}, u32[]{:S(2)}) collective-permute-start(bf16[384,128]{1,0:T(8,128)(2,1)S(1)} %get-tuple-element.131), channel_id=1, source_target_pairs={{0,12},{4,8},{8,4},{12,0},{1,13},{5,9},{9,5},{13,1},{2,14},{6,10},... | collective-permute-start | bytes 294920 | tf_op jit(solution)/shard_map/rest_values/ppermute | solution.py:356
  60.5 3.3 %attention_0.1 = (bf16[384,128]{1,0:T(8,128)(2,1)S(1)}, bf16[384,128]{1,0:T(8,128)(2,1)S(1)}, bf16[384,128]{1,0:T(8,128)(2,1)S(1)}, bf16[384,128]{1,0:T(8,128)(2...) custom-call(bf16[1152,128]{1,0:T(8,128)(2,1)S(1)} %get-tuple-element.87.refs_0_.refs_4_.refs_8_.refs_12_.refs_16_.refs_20_, ...), custom_call_target="tpu_custom_call" | custom-call | flops 1509949440 | bytes 3145728 | tf_op jit(solution)/shard_map/attention_0/pallas_call | solution.py:287
  64.4 2.0 %collective-permute-start.23 = (bf16[768,128]{1,0:T(8,128)(2,1)S(1)}, bf16[768,128]{1,0:T(8,128)(2,1)S(1)}, u32[]{:S(2)}, u32[]{:S(2)}) collective-permute-start(bf16[768,128]{1,0:T(8,128)(2,1)S(1)} %get-tuple-element.138), channel_id=1, source_target_pairs={{0,16},{16,0},{1,17},{17,1},{2,18},{18,2},{3,19},{19,3},{4,20},{20... | collective-permute-start | bytes 589832 | tf_op jit(solution)/shard_map/halo_query_grads_0/ppermute | solution.py:505
  66.4 2.8 %collective-permute-start.17 = (bf16[384,128]{1,0:T(8,128)(2,1)S(1)}, bf16[384,128]{1,0:T(8,128)(2,1)S(1)}, u32[]{:S(2)}, u32[]{:S(2)}) collective-permute-start(bf16[384,128]{1,0:T(8,128)(2,1)S(1)} %get-tuple-element.125), channel_id=1, source_target_pairs={{0,8},{4,12},{8,0},{12,4},{1,9},{5,13},{9,1},{13,5},{2,10},{6,14},... | collective-permute-start | bytes 294920 | tf_op jit(solution)/shard_map/rest_values/ppermute | solution.py:356
  70.8 3.2 %collective-permute-done.17.refs_6_ = bf16[384,128]{1,0:T(8,128)(2,1)S(1)} collective-permute-done((bf16[384,128]{1,0:T(8,128)(2,1)S(1)}, bf16[384,128]{1,0:T(8,128)(2,1)S(1)}, u32[]{:S(2)}, u32[]{:S(2)}) %collective-permute-start.17) | collective-permute-done | bytes 98336 | tf_op jit(solution)/shard_map/rest_values/ppermute | solution.py:356
  74.6 3.4 %attention_1.1 = (bf16[576,128]{1,0:T(8,128)(2,1)S(1)}, bf16[576,128]{1,0:T(8,128)(2,1)S(1)}, bf16[576,128]{1,0:T(8,128)(2,1)S(1)}, bf16[576,128]{1,0:T(8,128)(2...) custom-call(bf16[1152,128]{1,0:T(8,128)(2,1)S(1)} %get-tuple-element.87.refs_0_.refs_4_.refs_8_.refs_12_.refs_16_.refs_20_, ...), custom_call_target="tpu_custom_call" | custom-call | flops 1509949440 | bytes 3145728 | tf_op jit(solution)/shard_map/attention_1/pallas_call | solution.py:287
  80.4 3.9 %collective-permute-start.15 = (bf16[384,128]{1,0:T(8,128)(2,1)S(1)}, bf16[384,128]{1,0:T(8,128)(2,1)S(1)}, u32[]{:S(2)}, u32[]{:S(2)}) collective-permute-start(bf16[384,128]{1,0:T(8,128)(2,1)S(1)} %get-tuple-element.120), channel_id=1, source_target_pairs={{0,4},{4,0},{8,12},{12,8},{1,5},{5,1},{9,13},{13,9},{2,6},{6,2},{1... | collective-permute-start | bytes 294920 | tf_op jit(solution)/shard_map/returns_0/ppermute | solution.py:356
  84.3 3.4 %attention_2.1 = (bf16[576,128]{1,0:T(8,128)(2,1)S(1)}, bf16[576,128]{1,0:T(8,128)(2,1)S(1)}, bf16[576,128]{1,0:T(8,128)(2,1)S(1)}, bf16[576,128]{1,0:T(8,128)(2...) custom-call(bf16[1152,128]{1,0:T(8,128)(2,1)S(1)} %get-tuple-element.87.refs_0_.refs_4_.refs_8_.refs_12_.refs_16_.refs_20_, ...), custom_call_target="tpu_custom_call" | custom-call | flops 1509949440 | bytes 3145728 | tf_op jit(solution)/shard_map/attention_2/pallas_call | solution.py:287
  89.0 2.2 %collective-permute-done.15.refs_1_ = bf16[384,128]{1,0:T(8,128)(2,1)S(1)} collective-permute-done((bf16[384,128]{1,0:T(8,128)(2,1)S(1)}, bf16[384,128]{1,0:T(8,128)(2,1)S(1)}, u32[]{:S(2)}, u32[]{:S(2)}) %collective-permute-start.15) | collective-permute-done | bytes 98336 | tf_op jit(solution)/shard_map/returns_0/ppermute | solution.py:356
  91.2 4.4 %collective-permute-start.30 = (bf16[576,128]{1,0:T(8,128)(2,1)S(1)}, bf16[576,128]{1,0:T(8,128)(2,1)S(1)}, u32[]{:S(2)}, u32[]{:S(2)}) collective-permute-start(bf16[576,128]{1,0:T(8,128)(2,1)S(1)} %get-tuple-element.156), channel_id=1, source_target_pairs={{0,12},{4,8},{8,4},{12,0},{1,13},{5,9},{9,5},{13,1},{2,14},{6,10},... | collective-permute-start | bytes 442376 | tf_op jit(solution)/shard_map/returns_2/ppermute | solution.py:356
  95.6 4.5 %collective-permute-done.35 = f32[12,128]{1,0:T(8,128)S(1)} collective-permute-done((f32[12,128]{1,0:T(8,128)S(1)}, f32[12,128]{1,0:T(8,128)S(1)}, u32[]{:S(2)}, u32[]{:S(2)}) %collective-permute-start.35) | collective-permute-done | bytes 6176 | tf_op jit(solution)/shard_map/gain/ppermute | solution.py:356
  100.0 3.7 %collective-permute-start.36 = (f32[12,128]{1,0:T(8,128)S(1)}, f32[12,128]{1,0:T(8,128)S(1)}, u32[]{:S(2)}, u32[]{:S(2)}) collective-permute-start(f32[12,128]{1,0:T(8,128)S(1)} %add.34), channel_id=1, source_target_pairs={{0,8},{4,12},{8,0},{12,4},{1,9},{5,13},{9,1},{13,5},{2,10},{6,14},... | collective-permute-start | bytes 18440 | tf_op jit(solution)/shard_map/gain/ppermute | solution.py:356
  103.8 1.9 %collective-permute-start.28 = (bf16[576,128]{1,0:T(8,128)(2,1)S(1)}, bf16[576,128]{1,0:T(8,128)(2,1)S(1)}, u32[]{:S(2)}, u32[]{:S(2)}) collective-permute-start(bf16[576,128]{1,0:T(8,128)(2,1)S(1)} %get-tuple-element.152), channel_id=1, source_target_pairs={{0,4},{4,0},{8,12},{12,8},{1,5},{5,1},{9,13},{13,9},{2,6},{6,2},{1... | collective-permute-start | bytes 442376 | tf_op jit(solution)/shard_map/returns_2/ppermute | solution.py:356
  106.1 2.7 %collective-permute-start.33 = (bf16[192,128]{1,0:T(8,128)(2,1)S(1)}, bf16[192,128]{1,0:T(8,128)(2,1)S(1)}, u32[]{:S(2)}, u32[]{:S(2)}) collective-permute-start(bf16[192,128]{1,0:T(8,128)(2,1)S(1)} %get-tuple-element.163), channel_id=1, source_target_pairs={{0,8},{4,12},{8,0},{12,4},{1,9},{5,13},{9,1},{13,5},{2,10},{6,14},... | collective-permute-start | bytes 147464 | tf_op jit(solution)/shard_map/returns_last/ppermute | solution.py:356
  111.8 2.9 %collective-permute-done.34.refs_15_ = bf16[192,128]{1,0:T(8,128)(2,1)S(1)} collective-permute-done((bf16[192,128]{1,0:T(8,128)(2,1)S(1)}, bf16[192,128]{1,0:T(8,128)(2,1)S(1)}, u32[]{:S(2)}, u32[]{:S(2)}) %collective-permute-start.34) | collective-permute-done | bytes 49184 | tf_op jit(solution)/shard_map/returns_last/ppermute | solution.py:356
  (82 shorter events, 32.7 us)
Async XLA Ops:
  3.3 15.6 %collective-permute-start = (bf16[1152,128]{1,0:T(8,128)(2,1)S(1)}, bf16[1152,128]{1,0:T(8,128)(2,1)S(1)}, u32[]{:S(2)}, u32[]{:S(2)}) collective-permute-start(bf16[1152,128]{1,0:T(8,128)(2,1)S(1)} %get-tuple-element.88), channel_id=1, source_target_pairs={{0,4},{4,0},{8,12},{12,8},{1,5},{5,1},{9,13},{13,9},{2,6},{6,2},{1... | collective-permute-start | bytes 884744 | tf_op jit(solution)/shard_map/keys_queries/ppermute | solution.py:356
  6.4 23.5 %collective-permute-start.1 = (bf16[1152,128]{1,0:T(8,128)(2,1)S(1)}, bf16[1152,128]{1,0:T(8,128)(2,1)S(1)}, u32[]{:S(2)}, u32[]{:S(2)}) collective-permute-start(bf16[1152,128]{1,0:T(8,128)(2,1)S(1)} %get-tuple-element.89), channel_id=1, source_target_pairs={{0,8},{4,12},{8,0},{12,4},{1,9},{5,13},{9,1},{13,5},{2,10},{6,14},... | collective-permute-start | bytes 884744 | tf_op jit(solution)/shard_map/keys_queries/ppermute | solution.py:356
  8.9 20.9 %collective-permute-start.2 = (bf16[1152,128]{1,0:T(8,128)(2,1)S(1)}, bf16[1152,128]{1,0:T(8,128)(2,1)S(1)}, u32[]{:S(2)}, u32[]{:S(2)}) collective-permute-start(bf16[1152,128]{1,0:T(8,128)(2,1)S(1)} %get-tuple-element.90), channel_id=1, source_target_pairs={{0,12},{4,8},{8,4},{12,0},{1,13},{5,9},{9,5},{13,1},{2,14},{6,10},... | collective-permute-start | bytes 884744 | tf_op jit(solution)/shard_map/keys_queries/ppermute | solution.py:356
  30.4 18.9 %collective-permute-start.8 = (bf16[1728,128]{1,0:T(8,128)(2,1)S(1)}, bf16[1728,128]{1,0:T(8,128)(2,1)S(1)}, u32[]{:S(2)}, u32[]{:S(2)}) collective-permute-start(bf16[1728,128]{1,0:T(8,128)(2,1)S(1)} %halo_queries.1), channel_id=1, source_target_pairs={{0,16},{16,0},{1,17},{17,1},{2,18},{18,2},{3,19},{19,3},{4,20},{20... | collective-permute-start | bytes 1327112 | tf_op jit(solution)/shard_map/halo_queries/ppermute | solution.py:425
  32.0 13.0 %collective-permute-start.5 = (bf16[400,128]{1,0:T(8,128)(2,1)S(1)}, bf16[400,128]{1,0:T(8,128)(2,1)S(1)}, u32[]{:S(2)}, u32[]{:S(2)}) collective-permute-start(bf16[400,128]{1,0:T(8,128)(2,1)S(1)} %get-tuple-element.98), channel_id=1, source_target_pairs={{0,12},{4,8},{8,4},{12,0},{1,13},{5,9},{9,5},{13,1},{2,14},{6,10},... | collective-permute-start | bytes 307208 | tf_op jit(solution)/shard_map/first_grads/ppermute | solution.py:356
  34.4 12.8 %collective-permute-start.4 = (bf16[400,128]{1,0:T(8,128)(2,1)S(1)}, bf16[400,128]{1,0:T(8,128)(2,1)S(1)}, u32[]{:S(2)}, u32[]{:S(2)}) collective-permute-start(bf16[400,128]{1,0:T(8,128)(2,1)S(1)} %get-tuple-element.96), channel_id=1, source_target_pairs={{0,8},{4,12},{8,0},{12,4},{1,9},{5,13},{9,1},{13,5},{2,10},{6,14},... | collective-permute-start | bytes 307208 | tf_op jit(solution)/shard_map/first_grads/ppermute | solution.py:356
  40.0 8.3 %collective-permute-start.3 = (bf16[400,128]{1,0:T(8,128)(2,1)S(1)}, bf16[400,128]{1,0:T(8,128)(2,1)S(1)}, u32[]{:S(2)}, u32[]{:S(2)}) collective-permute-start(bf16[400,128]{1,0:T(8,128)(2,1)S(1)} %get-tuple-element.94), channel_id=1, source_target_pairs={{0,4},{4,0},{8,12},{12,8},{1,5},{5,1},{9,13},{13,9},{2,6},{6,2},{1... | collective-permute-start | bytes 307208 | tf_op jit(solution)/shard_map/first_grads/ppermute | solution.py:356
  44.9 10.7 %collective-permute-start.19 = (bf16[384,128]{1,0:T(8,128)(2,1)S(1)}, bf16[384,128]{1,0:T(8,128)(2,1)S(1)}, u32[]{:S(2)}, u32[]{:S(2)}) collective-permute-start(bf16[384,128]{1,0:T(8,128)(2,1)S(1)} %get-tuple-element.130), channel_id=1, source_target_pairs={{0,12},{4,8},{8,4},{12,0},{1,13},{5,9},{9,5},{13,1},{2,14},{6,10},... | collective-permute-start | bytes 294920 | tf_op jit(solution)/shard_map/rest_grads/ppermute | solution.py:356
  47.3 9.3 %collective-permute-start.16 = (bf16[384,128]{1,0:T(8,128)(2,1)S(1)}, bf16[384,128]{1,0:T(8,128)(2,1)S(1)}, u32[]{:S(2)}, u32[]{:S(2)}) collective-permute-start(bf16[384,128]{1,0:T(8,128)(2,1)S(1)} %get-tuple-element.124), channel_id=1, source_target_pairs={{0,8},{4,12},{8,0},{12,4},{1,9},{5,13},{9,1},{13,5},{2,10},{6,14},... | collective-permute-start | bytes 294920 | tf_op jit(solution)/shard_map/rest_grads/ppermute | solution.py:356
  48.3 8.3 %collective-permute-start.13 = (bf16[384,128]{1,0:T(8,128)(2,1)S(1)}, bf16[384,128]{1,0:T(8,128)(2,1)S(1)}, u32[]{:S(2)}, u32[]{:S(2)}) collective-permute-start(bf16[384,128]{1,0:T(8,128)(2,1)S(1)} %get-tuple-element.118), channel_id=1, source_target_pairs={{0,4},{4,0},{8,12},{12,8},{1,5},{5,1},{9,13},{13,9},{2,6},{6,2},{1... | collective-permute-start | bytes 294920 | tf_op jit(solution)/shard_map/rest_grads/ppermute | solution.py:356
  53.0 7.5 %collective-permute-start.10 = (f32[6,768]{1,0:T(8,128)S(1)}, f32[6,768]{1,0:T(8,128)S(1)}, u32[]{:S(2)}, u32[]{:S(2)}) collective-permute-start(f32[6,768]{1,0:T(8,128)S(1)} %pad_maximum_fusion), channel_id=1, source_target_pairs={{0,16},{16,0},{1,17},{17,1},{2,18},{18,2},{3,19},{19,3},{4,20},{20... | collective-permute-start | bytes 55304 | tf_op jit(solution)/shard_map/totals/ppermute | solution.py:402
  57.4 17.2 %collective-permute-start.22 = (bf16[1536,128]{1,0:T(8,128)(2,1)S(1)}, bf16[1536,128]{1,0:T(8,128)(2,1)S(1)}, u32[]{:S(2)}, u32[]{:S(2)}) collective-permute-start(bf16[1536,128]{1,0:T(8,128)(2,1)S(1)} %halo_rest_grads.1), channel_id=1, source_target_pairs={{0,16},{16,0},{1,17},{17,1},{2,18},{18,2},{3,19},{19,3},{4,20},{20... | collective-permute-start | bytes 1179656 | tf_op jit(solution)/shard_map/halo_rest_grads/ppermute | solution.py:425
  64.4 10.2 %collective-permute-start.23 = (bf16[768,128]{1,0:T(8,128)(2,1)S(1)}, bf16[768,128]{1,0:T(8,128)(2,1)S(1)}, u32[]{:S(2)}, u32[]{:S(2)}) collective-permute-start(bf16[768,128]{1,0:T(8,128)(2,1)S(1)} %get-tuple-element.138), channel_id=1, source_target_pairs={{0,16},{16,0},{1,17},{17,1},{2,18},{18,2},{3,19},{19,3},{4,20},{20... | collective-permute-start | bytes 589832 | tf_op jit(solution)/shard_map/halo_query_grads_0/ppermute | solution.py:505
  66.4 7.6 %collective-permute-start.17 = (bf16[384,128]{1,0:T(8,128)(2,1)S(1)}, bf16[384,128]{1,0:T(8,128)(2,1)S(1)}, u32[]{:S(2)}, u32[]{:S(2)}) collective-permute-start(bf16[384,128]{1,0:T(8,128)(2,1)S(1)} %get-tuple-element.125), channel_id=1, source_target_pairs={{0,8},{4,12},{8,0},{12,4},{1,9},{5,13},{9,1},{13,5},{2,10},{6,14},... | collective-permute-start | bytes 294920 | tf_op jit(solution)/shard_map/rest_values/ppermute | solution.py:356
  69.3 8.7 %collective-permute-start.21 = (bf16[384,128]{1,0:T(8,128)(2,1)S(1)}, bf16[384,128]{1,0:T(8,128)(2,1)S(1)}, u32[]{:S(2)}, u32[]{:S(2)}) collective-permute-start(bf16[384,128]{1,0:T(8,128)(2,1)S(1)} %get-tuple-element.132), channel_id=1, source_target_pairs={{0,12},{4,8},{8,4},{12,0},{1,13},{5,9},{9,5},{13,1},{2,14},{6,10},... | collective-permute-start | bytes 294920 | tf_op jit(solution)/shard_map/returns_0/ppermute | solution.py:356
  79.9 7.8 %collective-permute-start.26 = (bf16[576,128]{1,0:T(8,128)(2,1)S(1)}, bf16[576,128]{1,0:T(8,128)(2,1)S(1)}, u32[]{:S(2)}, u32[]{:S(2)}) collective-permute-start(bf16[576,128]{1,0:T(8,128)(2,1)S(1)} %get-tuple-element.145), channel_id=1, source_target_pairs={{0,12},{4,8},{8,4},{12,0},{1,13},{5,9},{9,5},{13,1},{2,14},{6,10},... | collective-permute-start | bytes 442376 | tf_op jit(solution)/shard_map/returns_1/ppermute | solution.py:356
  79.9 11.2 %collective-permute-start.18 = (bf16[384,128]{1,0:T(8,128)(2,1)S(1)}, bf16[384,128]{1,0:T(8,128)(2,1)S(1)}, u32[]{:S(2)}, u32[]{:S(2)}) collective-permute-start(bf16[384,128]{1,0:T(8,128)(2,1)S(1)} %get-tuple-element.126), channel_id=1, source_target_pairs={{0,8},{4,12},{8,0},{12,4},{1,9},{5,13},{9,1},{13,5},{2,10},{6,14},... | collective-permute-start | bytes 294920 | tf_op jit(solution)/shard_map/returns_0/ppermute | solution.py:356
  80.4 10.8 %collective-permute-start.15 = (bf16[384,128]{1,0:T(8,128)(2,1)S(1)}, bf16[384,128]{1,0:T(8,128)(2,1)S(1)}, u32[]{:S(2)}, u32[]{:S(2)}) collective-permute-start(bf16[384,128]{1,0:T(8,128)(2,1)S(1)} %get-tuple-element.120), channel_id=1, source_target_pairs={{0,4},{4,0},{8,12},{12,8},{1,5},{5,1},{9,13},{13,9},{2,6},{6,2},{1... | collective-permute-start | bytes 294920 | tf_op jit(solution)/shard_map/returns_0/ppermute | solution.py:356
  87.7 18.1 %collective-permute-start.31 = (bf16[768,128]{1,0:T(8,128)(2,1)S(1)}, bf16[768,128]{1,0:T(8,128)(2,1)S(1)}, u32[]{:S(2)}, u32[]{:S(2)}) collective-permute-start(bf16[768,128]{1,0:T(8,128)(2,1)S(1)} %get-tuple-element.160), channel_id=1, source_target_pairs={{0,16},{16,0},{1,17},{17,1},{2,18},{18,2},{3,19},{19,3},{4,20},{20... | collective-permute-start | bytes 589832 | tf_op jit(solution)/shard_map/halo_query_grads_2/ppermute | solution.py:505
  91.2 12.5 %collective-permute-start.24 = (bf16[576,128]{1,0:T(8,128)(2,1)S(1)}, bf16[576,128]{1,0:T(8,128)(2,1)S(1)}, u32[]{:S(2)}, u32[]{:S(2)}) collective-permute-start(bf16[576,128]{1,0:T(8,128)(2,1)S(1)} %get-tuple-element.141), channel_id=1, source_target_pairs={{0,4},{4,0},{8,12},{12,8},{1,5},{5,1},{9,13},{13,9},{2,6},{6,2},{1... | collective-permute-start | bytes 442376 | tf_op jit(solution)/shard_map/returns_1/ppermute | solution.py:356
  91.2 12.5 %collective-permute-start.25 = (bf16[576,128]{1,0:T(8,128)(2,1)S(1)}, bf16[576,128]{1,0:T(8,128)(2,1)S(1)}, u32[]{:S(2)}, u32[]{:S(2)}) collective-permute-start(bf16[576,128]{1,0:T(8,128)(2,1)S(1)} %get-tuple-element.143), channel_id=1, source_target_pairs={{0,8},{4,12},{8,0},{12,4},{1,9},{5,13},{9,1},{13,5},{2,10},{6,14},... | collective-permute-start | bytes 442376 | tf_op jit(solution)/shard_map/returns_1/ppermute | solution.py:356
  91.2 17.6 %collective-permute-start.30 = (bf16[576,128]{1,0:T(8,128)(2,1)S(1)}, bf16[576,128]{1,0:T(8,128)(2,1)S(1)}, u32[]{:S(2)}, u32[]{:S(2)}) collective-permute-start(bf16[576,128]{1,0:T(8,128)(2,1)S(1)} %get-tuple-element.156), channel_id=1, source_target_pairs={{0,12},{4,8},{8,4},{12,0},{1,13},{5,9},{9,5},{13,1},{2,14},{6,10},... | collective-permute-start | bytes 442376 | tf_op jit(solution)/shard_map/returns_2/ppermute | solution.py:356
  103.7 7.4 %collective-permute-start.29 = (bf16[576,128]{1,0:T(8,128)(2,1)S(1)}, bf16[576,128]{1,0:T(8,128)(2,1)S(1)}, u32[]{:S(2)}, u32[]{:S(2)}) collective-permute-start(bf16[576,128]{1,0:T(8,128)(2,1)S(1)} %get-tuple-element.154), channel_id=1, source_target_pairs={{0,8},{4,12},{8,0},{12,4},{1,9},{5,13},{9,1},{13,5},{2,10},{6,14},... | collective-permute-start | bytes 442376 | tf_op jit(solution)/shard_map/returns_2/ppermute | solution.py:356
  103.8 7.3 %collective-permute-start.28 = (bf16[576,128]{1,0:T(8,128)(2,1)S(1)}, bf16[576,128]{1,0:T(8,128)(2,1)S(1)}, u32[]{:S(2)}, u32[]{:S(2)}) collective-permute-start(bf16[576,128]{1,0:T(8,128)(2,1)S(1)} %get-tuple-element.152), channel_id=1, source_target_pairs={{0,4},{4,0},{8,12},{12,8},{1,5},{5,1},{9,13},{13,9},{2,6},{6,2},{1... | collective-permute-start | bytes 442376 | tf_op jit(solution)/shard_map/returns_2/ppermute | solution.py:356
  (18 other events, 83.4 us)

commit v6 on v5

--- a/solution.py
+++ b/solution.py
@@ -75,7 +75,8 @@
     pairs = []
     place = 0
     for number, first, count in ranges:
-        pairs.append((arrays[number].at[first : first + count], out_ref.at[place : place + count]))
+        if number is not None:
+            pairs.append((arrays[number].at[first : first + count], out_ref.at[place : place + count]))
         place += count
     run_copies(pairs, semaphores)
 
@@ -223,9 +224,9 @@
     key_refs, value_refs = take(parts), take(parts)
     query_refs, grad_refs, dots_refs = take(parts * sources), take(parts * sources), take(parts * sources)
     total_refs = take(sources)
-    before_refs = take(sources) if before else ()
-    piece_refs, query_grad_refs = take(parts), take(sources)
-    weight_ref, score_ref = refs
+    before_refs = take(before)
+    piece_refs, query_grad_refs = take(parts), refs[:-2]
+    weight_ref, score_ref = refs[-2:]
     if before:
         closed = before_refs[0][...]
         for ref in before_refs[1:]:
@@ -263,17 +264,20 @@
                 place = low - part * rows
                 piece_refs[part][place : place + high - low] = key_grad[low - first : high - first]
                 piece_refs[part][rows + place : rows + place + high - low] = value_grad[low - first : high - first]
-    for source in range(sources):
-        query_grad = lax.dot_general(
-            score_ref[:, source * slab : (source + 1) * slab],
-            keys,
-            (((0,), (0,)), ((), ())),
-            preferred_element_type=jnp.float32,
-        )
-        query_grad_refs[source][...] = (query_grad * SCALE).astype(query_grad_refs[source].dtype)
-
-
-def attention(head, heads, rows, keys, values, queries, grads, dots, totals, before):
+    start = 0
+    for ref in query_grad_refs:
+        for first in range(0, ref.shape[0], slab):
+            query_grad = lax.dot_general(
+                score_ref[:, start : start + slab],
+                keys,
+                (((0,), (0,)), ((), ())),
+                preferred_element_type=jnp.float32,
+            )
+            ref[first : first + slab] = (query_grad * SCALE).astype(ref.dtype)
+            start += slab
+
+
+def attention(head, heads, rows, keys, values, queries, grads, dots, totals, before, query_grads):
     parts = len(keys)
     sources = len(totals)
     slab = parts * rows
@@ -283,15 +287,14 @@
     line = pl.BlockSpec((heads, slab), lambda step: (0, 0))
     depth = (3 if before else 2) * rows
     out_specs, _ = block_specs(depth, [(None, 0)] * parts)
-    query_specs, _ = block_specs(slab, [(None, 0)] * sources)
+    query_specs = [pl.BlockSpec((count * slab, HD), lambda step: (0, 0)) for count, _ in query_grads]
     outs = pl.pallas_call(
-        functools.partial(attention_kernel, parts, sources, head, rows, bool(before)),
+        functools.partial(attention_kernel, parts, sources, head, rows, len(before)),
         grid=(1,),
         in_specs=in_specs + dot_specs + [line] * sources + before_specs,
         out_specs=out_specs + query_specs,
         out_shape=[jax.ShapeDtypeStruct((depth, HD), jnp.bfloat16)] * parts
-        + [jax.ShapeDtypeStruct((slab, HD), jnp.float32)]
-        + [jax.ShapeDtypeStruct((slab, HD), jnp.bfloat16)] * (sources - 1),
+        + [jax.ShapeDtypeStruct((count * slab, HD), dtype) for count, dtype in query_grads],
         scratch_shapes=[pltpu.VMEM((slab, sources * slab), jnp.bfloat16)] * 2,
         compiler_params=params(),
         cost_estimate=pl.CostEstimate(
@@ -387,9 +390,6 @@
 def neighbours(size):
     if size == 1:
         return []
-    if size == 2:
-        swapped = [(0, 1), (1, 0)]
-        return [(swapped, swapped)]
     up = [(index, index + 1) for index in range(size - 1)]
     down = [(index + 1, index) for index in range(size - 1)]
     return [(up, down), (down, up)]
@@ -398,10 +398,6 @@
 def exchange_totals(partial, sides):
     if not sides:
         return partial
-    if len(sides) == 1:
-        other = lax.ppermute(jnp.concatenate(partial), "tm", sides[0][0])
-        heads = partial[0].shape[0]
-        return [join_totals([partial[0], other[heads:]]), join_totals([partial[1], other[:heads]])]
     position = lax.axis_index("tm")
     present = [position < lax.axis_size("tm") - 1, position > 0]
     values = [partial[0]]
@@ -409,6 +405,13 @@
         values.append(jnp.where(flag, lax.ppermute(value, "tm", back), -jnp.inf))
     own = join_totals(values)
     return [own] + [lax.ppermute(own, "tm", there) for there, _ in sides]
+
+
+def swap_totals(partial):
+    both = jnp.concatenate(partial)
+    heads = partial[0].shape[0]
+    joined = join_totals([both, swap(both, "tm", 1)])
+    return [joined[:heads], joined[heads:]]
 
 
 def local(queries, keys, values, attn_out, out_grad, out_gain):
@@ -419,10 +422,20 @@
     rest = list(range(1, heads))
     dots = dots_depth(rows, heads)
     every = list(range(parts))
+    paired = span == 2
     sides = neighbours(span)
+    slabs = 2 if paired else 1
 
     def forward(array):
+        if paired:
+            return [lax.all_gather(array, "tm", axis=0, tiled=True)]
         return [lax.ppermute(array, "tm", there) for there, _ in sides]
+
+    def forwarded(arrays, place):
+        return [(array, index * (array.shape[0] // slabs) + place) for array in arrays for index in range(slabs)]
+
+    def placed(arrays, depth, place):
+        return [(array, row // depth) for array, row in forwarded(arrays, place)]
 
     with jax.named_scope("keys_queries"):
         packed = pack([keys[0], queries[0]], parts, list(range(heads)))
@@ -451,19 +464,23 @@
         lead = swap_pieces(sent_lead, pairs)
     with jax.named_scope("halo_first_grads"):
         ranges = [(part, 0, rows) for part in every] + [(part, 2 * rows, dots) for part in every]
+        ranges.append((None, 0, -parts * dots % rows))
         lead_side = forward(gather_rows(lead, ranges))
     with jax.named_scope("totals"):
         key_places = [[(piece, head) for piece in pairs] for head in range(heads)]
-        query_places = [[[(piece, heads + head) for piece in pairs] for head in range(heads)]]
-        for first, others in zip(first_side, late_side):
+        query_places = []
+        if not paired:
+            query_places.append([[(piece, heads + head) for piece in pairs] for head in range(heads)])
+        for source in range(len(first_side) * slabs):
             query_places.append(
                 [
-                    [(first, head)] + [(others, (part - 1) * heads + head) for part in every[1:]]
+                    [placed(first_side, rows, head * rows)[source]]
+                    + [placed(late_side, rows, ((part - 1) * heads + head) * rows)[source] for part in every[1:]]
                     for head in range(heads)
                 ]
             )
         part_totals = partial_totals(key_places, query_places, rows)
-        totals = exchange_totals(part_totals, sides)
+        totals = swap_totals(part_totals) if paired else exchange_totals(part_totals, sides)
     gain = advance(after([gain], late)[0], 2)
     with jax.named_scope("rest_grads"):
         rest_grads = swap_pieces(after(sent_rest, gain), lead)
@@ -472,19 +489,22 @@
         rest_side = forward(gather_rows(rest_grads, ranges))
     with jax.named_scope("rest_values"):
         rest_values = swap_pieces(after(pack([values[0]], parts, rest), part_totals), rest_grads)
-    dot_places = [(piece, 2 * rows // dots) for piece in lead]
-    dot_places += [(array, parts * rows // dots + part) for array in lead_side for part in every]
+    dot_places = [] if paired else [(piece, 2 * rows // dots) for piece in lead]
+    for source in range(len(lead_side) * slabs):
+        dot_places += [placed(lead_side, dots, parts * rows + part * dots)[source] for part in every]
+    query_grad_kinds = [(2, jnp.float32)] if paired else [(1, jnp.float32)] + [(1, jnp.bfloat16)] * len(sides)
     stages, pieces, open_grads = [], [], []
     gate = rest_values
     for head in range(heads):
         if head == 0:
             value_places = [(piece, 1) for piece in lead]
-            grad_places = [(piece, 0) for piece in lead] + [(array, part) for array in lead_side for part in every]
+            own_grads, sent, start = lead, lead_side, 0
         else:
             value_places = [(piece, head - 1) for piece in rest_values]
-            grad_places = [(piece, head - 1) for piece in rest_grads]
-            grad_places += [(array, (head - 1) * parts + part) for array in rest_side for part in every]
-        final = head == heads - 1
+            own_grads, sent, start = rest_grads, rest_side, (head - 1) * parts
+        grad_places = [] if paired else [(piece, max(0, head - 1)) for piece in own_grads]
+        for source in range(len(sent) * slabs):
+            grad_places += [placed(sent, rows, (start + part) * rows)[source] for part in every]
         before = open_grads if head else ()
         with jax.named_scope("attention_%d" % head):
             leaving, query_grads = attention(
@@ -498,22 +518,25 @@
                 dot_places,
                 totals,
                 before,
+                query_grad_kinds,
             )
         stages.append([(1, head), (2, head)] + ([(0, head - 1)] if before else []))
-        query_grads = after(query_grads, gate[-1])
+        query_grads = after(query_grads, gate[1:])
         with jax.named_scope("halo_query_grads_%d" % head):
-            back_grads = [lax.ppermute(other, "tm", back) for other, (_, back) in zip(query_grads[1:], sides)]
-            open_grads = list(query_grads[:1]) + back_grads
+            if paired:
+                open_grads = [lax.psum_scatter(query_grads[0], "tm", scatter_dimension=0, tiled=True)]
+            else:
+                open_grads = [query_grads[0]]
+                for other, (_, back) in zip(query_grads[1:], sides):
+                    open_grads.append(lax.ppermute(other, "tm", back))
         with jax.named_scope("returns_%d" % head):
             pieces.append(swap_pieces(leaving, gate))
         gate = pieces[-1]
-        if not final:
-            gain = advance(after([gain], gate[-1])[0])
     with jax.named_scope("returns_last"):
         stages.append([(0, heads - 1)])
         pieces.append(swap_pieces(close(open_grads, parts)))
     result = unpack(stages, pieces, rows, heads)
-    gain = advance(gain, len(steps)).reshape(channels) / token_count
+    gain = advance(after([gain], pieces[-3])[0], len(steps)).reshape(channels) / token_count
     return tuple(grad[None] for grad in result) + (gain,)
 
 

time: 117 us -> 215 us (1.84)
  blocking collectives: 0 us -> 39 us
  local copies, waits for them, and re-layouts: 3.9 us -> 28.8 us
  Pallas kernels: 18.1 us -> 40 us
  between operations: 0.96 us -> 14.2 us
  starting transfers between devices: 57.1 us -> 51.1 us
  waiting for transfers between devices: 35.7 us -> 40 us
    all_gather x0 -> x4, blocking collectives: none -> 39 us  [forward(): return [lax.all_gather(array, 'tm', axis=0, tiled=True)]]
    unnamed x10 -> x124, local copies, waits for them, and re-layouts: 3.19 us -> 28.1 us
    pallas_call x1, Pallas kernels: 1.49 us -> 23.8 us  [unpack(): pl.pallas_call(functools.partial(unpack_kernel, parts, rows, heads, stage...]
    reduce_scatter x0 -> x3, waiting for transfers between devices: none -> 14.9 us  [local(): lax.psum_scatter(query_grads[0], 'tm', scatter_dimension=0, tiled=True)]
    ppermute x8 -> x0, starting transfers between devices: 9.98 us -> none  [the longest x3 5.28 us: local(): lax.ppermute(other, 'tm', back)]
    ppermute x29 -> x30, waiting for transfers between devices: 32.3 us -> 25 us  [swap(): lax.ppermute(value, axis, [(index, index ^ distance) for index in range(l...]
    ppermute x29 -> x30, starting transfers between devices: 47.1 us -> 51 us  [swap(): lax.ppermute(value, axis, [(index, index ^ distance) for index in range(l...]
    ppermute x8 -> x0, waiting for transfers between devices: 3.34 us -> none  [the longest x4 3.33 us: forward(): return [lax.ppermute(array, 'tm', there) for there, _ in sides]]
  transfers between devices with their start and end apart: 37 -> 33, of which waited for: 16 -> 8; matrix products, arithmetic and copies ran while one was open for 1% -> 1% of each run, Pallas kernels for 13% -> 5%
where the time goes in v6:
time: 215 us; the launch traced here: 214 us
  starting transfers between devices  51.1 us (24%)
  Pallas kernels  40 us (19%)
  waiting for transfers between devices  40 us (19%)
  blocking collectives  39 us (18%)
  local copies, waits for them, and re-layouts  28.8 us (13%)
  between operations  14.2 us (7%)
    ppermute x30, starting transfers between devices, swap(): lax.ppermute(value, axis, [(index, index ^ distance) for index in range(l...  51 us
    all_gather x4, blocking collectives, forward(): return [lax.all_gather(array, 'tm', axis=0, tiled=True)]  39 us
    unnamed x124, local copies, waits for them, and re-layouts  28.1 us
    ppermute x30, waiting for transfers between devices, swap(): lax.ppermute(value, axis, [(index, index ^ distance) for index in range(l...  25 us
    pallas_call x1, Pallas kernels, unpack(): pl.pallas_call(functools.partial(unpack_kernel, parts, rows, heads, stage...  23.8 us
    reduce_scatter x3, waiting for transfers between devices, local(): lax.psum_scatter(query_grads[0], 'tm', scatter_dimension=0, tiled=True)  14.9 us
    pallas_call x3, Pallas kernels, attention(): pl.pallas_call(functools.partial(attention_kernel, parts, sources, head,...  9.97 us
  transfers between devices with their start and end apart: 33, of which 8 were waited for; matrix products, arithmetic and copies ran while one was open for 1% of the time, Pallas kernels for 5%

profile of v6, /device:TPU:0, one launch (start us, length us, event | category | flops | bytes accessed | tf_op | source)
XLA Modules:
  0.0 214.4 jit_solution(3023230483295371507)
XLA Ops:
  9.9 3.1 %collective-permute-start = (bf16[1152,128]{1,0:T(8,128)(2,1)S(1)}, bf16[1152,128]{1,0:T(8,128)(2,1)S(1)}, u32[]{:S(2)}, u32[]{:S(2)}) collective-permute-start(bf16[1152,128]{1,0:T(8,128)(2,1)S(1)} %get-tuple-element.81), channel_id=1, source_target_pairs={{0,4},{4,0},{8,12},{12,8},{1,5},{5,1},{9,13},{13,9},{2,6},{6,2},{1... | collective-permute-start | bytes 884744 | tf_op jit(solution)/shard_map/keys_queries/ppermute | solution.py:359
  12.9 2.6 %collective-permute-start.1 = (bf16[1152,128]{1,0:T(8,128)(2,1)S(1)}, bf16[1152,128]{1,0:T(8,128)(2,1)S(1)}, u32[]{:S(2)}, u32[]{:S(2)}) collective-permute-start(bf16[1152,128]{1,0:T(8,128)(2,1)S(1)} %get-tuple-element.82), channel_id=1, source_target_pairs={{0,8},{4,12},{8,0},{12,4},{1,9},{5,13},{9,1},{13,5},{2,10},{6,14},... | collective-permute-start | bytes 884744 | tf_op jit(solution)/shard_map/keys_queries/ppermute | solution.py:359
  22.9 5.8 %all_gather.12.refs_12_.refs_16_.refs_20_.refs_24_.refs_28_.refs_32_.refs_8_ = bf16[1152,128]{1,0:T(8,128)(2,1)S(1)} all-gather(bf16[576,128]{1,0:T(8,128)(2,1)S(1)} %slice.9), channel_id=1, replica_groups=mesh['tm'=2,'ulysses'=4,'dp'=4] {'tm'}, dimensions={0}, use_global_device_ids=true | all-gather | bytes 442368 | tf_op jit(solution)/shard_map/halo_queries/all_gather | solution.py:431
  28.7 7.7 %collective-permute-done.1.refs_1_.refs_2_.refs_6_.refs_10_ = bf16[1152,128]{1,0:T(8,128)(2,1)S(1)} collective-permute-done((bf16[1152,128]{1,0:T(8,128)(2,1)S(1)}, bf16[1152,128]{1,0:T(8,128)(2,1)S(1)}, u32[]{:S(2)}, u32[]{:S(2)}) %collective-permute-start.1) | collective-permute-done | bytes 294944 | tf_op jit(solution)/shard_map/keys_queries/ppermute | solution.py:359
  37.0 10.1 %all_gather.13.refs_13_.refs_14_.refs_15_.refs_17_.refs_18_.refs_19_.refs_21_.refs_22_.refs_23_.refs_25_.refs_26_.refs_27_.refs_29_.refs_30_.refs_31_.refs_33_.refs_34_.refs_35_.refs_9_.refs_10_.refs_11_ = bf16[3456,128]{1,0:T(8,128)(2,1)S(1)} all-gather(bf16[1728,128]{1,0:T(8,128)(2,1)S(1)} %halo_queries.1), channel_id=1, replica_groups=mesh['tm'=2,'ulysses'=4,'dp'=4] {'tm'}, dimensions={0}, use_global_device_ids=true | all-gather | bytes 1327104 | tf_op jit(solution)/shard_map/halo_queries/all_gather | solution.py:431
  47.1 3.6 %totals.1 = (f32[3,768]{1,0:T(4,128)S(1)}, f32[3,768]{1,0:T(4,128)S(1)}) custom-call(bf16[1152,128]{1,0:T(8,128)(2,1)S(1)} %get-tuple-element.80.refs_0_.refs_4_.refs_8_, bf16[1152,128]{1,0:T(8,128)(2,1)S(1)} %collective-permute-done.refs_0_.refs_1_.refs_5_.refs_9_, bf16[1152,128]{1,0:T(8,128)(2,1)S(1)} %collective-permute-done.1.refs_1_.refs_2_.refs_6_.refs_10_, ...), custom_call_target="tpu_custom_call" | custom-call | flops 905969664 | bytes 2359296 | tf_op jit(solution)/shard_map/totals/pallas_call | solution.py:195
  56.7 6.9 %collective-permute-start.4 = (bf16[400,128]{1,0:T(8,128)(2,1)S(1)}, bf16[400,128]{1,0:T(8,128)(2,1)S(1)}, u32[]{:S(2)}, u32[]{:S(2)}) collective-permute-start(bf16[400,128]{1,0:T(8,128)(2,1)S(1)} %copy-done.52), channel_id=1, source_target_pairs={{0,8},{4,12},{8,0},{12,4},{1,9},{5,13},{9,1},{13,5},{2,10},{6,14},... | collective-permute-start | bytes 307208 | tf_op jit(solution)/shard_map/first_grads/ppermute | solution.py:359
  66.8 7.0 %collective-permute-done.4.refs_2_.refs_6_ = bf16[400,128]{1,0:T(8,128)(2,1)S(1)} collective-permute-done((bf16[400,128]{1,0:T(8,128)(2,1)S(1)}, bf16[400,128]{1,0:T(8,128)(2,1)S(1)}, u32[]{:S(2)}, u32[]{:S(2)}) %collective-permute-start.4) | collective-permute-done | bytes 102432 | tf_op jit(solution)/shard_map/first_grads/ppermute | solution.py:359
  73.8 4.2 %collective-permute-start.10 = (bf16[384,128]{1,0:T(8,128)(2,1)S(1)}, bf16[384,128]{1,0:T(8,128)(2,1)S(1)}, u32[]{:S(2)}, u32[]{:S(2)}) collective-permute-start(bf16[384,128]{1,0:T(8,128)(2,1)S(1)} %copy-done.60), channel_id=1, source_target_pairs={{0,4},{4,0},{8,12},{12,8},{1,5},{5,1},{9,13},{13,9},{2,6},{6,2},{1... | collective-permute-start | bytes 294920 | tf_op jit(solution)/shard_map/rest_grads/ppermute | solution.py:359
  78.3 6.9 %all_gather.14.refs_16_.refs_17_.refs_18_.refs_19_.refs_20_.refs_21_.refs_22_.refs_23_.refs_24_.refs_25_.refs_26_.refs_27_.refs_28_.refs_29_.refs_30_.refs_31_ = bf16[1920,128]{1,0:T(8,128)(2,1)S(1)} all-gather(bf16[960,128]{1,0:T(8,128)(2,1)S(1)} %halo_first_grads.1), channel_id=1, replica_groups=mesh['tm'=2,'ulysses'=4,'dp'=4] {'tm'}, dimensions={0}, use_global_device_ids=true | all-gather | bytes 737280 | tf_op jit(solution)/shard_map/halo_first_grads/all_gather | solution.py:431
  88.6 2.9 %collective-permute-start.11 = (bf16[384,128]{1,0:T(8,128)(2,1)S(1)}, bf16[384,128]{1,0:T(8,128)(2,1)S(1)}, u32[]{:S(2)}, u32[]{:S(2)}) collective-permute-start(bf16[384,128]{1,0:T(8,128)(2,1)S(1)} %get-tuple-element.112), channel_id=1, source_target_pairs={{0,4},{4,0},{8,12},{12,8},{1,5},{5,1},{9,13},{13,9},{2,6},{6,2},{1... | collective-permute-start | bytes 294920 | tf_op jit(solution)/shard_map/rest_values/ppermute | solution.py:359
  91.5 3.3 %attention_0.1 = (bf16[384,128]{1,0:T(8,128)(2,1)S(1)}, bf16[384,128]{1,0:T(8,128)(2,1)}, bf16[384,128]{1,0:T(8,128)(2,1)}, bf16[384,128]{1,0:T(8,128)(2,1)}, f32[1536,128]{1,0:T(8,128)S(1)}) custom-call(bf16[1152,128]{1,0:T(8,128)(2,1)S(1)} %get-tuple-element.80.refs_0_.refs_4_.refs_8_, ...), custom_call_target="tpu_custom_call" | custom-call | flops 1509949440 | bytes 3145728 | tf_op jit(solution)/shard_map/attention_0/pallas_call | solution.py:291
  98.7 16.2 %all_gather.15.refs_16_.refs_17_.refs_18_.refs_19_.refs_20_.refs_21_.refs_22_.refs_23_ = bf16[3072,128]{1,0:T(8,128)(2,1)S(1)} all-gather(bf16[1536,128]{1,0:T(8,128)(2,1)S(1)} %halo_rest_grads.1), channel_id=1, replica_groups=mesh['tm'=2,'ulysses'=4,'dp'=4] {'tm'}, dimensions={0}, use_global_device_ids=true | all-gather | bytes 1179648 | tf_op jit(solution)/shard_map/halo_rest_grads/all_gather | solution.py:431
  116.8 2.5 %collective-permute-start.12 = (bf16[384,128]{1,0:T(8,128)(2,1)}, bf16[384,128]{1,0:T(8,128)(2,1)}, u32[]{:S(2)}, u32[]{:S(2)}) collective-permute-start(bf16[384,128]{1,0:T(8,128)(2,1)} %get-tuple-element.113), channel_id=1, source_target_pairs={{0,4},{4,0},{8,12},{12,8},{1,5},{5,1},{9,13},{13,9},{2,6},{6,2},{1... | collective-permute-start | bytes 294920 | tf_op jit(solution)/shard_map/returns_0/ppermute | solution.py:359
  123.8 3.3 %attention_1.1 = (bf16[576,128]{1,0:T(8,128)(2,1)S(1)}, bf16[576,128]{1,0:T(8,128)(2,1)S(1)}, bf16[576,128]{1,0:T(8,128)(2,1)S(1)}, bf16[576,128]{1,0:T(8,128)(2,1)S(1)}, f32[1536,128]{1,0:T(8,128)S(1)}) custom-call(bf16[1152,128]{1,0:T(8,128)(2,1)S(1)} %copy-done.1, bf16[1152,128]{1,0:T(8,128)(2,1)S(1)} %collective-permute-done.refs_0_.refs_1_.refs_5_.refs_9_, ...), custom_call_target="tpu_custom_call" | custom-call | flops 1509949440 | bytes 3145728 | tf_op jit(solution)/shard_map/attention_1/pallas_call | solution.py:291
  131.0 2.9 %collective-permute-start.19 = (bf16[576,128]{1,0:T(8,128)(2,1)}, bf16[576,128]{1,0:T(8,128)(2,1)}, u32[]{:S(2)}, u32[]{:S(2)}) collective-permute-start(bf16[576,128]{1,0:T(8,128)(2,1)} %copy-done.46), channel_id=1, source_target_pairs={{0,4},{4,0},{8,12},{12,8},{1,5},{5,1},{9,13},{13,9},{2,6},{6,2},{1... | collective-permute-start | bytes 442376 | tf_op jit(solution)/shard_map/returns_1/ppermute | solution.py:359
  134.0 10.2 %reduce-scatter.6.cloned.1.call-done.refs_34_ = f32[768,128]{1,0:T(8,128)} async-done(((f32[1536,128]{1,0:T(8,128)}), f32[768,128]{1,0:T(8,128)}) %reduce-scatter.6.cloned.1.call-update) | async-done | bytes 393232 | tf_op jit(solution)/shard_map/halo_query_grads_1/reduce_scatter | solution.py:527
  148.6 3.3 %attention_2.1 = (bf16[576,128]{1,0:T(8,128)(2,1)S(1)}, bf16[576,128]{1,0:T(8,128)(2,1)S(1)}, bf16[576,128]{1,0:T(8,128)(2,1)S(1)}, bf16[576,128]{1,0:T(8,128)(2,1)S(1)}, f32[1536,128]{1,0:T(8,128)S(1)}) custom-call(bf16[1152,128]{1,0:T(8,128)(2,1)S(1)} %copy-done.2, bf16[1152,128]{1,0:T(8,128)(2,1)S(1)} %collective-permute-done.refs_0_.refs_1_.refs_5_.refs_9_, ...), custom_call_target="tpu_custom_call" | custom-call | flops 1509949440 | bytes 3145728 | tf_op jit(solution)/shard_map/attention_2/pallas_call | solution.py:291
  156.4 3.3 %collective-permute-start.24 = (bf16[576,128]{1,0:T(8,128)(2,1)S(1)}, bf16[576,128]{1,0:T(8,128)(2,1)S(1)}, u32[]{:S(2)}, u32[]{:S(2)}) collective-permute-start(bf16[576,128]{1,0:T(8,128)(2,1)S(1)} %copy-done.45), channel_id=1, source_target_pairs={{0,12},{4,8},{8,4},{12,0},{1,13},{5,9},{9,5},{13,1},{2,14},{6,10},... | collective-permute-start | bytes 442376 | tf_op jit(solution)/shard_map/returns_2/ppermute | solution.py:359
  159.7 4.3 %collective-permute-done.28 = f32[12,128]{1,0:T(8,128)S(1)} collective-permute-done((f32[12,128]{1,0:T(8,128)S(1)}, f32[12,128]{1,0:T(8,128)S(1)}, u32[]{:S(2)}, u32[]{:S(2)}) %collective-permute-start.28) | collective-permute-done | bytes 6176 | tf_op jit(solution)/shard_map/gain/ppermute | solution.py:359
  164.6 2.4 %collective-permute-start.23 = (bf16[576,128]{1,0:T(8,128)(2,1)S(1)}, bf16[576,128]{1,0:T(8,128)(2,1)S(1)}, u32[]{:S(2)}, u32[]{:S(2)}) collective-permute-start(bf16[576,128]{1,0:T(8,128)(2,1)S(1)} %copy-done.43), channel_id=1, source_target_pairs={{0,8},{4,12},{8,0},{12,4},{1,9},{5,13},{9,1},{13,5},{2,10},{6,14},... | collective-permute-start | bytes 442376 | tf_op jit(solution)/shard_map/returns_2/ppermute | solution.py:359
  168.5 4.7 %reduce-scatter.8.cloned.1.call-done.refs_0_ = f32[768,128]{1,0:T(8,128)} async-done(((f32[1536,128]{1,0:T(8,128)}), f32[768,128]{1,0:T(8,128)}) %reduce-scatter.8.cloned.1.call-update) | async-done | bytes 393232 | tf_op jit(solution)/shard_map/halo_query_grads_2/reduce_scatter | solution.py:527
  181.6 2.5 %collective-permute-done.27.refs_15_ = bf16[192,128]{1,0:T(8,128)(2,1)S(1)} collective-permute-done((bf16[192,128]{1,0:T(8,128)(2,1)S(1)}, bf16[192,128]{1,0:T(8,128)(2,1)S(1)}, u32[]{:S(2)}, u32[]{:S(2)}) %collective-permute-start.27) | collective-permute-done | bytes 49184 | tf_op jit(solution)/shard_map/returns_last/ppermute | solution.py:359
  184.0 23.8 %shard_map.93 = (bf16[192,1536]{1,0:T(8,128)(2,1)}, bf16[192,1536]{1,0:T(8,128)(2,1)}, bf16[192,1536]{1,0:T(8,128)(2,1)}) custom-call(bf16[384,128]{1,0:T(8,128)(2,1)S(1)} %copy-done.31, bf16[384,128]{1,0:T(8,128)(2,1)} %collective-permute-done.12.refs_1_, bf16[384,128]{1,0:T(8,128)(2,1)} %collective-permute-done.15.refs_2_, ...), custom_call_target="tpu_custom_call" | custom-call | flops 1 | bytes 1 | tf_op jit(solution)/shard_map/pallas_call | solution.py:347
  (196 shorter events, 56.7 us)
Async XLA Ops:
  7.2 112.1 %reduce-scatter.4.cloned.1.call-start = ((), (), s32[]{:S(2)}) async-start(), calls=%async_computation.3 | async-start | bytes 1179648 | tf_op jit(solution)/shard_map/halo_query_grads_0/reduce_scatter | solution.py:527
  9.9 18.9 %collective-permute-start = (bf16[1152,128]{1,0:T(8,128)(2,1)S(1)}, bf16[1152,128]{1,0:T(8,128)(2,1)S(1)}, u32[]{:S(2)}, u32[]{:S(2)}) collective-permute-start(bf16[1152,128]{1,0:T(8,128)(2,1)S(1)} %get-tuple-element.81), channel_id=1, source_target_pairs={{0,4},{4,0},{8,12},{12,8},{1,5},{5,1},{9,13},{13,9},{2,6},{6,2},{1... | collective-permute-start | bytes 884744 | tf_op jit(solution)/shard_map/keys_queries/ppermute | solution.py:359
  12.9 23.5 %collective-permute-start.1 = (bf16[1152,128]{1,0:T(8,128)(2,1)S(1)}, bf16[1152,128]{1,0:T(8,128)(2,1)S(1)}, u32[]{:S(2)}, u32[]{:S(2)}) collective-permute-start(bf16[1152,128]{1,0:T(8,128)(2,1)S(1)} %get-tuple-element.82), channel_id=1, source_target_pairs={{0,8},{4,12},{8,0},{12,4},{1,9},{5,13},{9,1},{13,5},{2,10},{6,14},... | collective-permute-start | bytes 884744 | tf_op jit(solution)/shard_map/keys_queries/ppermute | solution.py:359
  15.5 20.9 %collective-permute-start.2 = (bf16[1152,128]{1,0:T(8,128)(2,1)S(1)}, bf16[1152,128]{1,0:T(8,128)(2,1)S(1)}, u32[]{:S(2)}, u32[]{:S(2)}) collective-permute-start(bf16[1152,128]{1,0:T(8,128)(2,1)S(1)} %get-tuple-element.83), channel_id=1, source_target_pairs={{0,12},{4,8},{8,4},{12,0},{1,13},{5,9},{9,5},{13,1},{2,14},{6,10},... | collective-permute-start | bytes 884744 | tf_op jit(solution)/shard_map/keys_queries/ppermute | solution.py:359
  50.7 13.6 %collective-permute-start.7 = (f32[6,768]{1,0:T(8,128)S(1)}, f32[6,768]{1,0:T(8,128)S(1)}, u32[]{:S(2)}, u32[]{:S(2)}) collective-permute-start(f32[6,768]{1,0:T(8,128)S(1)} %pad_maximum_fusion), channel_id=1, source_target_pairs={{0,16},{16,0},{1,17},{17,1},{2,18},{18,2},{3,19},{19,3},{4,20},{20... | collective-permute-start | bytes 55304 | tf_op jit(solution)/shard_map/totals/ppermute | solution.py:359
  53.5 10.3 %collective-permute-start.9 = (f32[12,128]{1,0:T(8,128)S(1)}, f32[12,128]{1,0:T(8,128)S(1)}, u32[]{:S(2)}, u32[]{:S(2)}) collective-permute-start(f32[12,128]{1,0:T(8,128)S(1)} %add.30), channel_id=1, source_target_pairs={{0,2},{1,3},{2,0},{3,1},{4,6},{5,7},{6,4},{7,5},{8,10},{9,11},{10,... | collective-permute-start | bytes 18440 | tf_op jit(solution)/shard_map/gain/ppermute | solution.py:359
  56.7 17.1 %collective-permute-start.4 = (bf16[400,128]{1,0:T(8,128)(2,1)S(1)}, bf16[400,128]{1,0:T(8,128)(2,1)S(1)}, u32[]{:S(2)}, u32[]{:S(2)}) collective-permute-start(bf16[400,128]{1,0:T(8,128)(2,1)S(1)} %copy-done.52), channel_id=1, source_target_pairs={{0,8},{4,12},{8,0},{12,4},{1,9},{5,13},{9,1},{13,5},{2,10},{6,14},... | collective-permute-start | bytes 307208 | tf_op jit(solution)/shard_map/first_grads/ppermute | solution.py:359
  63.6 10.2 %collective-permute-start.3 = (bf16[400,128]{1,0:T(8,128)(2,1)S(1)}, bf16[400,128]{1,0:T(8,128)(2,1)S(1)}, u32[]{:S(2)}, u32[]{:S(2)}) collective-permute-start(bf16[400,128]{1,0:T(8,128)(2,1)S(1)} %copy-done.50), channel_id=1, source_target_pairs={{0,4},{4,0},{8,12},{12,8},{1,5},{5,1},{9,13},{13,9},{2,6},{6,2},{1... | collective-permute-start | bytes 307208 | tf_op jit(solution)/shard_map/first_grads/ppermute | solution.py:359
  64.4 22.1 %collective-permute-start.16 = (bf16[384,128]{1,0:T(8,128)(2,1)S(1)}, bf16[384,128]{1,0:T(8,128)(2,1)S(1)}, u32[]{:S(2)}, u32[]{:S(2)}) collective-permute-start(bf16[384,128]{1,0:T(8,128)(2,1)S(1)} %copy-done.56), channel_id=1, source_target_pairs={{0,12},{4,8},{8,4},{12,0},{1,13},{5,9},{9,5},{13,1},{2,14},{6,10},... | collective-permute-start | bytes 294920 | tf_op jit(solution)/shard_map/rest_grads/ppermute | solution.py:359
  73.8 12.1 %collective-permute-start.13 = (bf16[384,128]{1,0:T(8,128)(2,1)S(1)}, bf16[384,128]{1,0:T(8,128)(2,1)S(1)}, u32[]{:S(2)}, u32[]{:S(2)}) collective-permute-start(bf16[384,128]{1,0:T(8,128)(2,1)S(1)} %copy-done.58), channel_id=1, source_target_pairs={{0,8},{4,12},{8,0},{12,4},{1,9},{5,13},{9,1},{13,5},{2,10},{6,14},... | collective-permute-start | bytes 294920 | tf_op jit(solution)/shard_map/rest_grads/ppermute | solution.py:359
  73.8 11.4 %collective-permute-start.10 = (bf16[384,128]{1,0:T(8,128)(2,1)S(1)}, bf16[384,128]{1,0:T(8,128)(2,1)S(1)}, u32[]{:S(2)}, u32[]{:S(2)}) collective-permute-start(bf16[384,128]{1,0:T(8,128)(2,1)S(1)} %copy-done.60), channel_id=1, source_target_pairs={{0,4},{4,0},{8,12},{12,8},{1,5},{5,1},{9,13},{13,9},{2,6},{6,2},{1... | collective-permute-start | bytes 294920 | tf_op jit(solution)/shard_map/rest_grads/ppermute | solution.py:359
  87.1 9.3 %collective-permute-start.17 = (bf16[384,128]{1,0:T(8,128)(2,1)S(1)}, bf16[384,128]{1,0:T(8,128)(2,1)S(1)}, u32[]{:S(2)}, u32[]{:S(2)}) collective-permute-start(bf16[384,128]{1,0:T(8,128)(2,1)S(1)} %get-tuple-element.124), channel_id=1, source_target_pairs={{0,12},{4,8},{8,4},{12,0},{1,13},{5,9},{9,5},{13,1},{2,14},{6,10},... | collective-permute-start | bytes 294920 | tf_op jit(solution)/shard_map/rest_values/ppermute | solution.py:359
  97.2 47.0 %reduce-scatter.6.cloned.1.call-start = ((), (), s32[]{:S(2)}) async-start(), calls=%async_computation.4 | async-start | bytes 1179648 | tf_op jit(solution)/shard_map/halo_query_grads_1/reduce_scatter | solution.py:527
  114.9 13.7 %collective-permute-start.18 = (bf16[384,128]{1,0:T(8,128)(2,1)}, bf16[384,128]{1,0:T(8,128)(2,1)}, u32[]{:S(2)}, u32[]{:S(2)}) collective-permute-start(bf16[384,128]{1,0:T(8,128)(2,1)} %get-tuple-element.125), channel_id=1, source_target_pairs={{0,12},{4,8},{8,4},{12,0},{1,13},{5,9},{9,5},{13,1},{2,14},{6,10},... | collective-permute-start | bytes 294920 | tf_op jit(solution)/shard_map/returns_0/ppermute | solution.py:359
  114.9 14.4 %collective-permute-start.15 = (bf16[384,128]{1,0:T(8,128)(2,1)}, bf16[384,128]{1,0:T(8,128)(2,1)}, u32[]{:S(2)}, u32[]{:S(2)}) collective-permute-start(bf16[384,128]{1,0:T(8,128)(2,1)} %get-tuple-element.119), channel_id=1, source_target_pairs={{0,8},{4,12},{8,0},{12,4},{1,9},{5,13},{9,1},{13,5},{2,10},{6,14},... | collective-permute-start | bytes 294920 | tf_op jit(solution)/shard_map/returns_0/ppermute | solution.py:359
  116.8 12.6 %collective-permute-start.12 = (bf16[384,128]{1,0:T(8,128)(2,1)}, bf16[384,128]{1,0:T(8,128)(2,1)}, u32[]{:S(2)}, u32[]{:S(2)}) collective-permute-start(bf16[384,128]{1,0:T(8,128)(2,1)} %get-tuple-element.113), channel_id=1, source_target_pairs={{0,4},{4,0},{8,12},{12,8},{1,5},{5,1},{9,13},{13,9},{2,6},{6,2},{1... | collective-permute-start | bytes 294920 | tf_op jit(solution)/shard_map/returns_0/ppermute | solution.py:359
  129.4 43.7 %reduce-scatter.8.cloned.1.call-start = ((), (), s32[]{:S(2)}) async-start(), calls=%async_computation.5 | async-start | bytes 1179648 | tf_op jit(solution)/shard_map/halo_query_grads_2/reduce_scatter | solution.py:527
  129.5 26.0 %collective-permute-start.21 = (bf16[576,128]{1,0:T(8,128)(2,1)}, bf16[576,128]{1,0:T(8,128)(2,1)}, u32[]{:S(2)}, u32[]{:S(2)}) collective-permute-start(bf16[576,128]{1,0:T(8,128)(2,1)} %copy-done.48), channel_id=1, source_target_pairs={{0,12},{4,8},{8,4},{12,0},{1,13},{5,9},{9,5},{13,1},{2,14},{6,10},... | collective-permute-start | bytes 442376 | tf_op jit(solution)/shard_map/returns_1/ppermute | solution.py:359
  129.6 25.9 %collective-permute-start.20 = (bf16[576,128]{1,0:T(8,128)(2,1)}, bf16[576,128]{1,0:T(8,128)(2,1)}, u32[]{:S(2)}, u32[]{:S(2)}) collective-permute-start(bf16[576,128]{1,0:T(8,128)(2,1)} %copy-done.47), channel_id=1, source_target_pairs={{0,8},{4,12},{8,0},{12,4},{1,9},{5,13},{9,1},{13,5},{2,10},{6,14},... | collective-permute-start | bytes 442376 | tf_op jit(solution)/shard_map/returns_1/ppermute | solution.py:359
  131.0 24.5 %collective-permute-start.19 = (bf16[576,128]{1,0:T(8,128)(2,1)}, bf16[576,128]{1,0:T(8,128)(2,1)}, u32[]{:S(2)}, u32[]{:S(2)}) collective-permute-start(bf16[576,128]{1,0:T(8,128)(2,1)} %copy-done.46), channel_id=1, source_target_pairs={{0,4},{4,0},{8,12},{12,8},{1,5},{5,1},{9,13},{13,9},{2,6},{6,2},{1... | collective-permute-start | bytes 442376 | tf_op jit(solution)/shard_map/returns_1/ppermute | solution.py:359
  156.4 21.7 %collective-permute-start.24 = (bf16[576,128]{1,0:T(8,128)(2,1)S(1)}, bf16[576,128]{1,0:T(8,128)(2,1)S(1)}, u32[]{:S(2)}, u32[]{:S(2)}) collective-permute-start(bf16[576,128]{1,0:T(8,128)(2,1)S(1)} %copy-done.45), channel_id=1, source_target_pairs={{0,12},{4,8},{8,4},{12,0},{1,13},{5,9},{9,5},{13,1},{2,14},{6,10},... | collective-permute-start | bytes 442376 | tf_op jit(solution)/shard_map/returns_2/ppermute | solution.py:359
  164.1 11.6 %collective-permute-start.29 = (f32[12,128]{1,0:T(8,128)S(1)}, f32[12,128]{1,0:T(8,128)S(1)}, u32[]{:S(2)}, u32[]{:S(2)}) collective-permute-start(f32[12,128]{1,0:T(8,128)S(1)} %add.32), channel_id=1, source_target_pairs={{0,8},{4,12},{8,0},{12,4},{1,9},{5,13},{9,1},{13,5},{2,10},{6,14},... | collective-permute-start | bytes 18440 | tf_op jit(solution)/shard_map/gain/ppermute | solution.py:359
  164.6 14.6 %collective-permute-start.23 = (bf16[576,128]{1,0:T(8,128)(2,1)S(1)}, bf16[576,128]{1,0:T(8,128)(2,1)S(1)}, u32[]{:S(2)}, u32[]{:S(2)}) collective-permute-start(bf16[576,128]{1,0:T(8,128)(2,1)S(1)} %copy-done.43), channel_id=1, source_target_pairs={{0,8},{4,12},{8,0},{12,4},{1,9},{5,13},{9,1},{13,5},{2,10},{6,14},... | collective-permute-start | bytes 442376 | tf_op jit(solution)/shard_map/returns_2/ppermute | solution.py:359
  167.0 12.2 %collective-permute-start.22 = (bf16[576,128]{1,0:T(8,128)(2,1)S(1)}, bf16[576,128]{1,0:T(8,128)(2,1)S(1)}, u32[]{:S(2)}, u32[]{:S(2)}) collective-permute-start(bf16[576,128]{1,0:T(8,128)(2,1)S(1)} %copy-done.41), channel_id=1, source_target_pairs={{0,4},{4,0},{8,12},{12,8},{1,5},{5,1},{9,13},{13,9},{2,6},{6,2},{1... | collective-permute-start | bytes 442376 | tf_op jit(solution)/shard_map/returns_2/ppermute | solution.py:359
  (71 other events, 360.9 us)
Sparse Core Ops, SparseCore 0:
  97.3 18.3 reduce-scatter.3
  129.6 14.5 reduce-scatter.5
  155.7 17.4 reduce-scatter.7

commit v7 on v5

--- a/solution.py
+++ b/solution.py
@@ -102,49 +102,98 @@
     return -(-2 * heads * dot_groups(rows) // TILE_ROWS) * TILE_ROWS
 
 
-def pack_grads_kernel(parts, out_grad_ref, attn_ref, value_ref, gain_ref, *refs):
-    leads, rests, gain_part_ref = refs[:parts], refs[parts:-1], refs[-1]
+def gain_kernel(out_grad_ref, attn_ref, out_ref):
+    product = out_grad_ref[...].astype(jnp.float32) * attn_ref[...].astype(jnp.float32)
+    out_ref[...] = jnp.sum(product, axis=0, keepdims=True)
+
+
+def gain_partial(out_grad, attn_out):
+    return pl.pallas_call(
+        gain_kernel,
+        out_shape=jax.ShapeDtypeStruct((1, out_grad.shape[1]), jnp.float32),
+        compiler_params=params(),
+        cost_estimate=COST,
+    )(out_grad, attn_out)
+
+
+def split_terms(value, count):
+    terms = []
+    for _ in range(count):
+        term = value.astype(jnp.bfloat16).astype(jnp.float32)
+        terms.append(term)
+        value = value - term
+    return terms
+
+
+def gain_depth(channels):
+    return -(-3 * channels // LANES // TILE_ROWS) * TILE_ROWS
+
+
+def pack_grads_kernel(parts, out_grad_ref, attn_ref, value_ref, gain_ref, partial_ref, *refs):
+    leads, rests = refs[:parts], refs[parts:]
     rows, channels = out_grad_ref.shape
     heads = channels // (parts * HD)
+    depth = 2 * rows + dots_depth(rows, heads)
+    lines = partial_ref.shape[0]
+    partial = jnp.concatenate(split_terms(partial_ref[...], 3), axis=0)
+    spare = gain_depth(channels) - partial.shape[0]
+    if spare:
+        partial = jnp.concatenate([partial, jnp.zeros((spare, LANES), jnp.float32)], axis=0)
     for distance in range(parts):
         terms = []
         for head in range(heads):
             columns = pl.ds(column_of(distance, heads, head), HD)
-            out_grad = out_grad_ref[:, columns].astype(jnp.float32)
-            attn = attn_ref[:, columns].astype(jnp.float32)
-            grad = (out_grad * gain_ref[:, columns]).astype(jnp.bfloat16)
-            gain_part_ref[:, columns] = jnp.sum(out_grad * attn, axis=0, keepdims=True)
+            grad = (out_grad_ref[:, columns].astype(jnp.float32) * gain_ref[:, columns]).astype(jnp.bfloat16)
             if head:
                 rests[distance][(head - 1) * rows : head * rows] = grad
             else:
                 leads[distance][:rows] = grad
                 leads[distance][rows : 2 * rows] = value_ref[:, columns]
-            dots = jnp.sum(jnp.transpose(grad.astype(jnp.float32) * attn), axis=0, keepdims=True)
+            product = grad.astype(jnp.float32) * attn_ref[:, columns].astype(jnp.float32)
+            dots = jnp.sum(jnp.transpose(product), axis=0, keepdims=True)
             for first in range(0, rows, LANES):
                 value = dots[:, first : first + LANES]
                 if value.shape[1] < LANES:
                     rest = jnp.zeros((1, LANES - value.shape[1]), jnp.float32)
                     value = jnp.concatenate([value, rest], axis=1)
-                high = value.astype(jnp.bfloat16).astype(jnp.float32)
-                terms += [high, value - high]
+                terms += split_terms(value, 2)
         rest = dots_depth(rows, heads) - len(terms)
         if rest:
             terms.append(jnp.zeros((rest, LANES), jnp.float32))
-        leads[distance][2 * rows :] = jnp.concatenate(terms, axis=0).astype(jnp.bfloat16)
-
-
-def pack_grads(out_grad, attn_out, values, out_gain, parts):
+        leads[distance][2 * rows : depth] = jnp.concatenate(terms, axis=0).astype(jnp.bfloat16)
+        leads[distance][depth:] = partial.astype(jnp.bfloat16)
+
+
+def pack_grads(out_grad, attn_out, values, out_gain, partial, parts):
     rows, channels = out_grad.shape
     heads = channels // (parts * HD)
-    lead = jax.ShapeDtypeStruct((2 * rows + dots_depth(rows, heads), HD), jnp.bfloat16)
+    depth = 2 * rows + dots_depth(rows, heads) + gain_depth(channels)
+    lead = jax.ShapeDtypeStruct((depth, HD), jnp.bfloat16)
     rest = jax.ShapeDtypeStruct(((heads - 1) * rows, HD), jnp.bfloat16)
     outs = pl.pallas_call(
         functools.partial(pack_grads_kernel, parts),
-        out_shape=[lead] * parts + [rest] * parts + [jax.ShapeDtypeStruct((1, channels), jnp.float32)],
-        compiler_params=params(),
-        cost_estimate=COST,
-    )(out_grad, attn_out, values, out_gain.reshape(1, channels))
-    return outs[:parts], outs[parts : 2 * parts], outs[2 * parts]
+        out_shape=[lead] * parts + [rest] * parts,
+        compiler_params=params(),
+        cost_estimate=COST,
+    )(out_grad, attn_out, values, out_gain.reshape(1, channels), partial)
+    return outs[:parts], outs[parts:]
+
+
+def gain_total_kernel(lines, starts, scale, *refs):
+    values = []
+    for ref, start in zip(refs[:-1], starts):
+        terms = [ref[start + index * lines : start + (index + 1) * lines].astype(jnp.float32) for index in range(3)]
+        values.append(terms[0] + terms[1] + terms[2])
+    refs[-1][...] = tree_sum(values) * scale
+
+
+def gain_total(places, lines, scale):
+    return pl.pallas_call(
+        functools.partial(gain_total_kernel, lines, [start for _, start in places], scale),
+        out_shape=jax.ShapeDtypeStruct((lines, LANES), jnp.float32),
+        compiler_params=params(),
+        cost_estimate=COST,
+    )(*[array for array, _ in places])
 
 
 def stacked(refs):
@@ -366,18 +415,17 @@
     return held
 
 
-def sum_steps(axes):
-    steps = []
-    for axis in axes:
-        size = lax.axis_size(axis)
-        if size & (size - 1):
-            steps.append(functools.partial(lax.psum, axis_name=axis))
-            continue
-        distance = 1
-        while distance < size:
-            steps.append(lambda value, axis=axis, distance=distance: value + swap(value, axis, distance))
-            distance *= 2
-    return steps
+def tree_sum(values):
+    while len(values) > 1:
+        values = [functools.reduce(jnp.add, values[index : index + 2]) for index in range(0, len(values), 2)]
+    return values[0]
+
+
+def sum_over(value, axis):
+    size = lax.axis_size(axis)
+    if size & (size - 1):
+        return lax.psum(value, axis)
+    return tree_sum([value] + [swap(value, axis, distance) for distance in range(1, size)])
 
 
 def after(values, *earlier):
@@ -427,30 +475,26 @@
     with jax.named_scope("keys_queries"):
         packed = pack([keys[0], queries[0]], parts, list(range(heads)))
         pairs = swap_pieces(packed)
+    paired = span == 2
+    with jax.named_scope("gain"):
+        out_grad = after([out_grad], packed[0])[0]
+        gain = gain_partial(out_grad[0], attn_out[0]).reshape(-1, LANES)
+        gain = sum_over(gain, "dp")
+        if not paired:
+            gain = sum_over(gain, "tm")
     with jax.named_scope("grads"):
-        out_grad = after([out_grad], packed[0])[0]
-        sent_lead, sent_rest, gain_part = pack_grads(out_grad[0], attn_out[0], values[0], out_gain, parts)
-    token_count = rows * span * parts * lax.axis_size("dp")
-    gain = gain_part.reshape(-1, LANES)
-    steps = sum_steps(("tm", "dp", "ulysses"))
-
-    def advance(value, count=1):
-        with jax.named_scope("gain"):
-            for step in steps[:count]:
-                value = step(value)
-        del steps[:count]
-        return value
-
-    gain = advance(gain, max(1, len(steps) - 4))
+        sent_lead, sent_rest = pack_grads(out_grad[0], attn_out[0], values[0], out_gain, gain, parts)
     with jax.named_scope("halo_queries"):
         width = heads * rows
         first_side = forward(pairs[0][width:])
-        late = after(pairs[1:], gain, first_side)
+        late = after(pairs[1:], sent_lead[0], first_side)
         late_side = forward(gather_rows(late, [(number, width, width) for number in range(parts - 1)]))
     with jax.named_scope("first_grads"):
         lead = swap_pieces(sent_lead, pairs)
     with jax.named_scope("halo_first_grads"):
+        extra = gain_depth(channels) if paired else 0
         ranges = [(part, 0, rows) for part in every] + [(part, 2 * rows, dots) for part in every]
+        ranges += [(part, 2 * rows + dots, extra) for part in every] * paired
         lead_side = forward(gather_rows(lead, ranges))
     with jax.named_scope("totals"):
         key_places = [[(piece, head) for piece in pairs] for head in range(heads)]
@@ -464,7 +508,6 @@
             )
         part_totals = partial_totals(key_places, query_places, rows)
         totals = exchange_totals(part_totals, sides)
-    gain = advance(after([gain], late)[0], 2)
     with jax.named_scope("rest_grads"):
         rest_grads = swap_pieces(after(sent_rest, gain), lead)
     with jax.named_scope("halo_rest_grads"):
@@ -484,7 +527,6 @@
             value_places = [(piece, head - 1) for piece in rest_values]
             grad_places = [(piece, head - 1) for piece in rest_grads]
             grad_places += [(array, (head - 1) * parts + part) for array in rest_side for part in every]
-        final = head == heads - 1
         before = open_grads if head else ()
         with jax.named_scope("attention_%d" % head):
             leaving, query_grads = attention(
@@ -500,21 +542,23 @@
                 before,
             )
         stages.append([(1, head), (2, head)] + ([(0, head - 1)] if before else []))
-        query_grads = after(query_grads, gate[-1])
+        query_grads = after(query_grads, gate[1:])
         with jax.named_scope("halo_query_grads_%d" % head):
             back_grads = [lax.ppermute(other, "tm", back) for other, (_, back) in zip(query_grads[1:], sides)]
             open_grads = list(query_grads[:1]) + back_grads
         with jax.named_scope("returns_%d" % head):
             pieces.append(swap_pieces(leaving, gate))
         gate = pieces[-1]
-        if not final:
-            gain = advance(after([gain], gate[-1])[0])
     with jax.named_scope("returns_last"):
         stages.append([(0, heads - 1)])
         pieces.append(swap_pieces(close(open_grads, parts)))
     result = unpack(stages, pieces, rows, heads)
-    gain = advance(gain, len(steps)).reshape(channels) / token_count
-    return tuple(grad[None] for grad in result) + (gain,)
+    with jax.named_scope("gain"):
+        places = [(piece, 2 * rows + dots) for piece in lead]
+        if paired:
+            places += [(lead_side[0], parts * (rows + dots) + part * extra) for part in every]
+        gain = gain_total(places, channels // LANES, 1.0 / (rows * span * parts * lax.axis_size("dp")))
+    return tuple(grad[None] for grad in result) + (gain.reshape(channels),)
 
 
 def solution(mesh):

time: 117 us -> 124 us (1.060)
  waiting for transfers between devices: 35.7 us -> 48.9 us
  starting transfers between devices: 57.1 us -> 52 us
  local copies, waits for them, and re-layouts: 3.9 us -> 2.16 us
    ppermute x29 -> x27, waiting for transfers between devices: 32.3 us -> 44.5 us  [swap(): lax.ppermute(value, axis, [(index, index ^ distance) for index in range(l...]
    ppermute x29 -> x27, starting transfers between devices: 47.1 us -> 42.7 us  [swap(): lax.ppermute(value, axis, [(index, index ^ distance) for index in range(l...]
    ppermute x3, starting transfers between devices: 5.28 us -> 2.56 us  [local(): lax.ppermute(other, 'tm', back)]
    ppermute x3, waiting for transfers between devices: 0.01 us -> 1.26 us  [local(): lax.ppermute(other, 'tm', back)]
    unnamed x10 -> x12, local copies, waits for them, and re-layouts: 3.19 us -> 2.14 us
  transfers between devices with their start and end apart: 37 -> 35, of which waited for: 16 -> 14; matrix products, arithmetic and copies ran while one was open for 1% -> 0% of each run, Pallas kernels for 13% -> 13%
where the time goes in v7:
time: 124 us
  starting transfers between devices  52 us (42%)
  waiting for transfers between devices  48.9 us (39%)
  Pallas kernels  19.3 us (16%)
  local copies, waits for them, and re-layouts  2.16 us (2%)
    ppermute x27, waiting for transfers between devices, swap(): lax.ppermute(value, axis, [(index, index ^ distance) for index in range(l...  44.5 us
    ppermute x27, starting transfers between devices, swap(): lax.ppermute(value, axis, [(index, index ^ distance) for index in range(l...  42.7 us
    pallas_call x3, Pallas kernels, attention(): pl.pallas_call(functools.partial(attention_kernel, parts, sources, head,...  10 us
    ppermute x4, starting transfers between devices, forward(): return [lax.ppermute(array, 'tm', there) for there, _ in sides]  5.2 us
    pallas_call x1, Pallas kernels, partial_totals(): pl.pallas_call(functools.partial(totals_kernel, parts, sources, heads), g...  3.61 us
    ppermute x4, waiting for transfers between devices, forward(): return [lax.ppermute(array, 'tm', there) for there, _ in sides]  3.21 us
    ppermute x3, starting transfers between devices, local(): lax.ppermute(other, 'tm', back)  2.56 us
  transfers between devices with their start and end apart: 35, of which 14 were waited for; matrix products, arithmetic and copies ran while one was open for 0% of the time, Pallas kernels for 13%

profile of v7, /device:TPU:0, one launch (start us, length us, event | category | flops | bytes accessed | tf_op | source)
XLA Modules:
  0.0 123.5 jit_solution(8496286943610502007)
XLA Ops:
  3.8 3.1 %collective-permute-start = (bf16[1152,128]{1,0:T(8,128)(2,1)}, bf16[1152,128]{1,0:T(8,128)(2,1)S(1)}, u32[]{:S(2)}, u32[]{:S(2)}) collective-permute-start(bf16[1152,128]{1,0:T(8,128)(2,1)} %get-tuple-element.84), channel_id=1, source_target_pairs={{0,4},{4,0},{8,12},{12,8},{1,5},{5,1},{9,13},{13,9},{2,6},{6,2},{1... | collective-permute-start | bytes 884744 | tf_op jit(solution)/shard_map/keys_queries/ppermute | solution.py:405
  6.9 2.6 %collective-permute-start.1 = (bf16[1152,128]{1,0:T(8,128)(2,1)S(1)}, bf16[1152,128]{1,0:T(8,128)(2,1)S(1)}, u32[]{:S(2)}, u32[]{:S(2)}) collective-permute-start(bf16[1152,128]{1,0:T(8,128)(2,1)S(1)} %get-tuple-element.85), channel_id=1, source_target_pairs={{0,8},{4,12},{8,0},{12,4},{1,9},{5,13},{9,1},{13,5},{2,10},{6,14},... | collective-permute-start | bytes 884744 | tf_op jit(solution)/shard_map/keys_queries/ppermute | solution.py:405
  9.6 1.8 %collective-permute-start.4 = (f32[12,128]{1,0:T(8,128)S(1)}, f32[12,128]{1,0:T(8,128)S(1)}, u32[]{:S(2)}, u32[]{:S(2)}) collective-permute-start(f32[12,128]{1,0:T(8,128)S(1)} %bitcast.19), channel_id=1, source_target_pairs={{0,2},{1,3},{2,0},{3,1},{4,6},{5,7},{6,4},{7,5},{8,10},{9,11},{10,... | collective-permute-start | bytes 18440 | tf_op jit(solution)/shard_map/gain/ppermute | solution.py:405
  11.4 1.9 %collective-permute-done.4 = f32[12,128]{1,0:T(8,128)S(1)} collective-permute-done((f32[12,128]{1,0:T(8,128)S(1)}, f32[12,128]{1,0:T(8,128)S(1)}, u32[]{:S(2)}, u32[]{:S(2)}) %collective-permute-start.4) | collective-permute-done | bytes 6176 | tf_op jit(solution)/shard_map/gain/ppermute | solution.py:405
  16.5 3.2 %collective-permute-done.9.refs_24_.refs_28_.refs_32_.refs_12_ = bf16[576,128]{1,0:T(8,128)(2,1)S(1)} collective-permute-done((bf16[576,128]{1,0:T(8,128)(2,1)S(1)}, bf16[576,128]{1,0:T(8,128)(2,1)S(1)}, u32[]{:S(2)}, u32[]{:S(2)}) %collective-permute-start.9) | collective-permute-done | bytes 147488 | tf_op jit(solution)/shard_map/halo_queries/ppermute | solution.py:473
  19.7 10.6 %collective-permute-done.1.refs_1_.refs_2_.refs_6_.refs_10_.refs_14_.refs_18_.refs_22_ = bf16[1152,128]{1,0:T(8,128)(2,1)S(1)} collective-permute-done((bf16[1152,128]{1,0:T(8,128)(2,1)S(1)}, bf16[1152,128]{1,0:T(8,128)(2,1)S(1)}, u32[]{:S(2)}, u32[]{:S(2)}) %collective-permute-start.1) | collective-permute-done | bytes 294944 | tf_op jit(solution)/shard_map/keys_queries/ppermute | solution.py:405
  32.5 5.4 %collective-permute-start.6 = (bf16[448,128]{1,0:T(8,128)(2,1)S(1)}, bf16[448,128]{1,0:T(8,128)(2,1)S(1)}, u32[]{:S(2)}, u32[]{:S(2)}) collective-permute-start(bf16[448,128]{1,0:T(8,128)(2,1)S(1)} %get-tuple-element.90), channel_id=1, source_target_pairs={{0,4},{4,0},{8,12},{12,8},{1,5},{5,1},{9,13},{13,9},{2,6},{6,2},{1... | collective-permute-start | bytes 344072 | tf_op jit(solution)/shard_map/first_grads/ppermute | solution.py:405
  41.8 6.4 %collective-permute-done.7.refs_2_.refs_6_.refs_18_.refs_26_ = bf16[448,128]{1,0:T(8,128)(2,1)S(1)} collective-permute-done((bf16[448,128]{1,0:T(8,128)(2,1)S(1)}, bf16[448,128]{1,0:T(8,128)(2,1)S(1)}, u32[]{:S(2)}, u32[]{:S(2)}) %collective-permute-start.7) | collective-permute-done | bytes 114720 | tf_op jit(solution)/shard_map/first_grads/ppermute | solution.py:405
  49.3 1.8 %collective-permute-start.13 = (bf16[384,128]{1,0:T(8,128)(2,1)S(1)}, bf16[384,128]{1,0:T(8,128)(2,1)S(1)}, u32[]{:S(2)}, u32[]{:S(2)}) collective-permute-start(bf16[384,128]{1,0:T(8,128)(2,1)S(1)} %get-tuple-element.112), channel_id=1, source_target_pairs={{0,4},{4,0},{8,12},{12,8},{1,5},{5,1},{9,13},{13,9},{2,6},{6,2},{1... | collective-permute-start | bytes 294920 | tf_op jit(solution)/shard_map/rest_grads/ppermute | solution.py:405
  51.9 1.7 %collective-permute-start.19 = (bf16[384,128]{1,0:T(8,128)(2,1)S(1)}, bf16[384,128]{1,0:T(8,128)(2,1)S(1)}, u32[]{:S(2)}, u32[]{:S(2)}) collective-permute-start(bf16[384,128]{1,0:T(8,128)(2,1)S(1)} %get-tuple-element.124), channel_id=1, source_target_pairs={{0,12},{4,8},{8,4},{12,0},{1,13},{5,9},{9,5},{13,1},{2,14},{6,10},... | collective-permute-start | bytes 294920 | tf_op jit(solution)/shard_map/rest_grads/ppermute | solution.py:405
  53.6 3.6 %totals.1 = (f32[3,768]{1,0:T(4,128)S(1)}, f32[3,768]{1,0:T(4,128)S(1)}) custom-call(bf16[1152,128]{1,0:T(8,128)(2,1)S(1)} %get-tuple-element.83.refs_0_.refs_4_.refs_8_.refs_12_.refs_16_.refs_20_, bf16[1152,128]{1,0:T(8,128)(2,1)S(1)} %collective-permute-done.refs_0_.refs_1_.refs_5_.refs_9_.refs_13_.refs_17_.refs_21_, ...), custom_call_target="tpu_custom_call" | custom-call | flops 905969664 | bytes 2359296 | tf_op jit(solution)/shard_map/totals/pallas_call | solution.py:243
  65.4 1.7 %collective-permute-start.20 = (bf16[384,128]{1,0:T(8,128)(2,1)S(1)}, bf16[384,128]{1,0:T(8,128)(2,1)S(1)}, u32[]{:S(2)}, u32[]{:S(2)}) collective-permute-start(bf16[384,128]{1,0:T(8,128)(2,1)S(1)} %get-tuple-element.125), channel_id=1, source_target_pairs={{0,12},{4,8},{8,4},{12,0},{1,13},{5,9},{9,5},{13,1},{2,14},{6,10},... | collective-permute-start | bytes 294920 | tf_op jit(solution)/shard_map/rest_values/ppermute | solution.py:405
  67.1 3.3 %attention_0.1 = (bf16[384,128]{1,0:T(8,128)(2,1)S(1)}, bf16[384,128]{1,0:T(8,128)(2,1)S(1)}, bf16[384,128]{1,0:T(8,128)(2,1)S(1)}, bf16[384,128]{1,0:T(8,128)(2...) custom-call(bf16[1152,128]{1,0:T(8,128)(2,1)S(1)} %get-tuple-element.83.refs_0_.refs_4_.refs_8_.refs_12_.refs_16_.refs_20_, ...), custom_call_target="tpu_custom_call" | custom-call | flops 1509949440 | bytes 3145728 | tf_op jit(solution)/shard_map/attention_0/pallas_call | solution.py:336
  70.5 3.1 %collective-permute-done.17.refs_6_ = bf16[384,128]{1,0:T(8,128)(2,1)S(1)} collective-permute-done((bf16[384,128]{1,0:T(8,128)(2,1)S(1)}, bf16[384,128]{1,0:T(8,128)(2,1)S(1)}, u32[]{:S(2)}, u32[]{:S(2)}) %collective-permute-start.17) | collective-permute-done | bytes 98336 | tf_op jit(solution)/shard_map/rest_values/ppermute | solution.py:405
  76.8 1.6 %collective-permute-start.21 = (bf16[384,128]{1,0:T(8,128)(2,1)S(1)}, bf16[384,128]{1,0:T(8,128)(2,1)S(1)}, u32[]{:S(2)}, u32[]{:S(2)}) collective-permute-start(bf16[384,128]{1,0:T(8,128)(2,1)S(1)} %get-tuple-element.126), channel_id=1, source_target_pairs={{0,12},{4,8},{8,4},{12,0},{1,13},{5,9},{9,5},{13,1},{2,14},{6,10},... | collective-permute-start | bytes 294920 | tf_op jit(solution)/shard_map/returns_0/ppermute | solution.py:405
  79.2 3.3 %attention_1.1 = (bf16[576,128]{1,0:T(8,128)(2,1)S(1)}, bf16[576,128]{1,0:T(8,128)(2,1)S(1)}, bf16[576,128]{1,0:T(8,128)(2,1)S(1)}, bf16[576,128]{1,0:T(8,128)(2...) custom-call(bf16[1152,128]{1,0:T(8,128)(2,1)S(1)} %get-tuple-element.83.refs_0_.refs_4_.refs_8_.refs_12_.refs_16_.refs_20_, ...), custom_call_target="tpu_custom_call" | custom-call | flops 1509949440 | bytes 3145728 | tf_op jit(solution)/shard_map/attention_1/pallas_call | solution.py:336
  82.6 2.4 %collective-permute-done.18.refs_2_ = bf16[384,128]{1,0:T(8,128)(2,1)S(1)} collective-permute-done((bf16[384,128]{1,0:T(8,128)(2,1)S(1)}, bf16[384,128]{1,0:T(8,128)(2,1)S(1)}, u32[]{:S(2)}, u32[]{:S(2)}) %collective-permute-start.18) | collective-permute-done | bytes 98336 | tf_op jit(solution)/shard_map/returns_0/ppermute | solution.py:405
  89.2 1.6 %collective-permute-start.26 = (bf16[576,128]{1,0:T(8,128)(2,1)S(1)}, bf16[576,128]{1,0:T(8,128)(2,1)S(1)}, u32[]{:S(2)}, u32[]{:S(2)}) collective-permute-start(bf16[576,128]{1,0:T(8,128)(2,1)S(1)} %get-tuple-element.139), channel_id=1, source_target_pairs={{0,12},{4,8},{8,4},{12,0},{1,13},{5,9},{9,5},{13,1},{2,14},{6,10},... | collective-permute-start | bytes 442376 | tf_op jit(solution)/shard_map/returns_1/ppermute | solution.py:405
  90.8 3.3 %attention_2.1 = (bf16[576,128]{1,0:T(8,128)(2,1)S(1)}, bf16[576,128]{1,0:T(8,128)(2,1)S(1)}, bf16[576,128]{1,0:T(8,128)(2,1)S(1)}, bf16[576,128]{1,0:T(8,128)(2...) custom-call(bf16[1152,128]{1,0:T(8,128)(2,1)S(1)} %get-tuple-element.83.refs_0_.refs_4_.refs_8_.refs_12_.refs_16_.refs_20_, ...), custom_call_target="tpu_custom_call" | custom-call | flops 1509949440 | bytes 3145728 | tf_op jit(solution)/shard_map/attention_2/pallas_call | solution.py:336
  94.2 6.7 %collective-permute-done.25.refs_6_ = bf16[576,128]{1,0:T(8,128)(2,1)S(1)} collective-permute-done((bf16[576,128]{1,0:T(8,128)(2,1)S(1)}, bf16[576,128]{1,0:T(8,128)(2,1)S(1)}, u32[]{:S(2)}, u32[]{:S(2)}) %collective-permute-start.25) | collective-permute-done | bytes 147488 | tf_op jit(solution)/shard_map/returns_1/ppermute | solution.py:405
  101.4 2.1 %collective-permute-start.28 = (bf16[576,128]{1,0:T(8,128)(2,1)S(1)}, bf16[576,128]{1,0:T(8,128)(2,1)S(1)}, u32[]{:S(2)}, u32[]{:S(2)}) collective-permute-start(bf16[576,128]{1,0:T(8,128)(2,1)S(1)} %get-tuple-element.146), channel_id=1, source_target_pairs={{0,4},{4,0},{8,12},{12,8},{1,5},{5,1},{9,13},{13,9},{2,6},{6,2},{1... | collective-permute-start | bytes 442376 | tf_op jit(solution)/shard_map/returns_2/ppermute | solution.py:405
  106.6 2.2 %collective-permute-start.32 = (bf16[192,128]{1,0:T(8,128)(2,1)S(1)}, bf16[192,128]{1,0:T(8,128)(2,1)S(1)}, u32[]{:S(2)}, u32[]{:S(2)}) collective-permute-start(bf16[192,128]{1,0:T(8,128)(2,1)S(1)} %get-tuple-element.156), channel_id=1, source_target_pairs={{0,4},{4,0},{8,12},{12,8},{1,5},{5,1},{9,13},{13,9},{2,6},{6,2},{1... | collective-permute-start | bytes 147464 | tf_op jit(solution)/shard_map/returns_last/ppermute | solution.py:405
  112.4 6.6 %collective-permute-done.29.refs_10_ = bf16[576,128]{1,0:T(8,128)(2,1)S(1)} collective-permute-done((bf16[576,128]{1,0:T(8,128)(2,1)S(1)}, bf16[576,128]{1,0:T(8,128)(2,1)S(1)}, u32[]{:S(2)}, u32[]{:S(2)}) %collective-permute-start.29) | collective-permute-done | bytes 147488 | tf_op jit(solution)/shard_map/returns_2/ppermute | solution.py:405
  119.0 2.9 %collective-permute-done.33.refs_14_ = bf16[192,128]{1,0:T(8,128)(2,1)S(1)} collective-permute-done((bf16[192,128]{1,0:T(8,128)(2,1)S(1)}, bf16[192,128]{1,0:T(8,128)(2,1)S(1)}, u32[]{:S(2)}, u32[]{:S(2)}) %collective-permute-start.33) | collective-permute-done | bytes 49184 | tf_op jit(solution)/shard_map/returns_last/ppermute | solution.py:405
  (78 shorter events, 39.5 us)
Async XLA Ops:
  3.8 16.0 %collective-permute-start = (bf16[1152,128]{1,0:T(8,128)(2,1)}, bf16[1152,128]{1,0:T(8,128)(2,1)S(1)}, u32[]{:S(2)}, u32[]{:S(2)}) collective-permute-start(bf16[1152,128]{1,0:T(8,128)(2,1)} %get-tuple-element.84), channel_id=1, source_target_pairs={{0,4},{4,0},{8,12},{12,8},{1,5},{5,1},{9,13},{13,9},{2,6},{6,2},{1... | collective-permute-start | bytes 884744 | tf_op jit(solution)/shard_map/keys_queries/ppermute | solution.py:405
  6.9 23.5 %collective-permute-start.1 = (bf16[1152,128]{1,0:T(8,128)(2,1)S(1)}, bf16[1152,128]{1,0:T(8,128)(2,1)S(1)}, u32[]{:S(2)}, u32[]{:S(2)}) collective-permute-start(bf16[1152,128]{1,0:T(8,128)(2,1)S(1)} %get-tuple-element.85), channel_id=1, source_target_pairs={{0,8},{4,12},{8,0},{12,4},{1,9},{5,13},{9,1},{13,5},{2,10},{6,14},... | collective-permute-start | bytes 884744 | tf_op jit(solution)/shard_map/keys_queries/ppermute | solution.py:405
  9.4 20.9 %collective-permute-start.2 = (bf16[1152,128]{1,0:T(8,128)(2,1)S(1)}, bf16[1152,128]{1,0:T(8,128)(2,1)S(1)}, u32[]{:S(2)}, u32[]{:S(2)}) collective-permute-start(bf16[1152,128]{1,0:T(8,128)(2,1)S(1)} %get-tuple-element.86), channel_id=1, source_target_pairs={{0,12},{4,8},{8,4},{12,0},{1,13},{5,9},{9,5},{13,1},{2,14},{6,10},... | collective-permute-start | bytes 884744 | tf_op jit(solution)/shard_map/keys_queries/ppermute | solution.py:405
  30.9 22.7 %collective-permute-start.10 = (bf16[1728,128]{1,0:T(8,128)(2,1)S(1)}, bf16[1728,128]{1,0:T(8,128)(2,1)S(1)}, u32[]{:S(2)}, u32[]{:S(2)}) collective-permute-start(bf16[1728,128]{1,0:T(8,128)(2,1)S(1)} %halo_queries.1), channel_id=1, source_target_pairs={{0,16},{16,0},{1,17},{17,1},{2,18},{18,2},{3,19},{19,3},{4,20},{20... | collective-permute-start | bytes 1327112 | tf_op jit(solution)/shard_map/halo_queries/ppermute | solution.py:473
  32.5 9.3 %collective-permute-start.6 = (bf16[448,128]{1,0:T(8,128)(2,1)S(1)}, bf16[448,128]{1,0:T(8,128)(2,1)S(1)}, u32[]{:S(2)}, u32[]{:S(2)}) collective-permute-start(bf16[448,128]{1,0:T(8,128)(2,1)S(1)} %get-tuple-element.90), channel_id=1, source_target_pairs={{0,4},{4,0},{8,12},{12,8},{1,5},{5,1},{9,13},{13,9},{2,6},{6,2},{1... | collective-permute-start | bytes 344072 | tf_op jit(solution)/shard_map/first_grads/ppermute | solution.py:405
  37.9 10.3 %collective-permute-start.7 = (bf16[448,128]{1,0:T(8,128)(2,1)S(1)}, bf16[448,128]{1,0:T(8,128)(2,1)S(1)}, u32[]{:S(2)}, u32[]{:S(2)}) collective-permute-start(bf16[448,128]{1,0:T(8,128)(2,1)S(1)} %get-tuple-element.92), channel_id=1, source_target_pairs={{0,8},{4,12},{8,0},{12,4},{1,9},{5,13},{9,1},{13,5},{2,10},{6,14},... | collective-permute-start | bytes 344072 | tf_op jit(solution)/shard_map/first_grads/ppermute | solution.py:405
  38.9 9.3 %collective-permute-start.8 = (bf16[448,128]{1,0:T(8,128)(2,1)S(1)}, bf16[448,128]{1,0:T(8,128)(2,1)S(1)}, u32[]{:S(2)}, u32[]{:S(2)}) collective-permute-start(bf16[448,128]{1,0:T(8,128)(2,1)S(1)} %get-tuple-element.94), channel_id=1, source_target_pairs={{0,12},{4,8},{8,4},{12,0},{1,13},{5,9},{9,5},{13,1},{2,14},{6,10},... | collective-permute-start | bytes 344072 | tf_op jit(solution)/shard_map/first_grads/ppermute | solution.py:405
  48.7 18.5 %collective-permute-start.11 = (bf16[1024,128]{1,0:T(8,128)(2,1)S(1)}, bf16[1024,128]{1,0:T(8,128)(2,1)S(1)}, u32[]{:S(2)}, u32[]{:S(2)}) collective-permute-start(bf16[1024,128]{1,0:T(8,128)(2,1)S(1)} %halo_first_grads.1), channel_id=1, source_target_pairs={{0,16},{16,0},{1,17},{17,1},{2,18},{18,2},{3,19},{19,3},{4,20},{20... | collective-permute-start | bytes 786440 | tf_op jit(solution)/shard_map/halo_first_grads/ppermute | solution.py:473
  49.3 9.8 %collective-permute-start.13 = (bf16[384,128]{1,0:T(8,128)(2,1)S(1)}, bf16[384,128]{1,0:T(8,128)(2,1)S(1)}, u32[]{:S(2)}, u32[]{:S(2)}) collective-permute-start(bf16[384,128]{1,0:T(8,128)(2,1)S(1)} %get-tuple-element.112), channel_id=1, source_target_pairs={{0,4},{4,0},{8,12},{12,8},{1,5},{5,1},{9,13},{13,9},{2,6},{6,2},{1... | collective-permute-start | bytes 294920 | tf_op jit(solution)/shard_map/rest_grads/ppermute | solution.py:405
  51.0 9.3 %collective-permute-start.16 = (bf16[384,128]{1,0:T(8,128)(2,1)S(1)}, bf16[384,128]{1,0:T(8,128)(2,1)S(1)}, u32[]{:S(2)}, u32[]{:S(2)}) collective-permute-start(bf16[384,128]{1,0:T(8,128)(2,1)S(1)} %get-tuple-element.118), channel_id=1, source_target_pairs={{0,8},{4,12},{8,0},{12,4},{1,9},{5,13},{9,1},{13,5},{2,10},{6,14},... | collective-permute-start | bytes 294920 | tf_op jit(solution)/shard_map/rest_grads/ppermute | solution.py:405
  51.9 8.4 %collective-permute-start.19 = (bf16[384,128]{1,0:T(8,128)(2,1)S(1)}, bf16[384,128]{1,0:T(8,128)(2,1)S(1)}, u32[]{:S(2)}, u32[]{:S(2)}) collective-permute-start(bf16[384,128]{1,0:T(8,128)(2,1)S(1)} %get-tuple-element.124), channel_id=1, source_target_pairs={{0,12},{4,8},{8,4},{12,0},{1,13},{5,9},{9,5},{13,1},{2,14},{6,10},... | collective-permute-start | bytes 294920 | tf_op jit(solution)/shard_map/rest_grads/ppermute | solution.py:405
  61.1 17.4 %collective-permute-start.22 = (bf16[1536,128]{1,0:T(8,128)(2,1)S(1)}, bf16[1536,128]{1,0:T(8,128)(2,1)S(1)}, u32[]{:S(2)}, u32[]{:S(2)}) collective-permute-start(bf16[1536,128]{1,0:T(8,128)(2,1)S(1)} %halo_rest_grads.1), channel_id=1, source_target_pairs={{0,16},{16,0},{1,17},{17,1},{2,18},{18,2},{3,19},{19,3},{4,20},{20... | collective-permute-start | bytes 1179656 | tf_op jit(solution)/shard_map/halo_rest_grads/ppermute | solution.py:473
  64.3 9.3 %collective-permute-start.17 = (bf16[384,128]{1,0:T(8,128)(2,1)S(1)}, bf16[384,128]{1,0:T(8,128)(2,1)S(1)}, u32[]{:S(2)}, u32[]{:S(2)}) collective-permute-start(bf16[384,128]{1,0:T(8,128)(2,1)S(1)} %get-tuple-element.119), channel_id=1, source_target_pairs={{0,8},{4,12},{8,0},{12,4},{1,9},{5,13},{9,1},{13,5},{2,10},{6,14},... | collective-permute-start | bytes 294920 | tf_op jit(solution)/shard_map/rest_values/ppermute | solution.py:405
  65.4 8.1 %collective-permute-start.20 = (bf16[384,128]{1,0:T(8,128)(2,1)S(1)}, bf16[384,128]{1,0:T(8,128)(2,1)S(1)}, u32[]{:S(2)}, u32[]{:S(2)}) collective-permute-start(bf16[384,128]{1,0:T(8,128)(2,1)S(1)} %get-tuple-element.125), channel_id=1, source_target_pairs={{0,12},{4,8},{8,4},{12,0},{1,13},{5,9},{9,5},{13,1},{2,14},{6,10},... | collective-permute-start | bytes 294920 | tf_op jit(solution)/shard_map/rest_values/ppermute | solution.py:405
  74.1 8.5 %collective-permute-start.15 = (bf16[384,128]{1,0:T(8,128)(2,1)S(1)}, bf16[384,128]{1,0:T(8,128)(2,1)S(1)}, u32[]{:S(2)}, u32[]{:S(2)}) collective-permute-start(bf16[384,128]{1,0:T(8,128)(2,1)S(1)} %get-tuple-element.114), channel_id=1, source_target_pairs={{0,4},{4,0},{8,12},{12,8},{1,5},{5,1},{9,13},{13,9},{2,6},{6,2},{1... | collective-permute-start | bytes 294920 | tf_op jit(solution)/shard_map/returns_0/ppermute | solution.py:405
  75.7 9.3 %collective-permute-start.18 = (bf16[384,128]{1,0:T(8,128)(2,1)S(1)}, bf16[384,128]{1,0:T(8,128)(2,1)S(1)}, u32[]{:S(2)}, u32[]{:S(2)}) collective-permute-start(bf16[384,128]{1,0:T(8,128)(2,1)S(1)} %get-tuple-element.120), channel_id=1, source_target_pairs={{0,8},{4,12},{8,0},{12,4},{1,9},{5,13},{9,1},{13,5},{2,10},{6,14},... | collective-permute-start | bytes 294920 | tf_op jit(solution)/shard_map/returns_0/ppermute | solution.py:405
  88.1 12.8 %collective-permute-start.25 = (bf16[576,128]{1,0:T(8,128)(2,1)S(1)}, bf16[576,128]{1,0:T(8,128)(2,1)S(1)}, u32[]{:S(2)}, u32[]{:S(2)}) collective-permute-start(bf16[576,128]{1,0:T(8,128)(2,1)S(1)} %get-tuple-element.137), channel_id=1, source_target_pairs={{0,8},{4,12},{8,0},{12,4},{1,9},{5,13},{9,1},{13,5},{2,10},{6,14},... | collective-permute-start | bytes 442376 | tf_op jit(solution)/shard_map/returns_1/ppermute | solution.py:405
  89.2 11.7 %collective-permute-start.26 = (bf16[576,128]{1,0:T(8,128)(2,1)S(1)}, bf16[576,128]{1,0:T(8,128)(2,1)S(1)}, u32[]{:S(2)}, u32[]{:S(2)}) collective-permute-start(bf16[576,128]{1,0:T(8,128)(2,1)S(1)} %get-tuple-element.139), channel_id=1, source_target_pairs={{0,12},{4,8},{8,4},{12,0},{1,13},{5,9},{9,5},{13,1},{2,14},{6,10},... | collective-permute-start | bytes 442376 | tf_op jit(solution)/shard_map/returns_1/ppermute | solution.py:405
  101.4 8.9 %collective-permute-start.28 = (bf16[576,128]{1,0:T(8,128)(2,1)S(1)}, bf16[576,128]{1,0:T(8,128)(2,1)S(1)}, u32[]{:S(2)}, u32[]{:S(2)}) collective-permute-start(bf16[576,128]{1,0:T(8,128)(2,1)S(1)} %get-tuple-element.146), channel_id=1, source_target_pairs={{0,4},{4,0},{8,12},{12,8},{1,5},{5,1},{9,13},{13,9},{2,6},{6,2},{1... | collective-permute-start | bytes 442376 | tf_op jit(solution)/shard_map/returns_2/ppermute | solution.py:405
  103.6 15.4 %collective-permute-start.29 = (bf16[576,128]{1,0:T(8,128)(2,1)S(1)}, bf16[576,128]{1,0:T(8,128)(2,1)S(1)}, u32[]{:S(2)}, u32[]{:S(2)}) collective-permute-start(bf16[576,128]{1,0:T(8,128)(2,1)S(1)} %get-tuple-element.148), channel_id=1, source_target_pairs={{0,8},{4,12},{8,0},{12,4},{1,9},{5,13},{9,1},{13,5},{2,10},{6,14},... | collective-permute-start | bytes 442376 | tf_op jit(solution)/shard_map/returns_2/ppermute | solution.py:405
  104.6 14.4 %collective-permute-start.30 = (bf16[576,128]{1,0:T(8,128)(2,1)S(1)}, bf16[576,128]{1,0:T(8,128)(2,1)S(1)}, u32[]{:S(2)}, u32[]{:S(2)}) collective-permute-start(bf16[576,128]{1,0:T(8,128)(2,1)S(1)} %get-tuple-element.150), channel_id=1, source_target_pairs={{0,12},{4,8},{8,4},{12,0},{1,13},{5,9},{9,5},{13,1},{2,14},{6,10},... | collective-permute-start | bytes 442376 | tf_op jit(solution)/shard_map/returns_2/ppermute | solution.py:405
  106.6 12.4 %collective-permute-start.32 = (bf16[192,128]{1,0:T(8,128)(2,1)S(1)}, bf16[192,128]{1,0:T(8,128)(2,1)S(1)}, u32[]{:S(2)}, u32[]{:S(2)}) collective-permute-start(bf16[192,128]{1,0:T(8,128)(2,1)S(1)} %get-tuple-element.156), channel_id=1, source_target_pairs={{0,4},{4,0},{8,12},{12,8},{1,5},{5,1},{9,13},{13,9},{2,6},{6,2},{1... | collective-permute-start | bytes 147464 | tf_op jit(solution)/shard_map/returns_last/ppermute | solution.py:405
  108.8 13.0 %collective-permute-start.33 = (bf16[192,128]{1,0:T(8,128)(2,1)S(1)}, bf16[192,128]{1,0:T(8,128)(2,1)S(1)}, u32[]{:S(2)}, u32[]{:S(2)}) collective-permute-start(bf16[192,128]{1,0:T(8,128)(2,1)S(1)} %get-tuple-element.157), channel_id=1, source_target_pairs={{0,8},{4,12},{8,0},{12,4},{1,9},{5,13},{9,1},{13,5},{2,10},{6,14},... | collective-permute-start | bytes 147464 | tf_op jit(solution)/shard_map/returns_last/ppermute | solution.py:405
  110.4 11.5 %collective-permute-start.34 = (bf16[192,128]{1,0:T(8,128)(2,1)S(1)}, bf16[192,128]{1,0:T(8,128)(2,1)S(1)}, u32[]{:S(2)}, u32[]{:S(2)}) collective-permute-start(bf16[192,128]{1,0:T(8,128)(2,1)S(1)} %get-tuple-element.158), channel_id=1, source_target_pairs={{0,12},{4,8},{8,4},{12,0},{1,13},{5,9},{9,5},{13,1},{2,14},{6,10},... | collective-permute-start | bytes 147464 | tf_op jit(solution)/shard_map/returns_last/ppermute | solution.py:405
  (17 other events, 89.4 us)

commit v8 on v7

--- a/solution.py
+++ b/solution.py
@@ -23,12 +23,13 @@
     return pltpu.CompilerParams(vmem_limit_bytes=VMEM_LIMIT)
 
 
-def partner(distance):
-    return lax.axis_index("ulysses") ^ distance
-
-
-def column_of(distance, heads, head):
-    return pl.multiple_of((partner(distance) * heads + head) * HD, HD)
+def distances(parts):
+    return [0] + list(range(parts - 1, 0, -1))
+
+
+def column_of(parts, place, heads, head):
+    partner = lax.axis_index("ulysses") ^ distances(parts)[place]
+    return pl.multiple_of((partner * heads + head) * HD, HD)
 
 
 def run_copies(pairs, semaphores):
@@ -49,7 +50,7 @@
     for distance in range(parts):
         for half, ref in enumerate(sources):
             for place, head in enumerate(chosen):
-                columns = pl.ds(column_of(distance, heads, head), HD)
+                columns = pl.ds(column_of(parts, distance, heads, head), HD)
                 start = (half * len(chosen) + place) * rows
                 pairs.append((ref.at[:, columns], pieces[distance].at[start : start + rows]))
     run_copies(pairs, semaphores)
@@ -142,7 +143,7 @@
     for distance in range(parts):
         terms = []
         for head in range(heads):
-            columns = pl.ds(column_of(distance, heads, head), HD)
+            columns = pl.ds(column_of(parts, distance, heads, head), HD)
             grad = (out_grad_ref[:, columns].astype(jnp.float32) * gain_ref[:, columns]).astype(jnp.bfloat16)
             if head:
                 rests[distance][(head - 1) * rows : head * rows] = grad
@@ -381,7 +382,7 @@
         for distance in range(parts):
             piece = pieces[number * parts + distance]
             for index, (output, head) in enumerate(blocks):
-                columns = pl.ds(column_of(distance, heads, head), HD)
+                columns = pl.ds(column_of(parts, distance, heads, head), HD)
                 pairs.append((piece.at[index * rows : (index + 1) * rows], outs[output].at[:, columns]))
     run_copies(pairs, semaphores)
 
@@ -407,11 +408,11 @@
 
 def swap_pieces(pieces, earlier=None):
     held = [pieces[0]]
-    for distance in range(1, len(pieces)):
-        piece = pieces[distance]
-        if earlier is not None:
-            piece = after([piece], earlier[distance])[0]
-        held.append(swap(piece, "ulysses", distance))
+    if earlier is not None:
+        pieces = after(pieces, earlier[1:])
+    for place, distance in enumerate(distances(len(pieces))):
+        if distance:
+            held.append(swap(pieces[place], "ulysses", distance))
     return held
 
 
@@ -487,15 +488,18 @@
     with jax.named_scope("halo_queries"):
         width = heads * rows
         first_side = forward(pairs[0][width:])
+    with jax.named_scope("first_grads"):
+        lead = swap_pieces(sent_lead, pairs)
+    with jax.named_scope("rest_grads"):
+        rest_grads = swap_pieces(sent_rest, lead)
+    with jax.named_scope("halo_queries"):
         late = after(pairs[1:], sent_lead[0], first_side)
         late_side = forward(gather_rows(late, [(number, width, width) for number in range(parts - 1)]))
-    with jax.named_scope("first_grads"):
-        lead = swap_pieces(sent_lead, pairs)
     with jax.named_scope("halo_first_grads"):
         extra = gain_depth(channels) if paired else 0
         ranges = [(part, 0, rows) for part in every] + [(part, 2 * rows, dots) for part in every]
         ranges += [(part, 2 * rows + dots, extra) for part in every] * paired
-        lead_side = forward(gather_rows(lead, ranges))
+        lead_side = forward(gather_rows(after(lead, rest_grads[-1]), ranges))
     with jax.named_scope("totals"):
         key_places = [[(piece, head) for piece in pairs] for head in range(heads)]
         query_places = [[[(piece, heads + head) for piece in pairs] for head in range(heads)]]
@@ -508,13 +512,11 @@
             )
         part_totals = partial_totals(key_places, query_places, rows)
         totals = exchange_totals(part_totals, sides)
-    with jax.named_scope("rest_grads"):
-        rest_grads = swap_pieces(after(sent_rest, gain), lead)
+    with jax.named_scope("rest_values"):
+        rest_values = swap_pieces(after(pack([values[0]], parts, rest), part_totals), rest_grads)
     with jax.named_scope("halo_rest_grads"):
         ranges = [(part, place * rows, rows) for place in range(heads - 1) for part in every]
-        rest_side = forward(gather_rows(rest_grads, ranges))
-    with jax.named_scope("rest_values"):
-        rest_values = swap_pieces(after(pack([values[0]], parts, rest), part_totals), rest_grads)
+        rest_side = forward(gather_rows(after(rest_grads, rest_values[-1]), ranges))
     dot_places = [(piece, 2 * rows // dots) for piece in lead]
     dot_places += [(array, parts * rows // dots + part) for array in lead_side for part in every]
     stages, pieces, open_grads = [], [], []

time: 124 us -> 118 us (0.952)
  starting transfers between devices: 52 us -> 45.9 us
    ppermute x27, starting transfers between devices: 42.7 us -> 38.3 us  [swap(): lax.ppermute(value, axis, [(index, index ^ distance) for index in range(l...]
    ppermute x3, waiting for transfers between devices: 1.26 us -> 2.91 us  [local(): lax.ppermute(other, 'tm', back)]
    ppermute x4, starting transfers between devices: 5.2 us -> 3.72 us  [forward(): return [lax.ppermute(array, 'tm', there) for there, _ in sides]]
    ppermute x27, waiting for transfers between devices: 44.5 us -> 43.1 us  [swap(): lax.ppermute(value, axis, [(index, index ^ distance) for index in range(l...]
  transfers between devices with their start and end apart: 35 -> 35, of which waited for: 14 -> 17; matrix products, arithmetic and copies ran while one was open for 0% -> 0% of each run, Pallas kernels for 13% -> 14%
where the time goes in v8:
time: 118 us
  waiting for transfers between devices  49.3 us (42%)
  starting transfers between devices  45.9 us (39%)
  Pallas kernels  19.3 us (16%)
  local copies, waits for them, and re-layouts  2.16 us (2%)
    ppermute x27, waiting for transfers between devices, swap(): lax.ppermute(value, axis, [(index, index ^ distance) for index in range(l...  43.1 us
    ppermute x27, starting transfers between devices, swap(): lax.ppermute(value, axis, [(index, index ^ distance) for index in range(l...  38.3 us
    pallas_call x3, Pallas kernels, attention(): pl.pallas_call(functools.partial(attention_kernel, parts, sources, head,...  10 us
    ppermute x4, starting transfers between devices, forward(): return [lax.ppermute(array, 'tm', there) for there, _ in sides]  3.72 us
    pallas_call x1, Pallas kernels, partial_totals(): pl.pallas_call(functools.partial(totals_kernel, parts, sources, heads), g...  3.61 us
    ppermute x3, starting transfers between devices, local(): lax.ppermute(other, 'tm', back)  3.36 us
    ppermute x4, waiting for transfers between devices, forward(): return [lax.ppermute(array, 'tm', there) for there, _ in sides]  3.27 us
    ppermute x3, waiting for transfers between devices, local(): lax.ppermute(other, 'tm', back)  2.91 us
  transfers between devices with their start and end apart: 35, of which 17 were waited for; matrix products, arithmetic and copies ran while one was open for 0% of the time, Pallas kernels for 14%

profile of v8, /device:TPU:0, one launch (start us, length us, event | category | flops | bytes accessed | tf_op | source)
XLA Modules:
  0.0 117.8 jit_solution(15004787765649301116)
XLA Ops:
  3.8 5.1 %collective-permute-start = (bf16[1152,128]{1,0:T(8,128)(2,1)}, bf16[1152,128]{1,0:T(8,128)(2,1)S(1)}, u32[]{:S(2)}, u32[]{:S(2)}) collective-permute-start(bf16[1152,128]{1,0:T(8,128)(2,1)} %get-tuple-element.88), channel_id=1, source_target_pairs={{0,12},{4,8},{8,4},{12,0},{1,13},{5,9},{9,5},{13,1},{2,14},{6,10},... | collective-permute-start | bytes 884744 | tf_op jit(solution)/shard_map/keys_queries/ppermute | solution.py:406
  11.4 2.0 %collective-permute-done.4 = f32[12,128]{1,0:T(8,128)S(1)} collective-permute-done((f32[12,128]{1,0:T(8,128)S(1)}, f32[12,128]{1,0:T(8,128)S(1)}, u32[]{:S(2)}, u32[]{:S(2)}) %collective-permute-start.4) | collective-permute-done | bytes 6176 | tf_op jit(solution)/shard_map/gain/ppermute | solution.py:406
  16.5 3.3 %collective-permute-done.9.refs_24_.refs_28_.refs_32_.refs_12_ = bf16[576,128]{1,0:T(8,128)(2,1)S(1)} collective-permute-done((bf16[576,128]{1,0:T(8,128)(2,1)S(1)}, bf16[576,128]{1,0:T(8,128)(2,1)S(1)}, u32[]{:S(2)}, u32[]{:S(2)}) %collective-permute-start.9) | collective-permute-done | bytes 147488 | tf_op jit(solution)/shard_map/halo_queries/ppermute | solution.py:474
  19.7 14.5 %collective-permute-done.1.refs_1_.refs_2_.refs_6_.refs_10_.refs_14_.refs_18_.refs_22_ = bf16[1152,128]{1,0:T(8,128)(2,1)S(1)} collective-permute-done((bf16[1152,128]{1,0:T(8,128)(2,1)S(1)}, bf16[1152,128]{1,0:T(8,128)(2,1)S(1)}, u32[]{:S(2)}, u32[]{:S(2)}) %collective-permute-start.1) | collective-permute-done | bytes 294944 | tf_op jit(solution)/shard_map/keys_queries/ppermute | solution.py:406
  36.4 2.5 %collective-permute-start.6 = (bf16[448,128]{1,0:T(8,128)(2,1)S(1)}, bf16[448,128]{1,0:T(8,128)(2,1)S(1)}, u32[]{:S(2)}, u32[]{:S(2)}) collective-permute-start(bf16[448,128]{1,0:T(8,128)(2,1)S(1)} %get-tuple-element.96), channel_id=1, source_target_pairs={{0,12},{4,8},{8,4},{12,0},{1,13},{5,9},{9,5},{13,1},{2,14},{6,10},... | collective-permute-start | bytes 344072 | tf_op jit(solution)/shard_map/first_grads/ppermute | solution.py:406
  38.8 1.9 %collective-permute-start.8 = (bf16[448,128]{1,0:T(8,128)(2,1)S(1)}, bf16[448,128]{1,0:T(8,128)(2,1)S(1)}, u32[]{:S(2)}, u32[]{:S(2)}) collective-permute-start(bf16[448,128]{1,0:T(8,128)(2,1)S(1)} %get-tuple-element.98), channel_id=1, source_target_pairs={{0,4},{4,0},{8,12},{12,8},{1,5},{5,1},{9,13},{13,9},{2,6},{6,2},{1... | collective-permute-start | bytes 344072 | tf_op jit(solution)/shard_map/first_grads/ppermute | solution.py:406
  40.7 3.5 %collective-permute-done.6.refs_1_.refs_5_.refs_17_.refs_25_ = bf16[448,128]{1,0:T(8,128)(2,1)S(1)} collective-permute-done((bf16[448,128]{1,0:T(8,128)(2,1)S(1)}, bf16[448,128]{1,0:T(8,128)(2,1)S(1)}, u32[]{:S(2)}, u32[]{:S(2)}) %collective-permute-start.6) | collective-permute-done | bytes 114720 | tf_op jit(solution)/shard_map/first_grads/ppermute | solution.py:406
  44.2 3.4 %collective-permute-done.7.refs_2_.refs_6_.refs_18_.refs_26_ = bf16[448,128]{1,0:T(8,128)(2,1)S(1)} collective-permute-done((bf16[448,128]{1,0:T(8,128)(2,1)S(1)}, bf16[448,128]{1,0:T(8,128)(2,1)S(1)}, u32[]{:S(2)}, u32[]{:S(2)}) %collective-permute-start.7) | collective-permute-done | bytes 114720 | tf_op jit(solution)/shard_map/first_grads/ppermute | solution.py:406
  54.0 3.6 %totals.1 = (f32[3,768]{1,0:T(4,128)S(1)}, f32[3,768]{1,0:T(4,128)S(1)}) custom-call(bf16[1152,128]{1,0:T(8,128)(2,1)S(1)} %get-tuple-element.87.refs_0_.refs_4_.refs_8_.refs_12_.refs_16_.refs_20_, bf16[1152,128]{1,0:T(8,128)(2,1)S(1)} %collective-permute-done.refs_0_.refs_1_.refs_5_.refs_9_.refs_13_.refs_17_.refs_21_, ...), custom_call_target="tpu_custom_call" | custom-call | flops 905969664 | bytes 2359296 | tf_op jit(solution)/shard_map/totals/pallas_call | solution.py:244
  57.6 1.9 %collective-permute-done.15.refs_2_.refs_18_ = bf16[384,128]{1,0:T(8,128)(2,1)S(1)} collective-permute-done((bf16[384,128]{1,0:T(8,128)(2,1)S(1)}, bf16[384,128]{1,0:T(8,128)(2,1)S(1)}, u32[]{:S(2)}, u32[]{:S(2)}) %collective-permute-start.15) | collective-permute-done | bytes 98336 | tf_op jit(solution)/shard_map/rest_grads/ppermute | solution.py:406
  60.1 2.1 %collective-permute-start.16 = (bf16[384,128]{1,0:T(8,128)(2,1)S(1)}, bf16[384,128]{1,0:T(8,128)(2,1)S(1)}, u32[]{:S(2)}, u32[]{:S(2)}) collective-permute-start(bf16[384,128]{1,0:T(8,128)(2,1)S(1)} %get-tuple-element.127), channel_id=1, source_target_pairs={{0,12},{4,8},{8,4},{12,0},{1,13},{5,9},{9,5},{13,1},{2,14},{6,10},... | collective-permute-start | bytes 294920 | tf_op jit(solution)/shard_map/rest_values/ppermute | solution.py:406
  63.6 2.0 %collective-permute-done.18.refs_7_ = bf16[384,128]{1,0:T(8,128)(2,1)S(1)} collective-permute-done((bf16[384,128]{1,0:T(8,128)(2,1)S(1)}, bf16[384,128]{1,0:T(8,128)(2,1)S(1)}, u32[]{:S(2)}, u32[]{:S(2)}) %collective-permute-start.18) | collective-permute-done | bytes 98336 | tf_op jit(solution)/shard_map/rest_values/ppermute | solution.py:406
  66.5 3.3 %attention_0.1 = (bf16[384,128]{1,0:T(8,128)(2,1)S(1)}, bf16[384,128]{1,0:T(8,128)(2,1)S(1)}, bf16[384,128]{1,0:T(8,128)(2,1)S(1)}, bf16[384,128]{1,0:T(8,128)(2...) custom-call(bf16[1152,128]{1,0:T(8,128)(2,1)S(1)} %get-tuple-element.87.refs_0_.refs_4_.refs_8_.refs_12_.refs_16_.refs_20_, ...), custom_call_target="tpu_custom_call" | custom-call | flops 1509949440 | bytes 3145728 | tf_op jit(solution)/shard_map/attention_0/pallas_call | solution.py:337
  72.2 2.6 %collective-permute-start.19 = (bf16[384,128]{1,0:T(8,128)(2,1)S(1)}, bf16[384,128]{1,0:T(8,128)(2,1)S(1)}, u32[]{:S(2)}, u32[]{:S(2)}) collective-permute-start(bf16[384,128]{1,0:T(8,128)(2,1)S(1)} %get-tuple-element.130), channel_id=1, source_target_pairs={{0,12},{4,8},{8,4},{12,0},{1,13},{5,9},{9,5},{13,1},{2,14},{6,10},... | collective-permute-start | bytes 294920 | tf_op jit(solution)/shard_map/returns_0/ppermute | solution.py:406
  78.4 3.3 %attention_1.1 = (bf16[576,128]{1,0:T(8,128)(2,1)S(1)}, bf16[576,128]{1,0:T(8,128)(2,1)S(1)}, bf16[576,128]{1,0:T(8,128)(2,1)S(1)}, bf16[576,128]{1,0:T(8,128)(2...) custom-call(bf16[1152,128]{1,0:T(8,128)(2,1)S(1)} %get-tuple-element.87.refs_0_.refs_4_.refs_8_.refs_12_.refs_16_.refs_20_, ...), custom_call_target="tpu_custom_call" | custom-call | flops 1509949440 | bytes 3145728 | tf_op jit(solution)/shard_map/attention_1/pallas_call | solution.py:337
  82.8 2.4 %collective-permute-start.24 = (bf16[576,128]{1,0:T(8,128)(2,1)S(1)}, bf16[576,128]{1,0:T(8,128)(2,1)S(1)}, u32[]{:S(2)}, u32[]{:S(2)}) collective-permute-start(bf16[576,128]{1,0:T(8,128)(2,1)S(1)} %get-tuple-element.145), channel_id=1, source_target_pairs={{0,12},{4,8},{8,4},{12,0},{1,13},{5,9},{9,5},{13,1},{2,14},{6,10},... | collective-permute-start | bytes 442376 | tf_op jit(solution)/shard_map/returns_1/ppermute | solution.py:406
  85.2 2.0 %collective-permute-start.26 = (bf16[576,128]{1,0:T(8,128)(2,1)S(1)}, bf16[576,128]{1,0:T(8,128)(2,1)S(1)}, u32[]{:S(2)}, u32[]{:S(2)}) collective-permute-start(bf16[576,128]{1,0:T(8,128)(2,1)S(1)} %get-tuple-element.147), channel_id=1, source_target_pairs={{0,4},{4,0},{8,12},{12,8},{1,5},{5,1},{9,13},{13,9},{2,6},{6,2},{1... | collective-permute-start | bytes 442376 | tf_op jit(solution)/shard_map/returns_1/ppermute | solution.py:406
  88.3 3.3 %attention_2.1 = (bf16[576,128]{1,0:T(8,128)(2,1)S(1)}, bf16[576,128]{1,0:T(8,128)(2,1)S(1)}, bf16[576,128]{1,0:T(8,128)(2,1)S(1)}, bf16[576,128]{1,0:T(8,128)(2...) custom-call(bf16[1152,128]{1,0:T(8,128)(2,1)S(1)} %get-tuple-element.87.refs_0_.refs_4_.refs_8_.refs_12_.refs_16_.refs_20_, ...), custom_call_target="tpu_custom_call" | custom-call | flops 1509949440 | bytes 3145728 | tf_op jit(solution)/shard_map/attention_2/pallas_call | solution.py:337
  91.6 5.5 %collective-permute-done.25.refs_6_ = bf16[576,128]{1,0:T(8,128)(2,1)S(1)} collective-permute-done((bf16[576,128]{1,0:T(8,128)(2,1)S(1)}, bf16[576,128]{1,0:T(8,128)(2,1)S(1)}, u32[]{:S(2)}, u32[]{:S(2)}) %collective-permute-start.25) | collective-permute-done | bytes 147488 | tf_op jit(solution)/shard_map/returns_1/ppermute | solution.py:406
  98.7 1.8 %collective-permute-start.28 = (bf16[576,128]{1,0:T(8,128)(2,1)S(1)}, bf16[576,128]{1,0:T(8,128)(2,1)S(1)}, u32[]{:S(2)}, u32[]{:S(2)}) collective-permute-start(bf16[576,128]{1,0:T(8,128)(2,1)S(1)} %get-tuple-element.156), channel_id=1, source_target_pairs={{0,12},{4,8},{8,4},{12,0},{1,13},{5,9},{9,5},{13,1},{2,14},{6,10},... | collective-permute-start | bytes 442376 | tf_op jit(solution)/shard_map/returns_2/ppermute | solution.py:406
  100.5 2.6 %collective-permute-start.30 = (bf16[576,128]{1,0:T(8,128)(2,1)S(1)}, bf16[576,128]{1,0:T(8,128)(2,1)S(1)}, u32[]{:S(2)}, u32[]{:S(2)}) collective-permute-start(bf16[576,128]{1,0:T(8,128)(2,1)S(1)} %get-tuple-element.158), channel_id=1, source_target_pairs={{0,4},{4,0},{8,12},{12,8},{1,5},{5,1},{9,13},{13,9},{2,6},{6,2},{1... | collective-permute-start | bytes 442376 | tf_op jit(solution)/shard_map/returns_2/ppermute | solution.py:406
  103.1 2.3 %collective-permute-start.32 = (bf16[192,128]{1,0:T(8,128)(2,1)S(1)}, bf16[192,128]{1,0:T(8,128)(2,1)S(1)}, u32[]{:S(2)}, u32[]{:S(2)}) collective-permute-start(bf16[192,128]{1,0:T(8,128)(2,1)S(1)} %get-tuple-element.164), channel_id=1, source_target_pairs={{0,12},{4,8},{8,4},{12,0},{1,13},{5,9},{9,5},{13,1},{2,14},{6,10},... | collective-permute-start | bytes 147464 | tf_op jit(solution)/shard_map/returns_last/ppermute | solution.py:406
  107.3 3.9 %collective-permute-start.34 = (bf16[192,128]{1,0:T(8,128)(2,1)S(1)}, bf16[192,128]{1,0:T(8,128)(2,1)S(1)}, u32[]{:S(2)}, u32[]{:S(2)}) collective-permute-start(bf16[192,128]{1,0:T(8,128)(2,1)S(1)} %get-tuple-element.166), channel_id=1, source_target_pairs={{0,4},{4,0},{8,12},{12,8},{1,5},{5,1},{9,13},{13,9},{2,6},{6,2},{1... | collective-permute-start | bytes 147464 | tf_op jit(solution)/shard_map/returns_last/ppermute | solution.py:406
  111.8 3.0 %collective-permute-done.29.refs_10_ = bf16[576,128]{1,0:T(8,128)(2,1)S(1)} collective-permute-done((bf16[576,128]{1,0:T(8,128)(2,1)S(1)}, bf16[576,128]{1,0:T(8,128)(2,1)S(1)}, u32[]{:S(2)}, u32[]{:S(2)}) %collective-permute-start.29) | collective-permute-done | bytes 147488 | tf_op jit(solution)/shard_map/returns_2/ppermute | solution.py:406
  (78 shorter events, 35.0 us)
Async XLA Ops:
  3.8 16.0 %collective-permute-start = (bf16[1152,128]{1,0:T(8,128)(2,1)}, bf16[1152,128]{1,0:T(8,128)(2,1)S(1)}, u32[]{:S(2)}, u32[]{:S(2)}) collective-permute-start(bf16[1152,128]{1,0:T(8,128)(2,1)} %get-tuple-element.88), channel_id=1, source_target_pairs={{0,12},{4,8},{8,4},{12,0},{1,13},{5,9},{9,5},{13,1},{2,14},{6,10},... | collective-permute-start | bytes 884744 | tf_op jit(solution)/shard_map/keys_queries/ppermute | solution.py:406
  8.9 25.3 %collective-permute-start.1 = (bf16[1152,128]{1,0:T(8,128)(2,1)S(1)}, bf16[1152,128]{1,0:T(8,128)(2,1)S(1)}, u32[]{:S(2)}, u32[]{:S(2)}) collective-permute-start(bf16[1152,128]{1,0:T(8,128)(2,1)S(1)} %get-tuple-element.89), channel_id=1, source_target_pairs={{0,8},{4,12},{8,0},{12,4},{1,9},{5,13},{9,1},{13,5},{2,10},{6,14},... | collective-permute-start | bytes 884744 | tf_op jit(solution)/shard_map/keys_queries/ppermute | solution.py:406
  8.9 25.3 %collective-permute-start.2 = (bf16[1152,128]{1,0:T(8,128)(2,1)S(1)}, bf16[1152,128]{1,0:T(8,128)(2,1)S(1)}, u32[]{:S(2)}, u32[]{:S(2)}) collective-permute-start(bf16[1152,128]{1,0:T(8,128)(2,1)S(1)} %get-tuple-element.90), channel_id=1, source_target_pairs={{0,4},{4,0},{8,12},{12,8},{1,5},{5,1},{9,13},{13,9},{2,6},{6,2},{1... | collective-permute-start | bytes 884744 | tf_op jit(solution)/shard_map/keys_queries/ppermute | solution.py:406
  34.8 19.2 %collective-permute-start.10 = (bf16[1728,128]{1,0:T(8,128)(2,1)S(1)}, bf16[1728,128]{1,0:T(8,128)(2,1)S(1)}, u32[]{:S(2)}, u32[]{:S(2)}) collective-permute-start(bf16[1728,128]{1,0:T(8,128)(2,1)S(1)} %halo_queries.1), channel_id=1, source_target_pairs={{0,16},{16,0},{1,17},{17,1},{2,18},{18,2},{3,19},{19,3},{4,20},{20... | collective-permute-start | bytes 1327112 | tf_op jit(solution)/shard_map/halo_queries/ppermute | solution.py:474
  36.4 7.9 %collective-permute-start.6 = (bf16[448,128]{1,0:T(8,128)(2,1)S(1)}, bf16[448,128]{1,0:T(8,128)(2,1)S(1)}, u32[]{:S(2)}, u32[]{:S(2)}) collective-permute-start(bf16[448,128]{1,0:T(8,128)(2,1)S(1)} %get-tuple-element.96), channel_id=1, source_target_pairs={{0,12},{4,8},{8,4},{12,0},{1,13},{5,9},{9,5},{13,1},{2,14},{6,10},... | collective-permute-start | bytes 344072 | tf_op jit(solution)/shard_map/first_grads/ppermute | solution.py:406
  38.8 8.8 %collective-permute-start.7 = (bf16[448,128]{1,0:T(8,128)(2,1)S(1)}, bf16[448,128]{1,0:T(8,128)(2,1)S(1)}, u32[]{:S(2)}, u32[]{:S(2)}) collective-permute-start(bf16[448,128]{1,0:T(8,128)(2,1)S(1)} %get-tuple-element.97), channel_id=1, source_target_pairs={{0,8},{4,12},{8,0},{12,4},{1,9},{5,13},{9,1},{13,5},{2,10},{6,14},... | collective-permute-start | bytes 344072 | tf_op jit(solution)/shard_map/first_grads/ppermute | solution.py:406
  38.8 8.8 %collective-permute-start.8 = (bf16[448,128]{1,0:T(8,128)(2,1)S(1)}, bf16[448,128]{1,0:T(8,128)(2,1)S(1)}, u32[]{:S(2)}, u32[]{:S(2)}) collective-permute-start(bf16[448,128]{1,0:T(8,128)(2,1)S(1)} %get-tuple-element.98), channel_id=1, source_target_pairs={{0,4},{4,0},{8,12},{12,8},{1,5},{5,1},{9,13},{13,9},{2,6},{6,2},{1... | collective-permute-start | bytes 344072 | tf_op jit(solution)/shard_map/first_grads/ppermute | solution.py:406
  47.6 10.0 %collective-permute-start.14 = (bf16[384,128]{1,0:T(8,128)(2,1)S(1)}, bf16[384,128]{1,0:T(8,128)(2,1)S(1)}, u32[]{:S(2)}, u32[]{:S(2)}) collective-permute-start(bf16[384,128]{1,0:T(8,128)(2,1)S(1)} %get-tuple-element.125), channel_id=1, source_target_pairs={{0,12},{4,8},{8,4},{12,0},{1,13},{5,9},{9,5},{13,1},{2,14},{6,10},... | collective-permute-start | bytes 294920 | tf_op jit(solution)/shard_map/rest_grads/ppermute | solution.py:406
  49.3 10.2 %collective-permute-start.15 = (bf16[384,128]{1,0:T(8,128)(2,1)S(1)}, bf16[384,128]{1,0:T(8,128)(2,1)S(1)}, u32[]{:S(2)}, u32[]{:S(2)}) collective-permute-start(bf16[384,128]{1,0:T(8,128)(2,1)S(1)} %get-tuple-element.126), channel_id=1, source_target_pairs={{0,8},{4,12},{8,0},{12,4},{1,9},{5,13},{9,1},{13,5},{2,10},{6,14},... | collective-permute-start | bytes 294920 | tf_op jit(solution)/shard_map/rest_grads/ppermute | solution.py:406
  53.4 13.1 %collective-permute-start.12 = (bf16[1024,128]{1,0:T(8,128)(2,1)S(1)}, bf16[1024,128]{1,0:T(8,128)(2,1)S(1)}, u32[]{:S(2)}, u32[]{:S(2)}) collective-permute-start(bf16[1024,128]{1,0:T(8,128)(2,1)S(1)} %halo_first_grads.1), channel_id=1, source_target_pairs={{0,16},{16,0},{1,17},{17,1},{2,18},{18,2},{3,19},{19,3},{4,20},{20... | collective-permute-start | bytes 786440 | tf_op jit(solution)/shard_map/halo_first_grads/ppermute | solution.py:474
  60.1 9.8 %collective-permute-start.16 = (bf16[384,128]{1,0:T(8,128)(2,1)S(1)}, bf16[384,128]{1,0:T(8,128)(2,1)S(1)}, u32[]{:S(2)}, u32[]{:S(2)}) collective-permute-start(bf16[384,128]{1,0:T(8,128)(2,1)S(1)} %get-tuple-element.127), channel_id=1, source_target_pairs={{0,12},{4,8},{8,4},{12,0},{1,13},{5,9},{9,5},{13,1},{2,14},{6,10},... | collective-permute-start | bytes 294920 | tf_op jit(solution)/shard_map/rest_values/ppermute | solution.py:406
  62.2 8.7 %collective-permute-start.17 = (bf16[384,128]{1,0:T(8,128)(2,1)S(1)}, bf16[384,128]{1,0:T(8,128)(2,1)S(1)}, u32[]{:S(2)}, u32[]{:S(2)}) collective-permute-start(bf16[384,128]{1,0:T(8,128)(2,1)S(1)} %get-tuple-element.128), channel_id=1, source_target_pairs={{0,8},{4,12},{8,0},{12,4},{1,9},{5,13},{9,1},{13,5},{2,10},{6,14},... | collective-permute-start | bytes 294920 | tf_op jit(solution)/shard_map/rest_values/ppermute | solution.py:406
  66.4 12.1 %collective-permute-start.22 = (bf16[1536,128]{1,0:T(8,128)(2,1)S(1)}, bf16[1536,128]{1,0:T(8,128)(2,1)S(1)}, u32[]{:S(2)}, u32[]{:S(2)}) collective-permute-start(bf16[1536,128]{1,0:T(8,128)(2,1)S(1)} %halo_rest_grads.1), channel_id=1, source_target_pairs={{0,16},{16,0},{1,17},{17,1},{2,18},{18,2},{3,19},{19,3},{4,20},{20... | collective-permute-start | bytes 1179656 | tf_op jit(solution)/shard_map/halo_rest_grads/ppermute | solution.py:474
  70.9 7.5 %collective-permute-start.23 = (bf16[768,128]{1,0:T(8,128)(2,1)S(1)}, bf16[768,128]{1,0:T(8,128)(2,1)S(1)}, u32[]{:S(2)}, u32[]{:S(2)}) collective-permute-start(bf16[768,128]{1,0:T(8,128)(2,1)S(1)} %get-tuple-element.140), channel_id=1, source_target_pairs={{0,16},{16,0},{1,17},{17,1},{2,18},{18,2},{3,19},{19,3},{4,20},{20... | collective-permute-start | bytes 589832 | tf_op jit(solution)/shard_map/halo_query_grads_0/ppermute | solution.py:549
  72.2 9.5 %collective-permute-start.19 = (bf16[384,128]{1,0:T(8,128)(2,1)S(1)}, bf16[384,128]{1,0:T(8,128)(2,1)S(1)}, u32[]{:S(2)}, u32[]{:S(2)}) collective-permute-start(bf16[384,128]{1,0:T(8,128)(2,1)S(1)} %get-tuple-element.130), channel_id=1, source_target_pairs={{0,12},{4,8},{8,4},{12,0},{1,13},{5,9},{9,5},{13,1},{2,14},{6,10},... | collective-permute-start | bytes 294920 | tf_op jit(solution)/shard_map/returns_0/ppermute | solution.py:406
  82.8 8.8 %collective-permute-start.24 = (bf16[576,128]{1,0:T(8,128)(2,1)S(1)}, bf16[576,128]{1,0:T(8,128)(2,1)S(1)}, u32[]{:S(2)}, u32[]{:S(2)}) collective-permute-start(bf16[576,128]{1,0:T(8,128)(2,1)S(1)} %get-tuple-element.145), channel_id=1, source_target_pairs={{0,12},{4,8},{8,4},{12,0},{1,13},{5,9},{9,5},{13,1},{2,14},{6,10},... | collective-permute-start | bytes 442376 | tf_op jit(solution)/shard_map/returns_1/ppermute | solution.py:406
  85.2 11.9 %collective-permute-start.25 = (bf16[576,128]{1,0:T(8,128)(2,1)S(1)}, bf16[576,128]{1,0:T(8,128)(2,1)S(1)}, u32[]{:S(2)}, u32[]{:S(2)}) collective-permute-start(bf16[576,128]{1,0:T(8,128)(2,1)S(1)} %get-tuple-element.146), channel_id=1, source_target_pairs={{0,8},{4,12},{8,0},{12,4},{1,9},{5,13},{9,1},{13,5},{2,10},{6,14},... | collective-permute-start | bytes 442376 | tf_op jit(solution)/shard_map/returns_1/ppermute | solution.py:406
  85.2 11.9 %collective-permute-start.26 = (bf16[576,128]{1,0:T(8,128)(2,1)S(1)}, bf16[576,128]{1,0:T(8,128)(2,1)S(1)}, u32[]{:S(2)}, u32[]{:S(2)}) collective-permute-start(bf16[576,128]{1,0:T(8,128)(2,1)S(1)} %get-tuple-element.147), channel_id=1, source_target_pairs={{0,4},{4,0},{8,12},{12,8},{1,5},{5,1},{9,13},{13,9},{2,6},{6,2},{1... | collective-permute-start | bytes 442376 | tf_op jit(solution)/shard_map/returns_1/ppermute | solution.py:406
  98.7 8.6 %collective-permute-start.28 = (bf16[576,128]{1,0:T(8,128)(2,1)S(1)}, bf16[576,128]{1,0:T(8,128)(2,1)S(1)}, u32[]{:S(2)}, u32[]{:S(2)}) collective-permute-start(bf16[576,128]{1,0:T(8,128)(2,1)S(1)} %get-tuple-element.156), channel_id=1, source_target_pairs={{0,12},{4,8},{8,4},{12,0},{1,13},{5,9},{9,5},{13,1},{2,14},{6,10},... | collective-permute-start | bytes 442376 | tf_op jit(solution)/shard_map/returns_2/ppermute | solution.py:406
  100.5 14.3 %collective-permute-start.29 = (bf16[576,128]{1,0:T(8,128)(2,1)S(1)}, bf16[576,128]{1,0:T(8,128)(2,1)S(1)}, u32[]{:S(2)}, u32[]{:S(2)}) collective-permute-start(bf16[576,128]{1,0:T(8,128)(2,1)S(1)} %get-tuple-element.157), channel_id=1, source_target_pairs={{0,8},{4,12},{8,0},{12,4},{1,9},{5,13},{9,1},{13,5},{2,10},{6,14},... | collective-permute-start | bytes 442376 | tf_op jit(solution)/shard_map/returns_2/ppermute | solution.py:406
  100.5 14.3 %collective-permute-start.30 = (bf16[576,128]{1,0:T(8,128)(2,1)S(1)}, bf16[576,128]{1,0:T(8,128)(2,1)S(1)}, u32[]{:S(2)}, u32[]{:S(2)}) collective-permute-start(bf16[576,128]{1,0:T(8,128)(2,1)S(1)} %get-tuple-element.158), channel_id=1, source_target_pairs={{0,4},{4,0},{8,12},{12,8},{1,5},{5,1},{9,13},{13,9},{2,6},{6,2},{1... | collective-permute-start | bytes 442376 | tf_op jit(solution)/shard_map/returns_2/ppermute | solution.py:406
  103.1 11.7 %collective-permute-start.32 = (bf16[192,128]{1,0:T(8,128)(2,1)S(1)}, bf16[192,128]{1,0:T(8,128)(2,1)S(1)}, u32[]{:S(2)}, u32[]{:S(2)}) collective-permute-start(bf16[192,128]{1,0:T(8,128)(2,1)S(1)} %get-tuple-element.164), channel_id=1, source_target_pairs={{0,12},{4,8},{8,4},{12,0},{1,13},{5,9},{9,5},{13,1},{2,14},{6,10},... | collective-permute-start | bytes 147464 | tf_op jit(solution)/shard_map/returns_last/ppermute | solution.py:406
  105.5 10.6 %collective-permute-start.33 = (bf16[192,128]{1,0:T(8,128)(2,1)S(1)}, bf16[192,128]{1,0:T(8,128)(2,1)S(1)}, u32[]{:S(2)}, u32[]{:S(2)}) collective-permute-start(bf16[192,128]{1,0:T(8,128)(2,1)S(1)} %get-tuple-element.165), channel_id=1, source_target_pairs={{0,8},{4,12},{8,0},{12,4},{1,9},{5,13},{9,1},{13,5},{2,10},{6,14},... | collective-permute-start | bytes 147464 | tf_op jit(solution)/shard_map/returns_last/ppermute | solution.py:406
  107.3 8.8 %collective-permute-start.34 = (bf16[192,128]{1,0:T(8,128)(2,1)S(1)}, bf16[192,128]{1,0:T(8,128)(2,1)S(1)}, u32[]{:S(2)}, u32[]{:S(2)}) collective-permute-start(bf16[192,128]{1,0:T(8,128)(2,1)S(1)} %get-tuple-element.166), channel_id=1, source_target_pairs={{0,4},{4,0},{8,12},{12,8},{1,5},{5,1},{9,13},{13,9},{2,6},{6,2},{1... | collective-permute-start | bytes 147464 | tf_op jit(solution)/shard_map/returns_last/ppermute | solution.py:406
  (17 other events, 85.7 us)

commit v9 on v8

--- a/solution.py
+++ b/solution.py
@@ -131,11 +131,10 @@
 
 
 def pack_grads_kernel(parts, out_grad_ref, attn_ref, value_ref, gain_ref, partial_ref, *refs):
-    leads, rests = refs[:parts], refs[parts:]
     rows, channels = out_grad_ref.shape
     heads = channels // (parts * HD)
-    depth = 2 * rows + dots_depth(rows, heads)
-    lines = partial_ref.shape[0]
+    base = (heads + 1) * rows
+    depth = base + dots_depth(rows, heads)
     partial = jnp.concatenate(split_terms(partial_ref[...], 3), axis=0)
     spare = gain_depth(channels) - partial.shape[0]
     if spare:
@@ -145,11 +144,10 @@
         for head in range(heads):
             columns = pl.ds(column_of(parts, distance, heads, head), HD)
             grad = (out_grad_ref[:, columns].astype(jnp.float32) * gain_ref[:, columns]).astype(jnp.bfloat16)
-            if head:
-                rests[distance][(head - 1) * rows : head * rows] = grad
-            else:
-                leads[distance][:rows] = grad
-                leads[distance][rows : 2 * rows] = value_ref[:, columns]
+            place = head + 1 if head else 0
+            refs[distance][place * rows : (place + 1) * rows] = grad
+            if head == 0:
+                refs[distance][rows : 2 * rows] = value_ref[:, columns]
             product = grad.astype(jnp.float32) * attn_ref[:, columns].astype(jnp.float32)
             dots = jnp.sum(jnp.transpose(product), axis=0, keepdims=True)
             for first in range(0, rows, LANES):
@@ -161,23 +159,20 @@
         rest = dots_depth(rows, heads) - len(terms)
         if rest:
             terms.append(jnp.zeros((rest, LANES), jnp.float32))
-        leads[distance][2 * rows : depth] = jnp.concatenate(terms, axis=0).astype(jnp.bfloat16)
-        leads[distance][depth:] = partial.astype(jnp.bfloat16)
+        refs[distance][base:depth] = jnp.concatenate(terms, axis=0).astype(jnp.bfloat16)
+        refs[distance][depth:] = partial.astype(jnp.bfloat16)
 
 
 def pack_grads(out_grad, attn_out, values, out_gain, partial, parts):
     rows, channels = out_grad.shape
     heads = channels // (parts * HD)
-    depth = 2 * rows + dots_depth(rows, heads) + gain_depth(channels)
-    lead = jax.ShapeDtypeStruct((depth, HD), jnp.bfloat16)
-    rest = jax.ShapeDtypeStruct(((heads - 1) * rows, HD), jnp.bfloat16)
-    outs = pl.pallas_call(
+    depth = (heads + 1) * rows + dots_depth(rows, heads) + gain_depth(channels)
+    return pl.pallas_call(
         functools.partial(pack_grads_kernel, parts),
-        out_shape=[lead] * parts + [rest] * parts,
+        out_shape=[jax.ShapeDtypeStruct((depth, HD), jnp.bfloat16)] * parts,
         compiler_params=params(),
         cost_estimate=COST,
     )(out_grad, attn_out, values, out_gain.reshape(1, channels), partial)
-    return outs[:parts], outs[parts:]
 
 
 def gain_total_kernel(lines, starts, scale, *refs):
@@ -262,7 +257,7 @@
     return top + jnp.log2(functools.reduce(jnp.add, [jnp.exp2(value - top) for value in values]))
 
 
-def attention_kernel(parts, sources, head, rows, before, *refs):
+def attention_kernel(parts, sources, chosen, rows, *refs):
     slab = parts * rows
 
     def take(count):
@@ -270,108 +265,103 @@
         taken, refs = refs[:count], refs[count:]
         return taken
 
-    key_refs, value_refs = take(parts), take(parts)
-    query_refs, grad_refs, dots_refs = take(parts * sources), take(parts * sources), take(parts * sources)
-    total_refs = take(sources)
-    before_refs = take(sources) if before else ()
+    dots_refs, total_refs = take(parts * sources), take(sources)
+    inputs = [[take(parts), take(parts), take(parts * sources), take(parts * sources)] for _ in chosen]
     piece_refs, query_grad_refs = take(parts), take(sources)
     weight_ref, score_ref = refs
-    if before:
-        closed = before_refs[0][...]
-        for ref in before_refs[1:]:
-            closed = closed + ref[...].astype(jnp.float32)
-        closed = closed.astype(jnp.bfloat16)
-        for part in range(parts):
-            piece_refs[part][2 * rows :] = closed[part * rows : (part + 1) * rows]
-    keys, values, queries, grads = stacked(key_refs), stacked(value_refs), stacked(query_refs), stacked(grad_refs)
-    query_flip, grad_flip = jnp.transpose(queries), jnp.transpose(grads)
-    lines = []
-    for ref in dots_refs:
-        terms = ref[...].astype(jnp.float32)
-        for index in range(dot_groups(rows)):
-            line = 2 * (head * dot_groups(rows) + index)
-            count = min(LANES, rows - index * LANES)
-            lines.append((terms[line : line + 1] + terms[line + 1 : line + 2])[:, :count])
-    dots = jnp.concatenate(lines, axis=1)
-    totals = jnp.concatenate([ref[head : head + 1] for ref in total_refs], axis=1)
-    width = sources * slab
-    for first in range(0, slab, KEY_BLOCK):
-        stretch = slice(first, first + KEY_BLOCK)
-        for start in range(0, width, QUERY_BLOCK):
-            span = slice(start, start + QUERY_BLOCK)
-            scores = jnp.dot(keys[stretch], query_flip[:, span], preferred_element_type=jnp.float32)
-            weights = jnp.exp2(scores * SCALE_LOG2 - totals[:, span])
-            grad_weights = jnp.dot(values[stretch], grad_flip[:, span], preferred_element_type=jnp.float32)
-            weight_ref[stretch, span] = weights.astype(jnp.bfloat16)
-            score_ref[stretch, span] = (weights * (grad_weights - dots[:, span])).astype(jnp.bfloat16)
-        value_grad = jnp.dot(weight_ref[stretch], grads, preferred_element_type=jnp.float32)
-        key_grad = jnp.dot(score_ref[stretch], queries, preferred_element_type=jnp.float32) * SCALE
-        key_grad, value_grad = key_grad.astype(jnp.bfloat16), value_grad.astype(jnp.bfloat16)
-        for part in range(parts):
-            low, high = max(first, part * rows), min(first + KEY_BLOCK, (part + 1) * rows)
-            if low < high:
-                place = low - part * rows
-                piece_refs[part][place : place + high - low] = key_grad[low - first : high - first]
-                piece_refs[part][rows + place : rows + place + high - low] = value_grad[low - first : high - first]
-    for source in range(sources):
-        query_grad = lax.dot_general(
-            score_ref[:, source * slab : (source + 1) * slab],
-            keys,
-            (((0,), (0,)), ((), ())),
-            preferred_element_type=jnp.float32,
-        )
-        query_grad_refs[source][...] = (query_grad * SCALE).astype(query_grad_refs[source].dtype)
-
-
-def attention(head, heads, rows, keys, values, queries, grads, dots, totals, before):
-    parts = len(keys)
+    for number, head in enumerate(chosen):
+        keys, values, queries, grads = [stacked(held) for held in inputs[number]]
+        query_flip, grad_flip = jnp.transpose(queries), jnp.transpose(grads)
+        lines = []
+        for ref in dots_refs:
+            terms = ref[...].astype(jnp.float32)
+            for index in range(dot_groups(rows)):
+                line = 2 * (head * dot_groups(rows) + index)
+                count = min(LANES, rows - index * LANES)
+                lines.append((terms[line : line + 1] + terms[line + 1 : line + 2])[:, :count])
+        dots = jnp.concatenate(lines, axis=1)
+        totals = jnp.concatenate([ref[head : head + 1] for ref in total_refs], axis=1)
+        base = 2 * number * rows
+        for first in range(0, slab, KEY_BLOCK):
+            stretch = slice(first, first + KEY_BLOCK)
+            for start in range(0, sources * slab, QUERY_BLOCK):
+                span = slice(start, start + QUERY_BLOCK)
+                scores = jnp.dot(keys[stretch], query_flip[:, span], preferred_element_type=jnp.float32)
+                weights = jnp.exp2(scores * SCALE_LOG2 - totals[:, span])
+                grad_weights = jnp.dot(values[stretch], grad_flip[:, span], preferred_element_type=jnp.float32)
+                weight_ref[stretch, span] = weights.astype(jnp.bfloat16)
+                score_ref[stretch, span] = (weights * (grad_weights - dots[:, span])).astype(jnp.bfloat16)
+            value_grad = jnp.dot(weight_ref[stretch], grads, preferred_element_type=jnp.float32)
+            key_grad = jnp.dot(score_ref[stretch], queries, preferred_element_type=jnp.float32) * SCALE
+            key_grad, value_grad = key_grad.astype(jnp.bfloat16), value_grad.astype(jnp.bfloat16)
+            for part in range(parts):
+                low, high = max(first, part * rows), min(first + KEY_BLOCK, (part + 1) * rows)
+                if low < high:
+                    place = base + low - part * rows
+                    local_rows = slice(low - first, high - first)
+                    piece_refs[part][place : place + high - low] = key_grad[local_rows]
+                    piece_refs[part][place + rows : place + rows + high - low] = value_grad[local_rows]
+        for source, ref in enumerate(query_grad_refs):
+            query_grad = lax.dot_general(
+                score_ref[:, source * slab : (source + 1) * slab],
+                keys,
+                (((0,), (0,)), ((), ())),
+                preferred_element_type=jnp.float32,
+            )
+            ref[number * slab : (number + 1) * slab] = (query_grad * SCALE).astype(ref.dtype)
+
+
+def attention(chosen, heads, rows, inputs, dots, totals):
+    parts = len(inputs[0][0])
     sources = len(totals)
     slab = parts * rows
-    in_specs, operands = block_specs(rows, keys + values + queries + grads)
     dot_specs, dot_arrays = block_specs(dots_depth(rows, heads), dots)
-    before_specs, before_arrays = block_specs(slab, [(array, 0) for array in before])
+    in_specs, operands = block_specs(rows, [place for held in inputs for places in held for place in places])
     line = pl.BlockSpec((heads, slab), lambda step: (0, 0))
-    depth = (3 if before else 2) * rows
+    depth = 2 * len(chosen) * rows
     out_specs, _ = block_specs(depth, [(None, 0)] * parts)
-    query_specs, _ = block_specs(slab, [(None, 0)] * sources)
+    query_specs, _ = block_specs(len(chosen) * slab, [(None, 0)] * sources)
     outs = pl.pallas_call(
-        functools.partial(attention_kernel, parts, sources, head, rows, bool(before)),
+        functools.partial(attention_kernel, parts, sources, chosen, rows),
         grid=(1,),
-        in_specs=in_specs + dot_specs + [line] * sources + before_specs,
+        in_specs=dot_specs + [line] * sources + in_specs,
         out_specs=out_specs + query_specs,
         out_shape=[jax.ShapeDtypeStruct((depth, HD), jnp.bfloat16)] * parts
-        + [jax.ShapeDtypeStruct((slab, HD), jnp.float32)]
-        + [jax.ShapeDtypeStruct((slab, HD), jnp.bfloat16)] * (sources - 1),
+        + [jax.ShapeDtypeStruct((len(chosen) * slab, HD), jnp.float32)]
+        + [jax.ShapeDtypeStruct((len(chosen) * slab, HD), jnp.bfloat16)] * (sources - 1),
         scratch_shapes=[pltpu.VMEM((slab, sources * slab), jnp.bfloat16)] * 2,
         compiler_params=params(),
         cost_estimate=pl.CostEstimate(
-            flops=10 * slab * sources * slab * HD,
-            bytes_accessed=32 * slab * HD,
-            transcendentals=slab * sources * slab,
+            flops=10 * len(chosen) * slab * sources * slab * HD,
+            bytes_accessed=32 * len(chosen) * slab * HD,
+            transcendentals=len(chosen) * slab * sources * slab,
         ),
-    )(*operands, *dot_arrays, *totals, *before_arrays)
+    )(*dot_arrays, *totals, *operands)
     return outs[:parts], outs[parts:]
 
 
-def close_kernel(parts, *refs):
-    own_ref, side_refs, pieces = refs[0], refs[1:-parts], refs[-parts:]
-    rows = pieces[0].shape[0]
-    for part in range(parts):
-        span = slice(part * rows, (part + 1) * rows)
-        total = own_ref[span]
-        for ref in side_refs:
-            total = total + ref[span].astype(jnp.float32)
-        pieces[part][...] = total.astype(jnp.bfloat16)
-
-
-def close(query_grads, parts):
-    rows = query_grads[0].shape[0] // parts
-    return pl.pallas_call(
-        functools.partial(close_kernel, parts),
-        out_shape=[jax.ShapeDtypeStruct((rows, HD), jnp.bfloat16)] * parts,
-        compiler_params=params(),
-        cost_estimate=COST,
-    )(*query_grads)
+def close_kernel(parts, rows, sources, *refs):
+    terms, pieces = refs[:-parts], refs[-parts:]
+    place = 0
+    for first in range(0, len(terms), sources):
+        for start in range(0, terms[first].shape[0], parts * rows):
+            for part in range(parts):
+                span = slice(start + part * rows, start + (part + 1) * rows)
+                total = terms[first][span]
+                for ref in terms[first + 1 : first + sources]:
+                    total = total + ref[span].astype(jnp.float32)
+                pieces[part][place : place + rows] = total.astype(jnp.bfloat16)
+            place += rows
+
+
+def close(query_grads, parts, rows):
+    depth = sum(terms[0].shape[0] for terms in query_grads) // parts
+    return pl.pallas_call(
+        functools.partial(close_kernel, parts, rows, len(query_grads[0])),
+        out_shape=[jax.ShapeDtypeStruct((depth, HD), jnp.bfloat16)] * parts,
+        compiler_params=params(),
+        cost_estimate=COST,
+    )(*[term for terms in query_grads for term in terms])
 
 
 def unpack_kernel(parts, rows, heads, stages, *refs):
@@ -484,22 +474,19 @@
         if not paired:
             gain = sum_over(gain, "tm")
     with jax.named_scope("grads"):
-        sent_lead, sent_rest = pack_grads(out_grad[0], attn_out[0], values[0], out_gain, gain, parts)
+        sent_lead = pack_grads(out_grad[0], attn_out[0], values[0], out_gain, gain, parts)
+    with jax.named_scope("halo_own_grads"):
+        own_side = forward(sent_lead[0])
     with jax.named_scope("halo_queries"):
         width = heads * rows
         first_side = forward(pairs[0][width:])
-    with jax.named_scope("first_grads"):
+    with jax.named_scope("grads"):
         lead = swap_pieces(sent_lead, pairs)
-    with jax.named_scope("rest_grads"):
-        rest_grads = swap_pieces(sent_rest, lead)
     with jax.named_scope("halo_queries"):
-        late = after(pairs[1:], sent_lead[0], first_side)
+        late = after(pairs[1:], first_side, sent_lead[0])
         late_side = forward(gather_rows(late, [(number, width, width) for number in range(parts - 1)]))
-    with jax.named_scope("halo_first_grads"):
-        extra = gain_depth(channels) if paired else 0
-        ranges = [(part, 0, rows) for part in every] + [(part, 2 * rows, dots) for part in every]
-        ranges += [(part, 2 * rows + dots, extra) for part in every] * paired
-        lead_side = forward(gather_rows(after(lead, rest_grads[-1]), ranges))
+    base = (heads + 1) * rows
+    extra = gain_depth(channels)
     with jax.named_scope("totals"):
         key_places = [[(piece, head) for piece in pairs] for head in range(heads)]
         query_places = [[[(piece, heads + head) for piece in pairs] for head in range(heads)]]
@@ -511,54 +498,64 @@
                 ]
             )
         part_totals = partial_totals(key_places, query_places, rows)
-        totals = exchange_totals(part_totals, sides)
+        totals = exchange_totals(after(part_totals, lead[1:]), sides)
+    others = range(1, parts)
+    with jax.named_scope("halo_first_grads"):
+        ranges = [(part, 0, rows) for part in others] + [(part, base, dots + extra) for part in others]
+        lead_side = forward(gather_rows(after(lead, part_totals, own_side), ranges))
     with jax.named_scope("rest_values"):
-        rest_values = swap_pieces(after(pack([values[0]], parts, rest), part_totals), rest_grads)
-    with jax.named_scope("halo_rest_grads"):
-        ranges = [(part, place * rows, rows) for place in range(heads - 1) for part in every]
-        rest_side = forward(gather_rows(after(rest_grads, rest_values[-1]), ranges))
-    dot_places = [(piece, 2 * rows // dots) for piece in lead]
-    dot_places += [(array, parts * rows // dots + part) for array in lead_side for part in every]
+        rest_values = swap_pieces(after(pack([values[0]], parts, rest), part_totals), lead)
+    dot_places = [(piece, base // dots) for piece in lead]
+    for own, array in zip(own_side, lead_side):
+        dot_places.append((own, base // dots))
+        step = (dots + extra) // dots
+        dot_places += [(array, (parts - 1) * rows // dots + (part - 1) * step) for part in others]
+
+    def inputs_of(head):
+        queries_of = [place for source in query_places for place in source[head]]
+        if head == 0:
+            values_of = [(piece, 1) for piece in lead]
+            grads_of = [(piece, 0) for piece in lead]
+            for own, array in zip(own_side, lead_side):
+                grads_of += [(own, 0)] + [(array, part - 1) for part in others]
+        else:
+            values_of = [(piece, head - 1) for piece in rest_values]
+            grads_of = [(piece, head + 1) for piece in lead]
+            for own, array in zip(own_side, rest_side):
+                start = (head - 1) * (parts - 1)
+                grads_of += [(own, head + 1)] + [(array, start + part - 1) for part in others]
+        return [key_places[head], values_of, queries_of, grads_of]
+
     stages, pieces, open_grads = [], [], []
     gate = rest_values
-    for head in range(heads):
-        if head == 0:
-            value_places = [(piece, 1) for piece in lead]
-            grad_places = [(piece, 0) for piece in lead] + [(array, part) for array in lead_side for part in every]
-        else:
-            value_places = [(piece, head - 1) for piece in rest_values]
-            grad_places = [(piece, head - 1) for piece in rest_grads]
-            grad_places += [(array, (head - 1) * parts + part) for array in rest_side for part in every]
-        before = open_grads if head else ()
-        with jax.named_scope("attention_%d" % head):
-            leaving, query_grads = attention(
-                head,
-                heads,
-                rows,
-                key_places[head],
-                value_places,
-                [place for source in query_places for place in source[head]],
-                grad_places,
-                dot_places,
-                totals,
-                before,
-            )
-        stages.append([(1, head), (2, head)] + ([(0, head - 1)] if before else []))
-        query_grads = after(query_grads, gate[1:])
-        with jax.named_scope("halo_query_grads_%d" % head):
-            back_grads = [lax.ppermute(other, "tm", back) for other, (_, back) in zip(query_grads[1:], sides)]
-            open_grads = list(query_grads[:1]) + back_grads
-        with jax.named_scope("returns_%d" % head):
-            pieces.append(swap_pieces(leaving, gate))
-        gate = pieces[-1]
+    for number, chosen in enumerate([[0], rest]):
+        if number:
+            with jax.named_scope("halo_rest_grads"):
+                ranges = [(part, (head + 1) * rows, rows) for head in rest for part in others]
+                rest_side = forward(gather_rows(after(lead, leaving[0], rest_values[1:]), ranges))
+        with jax.named_scope("attention_%d" % number):
+            inputs = [inputs_of(head) for head in chosen]
+            leaving, query_grads = attention(chosen, heads, rows, inputs, dot_places, totals)
+            totals = after(totals, leaving[0])
+        if number:
+            query_grads = after(query_grads, gate[1:])
+        with jax.named_scope("halo_query_grads_%d" % number):
+            sent_back = [lax.ppermute(other, "tm", back) for other, (_, back) in zip(query_grads[1:], sides)]
+            open_grads.append(list(query_grads[:1]) + sent_back)
+        with jax.named_scope("returns_%d" % number):
+            gate = swap_pieces(leaving, gate)
+            pieces.append(gate)
+        stages.append([(output, head) for head in chosen for output in (1, 2)])
     with jax.named_scope("returns_last"):
-        stages.append([(0, heads - 1)])
-        pieces.append(swap_pieces(close(open_grads, parts)))
+        pieces.append(swap_pieces(close(open_grads, parts, rows), gate))
+        stages.append([(0, head) for head in range(heads)])
     result = unpack(stages, pieces, rows, heads)
     with jax.named_scope("gain"):
-        places = [(piece, 2 * rows + dots) for piece in lead]
+        places = [(piece, base + dots) for piece in lead]
         if paired:
-            places += [(lead_side[0], parts * (rows + dots) + part * extra) for part in every]
+            places.append((own_side[0], base + dots))
+            start = (parts - 1) * rows + dots
+            places += [(lead_side[0], start + (part - 1) * (dots + extra)) for part in others]
         gain = gain_total(places, channels // LANES, 1.0 / (rows * span * parts * lax.axis_size("dp")))
     return tuple(grad[None] for grad in result) + (gain.reshape(channels),)
 

time: 118 us -> 117 us (level)
  starting transfers between devices: 45.9 us -> 37.9 us
  waiting for transfers between devices: 49.3 us -> 56.5 us
    ppermute x4 -> x5, waiting for transfers between devices: 3.27 us -> 13.4 us  [forward(): return [lax.ppermute(array, 'tm', there) for there, _ in sides]]
    ppermute x27 -> x21, starting transfers between devices: 38.3 us -> 29.4 us  [swap(): lax.ppermute(value, axis, [(index, index ^ distance) for index in range(l...]
    ppermute x27 -> x21, waiting for transfers between devices: 43.1 us -> 35.7 us  [swap(): lax.ppermute(value, axis, [(index, index ^ distance) for index in range(l...]
    ppermute x3 -> x2, waiting for transfers between devices: 2.91 us -> 7.36 us  [local(): lax.ppermute(other, 'tm', back)]
    ppermute x4 -> x5, starting transfers between devices: 3.72 us -> 5.71 us  [forward(): return [lax.ppermute(array, 'tm', there) for there, _ in sides]]
    ppermute x3 -> x2, starting transfers between devices: 3.36 us -> 2.09 us  [local(): lax.ppermute(other, 'tm', back)]
    pallas_call x5 -> x4, Pallas kernels: 10.6 us -> 10.4 us  [the longest x2 9.8 us: attention(): pl.pallas_call(functools.partial(attention_kernel, parts, sources, chosen...]
  transfers between devices with their start and end apart: 35 -> 29, of which waited for: 17 -> 12; matrix products, arithmetic and copies ran while one was open for 0% -> 0% of each run, Pallas kernels for 14% -> 13%
where the time goes in v9:
time: 117 us; the launch traced here: 116 us
  waiting for transfers between devices  56.5 us (48%)
  starting transfers between devices  37.9 us (32%)
  Pallas kernels  18.9 us (16%)
  local copies, waits for them, and re-layouts  2.16 us (2%)
    ppermute x21, waiting for transfers between devices, swap(): lax.ppermute(value, axis, [(index, index ^ distance) for index in range(l...  35.7 us
    ppermute x21, starting transfers between devices, swap(): lax.ppermute(value, axis, [(index, index ^ distance) for index in range(l...  29.4 us
    ppermute x5, waiting for transfers between devices, forward(): return [lax.ppermute(array, 'tm', there) for there, _ in sides]  13.4 us
    pallas_call x2, Pallas kernels, attention(): pl.pallas_call(functools.partial(attention_kernel, parts, sources, chosen...  9.8 us
    ppermute x2, waiting for transfers between devices, local(): lax.ppermute(other, 'tm', back)  7.36 us
    ppermute x5, starting transfers between devices, forward(): return [lax.ppermute(array, 'tm', there) for there, _ in sides]  5.71 us
    pallas_call x1, Pallas kernels, partial_totals(): pl.pallas_call(functools.partial(totals_kernel, parts, sources, heads), g...  3.61 us
  transfers between devices with their start and end apart: 29, of which 12 were waited for; matrix products, arithmetic and copies ran while one was open for 0% of the time, Pallas kernels for 13%

profile of v9, /device:TPU:0, one launch (start us, length us, event | category | flops | bytes accessed | tf_op | source)
XLA Modules:
  0.0 116.4 jit_solution(16717907473089028337)
XLA Ops:
  3.8 5.1 %collective-permute-start.3 = (bf16[1152,128]{1,0:T(8,128)(2,1)}, bf16[1152,128]{1,0:T(8,128)(2,1)S(1)}, u32[]{:S(2)}, u32[]{:S(2)}) collective-permute-start(bf16[1152,128]{1,0:T(8,128)(2,1)} %get-tuple-element.80), channel_id=1, source_target_pairs={{0,12},{4,8},{8,4},{12,0},{1,13},{5,9},{9,5},{13,1},{2,14},{6,10},... | collective-permute-start | bytes 884744 | tf_op jit(solution)/shard_map/keys_queries/ppermute | solution.py:396
  9.6 1.7 %collective-permute-start.1 = (f32[12,128]{1,0:T(8,128)S(1)}, f32[12,128]{1,0:T(8,128)S(1)}, u32[]{:S(2)}, u32[]{:S(2)}) collective-permute-start(f32[12,128]{1,0:T(8,128)S(1)} %bitcast.19), channel_id=1, source_target_pairs={{0,2},{1,3},{2,0},{3,1},{4,6},{5,7},{6,4},{7,5},{8,10},{9,11},{10,... | collective-permute-start | bytes 18440 | tf_op jit(solution)/shard_map/gain/ppermute | solution.py:396
  11.4 2.0 %collective-permute-done.1 = f32[12,128]{1,0:T(8,128)S(1)} collective-permute-done((f32[12,128]{1,0:T(8,128)S(1)}, f32[12,128]{1,0:T(8,128)S(1)}, u32[]{:S(2)}, u32[]{:S(2)}) %collective-permute-start.1) | collective-permute-done | bytes 6176 | tf_op jit(solution)/shard_map/gain/ppermute | solution.py:396
  16.5 3.3 %collective-permute-done.10.refs_24_.refs_28_.refs_32_.refs_22_.refs_46_ = bf16[576,128]{1,0:T(8,128)(2,1)S(1)} collective-permute-done((bf16[576,128]{1,0:T(8,128)(2,1)S(1)}, bf16[576,128]{1,0:T(8,128)(2,1)S(1)}, u32[]{:S(2)}, u32[]{:S(2)}) %collective-permute-start.10) | collective-permute-done | bytes 147488 | tf_op jit(solution)/shard_map/halo_queries/ppermute | solution.py:464
  19.7 14.5 %collective-permute-done.4.refs_1_.refs_2_.refs_6_.refs_10_.refs_14_.refs_18_.refs_22_.refs_12_.refs_20_.refs_36_.refs_44_ = bf16[1152,128]{1,0:T(8,128)(2,1)S(1)} collective-permute-done((bf16[1152,128]{1,0:T(8,128)(2,1)S(1)}, bf16[1152,128]{1,0:T(8,128)(2,1)S(1)}, u32[]{:S(2)}, u32[]{:S(2)}) %collective-permute-start.4) | collective-permute-done | bytes 294944 | tf_op jit(solution)/shard_map/keys_queries/ppermute | solution.py:396
  36.4 2.5 %collective-permute-start.6 = (bf16[832,128]{1,0:T(8,128)(2,1)S(1)}, bf16[832,128]{1,0:T(8,128)(2,1)S(1)}, u32[]{:S(2)}, u32[]{:S(2)}) collective-permute-start(bf16[832,128]{1,0:T(8,128)(2,1)S(1)} %get-tuple-element.83), channel_id=1, source_target_pairs={{0,12},{4,8},{8,4},{12,0},{1,13},{5,9},{9,5},{13,1},{2,14},{6,10},... | collective-permute-start | bytes 638984 | tf_op jit(solution)/shard_map/grads/ppermute | solution.py:396
  38.8 1.9 %collective-permute-start.8 = (bf16[832,128]{1,0:T(8,128)(2,1)S(1)}, bf16[832,128]{1,0:T(8,128)(2,1)S(1)}, u32[]{:S(2)}, u32[]{:S(2)}) collective-permute-start(bf16[832,128]{1,0:T(8,128)(2,1)S(1)} %get-tuple-element.85), channel_id=1, source_target_pairs={{0,4},{4,0},{8,12},{12,8},{1,5},{5,1},{9,13},{13,9},{2,6},{6,2},{1... | collective-permute-start | bytes 638984 | tf_op jit(solution)/shard_map/grads/ppermute | solution.py:396
  41.3 6.7 %collective-permute-done.11.refs_25_.refs_26_.refs_27_.refs_29_.refs_30_.refs_31_.refs_33_.refs_34_.refs_35_.refs_23_.refs_24_.refs_47_.refs_48_.refs_49_ = bf16[1728,128]{1,0:T(8,128)(2,1)S(1)} collective-permute-done((bf16[1728,128]{1,0:T(8,128)(2,1)S(1)}, bf16[1728,128]{1,0:T(8,128)(2,1)S(1)}, u32[]{:S(2)}, u32[]{:S(2)}) %collective-permute-start.11) | collective-permute-done | bytes 442400 | tf_op jit(solution)/shard_map/halo_queries/ppermute | solution.py:464
  48.0 3.6 %totals.1 = (f32[3,768]{1,0:T(4,128)S(1)}, f32[3,768]{1,0:T(4,128)S(1)}) custom-call(bf16[1152,128]{1,0:T(8,128)(2,1)S(1)} %get-tuple-element.74.refs_0_.refs_4_.refs_8_.refs_12_.refs_16_.refs_20_.refs_10_.refs_18_.refs_34_.refs_42_, ...), custom_call_target="tpu_custom_call" | custom-call | flops 905969664 | bytes 2359296 | tf_op jit(solution)/shard_map/totals/pallas_call | solution.py:239
  51.6 3.4 %collective-permute-done.7.refs_2_.refs_16_.refs_28_.refs_52_ = bf16[832,128]{1,0:T(8,128)(2,1)S(1)} collective-permute-done((bf16[832,128]{1,0:T(8,128)(2,1)S(1)}, bf16[832,128]{1,0:T(8,128)(2,1)S(1)}, u32[]{:S(2)}, u32[]{:S(2)}) %collective-permute-start.7) | collective-permute-done | bytes 213024 | tf_op jit(solution)/shard_map/grads/ppermute | solution.py:396
  59.2 2.9 %collective-permute-start.16 = (bf16[384,128]{1,0:T(8,128)(2,1)S(1)}, bf16[384,128]{1,0:T(8,128)(2,1)S(1)}, u32[]{:S(2)}, u32[]{:S(2)}) collective-permute-start(bf16[384,128]{1,0:T(8,128)(2,1)S(1)} %get-tuple-element.111), channel_id=1, source_target_pairs={{0,4},{4,0},{8,12},{12,8},{1,5},{5,1},{9,13},{13,9},{2,6},{6,2},{1... | collective-permute-start | bytes 294920 | tf_op jit(solution)/shard_map/rest_values/ppermute | solution.py:396
  62.1 3.4 %attention_0.1 = (bf16[384,128]{1,0:T(8,128)(2,1)S(1)}, bf16[384,128]{1,0:T(8,128)(2,1)S(1)}, bf16[384,128]{1,0:T(8,128)(2,1)S(1)}, bf16[384,128]{1,0:T(8,128)(2...) custom-call(bf16[832,128]{1,0:T(8,128)(2,1)S(1)} %get-tuple-element.117.refs_0_.refs_14_.refs_26_.refs_50_, ...), custom_call_target="tpu_custom_call" | custom-call | flops 1509949440 | bytes 3145728 | tf_op jit(solution)/shard_map/attention_0/pallas_call | solution.py:324
  68.2 2.1 %collective-permute-start.17 = (bf16[384,128]{1,0:T(8,128)(2,1)S(1)}, bf16[384,128]{1,0:T(8,128)(2,1)S(1)}, u32[]{:S(2)}, u32[]{:S(2)}) collective-permute-start(bf16[384,128]{1,0:T(8,128)(2,1)S(1)} %get-tuple-element.112), channel_id=1, source_target_pairs={{0,12},{4,8},{8,4},{12,0},{1,13},{5,9},{9,5},{13,1},{2,14},{6,10},... | collective-permute-start | bytes 294920 | tf_op jit(solution)/shard_map/returns_0/ppermute | solution.py:396
  70.3 2.2 %collective-permute-start.19 = (bf16[384,128]{1,0:T(8,128)(2,1)S(1)}, bf16[384,128]{1,0:T(8,128)(2,1)S(1)}, u32[]{:S(2)}, u32[]{:S(2)}) collective-permute-start(bf16[384,128]{1,0:T(8,128)(2,1)S(1)} %get-tuple-element.114), channel_id=1, source_target_pairs={{0,4},{4,0},{8,12},{12,8},{1,5},{5,1},{9,13},{13,9},{2,6},{6,2},{1... | collective-permute-start | bytes 294920 | tf_op jit(solution)/shard_map/returns_0/ppermute | solution.py:396
  72.6 3.4 %collective-permute-done.20.refs_31_.refs_32_.refs_33_.refs_55_.refs_56_.refs_57_ = bf16[1152,128]{1,0:T(8,128)(2,1)S(1)} collective-permute-done((bf16[1152,128]{1,0:T(8,128)(2,1)S(1)}, bf16[1152,128]{1,0:T(8,128)(2,1)S(1)}, u32[]{:S(2)}, u32[]{:S(2)}) %collective-permute-start.20) | collective-permute-done | bytes 294944 | tf_op jit(solution)/shard_map/halo_rest_grads/ppermute | solution.py:464
  76.0 6.4 %attention_1.1 = (bf16[768,128]{1,0:T(8,128)(2,1)S(1)}, bf16[768,128]{1,0:T(8,128)(2,1)S(1)}, bf16[768,128]{1,0:T(8,128)(2,1)S(1)}, bf16[768,128]{1,0:T(8,128)(2...) custom-call(bf16[832,128]{1,0:T(8,128)(2,1)S(1)} %get-tuple-element.117.refs_0_.refs_14_.refs_26_.refs_50_, ...), custom_call_target="tpu_custom_call" | custom-call | flops 3019898880 | bytes 6291456 | tf_op jit(solution)/shard_map/attention_1/pallas_call | solution.py:324
  84.6 2.2 %collective-permute-start.21 = (bf16[768,128]{1,0:T(8,128)(2,1)S(1)}, bf16[768,128]{1,0:T(8,128)(2,1)S(1)}, u32[]{:S(2)}, u32[]{:S(2)}) collective-permute-start(bf16[768,128]{1,0:T(8,128)(2,1)S(1)} %get-tuple-element.125), channel_id=1, source_target_pairs={{0,12},{4,8},{8,4},{12,0},{1,13},{5,9},{9,5},{13,1},{2,14},{6,10},... | collective-permute-start | bytes 589832 | tf_op jit(solution)/shard_map/returns_1/ppermute | solution.py:396
  86.8 2.1 %collective-permute-start.23 = (bf16[768,128]{1,0:T(8,128)(2,1)S(1)}, bf16[768,128]{1,0:T(8,128)(2,1)S(1)}, u32[]{:S(2)}, u32[]{:S(2)}) collective-permute-start(bf16[768,128]{1,0:T(8,128)(2,1)S(1)} %get-tuple-element.127), channel_id=1, source_target_pairs={{0,4},{4,0},{8,12},{12,8},{1,5},{5,1},{9,13},{13,9},{2,6},{6,2},{1... | collective-permute-start | bytes 589832 | tf_op jit(solution)/shard_map/returns_1/ppermute | solution.py:396
  89.0 7.4 %collective-permute-done.24.refs_1_ = bf16[768,128]{1,0:T(8,128)(2,1)S(1)} collective-permute-done((bf16[768,128]{1,0:T(8,128)(2,1)S(1)}, bf16[768,128]{1,0:T(8,128)(2,1)S(1)}, u32[]{:S(2)}, u32[]{:S(2)}) %collective-permute-start.24) | collective-permute-done | bytes 196640 | tf_op jit(solution)/shard_map/halo_query_grads_0/ppermute | solution.py:543
  96.4 5.4 %collective-permute-done.22.refs_6_ = bf16[768,128]{1,0:T(8,128)(2,1)S(1)} collective-permute-done((bf16[768,128]{1,0:T(8,128)(2,1)S(1)}, bf16[768,128]{1,0:T(8,128)(2,1)S(1)}, u32[]{:S(2)}, u32[]{:S(2)}) %collective-permute-start.22) | collective-permute-done | bytes 196640 | tf_op jit(solution)/shard_map/returns_1/ppermute | solution.py:396
  101.9 1.6 %collective-permute-start.26 = (bf16[576,128]{1,0:T(8,128)(2,1)S(1)}, bf16[576,128]{1,0:T(8,128)(2,1)S(1)}, u32[]{:S(2)}, u32[]{:S(2)}) collective-permute-start(bf16[576,128]{1,0:T(8,128)(2,1)S(1)} %get-tuple-element.138), channel_id=1, source_target_pairs={{0,12},{4,8},{8,4},{12,0},{1,13},{5,9},{9,5},{13,1},{2,14},{6,10},... | collective-permute-start | bytes 442376 | tf_op jit(solution)/shard_map/returns_last/ppermute | solution.py:396
  103.5 2.7 %collective-permute-start.28 = (bf16[576,128]{1,0:T(8,128)(2,1)S(1)}, bf16[576,128]{1,0:T(8,128)(2,1)S(1)}, u32[]{:S(2)}, u32[]{:S(2)}) collective-permute-start(bf16[576,128]{1,0:T(8,128)(2,1)S(1)} %get-tuple-element.140), channel_id=1, source_target_pairs={{0,4},{4,0},{8,12},{12,8},{1,5},{5,1},{9,13},{13,9},{2,6},{6,2},{1... | collective-permute-start | bytes 442376 | tf_op jit(solution)/shard_map/returns_last/ppermute | solution.py:396
  106.9 3.6 %collective-permute-done.26.refs_9_ = bf16[576,128]{1,0:T(8,128)(2,1)S(1)} collective-permute-done((bf16[576,128]{1,0:T(8,128)(2,1)S(1)}, bf16[576,128]{1,0:T(8,128)(2,1)S(1)}, u32[]{:S(2)}, u32[]{:S(2)}) %collective-permute-start.26) | collective-permute-done | bytes 147488 | tf_op jit(solution)/shard_map/returns_last/ppermute | solution.py:396
  110.5 4.3 %collective-permute-done.27.refs_10_ = bf16[576,128]{1,0:T(8,128)(2,1)S(1)} collective-permute-done((bf16[576,128]{1,0:T(8,128)(2,1)S(1)}, bf16[576,128]{1,0:T(8,128)(2,1)S(1)}, u32[]{:S(2)}, u32[]{:S(2)}) %collective-permute-start.27) | collective-permute-done | bytes 147488 | tf_op jit(solution)/shard_map/returns_last/ppermute | solution.py:396
  (65 shorter events, 20.9 us)
Async XLA Ops:
  3.8 16.0 %collective-permute-start.3 = (bf16[1152,128]{1,0:T(8,128)(2,1)}, bf16[1152,128]{1,0:T(8,128)(2,1)S(1)}, u32[]{:S(2)}, u32[]{:S(2)}) collective-permute-start(bf16[1152,128]{1,0:T(8,128)(2,1)} %get-tuple-element.80), channel_id=1, source_target_pairs={{0,12},{4,8},{8,4},{12,0},{1,13},{5,9},{9,5},{13,1},{2,14},{6,10},... | collective-permute-start | bytes 884744 | tf_op jit(solution)/shard_map/keys_queries/ppermute | solution.py:396
  8.9 25.3 %collective-permute-start.4 = (bf16[1152,128]{1,0:T(8,128)(2,1)S(1)}, bf16[1152,128]{1,0:T(8,128)(2,1)S(1)}, u32[]{:S(2)}, u32[]{:S(2)}) collective-permute-start(bf16[1152,128]{1,0:T(8,128)(2,1)S(1)} %get-tuple-element.81), channel_id=1, source_target_pairs={{0,8},{4,12},{8,0},{12,4},{1,9},{5,13},{9,1},{13,5},{2,10},{6,14},... | collective-permute-start | bytes 884744 | tf_op jit(solution)/shard_map/keys_queries/ppermute | solution.py:396
  8.9 25.3 %collective-permute-start.5 = (bf16[1152,128]{1,0:T(8,128)(2,1)S(1)}, bf16[1152,128]{1,0:T(8,128)(2,1)S(1)}, u32[]{:S(2)}, u32[]{:S(2)}) collective-permute-start(bf16[1152,128]{1,0:T(8,128)(2,1)S(1)} %get-tuple-element.82), channel_id=1, source_target_pairs={{0,4},{4,0},{8,12},{12,8},{1,5},{5,1},{9,13},{13,9},{2,6},{6,2},{1... | collective-permute-start | bytes 884744 | tf_op jit(solution)/shard_map/keys_queries/ppermute | solution.py:396
  34.8 13.2 %collective-permute-start.11 = (bf16[1728,128]{1,0:T(8,128)(2,1)S(1)}, bf16[1728,128]{1,0:T(8,128)(2,1)S(1)}, u32[]{:S(2)}, u32[]{:S(2)}) collective-permute-start(bf16[1728,128]{1,0:T(8,128)(2,1)S(1)} %halo_queries.1), channel_id=1, source_target_pairs={{0,16},{16,0},{1,17},{17,1},{2,18},{18,2},{3,19},{19,3},{4,20},{20... | collective-permute-start | bytes 1327112 | tf_op jit(solution)/shard_map/halo_queries/ppermute | solution.py:464
  36.4 15.2 %collective-permute-start.6 = (bf16[832,128]{1,0:T(8,128)(2,1)S(1)}, bf16[832,128]{1,0:T(8,128)(2,1)S(1)}, u32[]{:S(2)}, u32[]{:S(2)}) collective-permute-start(bf16[832,128]{1,0:T(8,128)(2,1)S(1)} %get-tuple-element.83), channel_id=1, source_target_pairs={{0,12},{4,8},{8,4},{12,0},{1,13},{5,9},{9,5},{13,1},{2,14},{6,10},... | collective-permute-start | bytes 638984 | tf_op jit(solution)/shard_map/grads/ppermute | solution.py:396
  38.8 16.2 %collective-permute-start.7 = (bf16[832,128]{1,0:T(8,128)(2,1)S(1)}, bf16[832,128]{1,0:T(8,128)(2,1)S(1)}, u32[]{:S(2)}, u32[]{:S(2)}) collective-permute-start(bf16[832,128]{1,0:T(8,128)(2,1)S(1)} %get-tuple-element.84), channel_id=1, source_target_pairs={{0,8},{4,12},{8,0},{12,4},{1,9},{5,13},{9,1},{13,5},{2,10},{6,14},... | collective-permute-start | bytes 638984 | tf_op jit(solution)/shard_map/grads/ppermute | solution.py:396
  38.8 16.2 %collective-permute-start.8 = (bf16[832,128]{1,0:T(8,128)(2,1)S(1)}, bf16[832,128]{1,0:T(8,128)(2,1)S(1)}, u32[]{:S(2)}, u32[]{:S(2)}) collective-permute-start(bf16[832,128]{1,0:T(8,128)(2,1)S(1)} %get-tuple-element.85), channel_id=1, source_target_pairs={{0,4},{4,0},{8,12},{12,8},{1,5},{5,1},{9,13},{13,9},{2,6},{6,2},{1... | collective-permute-start | bytes 638984 | tf_op jit(solution)/shard_map/grads/ppermute | solution.py:396
  40.7 15.1 %collective-permute-start.9 = (bf16[832,128]{1,0:T(8,128)(2,1)S(1)}, bf16[832,128]{1,0:T(8,128)(2,1)S(1)}, u32[]{:S(2)}, u32[]{:S(2)}) collective-permute-start(bf16[832,128]{1,0:T(8,128)(2,1)S(1)} %get-tuple-element.117.refs_0_.refs_14_.refs_26_.refs_50_), channel_id=1, source_target_pairs={{0,16},{16,0},{1,17},{17,1},{2,18},{18,2},{3,19},{19,3},{4,20},{20... | collective-permute-start | bytes 638984 | tf_op jit(solution)/shard_map/halo_own_grads/ppermute | solution.py:464
  55.0 7.1 %collective-permute-start.13 = (f32[6,768]{1,0:T(8,128)S(1)}, f32[6,768]{1,0:T(8,128)S(1)}, u32[]{:S(2)}, u32[]{:S(2)}) collective-permute-start(f32[6,768]{1,0:T(8,128)S(1)} %pad_maximum_fusion), channel_id=1, source_target_pairs={{0,16},{16,0},{1,17},{17,1},{2,18},{18,2},{3,19},{19,3},{4,20},{20... | collective-permute-start | bytes 55304 | tf_op jit(solution)/shard_map/totals/ppermute | solution.py:441
  57.7 7.8 %collective-permute-start.14 = (bf16[384,128]{1,0:T(8,128)(2,1)S(1)}, bf16[384,128]{1,0:T(8,128)(2,1)S(1)}, u32[]{:S(2)}, u32[]{:S(2)}) collective-permute-start(bf16[384,128]{1,0:T(8,128)(2,1)S(1)} %get-tuple-element.109), channel_id=1, source_target_pairs={{0,12},{4,8},{8,4},{12,0},{1,13},{5,9},{9,5},{13,1},{2,14},{6,10},... | collective-permute-start | bytes 294920 | tf_op jit(solution)/shard_map/rest_values/ppermute | solution.py:396
  59.2 7.7 %collective-permute-start.15 = (bf16[384,128]{1,0:T(8,128)(2,1)S(1)}, bf16[384,128]{1,0:T(8,128)(2,1)S(1)}, u32[]{:S(2)}, u32[]{:S(2)}) collective-permute-start(bf16[384,128]{1,0:T(8,128)(2,1)S(1)} %get-tuple-element.110), channel_id=1, source_target_pairs={{0,8},{4,12},{8,0},{12,4},{1,9},{5,13},{9,1},{13,5},{2,10},{6,14},... | collective-permute-start | bytes 294920 | tf_op jit(solution)/shard_map/rest_values/ppermute | solution.py:396
  59.2 7.7 %collective-permute-start.16 = (bf16[384,128]{1,0:T(8,128)(2,1)S(1)}, bf16[384,128]{1,0:T(8,128)(2,1)S(1)}, u32[]{:S(2)}, u32[]{:S(2)}) collective-permute-start(bf16[384,128]{1,0:T(8,128)(2,1)S(1)} %get-tuple-element.111), channel_id=1, source_target_pairs={{0,4},{4,0},{8,12},{12,8},{1,5},{5,1},{9,13},{13,9},{2,6},{6,2},{1... | collective-permute-start | bytes 294920 | tf_op jit(solution)/shard_map/rest_values/ppermute | solution.py:396
  67.6 8.4 %collective-permute-start.20 = (bf16[1152,128]{1,0:T(8,128)(2,1)S(1)}, bf16[1152,128]{1,0:T(8,128)(2,1)S(1)}, u32[]{:S(2)}, u32[]{:S(2)}) collective-permute-start(bf16[1152,128]{1,0:T(8,128)(2,1)S(1)} %halo_rest_grads.1), channel_id=1, source_target_pairs={{0,16},{16,0},{1,17},{17,1},{2,18},{18,2},{3,19},{19,3},{4,20},{20... | collective-permute-start | bytes 884744 | tf_op jit(solution)/shard_map/halo_rest_grads/ppermute | solution.py:464
  68.2 14.3 %collective-permute-start.17 = (bf16[384,128]{1,0:T(8,128)(2,1)S(1)}, bf16[384,128]{1,0:T(8,128)(2,1)S(1)}, u32[]{:S(2)}, u32[]{:S(2)}) collective-permute-start(bf16[384,128]{1,0:T(8,128)(2,1)S(1)} %get-tuple-element.112), channel_id=1, source_target_pairs={{0,12},{4,8},{8,4},{12,0},{1,13},{5,9},{9,5},{13,1},{2,14},{6,10},... | collective-permute-start | bytes 294920 | tf_op jit(solution)/shard_map/returns_0/ppermute | solution.py:396
  70.3 12.2 %collective-permute-start.18 = (bf16[384,128]{1,0:T(8,128)(2,1)S(1)}, bf16[384,128]{1,0:T(8,128)(2,1)S(1)}, u32[]{:S(2)}, u32[]{:S(2)}) collective-permute-start(bf16[384,128]{1,0:T(8,128)(2,1)S(1)} %get-tuple-element.113), channel_id=1, source_target_pairs={{0,8},{4,12},{8,0},{12,4},{1,9},{5,13},{9,1},{13,5},{2,10},{6,14},... | collective-permute-start | bytes 294920 | tf_op jit(solution)/shard_map/returns_0/ppermute | solution.py:396
  70.3 12.2 %collective-permute-start.19 = (bf16[384,128]{1,0:T(8,128)(2,1)S(1)}, bf16[384,128]{1,0:T(8,128)(2,1)S(1)}, u32[]{:S(2)}, u32[]{:S(2)}) collective-permute-start(bf16[384,128]{1,0:T(8,128)(2,1)S(1)} %get-tuple-element.114), channel_id=1, source_target_pairs={{0,4},{4,0},{8,12},{12,8},{1,5},{5,1},{9,13},{13,9},{2,6},{6,2},{1... | collective-permute-start | bytes 294920 | tf_op jit(solution)/shard_map/returns_0/ppermute | solution.py:396
  82.5 13.8 %collective-permute-start.25 = (bf16[1536,128]{1,0:T(8,128)(2,1)S(1)}, bf16[1536,128]{1,0:T(8,128)(2,1)S(1)}, u32[]{:S(2)}, u32[]{:S(2)}) collective-permute-start(bf16[1536,128]{1,0:T(8,128)(2,1)S(1)} %get-tuple-element.133), channel_id=1, source_target_pairs={{0,16},{16,0},{1,17},{17,1},{2,18},{18,2},{3,19},{19,3},{4,20},{20... | collective-permute-start | bytes 1179656 | tf_op jit(solution)/shard_map/halo_query_grads_1/ppermute | solution.py:543
  83.1 13.2 %collective-permute-start.24 = (bf16[768,128]{1,0:T(8,128)(2,1)S(1)}, bf16[768,128]{1,0:T(8,128)(2,1)S(1)}, u32[]{:S(2)}, u32[]{:S(2)}) collective-permute-start(bf16[768,128]{1,0:T(8,128)(2,1)S(1)} %get-tuple-element.129), channel_id=1, source_target_pairs={{0,16},{16,0},{1,17},{17,1},{2,18},{18,2},{3,19},{19,3},{4,20},{20... | collective-permute-start | bytes 589832 | tf_op jit(solution)/shard_map/halo_query_grads_0/ppermute | solution.py:543
  84.6 11.9 %collective-permute-start.21 = (bf16[768,128]{1,0:T(8,128)(2,1)S(1)}, bf16[768,128]{1,0:T(8,128)(2,1)S(1)}, u32[]{:S(2)}, u32[]{:S(2)}) collective-permute-start(bf16[768,128]{1,0:T(8,128)(2,1)S(1)} %get-tuple-element.125), channel_id=1, source_target_pairs={{0,12},{4,8},{8,4},{12,0},{1,13},{5,9},{9,5},{13,1},{2,14},{6,10},... | collective-permute-start | bytes 589832 | tf_op jit(solution)/shard_map/returns_1/ppermute | solution.py:396
  86.8 15.1 %collective-permute-start.22 = (bf16[768,128]{1,0:T(8,128)(2,1)S(1)}, bf16[768,128]{1,0:T(8,128)(2,1)S(1)}, u32[]{:S(2)}, u32[]{:S(2)}) collective-permute-start(bf16[768,128]{1,0:T(8,128)(2,1)S(1)} %get-tuple-element.126), channel_id=1, source_target_pairs={{0,8},{4,12},{8,0},{12,4},{1,9},{5,13},{9,1},{13,5},{2,10},{6,14},... | collective-permute-start | bytes 589832 | tf_op jit(solution)/shard_map/returns_1/ppermute | solution.py:396
  86.8 15.1 %collective-permute-start.23 = (bf16[768,128]{1,0:T(8,128)(2,1)S(1)}, bf16[768,128]{1,0:T(8,128)(2,1)S(1)}, u32[]{:S(2)}, u32[]{:S(2)}) collective-permute-start(bf16[768,128]{1,0:T(8,128)(2,1)S(1)} %get-tuple-element.127), channel_id=1, source_target_pairs={{0,4},{4,0},{8,12},{12,8},{1,5},{5,1},{9,13},{13,9},{2,6},{6,2},{1... | collective-permute-start | bytes 589832 | tf_op jit(solution)/shard_map/returns_1/ppermute | solution.py:396
  101.9 8.6 %collective-permute-start.26 = (bf16[576,128]{1,0:T(8,128)(2,1)S(1)}, bf16[576,128]{1,0:T(8,128)(2,1)S(1)}, u32[]{:S(2)}, u32[]{:S(2)}) collective-permute-start(bf16[576,128]{1,0:T(8,128)(2,1)S(1)} %get-tuple-element.138), channel_id=1, source_target_pairs={{0,12},{4,8},{8,4},{12,0},{1,13},{5,9},{9,5},{13,1},{2,14},{6,10},... | collective-permute-start | bytes 442376 | tf_op jit(solution)/shard_map/returns_last/ppermute | solution.py:396
  103.5 11.2 %collective-permute-start.27 = (bf16[576,128]{1,0:T(8,128)(2,1)S(1)}, bf16[576,128]{1,0:T(8,128)(2,1)S(1)}, u32[]{:S(2)}, u32[]{:S(2)}) collective-permute-start(bf16[576,128]{1,0:T(8,128)(2,1)S(1)} %get-tuple-element.139), channel_id=1, source_target_pairs={{0,8},{4,12},{8,0},{12,4},{1,9},{5,13},{9,1},{13,5},{2,10},{6,14},... | collective-permute-start | bytes 442376 | tf_op jit(solution)/shard_map/returns_last/ppermute | solution.py:396
  103.5 11.2 %collective-permute-start.28 = (bf16[576,128]{1,0:T(8,128)(2,1)S(1)}, bf16[576,128]{1,0:T(8,128)(2,1)S(1)}, u32[]{:S(2)}, u32[]{:S(2)}) collective-permute-start(bf16[576,128]{1,0:T(8,128)(2,1)S(1)} %get-tuple-element.140), channel_id=1, source_target_pairs={{0,4},{4,0},{8,12},{12,8},{1,5},{5,1},{9,13},{13,9},{2,6},{6,2},{1... | collective-permute-start | bytes 442376 | tf_op jit(solution)/shard_map/returns_last/ppermute | solution.py:396
  (11 other events, 46.5 us)

commit v10 on v9

--- a/solution.py
+++ b/solution.py
@@ -14,6 +14,7 @@
 KEY_BLOCK = 256
 QUERY_BLOCK = 256
 VMEM_LIMIT = 48 * 1024 * 1024
+VMEM_WHOLE = 62 * 1024 * 1024
 SCALE = 1.0 / math.sqrt(HD)
 SCALE_LOG2 = SCALE / math.log(2.0)
 COST = pl.CostEstimate(flops=1, bytes_accessed=1, transcendentals=0)
@@ -56,7 +57,7 @@
     run_copies(pairs, semaphores)
 
 
-def pack(sources, parts, chosen):
+def pack(sources, parts, chosen, limit=VMEM_LIMIT):
     rows = sources[0].shape[0]
     depth = len(sources) * len(chosen) * rows
     whole = pl.BlockSpec(memory_space=pl.ANY)
@@ -66,7 +67,7 @@
         out_specs=[whole] * parts,
         out_shape=[jax.ShapeDtypeStruct((depth, HD), sources[0].dtype)] * parts,
         scratch_shapes=[pltpu.SemaphoreType.DMA((len(sources) * len(chosen) * parts,))],
-        compiler_params=params(),
+        compiler_params=pltpu.CompilerParams(vmem_limit_bytes=limit),
         cost_estimate=COST,
     )(*sources)
 
@@ -377,16 +378,16 @@
     run_copies(pairs, semaphores)
 
 
-def unpack(stages, pieces, rows, heads):
+def unpack(stages, pieces, rows, heads, outputs):
     parts = len(pieces[0])
     whole = pl.BlockSpec(memory_space=pl.ANY)
     channels = parts * heads * HD
     return pl.pallas_call(
         functools.partial(unpack_kernel, parts, rows, heads, stages),
         in_specs=[whole] * (parts * len(stages)),
-        out_specs=[whole] * 3,
-        out_shape=[jax.ShapeDtypeStruct((rows, channels), jnp.bfloat16)] * 3,
-        scratch_shapes=[pltpu.SemaphoreType.DMA((3 * heads * parts,))],
+        out_specs=[whole] * outputs,
+        out_shape=[jax.ShapeDtypeStruct((rows, channels), jnp.bfloat16)] * outputs,
+        scratch_shapes=[pltpu.SemaphoreType.DMA((outputs * heads * parts,))],
         compiler_params=params(),
         cost_estimate=COST,
     )(*[piece for stage in pieces for piece in stage])
@@ -398,11 +399,10 @@
 
 def swap_pieces(pieces, earlier=None):
     held = [pieces[0]]
-    if earlier is not None:
-        pieces = after(pieces, earlier[1:])
     for place, distance in enumerate(distances(len(pieces))):
         if distance:
-            held.append(swap(pieces[place], "ulysses", distance))
+            piece = pieces[place] if earlier is None else after([pieces[place]], earlier[place])[0]
+            held.append(swap(piece, "ulysses", distance))
     return held
 
 
@@ -464,7 +464,7 @@
         return [lax.ppermute(array, "tm", there) for there, _ in sides]
 
     with jax.named_scope("keys_queries"):
-        packed = pack([keys[0], queries[0]], parts, list(range(heads)))
+        packed = pack([keys[0], queries[0]], parts, list(range(heads)), VMEM_WHOLE)
         pairs = swap_pieces(packed)
     paired = span == 2
     with jax.named_scope("gain"):
@@ -538,18 +538,19 @@
             leaving, query_grads = attention(chosen, heads, rows, inputs, dot_places, totals)
             totals = after(totals, leaving[0])
         if number:
-            query_grads = after(query_grads, gate[1:])
+            query_grads = after(query_grads, gate[1:], open_grads[0][1:])
         with jax.named_scope("halo_query_grads_%d" % number):
             sent_back = [lax.ppermute(other, "tm", back) for other, (_, back) in zip(query_grads[1:], sides)]
             open_grads.append(list(query_grads[:1]) + sent_back)
         with jax.named_scope("returns_%d" % number):
             gate = swap_pieces(leaving, gate)
             pieces.append(gate)
-        stages.append([(output, head) for head in chosen for output in (1, 2)])
+        stages.append([(output, head) for head in chosen for output in (0, 1)])
+    key_grad, value_grad = unpack(stages, pieces, rows, heads, 2)
     with jax.named_scope("returns_last"):
-        pieces.append(swap_pieces(close(open_grads, parts, rows), gate))
-        stages.append([(0, head) for head in range(heads)])
-    result = unpack(stages, pieces, rows, heads)
+        last = swap_pieces(close(open_grads, parts, rows), gate)
+    (query_grad,) = unpack([[(0, head) for head in range(heads)]], [last], rows, heads, 1)
+    result = (query_grad, key_grad, value_grad)
     with jax.named_scope("gain"):
         places = [(piece, base + dots) for piece in lead]
         if paired:

time: 117 us -> 150 us (1.28)
  Pallas kernels: 18.9 us -> 55.6 us
  local copies, waits for them, and re-layouts: 2.16 us -> 0.04 us
  waiting for transfers between devices: 56.5 us -> 54.5 us
    pallas_call x2, Pallas kernels: 1.15 us -> 37.2 us  [pack(): pl.pallas_call(functools.partial(pack_kernel, parts, chosen), in_specs=[w...]
    ppermute x2, waiting for transfers between devices: 7.36 us -> 2.86 us  [local(): lax.ppermute(other, 'tm', back)]
    ppermute x21, waiting for transfers between devices: 35.7 us -> 38.2 us  [swap(): lax.ppermute(value, axis, [(index, index ^ distance) for index in range(l...]
    unnamed x12 -> x10, local copies, waits for them, and re-layouts: 2.14 us -> 0.02 us
  transfers between devices with their start and end apart: 29 -> 29, of which waited for: 12 -> 13; matrix products, arithmetic and copies ran while one was open for 0% -> 0% of each run, Pallas kernels for 13% -> 11%
where the time goes in v10:
time: 150 us
  Pallas kernels  55.6 us (37%)
  waiting for transfers between devices  54.5 us (36%)
  starting transfers between devices  39 us (26%)
    ppermute x21, waiting for transfers between devices, swap(): lax.ppermute(value, axis, [(index, index ^ distance) for index in range(l...  38.2 us
    pallas_call x2, Pallas kernels, pack(): pl.pallas_call(functools.partial(pack_kernel, parts, chosen), in_specs=[w...  37.2 us
    ppermute x21, starting transfers between devices, swap(): lax.ppermute(value, axis, [(index, index ^ distance) for index in range(l...  30.5 us
    ppermute x5, waiting for transfers between devices, forward(): return [lax.ppermute(array, 'tm', there) for there, _ in sides]  13.5 us
    pallas_call x2, Pallas kernels, attention(): pl.pallas_call(functools.partial(attention_kernel, parts, sources, chosen...  9.8 us
    ppermute x5, starting transfers between devices, forward(): return [lax.ppermute(array, 'tm', there) for there, _ in sides]  5.74 us
    pallas_call x1, Pallas kernels, partial_totals(): pl.pallas_call(functools.partial(totals_kernel, parts, sources, heads), g...  3.61 us
  transfers between devices with their start and end apart: 29, of which 13 were waited for; matrix products, arithmetic and copies ran while one was open for 0% of the time, Pallas kernels for 11%

profile of v10, /device:TPU:0, one launch (start us, length us, event | category | flops | bytes accessed | tf_op | source)
XLA Modules:
  0.0 150.2 jit_solution(7826573329208964573)
XLA Ops:
  0.7 37.1 %keys_queries.1 = (bf16[1152,128]{1,0:T(8,128)(2,1)}, bf16[1152,128]{1,0:T(8,128)(2,1)}, bf16[1152,128]{1,0:T(8,128)(2,1)}, bf16[1152,128]{1,0:T(8,128)(2,1)}) custom-call(bf16[192,1536]{1,0:T(8,128)(2,1)} %bitcast.17, bf16[192,1536]{1,0:T(8,128)(2,1)} %bitcast.18), custom_call_target="tpu_custom_call" | custom-call | flops 1 | bytes 1 | tf_op jit(solution)/shard_map/keys_queries/pallas_call | solution.py:64
  37.7 5.1 %collective-permute-start.3 = (bf16[1152,128]{1,0:T(8,128)(2,1)}, bf16[1152,128]{1,0:T(8,128)(2,1)S(1)}, u32[]{:S(2)}, u32[]{:S(2)}) collective-permute-start(bf16[1152,128]{1,0:T(8,128)(2,1)} %get-tuple-element.77), channel_id=1, source_target_pairs={{0,12},{4,8},{8,4},{12,0},{1,13},{5,9},{9,5},{13,1},{2,14},{6,10},... | collective-permute-start | bytes 884744 | tf_op jit(solution)/shard_map/keys_queries/ppermute | solution.py:397
  45.3 2.0 %collective-permute-done.1 = f32[12,128]{1,0:T(8,128)S(1)} collective-permute-done((f32[12,128]{1,0:T(8,128)S(1)}, f32[12,128]{1,0:T(8,128)S(1)}, u32[]{:S(2)}, u32[]{:S(2)}) %collective-permute-start.1) | collective-permute-done | bytes 6176 | tf_op jit(solution)/shard_map/gain/ppermute | solution.py:397
  50.4 3.3 %collective-permute-done.10.refs_24_.refs_28_.refs_32_.refs_22_.refs_46_ = bf16[576,128]{1,0:T(8,128)(2,1)S(1)} collective-permute-done((bf16[576,128]{1,0:T(8,128)(2,1)S(1)}, bf16[576,128]{1,0:T(8,128)(2,1)S(1)}, u32[]{:S(2)}, u32[]{:S(2)}) %collective-permute-start.10) | collective-permute-done | bytes 147488 | tf_op jit(solution)/shard_map/halo_queries/ppermute | solution.py:464
  53.7 14.5 %collective-permute-done.5.refs_1_.refs_2_.refs_6_.refs_10_.refs_14_.refs_18_.refs_22_.refs_12_.refs_20_.refs_36_.refs_44_ = bf16[1152,128]{1,0:T(8,128)(2,1)S(1)} collective-permute-done((bf16[1152,128]{1,0:T(8,128)(2,1)}, bf16[1152,128]{1,0:T(8,128)(2,1)S(1)}, u32[]{:S(2)}, u32[]{:S(2)}) %collective-permute-start.5) | collective-permute-done | bytes 294944 | tf_op jit(solution)/shard_map/keys_queries/ppermute | solution.py:397
  70.3 2.5 %collective-permute-start.4 = (bf16[832,128]{1,0:T(8,128)(2,1)S(1)}, bf16[832,128]{1,0:T(8,128)(2,1)S(1)}, u32[]{:S(2)}, u32[]{:S(2)}) collective-permute-start(bf16[832,128]{1,0:T(8,128)(2,1)S(1)} %get-tuple-element.78), channel_id=1, source_target_pairs={{0,12},{4,8},{8,4},{12,0},{1,13},{5,9},{9,5},{13,1},{2,14},{6,10},... | collective-permute-start | bytes 638984 | tf_op jit(solution)/shard_map/grads/ppermute | solution.py:397
  72.8 1.9 %collective-permute-start.8 = (bf16[832,128]{1,0:T(8,128)(2,1)S(1)}, bf16[832,128]{1,0:T(8,128)(2,1)S(1)}, u32[]{:S(2)}, u32[]{:S(2)}) collective-permute-start(bf16[832,128]{1,0:T(8,128)(2,1)S(1)} %get-tuple-element.84), channel_id=1, source_target_pairs={{0,4},{4,0},{8,12},{12,8},{1,5},{5,1},{9,13},{13,9},{2,6},{6,2},{1... | collective-permute-start | bytes 638984 | tf_op jit(solution)/shard_map/grads/ppermute | solution.py:397
  75.2 6.7 %collective-permute-done.11.refs_25_.refs_26_.refs_27_.refs_29_.refs_30_.refs_31_.refs_33_.refs_34_.refs_35_.refs_23_.refs_24_.refs_47_.refs_48_.refs_49_ = bf16[1728,128]{1,0:T(8,128)(2,1)S(1)} collective-permute-done((bf16[1728,128]{1,0:T(8,128)(2,1)S(1)}, bf16[1728,128]{1,0:T(8,128)(2,1)S(1)}, u32[]{:S(2)}, u32[]{:S(2)}) %collective-permute-start.11) | collective-permute-done | bytes 442400 | tf_op jit(solution)/shard_map/halo_queries/ppermute | solution.py:464
  81.9 3.6 %totals.1 = (f32[3,768]{1,0:T(4,128)S(1)}, f32[3,768]{1,0:T(4,128)S(1)}) custom-call(bf16[1152,128]{1,0:T(8,128)(2,1)S(1)} %copy-done, bf16[1152,128]{1,0:T(8,128)(2,1)S(1)} %collective-permute-done.3.refs_0_.refs_1_.refs_5_.refs_9_.refs_13_.refs_17_.refs_21_.refs_11_.refs_19_.refs_35_.refs_43_, ...), custom_call_target="tpu_custom_call" | custom-call | flops 905969664 | bytes 2359296 | tf_op jit(solution)/shard_map/totals/pallas_call | solution.py:240
  85.5 3.5 %collective-permute-done.6.refs_2_.refs_16_.refs_28_.refs_52_ = bf16[832,128]{1,0:T(8,128)(2,1)S(1)} collective-permute-done((bf16[832,128]{1,0:T(8,128)(2,1)S(1)}, bf16[832,128]{1,0:T(8,128)(2,1)S(1)}, u32[]{:S(2)}, u32[]{:S(2)}) %collective-permute-start.6) | collective-permute-done | bytes 213024 | tf_op jit(solution)/shard_map/grads/ppermute | solution.py:397
  93.3 2.9 %collective-permute-start.17 = (bf16[384,128]{1,0:T(8,128)(2,1)S(1)}, bf16[384,128]{1,0:T(8,128)(2,1)S(1)}, u32[]{:S(2)}, u32[]{:S(2)}) collective-permute-start(bf16[384,128]{1,0:T(8,128)(2,1)S(1)} %get-tuple-element.111), channel_id=1, source_target_pairs={{0,4},{4,0},{8,12},{12,8},{1,5},{5,1},{9,13},{13,9},{2,6},{6,2},{1... | collective-permute-start | bytes 294920 | tf_op jit(solution)/shard_map/rest_values/ppermute | solution.py:397
  96.2 3.4 %attention_0.1 = (bf16[384,128]{1,0:T(8,128)(2,1)S(1)}, bf16[384,128]{1,0:T(8,128)(2,1)S(1)}, bf16[384,128]{1,0:T(8,128)(2,1)S(1)}, bf16[384,128]{1,0:T(8,128)(2...) custom-call(bf16[832,128]{1,0:T(8,128)(2,1)S(1)} %get-tuple-element.112.refs_0_.refs_14_.refs_26_.refs_50_, ...), custom_call_target="tpu_custom_call" | custom-call | flops 1509949440 | bytes 3145728 | tf_op jit(solution)/shard_map/attention_0/pallas_call | solution.py:325
  103.6 2.2 %collective-permute-start.19 = (bf16[384,128]{1,0:T(8,128)(2,1)S(1)}, bf16[384,128]{1,0:T(8,128)(2,1)S(1)}, u32[]{:S(2)}, u32[]{:S(2)}) collective-permute-start(bf16[384,128]{1,0:T(8,128)(2,1)S(1)} %get-tuple-element.119), channel_id=1, source_target_pairs={{0,12},{4,8},{8,4},{12,0},{1,13},{5,9},{9,5},{13,1},{2,14},{6,10},... | collective-permute-start | bytes 294920 | tf_op jit(solution)/shard_map/returns_0/ppermute | solution.py:397
  105.8 2.2 %collective-permute-start.21 = (bf16[384,128]{1,0:T(8,128)(2,1)S(1)}, bf16[384,128]{1,0:T(8,128)(2,1)S(1)}, u32[]{:S(2)}, u32[]{:S(2)}) collective-permute-start(bf16[384,128]{1,0:T(8,128)(2,1)S(1)} %get-tuple-element.123), channel_id=1, source_target_pairs={{0,4},{4,0},{8,12},{12,8},{1,5},{5,1},{9,13},{13,9},{2,6},{6,2},{1... | collective-permute-start | bytes 294920 | tf_op jit(solution)/shard_map/returns_0/ppermute | solution.py:397
  108.0 3.5 %collective-permute-done.18.refs_31_.refs_32_.refs_33_.refs_55_.refs_56_.refs_57_ = bf16[1152,128]{1,0:T(8,128)(2,1)S(1)} collective-permute-done((bf16[1152,128]{1,0:T(8,128)(2,1)S(1)}, bf16[1152,128]{1,0:T(8,128)(2,1)S(1)}, u32[]{:S(2)}, u32[]{:S(2)}) %collective-permute-start.18) | collective-permute-done | bytes 294944 | tf_op jit(solution)/shard_map/halo_rest_grads/ppermute | solution.py:464
  111.5 6.4 %attention_1.1 = (bf16[768,128]{1,0:T(8,128)(2,1)S(1)}, bf16[768,128]{1,0:T(8,128)(2,1)S(1)}, bf16[768,128]{1,0:T(8,128)(2,1)S(1)}, bf16[768,128]{1,0:T(8,128)(2...) custom-call(bf16[832,128]{1,0:T(8,128)(2,1)S(1)} %get-tuple-element.112.refs_0_.refs_14_.refs_26_.refs_50_, ...), custom_call_target="tpu_custom_call" | custom-call | flops 3019898880 | bytes 6291456 | tf_op jit(solution)/shard_map/attention_1/pallas_call | solution.py:325
  118.6 2.2 %collective-permute-start.23 = (bf16[768,128]{1,0:T(8,128)(2,1)S(1)}, bf16[768,128]{1,0:T(8,128)(2,1)S(1)}, u32[]{:S(2)}, u32[]{:S(2)}) collective-permute-start(bf16[768,128]{1,0:T(8,128)(2,1)S(1)} %get-tuple-element.129), channel_id=1, source_target_pairs={{0,12},{4,8},{8,4},{12,0},{1,13},{5,9},{9,5},{13,1},{2,14},{6,10},... | collective-permute-start | bytes 589832 | tf_op jit(solution)/shard_map/returns_1/ppermute | solution.py:397
  120.8 2.2 %collective-permute-start.27 = (bf16[768,128]{1,0:T(8,128)(2,1)S(1)}, bf16[768,128]{1,0:T(8,128)(2,1)S(1)}, u32[]{:S(2)}, u32[]{:S(2)}) collective-permute-start(bf16[768,128]{1,0:T(8,128)(2,1)S(1)} %get-tuple-element.137), channel_id=1, source_target_pairs={{0,4},{4,0},{8,12},{12,8},{1,5},{5,1},{9,13},{13,9},{2,6},{6,2},{1... | collective-permute-start | bytes 589832 | tf_op jit(solution)/shard_map/returns_1/ppermute | solution.py:397
  123.0 2.9 %collective-permute-done.22.refs_3_ = bf16[1536,128]{1,0:T(8,128)(2,1)S(1)} collective-permute-done((bf16[1536,128]{1,0:T(8,128)(2,1)S(1)}, bf16[1536,128]{1,0:T(8,128)(2,1)S(1)}, u32[]{:S(2)}, u32[]{:S(2)}) %collective-permute-start.22) | collective-permute-done | bytes 393248 | tf_op jit(solution)/shard_map/halo_query_grads_1/ppermute | solution.py:543
  126.0 2.3 %collective-permute-done.23.refs_5_ = bf16[768,128]{1,0:T(8,128)(2,1)S(1)} collective-permute-done((bf16[768,128]{1,0:T(8,128)(2,1)S(1)}, bf16[768,128]{1,0:T(8,128)(2,1)S(1)}, u32[]{:S(2)}, u32[]{:S(2)}) %collective-permute-start.23) | collective-permute-done | bytes 196640 | tf_op jit(solution)/shard_map/returns_1/ppermute | solution.py:397
  128.3 2.1 %collective-permute-start.24 = (bf16[576,128]{1,0:T(8,128)(2,1)S(1)}, bf16[576,128]{1,0:T(8,128)(2,1)S(1)}, u32[]{:S(2)}, u32[]{:S(2)}) collective-permute-start(bf16[576,128]{1,0:T(8,128)(2,1)S(1)} %get-tuple-element.130), channel_id=1, source_target_pairs={{0,12},{4,8},{8,4},{12,0},{1,13},{5,9},{9,5},{13,1},{2,14},{6,10},... | collective-permute-start | bytes 442376 | tf_op jit(solution)/shard_map/returns_last/ppermute | solution.py:397
  130.5 10.7 %collective-permute-done.25.refs_6_ = bf16[768,128]{1,0:T(8,128)(2,1)S(1)} collective-permute-done((bf16[768,128]{1,0:T(8,128)(2,1)S(1)}, bf16[768,128]{1,0:T(8,128)(2,1)S(1)}, u32[]{:S(2)}, u32[]{:S(2)}) %collective-permute-start.25) | collective-permute-done | bytes 196640 | tf_op jit(solution)/shard_map/returns_1/ppermute | solution.py:397
  141.1 3.4 %collective-permute-start.28 = (bf16[576,128]{1,0:T(8,128)(2,1)S(1)}, bf16[576,128]{1,0:T(8,128)(2,1)S(1)}, u32[]{:S(2)}, u32[]{:S(2)}) collective-permute-start(bf16[576,128]{1,0:T(8,128)(2,1)S(1)} %get-tuple-element.138), channel_id=1, source_target_pairs={{0,4},{4,0},{8,12},{12,8},{1,5},{5,1},{9,13},{13,9},{2,6},{6,2},{1... | collective-permute-start | bytes 442376 | tf_op jit(solution)/shard_map/returns_last/ppermute | solution.py:397
  146.3 2.4 %collective-permute-done.26.refs_2_ = bf16[576,128]{1,0:T(8,128)(2,1)S(1)} collective-permute-done((bf16[576,128]{1,0:T(8,128)(2,1)S(1)}, bf16[576,128]{1,0:T(8,128)(2,1)S(1)}, u32[]{:S(2)}, u32[]{:S(2)}) %collective-permute-start.26) | collective-permute-done | bytes 147488 | tf_op jit(solution)/shard_map/returns_last/ppermute | solution.py:397
  (64 shorter events, 20.4 us)
Async XLA Ops:
  37.7 16.0 %collective-permute-start.3 = (bf16[1152,128]{1,0:T(8,128)(2,1)}, bf16[1152,128]{1,0:T(8,128)(2,1)S(1)}, u32[]{:S(2)}, u32[]{:S(2)}) collective-permute-start(bf16[1152,128]{1,0:T(8,128)(2,1)} %get-tuple-element.77), channel_id=1, source_target_pairs={{0,12},{4,8},{8,4},{12,0},{1,13},{5,9},{9,5},{13,1},{2,14},{6,10},... | collective-permute-start | bytes 884744 | tf_op jit(solution)/shard_map/keys_queries/ppermute | solution.py:397
  42.8 25.3 %collective-permute-start.5 = (bf16[1152,128]{1,0:T(8,128)(2,1)}, bf16[1152,128]{1,0:T(8,128)(2,1)S(1)}, u32[]{:S(2)}, u32[]{:S(2)}) collective-permute-start(bf16[1152,128]{1,0:T(8,128)(2,1)} %get-tuple-element.80), channel_id=1, source_target_pairs={{0,8},{4,12},{8,0},{12,4},{1,9},{5,13},{9,1},{13,5},{2,10},{6,14},... | collective-permute-start | bytes 884744 | tf_op jit(solution)/shard_map/keys_queries/ppermute | solution.py:397
  42.8 25.3 %collective-permute-start.7 = (bf16[1152,128]{1,0:T(8,128)(2,1)}, bf16[1152,128]{1,0:T(8,128)(2,1)S(1)}, u32[]{:S(2)}, u32[]{:S(2)}) collective-permute-start(bf16[1152,128]{1,0:T(8,128)(2,1)} %get-tuple-element.83), channel_id=1, source_target_pairs={{0,4},{4,0},{8,12},{12,8},{1,5},{5,1},{9,13},{13,9},{2,6},{6,2},{1... | collective-permute-start | bytes 884744 | tf_op jit(solution)/shard_map/keys_queries/ppermute | solution.py:397
  68.8 13.2 %collective-permute-start.11 = (bf16[1728,128]{1,0:T(8,128)(2,1)S(1)}, bf16[1728,128]{1,0:T(8,128)(2,1)S(1)}, u32[]{:S(2)}, u32[]{:S(2)}) collective-permute-start(bf16[1728,128]{1,0:T(8,128)(2,1)S(1)} %halo_queries.1), channel_id=1, source_target_pairs={{0,16},{16,0},{1,17},{17,1},{2,18},{18,2},{3,19},{19,3},{4,20},{20... | collective-permute-start | bytes 1327112 | tf_op jit(solution)/shard_map/halo_queries/ppermute | solution.py:464
  70.3 15.2 %collective-permute-start.4 = (bf16[832,128]{1,0:T(8,128)(2,1)S(1)}, bf16[832,128]{1,0:T(8,128)(2,1)S(1)}, u32[]{:S(2)}, u32[]{:S(2)}) collective-permute-start(bf16[832,128]{1,0:T(8,128)(2,1)S(1)} %get-tuple-element.78), channel_id=1, source_target_pairs={{0,12},{4,8},{8,4},{12,0},{1,13},{5,9},{9,5},{13,1},{2,14},{6,10},... | collective-permute-start | bytes 638984 | tf_op jit(solution)/shard_map/grads/ppermute | solution.py:397
  72.8 16.3 %collective-permute-start.6 = (bf16[832,128]{1,0:T(8,128)(2,1)S(1)}, bf16[832,128]{1,0:T(8,128)(2,1)S(1)}, u32[]{:S(2)}, u32[]{:S(2)}) collective-permute-start(bf16[832,128]{1,0:T(8,128)(2,1)S(1)} %get-tuple-element.81), channel_id=1, source_target_pairs={{0,8},{4,12},{8,0},{12,4},{1,9},{5,13},{9,1},{13,5},{2,10},{6,14},... | collective-permute-start | bytes 638984 | tf_op jit(solution)/shard_map/grads/ppermute | solution.py:397
  72.8 16.3 %collective-permute-start.8 = (bf16[832,128]{1,0:T(8,128)(2,1)S(1)}, bf16[832,128]{1,0:T(8,128)(2,1)S(1)}, u32[]{:S(2)}, u32[]{:S(2)}) collective-permute-start(bf16[832,128]{1,0:T(8,128)(2,1)S(1)} %get-tuple-element.84), channel_id=1, source_target_pairs={{0,4},{4,0},{8,12},{12,8},{1,5},{5,1},{9,13},{13,9},{2,6},{6,2},{1... | collective-permute-start | bytes 638984 | tf_op jit(solution)/shard_map/grads/ppermute | solution.py:397
  74.7 15.1 %collective-permute-start.9 = (bf16[832,128]{1,0:T(8,128)(2,1)S(1)}, bf16[832,128]{1,0:T(8,128)(2,1)S(1)}, u32[]{:S(2)}, u32[]{:S(2)}) collective-permute-start(bf16[832,128]{1,0:T(8,128)(2,1)S(1)} %get-tuple-element.112.refs_0_.refs_14_.refs_26_.refs_50_), channel_id=1, source_target_pairs={{0,16},{16,0},{1,17},{17,1},{2,18},{18,2},{3,19},{19,3},{4,20},{20... | collective-permute-start | bytes 638984 | tf_op jit(solution)/shard_map/halo_own_grads/ppermute | solution.py:464
  89.1 7.1 %collective-permute-start.13 = (f32[6,768]{1,0:T(8,128)S(1)}, f32[6,768]{1,0:T(8,128)S(1)}, u32[]{:S(2)}, u32[]{:S(2)}) collective-permute-start(f32[6,768]{1,0:T(8,128)S(1)} %pad_maximum_fusion), channel_id=1, source_target_pairs={{0,16},{16,0},{1,17},{17,1},{2,18},{18,2},{3,19},{19,3},{4,20},{20... | collective-permute-start | bytes 55304 | tf_op jit(solution)/shard_map/totals/ppermute | solution.py:441
  91.7 7.8 %collective-permute-start.15 = (bf16[384,128]{1,0:T(8,128)(2,1)S(1)}, bf16[384,128]{1,0:T(8,128)(2,1)S(1)}, u32[]{:S(2)}, u32[]{:S(2)}) collective-permute-start(bf16[384,128]{1,0:T(8,128)(2,1)S(1)} %get-tuple-element.107), channel_id=1, source_target_pairs={{0,12},{4,8},{8,4},{12,0},{1,13},{5,9},{9,5},{13,1},{2,14},{6,10},... | collective-permute-start | bytes 294920 | tf_op jit(solution)/shard_map/rest_values/ppermute | solution.py:397
  93.3 7.6 %collective-permute-start.16 = (bf16[384,128]{1,0:T(8,128)(2,1)S(1)}, bf16[384,128]{1,0:T(8,128)(2,1)S(1)}, u32[]{:S(2)}, u32[]{:S(2)}) collective-permute-start(bf16[384,128]{1,0:T(8,128)(2,1)S(1)} %get-tuple-element.109), channel_id=1, source_target_pairs={{0,8},{4,12},{8,0},{12,4},{1,9},{5,13},{9,1},{13,5},{2,10},{6,14},... | collective-permute-start | bytes 294920 | tf_op jit(solution)/shard_map/rest_values/ppermute | solution.py:397
  93.3 7.6 %collective-permute-start.17 = (bf16[384,128]{1,0:T(8,128)(2,1)S(1)}, bf16[384,128]{1,0:T(8,128)(2,1)S(1)}, u32[]{:S(2)}, u32[]{:S(2)}) collective-permute-start(bf16[384,128]{1,0:T(8,128)(2,1)S(1)} %get-tuple-element.111), channel_id=1, source_target_pairs={{0,4},{4,0},{8,12},{12,8},{1,5},{5,1},{9,13},{13,9},{2,6},{6,2},{1... | collective-permute-start | bytes 294920 | tf_op jit(solution)/shard_map/rest_values/ppermute | solution.py:397
  101.5 10.0 %collective-permute-start.18 = (bf16[1152,128]{1,0:T(8,128)(2,1)S(1)}, bf16[1152,128]{1,0:T(8,128)(2,1)S(1)}, u32[]{:S(2)}, u32[]{:S(2)}) collective-permute-start(bf16[1152,128]{1,0:T(8,128)(2,1)S(1)} %halo_rest_grads.1), channel_id=1, source_target_pairs={{0,16},{16,0},{1,17},{17,1},{2,18},{18,2},{3,19},{19,3},{4,20},{20... | collective-permute-start | bytes 884744 | tf_op jit(solution)/shard_map/halo_rest_grads/ppermute | solution.py:464
  102.1 15.9 %collective-permute-start.14 = (bf16[768,128]{1,0:T(8,128)(2,1)S(1)}, bf16[768,128]{1,0:T(8,128)(2,1)S(1)}, u32[]{:S(2)}, u32[]{:S(2)}) collective-permute-start(bf16[768,128]{1,0:T(8,128)(2,1)S(1)} %get-tuple-element.97), channel_id=1, source_target_pairs={{0,16},{16,0},{1,17},{17,1},{2,18},{18,2},{3,19},{19,3},{4,20},{20... | collective-permute-start | bytes 589832 | tf_op jit(solution)/shard_map/halo_query_grads_0/ppermute | solution.py:543
  103.6 14.4 %collective-permute-start.19 = (bf16[384,128]{1,0:T(8,128)(2,1)S(1)}, bf16[384,128]{1,0:T(8,128)(2,1)S(1)}, u32[]{:S(2)}, u32[]{:S(2)}) collective-permute-start(bf16[384,128]{1,0:T(8,128)(2,1)S(1)} %get-tuple-element.119), channel_id=1, source_target_pairs={{0,12},{4,8},{8,4},{12,0},{1,13},{5,9},{9,5},{13,1},{2,14},{6,10},... | collective-permute-start | bytes 294920 | tf_op jit(solution)/shard_map/returns_0/ppermute | solution.py:397
  105.8 12.2 %collective-permute-start.20 = (bf16[384,128]{1,0:T(8,128)(2,1)S(1)}, bf16[384,128]{1,0:T(8,128)(2,1)S(1)}, u32[]{:S(2)}, u32[]{:S(2)}) collective-permute-start(bf16[384,128]{1,0:T(8,128)(2,1)S(1)} %get-tuple-element.121), channel_id=1, source_target_pairs={{0,8},{4,12},{8,0},{12,4},{1,9},{5,13},{9,1},{13,5},{2,10},{6,14},... | collective-permute-start | bytes 294920 | tf_op jit(solution)/shard_map/returns_0/ppermute | solution.py:397
  105.8 12.2 %collective-permute-start.21 = (bf16[384,128]{1,0:T(8,128)(2,1)S(1)}, bf16[384,128]{1,0:T(8,128)(2,1)S(1)}, u32[]{:S(2)}, u32[]{:S(2)}) collective-permute-start(bf16[384,128]{1,0:T(8,128)(2,1)S(1)} %get-tuple-element.123), channel_id=1, source_target_pairs={{0,4},{4,0},{8,12},{12,8},{1,5},{5,1},{9,13},{13,9},{2,6},{6,2},{1... | collective-permute-start | bytes 294920 | tf_op jit(solution)/shard_map/returns_0/ppermute | solution.py:397
  118.0 7.8 %collective-permute-start.22 = (bf16[1536,128]{1,0:T(8,128)(2,1)S(1)}, bf16[1536,128]{1,0:T(8,128)(2,1)S(1)}, u32[]{:S(2)}, u32[]{:S(2)}) collective-permute-start(bf16[1536,128]{1,0:T(8,128)(2,1)S(1)} %get-tuple-element.125), channel_id=1, source_target_pairs={{0,16},{16,0},{1,17},{17,1},{2,18},{18,2},{3,19},{19,3},{4,20},{20... | collective-permute-start | bytes 1179656 | tf_op jit(solution)/shard_map/halo_query_grads_1/ppermute | solution.py:543
  118.6 9.7 %collective-permute-start.23 = (bf16[768,128]{1,0:T(8,128)(2,1)S(1)}, bf16[768,128]{1,0:T(8,128)(2,1)S(1)}, u32[]{:S(2)}, u32[]{:S(2)}) collective-permute-start(bf16[768,128]{1,0:T(8,128)(2,1)S(1)} %get-tuple-element.129), channel_id=1, source_target_pairs={{0,12},{4,8},{8,4},{12,0},{1,13},{5,9},{9,5},{13,1},{2,14},{6,10},... | collective-permute-start | bytes 589832 | tf_op jit(solution)/shard_map/returns_1/ppermute | solution.py:397
  120.8 20.3 %collective-permute-start.25 = (bf16[768,128]{1,0:T(8,128)(2,1)S(1)}, bf16[768,128]{1,0:T(8,128)(2,1)S(1)}, u32[]{:S(2)}, u32[]{:S(2)}) collective-permute-start(bf16[768,128]{1,0:T(8,128)(2,1)S(1)} %get-tuple-element.133), channel_id=1, source_target_pairs={{0,8},{4,12},{8,0},{12,4},{1,9},{5,13},{9,1},{13,5},{2,10},{6,14},... | collective-permute-start | bytes 589832 | tf_op jit(solution)/shard_map/returns_1/ppermute | solution.py:397
  120.8 20.3 %collective-permute-start.27 = (bf16[768,128]{1,0:T(8,128)(2,1)S(1)}, bf16[768,128]{1,0:T(8,128)(2,1)S(1)}, u32[]{:S(2)}, u32[]{:S(2)}) collective-permute-start(bf16[768,128]{1,0:T(8,128)(2,1)S(1)} %get-tuple-element.137), channel_id=1, source_target_pairs={{0,4},{4,0},{8,12},{12,8},{1,5},{5,1},{9,13},{13,9},{2,6},{6,2},{1... | collective-permute-start | bytes 589832 | tf_op jit(solution)/shard_map/returns_1/ppermute | solution.py:397
  128.3 18.0 %collective-permute-start.24 = (bf16[576,128]{1,0:T(8,128)(2,1)S(1)}, bf16[576,128]{1,0:T(8,128)(2,1)S(1)}, u32[]{:S(2)}, u32[]{:S(2)}) collective-permute-start(bf16[576,128]{1,0:T(8,128)(2,1)S(1)} %get-tuple-element.130), channel_id=1, source_target_pairs={{0,12},{4,8},{8,4},{12,0},{1,13},{5,9},{9,5},{13,1},{2,14},{6,10},... | collective-permute-start | bytes 442376 | tf_op jit(solution)/shard_map/returns_last/ppermute | solution.py:397
  141.1 7.6 %collective-permute-start.26 = (bf16[576,128]{1,0:T(8,128)(2,1)S(1)}, bf16[576,128]{1,0:T(8,128)(2,1)S(1)}, u32[]{:S(2)}, u32[]{:S(2)}) collective-permute-start(bf16[576,128]{1,0:T(8,128)(2,1)S(1)} %get-tuple-element.134), channel_id=1, source_target_pairs={{0,8},{4,12},{8,0},{12,4},{1,9},{5,13},{9,1},{13,5},{2,10},{6,14},... | collective-permute-start | bytes 442376 | tf_op jit(solution)/shard_map/returns_last/ppermute | solution.py:397
  141.1 8.0 %collective-permute-start.28 = (bf16[576,128]{1,0:T(8,128)(2,1)S(1)}, bf16[576,128]{1,0:T(8,128)(2,1)S(1)}, u32[]{:S(2)}, u32[]{:S(2)}) collective-permute-start(bf16[576,128]{1,0:T(8,128)(2,1)S(1)} %get-tuple-element.138), channel_id=1, source_target_pairs={{0,4},{4,0},{8,12},{12,8},{1,5},{5,1},{9,13},{13,9},{2,6},{6,2},{1... | collective-permute-start | bytes 442376 | tf_op jit(solution)/shard_map/returns_last/ppermute | solution.py:397
  (10 other events, 120.4 us)

commit v11 on v10

--- a/solution.py
+++ b/solution.py
@@ -14,7 +14,6 @@
 KEY_BLOCK = 256
 QUERY_BLOCK = 256
 VMEM_LIMIT = 48 * 1024 * 1024
-VMEM_WHOLE = 62 * 1024 * 1024
 SCALE = 1.0 / math.sqrt(HD)
 SCALE_LOG2 = SCALE / math.log(2.0)
 COST = pl.CostEstimate(flops=1, bytes_accessed=1, transcendentals=0)
@@ -57,7 +56,7 @@
     run_copies(pairs, semaphores)
 
 
-def pack(sources, parts, chosen, limit=VMEM_LIMIT):
+def pack(sources, parts, chosen):
     rows = sources[0].shape[0]
     depth = len(sources) * len(chosen) * rows
     whole = pl.BlockSpec(memory_space=pl.ANY)
@@ -67,7 +66,7 @@
         out_specs=[whole] * parts,
         out_shape=[jax.ShapeDtypeStruct((depth, HD), sources[0].dtype)] * parts,
         scratch_shapes=[pltpu.SemaphoreType.DMA((len(sources) * len(chosen) * parts,))],
-        compiler_params=pltpu.CompilerParams(vmem_limit_bytes=limit),
+        compiler_params=params(),
         cost_estimate=COST,
     )(*sources)
 
@@ -464,7 +463,7 @@
         return [lax.ppermute(array, "tm", there) for there, _ in sides]
 
     with jax.named_scope("keys_queries"):
-        packed = pack([keys[0], queries[0]], parts, list(range(heads)), VMEM_WHOLE)
+        packed = pack([keys[0], queries[0]], parts, list(range(heads)))
         pairs = swap_pieces(packed)
     paired = span == 2
     with jax.named_scope("gain"):
@@ -483,17 +482,20 @@
     with jax.named_scope("grads"):
         lead = swap_pieces(sent_lead, pairs)
     with jax.named_scope("halo_queries"):
-        late = after(pairs[1:], first_side, sent_lead[0])
-        late_side = forward(gather_rows(late, [(number, width, width) for number in range(parts - 1)]))
+        early_side = forward(pairs[1][width:])
+        late = after(pairs[2:], first_side, early_side, sent_lead[0])
+        late_side = forward(gather_rows(late, [(number, width, width) for number in range(parts - 2)]))
     base = (heads + 1) * rows
     extra = gain_depth(channels)
+    with jax.named_scope("halo_own_grads"):
+        own_side = forward(sent_lead[0])
     with jax.named_scope("totals"):
         key_places = [[(piece, head) for piece in pairs] for head in range(heads)]
         query_places = [[[(piece, heads + head) for piece in pairs] for head in range(heads)]]
-        for first, others in zip(first_side, late_side):
+        for first, second, array in zip(first_side, early_side, late_side):
             query_places.append(
                 [
-                    [(first, head)] + [(others, (part - 1) * heads + head) for part in every[1:]]
+                    [(first, head), (second, head)] + [(array, part * heads + head) for part in range(parts - 2)]
                     for head in range(heads)
                 ]
             )

time: 150 us -> 121 us (0.81)
  Pallas kernels: 55.6 us -> 19.3 us
  starting transfers between devices: 39 us -> 42.5 us
  local copies, waits for them, and re-layouts: 0.04 us -> 2.86 us
    pallas_call x2, Pallas kernels: 37.2 us -> 1.15 us  [pack(): pl.pallas_call(functools.partial(pack_kernel, parts, chosen), in_specs=[w...]
    ppermute x5 -> x6, waiting for transfers between devices: 13.5 us -> 7.9 us  [forward(): return [lax.ppermute(array, 'tm', there) for there, _ in sides]]
    ppermute x21, waiting for transfers between devices: 38.2 us -> 43 us  [swap(): lax.ppermute(value, axis, [(index, index ^ distance) for index in range(l...]
    ppermute x21, starting transfers between devices: 30.5 us -> 33.5 us  [swap(): lax.ppermute(value, axis, [(index, index ^ distance) for index in range(l...]
    unnamed x10, local copies, waits for them, and re-layouts: 0.02 us -> 2.13 us
    ppermute x5 -> x6, starting transfers between devices: 5.74 us -> 6.34 us  [forward(): return [lax.ppermute(array, 'tm', there) for there, _ in sides]]
  transfers between devices with their start and end apart: 29 -> 30, of which waited for: 13 -> 12; matrix products, arithmetic and copies ran while one was open for 0% -> 1% of each run, Pallas kernels for 11% -> 14%
where the time goes in v11:
time: 121 us; the launch traced here: 120 us
  waiting for transfers between devices  54.7 us (45%)
  starting transfers between devices  42.5 us (35%)
  Pallas kernels  19.3 us (16%)
  local copies, waits for them, and re-layouts  2.86 us (2%)
    ppermute x21, waiting for transfers between devices, swap(): lax.ppermute(value, axis, [(index, index ^ distance) for index in range(l...  43 us
    ppermute x21, starting transfers between devices, swap(): lax.ppermute(value, axis, [(index, index ^ distance) for index in range(l...  33.5 us
    pallas_call x2, Pallas kernels, attention(): pl.pallas_call(functools.partial(attention_kernel, parts, sources, chosen...  9.77 us
    ppermute x6, waiting for transfers between devices, forward(): return [lax.ppermute(array, 'tm', there) for there, _ in sides]  7.9 us
    ppermute x6, starting transfers between devices, forward(): return [lax.ppermute(array, 'tm', there) for there, _ in sides]  6.34 us
    ppermute x2, waiting for transfers between devices, local(): lax.ppermute(other, 'tm', back)  3.8 us
    pallas_call x1, Pallas kernels, partial_totals(): pl.pallas_call(functools.partial(totals_kernel, parts, sources, heads), g...  3.6 us
  transfers between devices with their start and end apart: 30, of which 12 were waited for; matrix products, arithmetic and copies ran while one was open for 1% of the time, Pallas kernels for 14%

profile of v11, /device:TPU:0, one launch (start us, length us, event | category | flops | bytes accessed | tf_op | source)
XLA Modules:
  0.0 120.5 jit_solution(10296996466076551755)
XLA Ops:
  3.8 5.1 %collective-permute-start.3 = (bf16[1152,128]{1,0:T(8,128)(2,1)}, bf16[1152,128]{1,0:T(8,128)(2,1)S(1)}, u32[]{:S(2)}, u32[]{:S(2)}) collective-permute-start(bf16[1152,128]{1,0:T(8,128)(2,1)} %get-tuple-element.76), channel_id=1, source_target_pairs={{0,12},{4,8},{8,4},{12,0},{1,13},{5,9},{9,5},{13,1},{2,14},{6,10},... | collective-permute-start | bytes 884744 | tf_op jit(solution)/shard_map/keys_queries/ppermute | solution.py:396
  11.4 5.7 %collective-permute-done.3.refs_1_.refs_5_.refs_9_.refs_13_.refs_17_.refs_21_.refs_11_.refs_19_.refs_35_.refs_43_ = bf16[1152,128]{1,0:T(8,128)(2,1)S(1)} collective-permute-done((bf16[1152,128]{1,0:T(8,128)(2,1)}, bf16[1152,128]{1,0:T(8,128)(2,1)S(1)}, u32[]{:S(2)}, u32[]{:S(2)}) %collective-permute-start.3) | collective-permute-done | bytes 294944 | tf_op jit(solution)/shard_map/keys_queries/ppermute | solution.py:396
  17.8 1.8 %collective-permute-start.10 = (bf16[576,128]{1,0:T(8,128)(2,1)S(1)}, bf16[576,128]{1,0:T(8,128)(2,1)S(1)}, u32[]{:S(2)}, u32[]{:S(2)}) collective-permute-start(bf16[576,128]{1,0:T(8,128)(2,1)S(1)} %slice.12), channel_id=1, source_target_pairs={{0,16},{16,0},{1,17},{17,1},{2,18},{18,2},{3,19},{19,3},{4,20},{20... | collective-permute-start | bytes 442376 | tf_op jit(solution)/shard_map/halo_queries/ppermute | solution.py:463
  20.4 4.1 %collective-permute-done.10.refs_24_.refs_28_.refs_32_.refs_22_.refs_46_ = bf16[576,128]{1,0:T(8,128)(2,1)S(1)} collective-permute-done((bf16[576,128]{1,0:T(8,128)(2,1)S(1)}, bf16[576,128]{1,0:T(8,128)(2,1)S(1)}, u32[]{:S(2)}, u32[]{:S(2)}) %collective-permute-start.10) | collective-permute-done | bytes 147488 | tf_op jit(solution)/shard_map/halo_queries/ppermute | solution.py:463
  24.5 9.7 %collective-permute-done.5.refs_0_.refs_2_.refs_6_.refs_10_.refs_14_.refs_18_.refs_22_.refs_12_.refs_20_.refs_36_.refs_44_ = bf16[1152,128]{1,0:T(8,128)(2,1)S(1)} collective-permute-done((bf16[1152,128]{1,0:T(8,128)(2,1)S(1)}, bf16[1152,128]{1,0:T(8,128)(2,1)S(1)}, u32[]{:S(2)}, u32[]{:S(2)}) %collective-permute-start.5) | collective-permute-done | bytes 294944 | tf_op jit(solution)/shard_map/keys_queries/ppermute | solution.py:396
  36.2 2.5 %collective-permute-start.4 = (bf16[832,128]{1,0:T(8,128)(2,1)S(1)}, bf16[832,128]{1,0:T(8,128)(2,1)S(1)}, u32[]{:S(2)}, u32[]{:S(2)}) collective-permute-start(bf16[832,128]{1,0:T(8,128)(2,1)S(1)} %get-tuple-element.77), channel_id=1, source_target_pairs={{0,12},{4,8},{8,4},{12,0},{1,13},{5,9},{9,5},{13,1},{2,14},{6,10},... | collective-permute-start | bytes 638984 | tf_op jit(solution)/shard_map/grads/ppermute | solution.py:396
  38.6 4.4 %collective-permute-start.6 = (bf16[832,128]{1,0:T(8,128)(2,1)S(1)}, bf16[832,128]{1,0:T(8,128)(2,1)S(1)}, u32[]{:S(2)}, u32[]{:S(2)}) collective-permute-start(bf16[832,128]{1,0:T(8,128)(2,1)S(1)} %get-tuple-element.80), channel_id=1, source_target_pairs={{0,8},{4,12},{8,0},{12,4},{1,9},{5,13},{9,1},{13,5},{2,10},{6,14},... | collective-permute-start | bytes 638984 | tf_op jit(solution)/shard_map/grads/ppermute | solution.py:396
  43.9 3.6 %totals.1 = (f32[3,768]{1,0:T(4,128)S(1)}, f32[3,768]{1,0:T(4,128)S(1)}) custom-call(bf16[1152,128]{1,0:T(8,128)(2,1)S(1)} %get-tuple-element.72.refs_0_.refs_4_.refs_8_.refs_12_.refs_16_.refs_20_.refs_10_.refs_18_.refs_34_.refs_42_, ...), custom_call_target="tpu_custom_call" | custom-call | flops 905969664 | bytes 2359296 | tf_op jit(solution)/shard_map/totals/pallas_call | solution.py:239
  47.5 10.2 %collective-permute-done.6.refs_2_.refs_16_.refs_28_.refs_52_ = bf16[832,128]{1,0:T(8,128)(2,1)S(1)} collective-permute-done((bf16[832,128]{1,0:T(8,128)(2,1)S(1)}, bf16[832,128]{1,0:T(8,128)(2,1)S(1)}, u32[]{:S(2)}, u32[]{:S(2)}) %collective-permute-start.6) | collective-permute-done | bytes 213024 | tf_op jit(solution)/shard_map/grads/ppermute | solution.py:396
  60.4 2.3 %collective-permute-start.16 = (bf16[384,128]{1,0:T(8,128)(2,1)S(1)}, bf16[384,128]{1,0:T(8,128)(2,1)S(1)}, u32[]{:S(2)}, u32[]{:S(2)}) collective-permute-start(bf16[384,128]{1,0:T(8,128)(2,1)S(1)} %get-tuple-element.105), channel_id=1, source_target_pairs={{0,12},{4,8},{8,4},{12,0},{1,13},{5,9},{9,5},{13,1},{2,14},{6,10},... | collective-permute-start | bytes 294920 | tf_op jit(solution)/shard_map/rest_values/ppermute | solution.py:396
  62.7 2.1 %collective-permute-start.18 = (bf16[384,128]{1,0:T(8,128)(2,1)S(1)}, bf16[384,128]{1,0:T(8,128)(2,1)S(1)}, u32[]{:S(2)}, u32[]{:S(2)}) collective-permute-start(bf16[384,128]{1,0:T(8,128)(2,1)S(1)} %get-tuple-element.109), channel_id=1, source_target_pairs={{0,4},{4,0},{8,12},{12,8},{1,5},{5,1},{9,13},{13,9},{2,6},{6,2},{1... | collective-permute-start | bytes 294920 | tf_op jit(solution)/shard_map/rest_values/ppermute | solution.py:396
  65.1 3.3 %attention_0.1 = (bf16[384,128]{1,0:T(8,128)(2,1)S(1)}, bf16[384,128]{1,0:T(8,128)(2,1)S(1)}, bf16[384,128]{1,0:T(8,128)(2,1)S(1)}, bf16[384,128]{1,0:T(8,128)(2...) custom-call(bf16[832,128]{1,0:T(8,128)(2,1)S(1)} %get-tuple-element.110.refs_0_.refs_14_.refs_26_.refs_50_, ...), custom_call_target="tpu_custom_call" | custom-call | flops 1509949440 | bytes 3145728 | tf_op jit(solution)/shard_map/attention_0/pallas_call | solution.py:324
  68.5 1.7 %collective-permute-done.17.refs_16_.refs_40_ = bf16[384,128]{1,0:T(8,128)(2,1)S(1)} collective-permute-done((bf16[384,128]{1,0:T(8,128)(2,1)S(1)}, bf16[384,128]{1,0:T(8,128)(2,1)S(1)}, u32[]{:S(2)}, u32[]{:S(2)}) %collective-permute-start.17) | collective-permute-done | bytes 98336 | tf_op jit(solution)/shard_map/rest_values/ppermute | solution.py:396
  72.9 2.3 %collective-permute-start.20 = (bf16[384,128]{1,0:T(8,128)(2,1)S(1)}, bf16[384,128]{1,0:T(8,128)(2,1)S(1)}, u32[]{:S(2)}, u32[]{:S(2)}) collective-permute-start(bf16[384,128]{1,0:T(8,128)(2,1)S(1)} %get-tuple-element.117), channel_id=1, source_target_pairs={{0,12},{4,8},{8,4},{12,0},{1,13},{5,9},{9,5},{13,1},{2,14},{6,10},... | collective-permute-start | bytes 294920 | tf_op jit(solution)/shard_map/returns_0/ppermute | solution.py:396
  75.2 2.1 %collective-permute-start.22 = (bf16[384,128]{1,0:T(8,128)(2,1)S(1)}, bf16[384,128]{1,0:T(8,128)(2,1)S(1)}, u32[]{:S(2)}, u32[]{:S(2)}) collective-permute-start(bf16[384,128]{1,0:T(8,128)(2,1)S(1)} %get-tuple-element.121), channel_id=1, source_target_pairs={{0,4},{4,0},{8,12},{12,8},{1,5},{5,1},{9,13},{13,9},{2,6},{6,2},{1... | collective-permute-start | bytes 294920 | tf_op jit(solution)/shard_map/returns_0/ppermute | solution.py:396
  77.3 3.5 %collective-permute-done.19.refs_31_.refs_32_.refs_33_.refs_55_.refs_56_.refs_57_ = bf16[1152,128]{1,0:T(8,128)(2,1)S(1)} collective-permute-done((bf16[1152,128]{1,0:T(8,128)(2,1)S(1)}, bf16[1152,128]{1,0:T(8,128)(2,1)S(1)}, u32[]{:S(2)}, u32[]{:S(2)}) %collective-permute-start.19) | collective-permute-done | bytes 294944 | tf_op jit(solution)/shard_map/halo_rest_grads/ppermute | solution.py:463
  80.8 6.4 %attention_1.1 = (bf16[768,128]{1,0:T(8,128)(2,1)S(1)}, bf16[768,128]{1,0:T(8,128)(2,1)S(1)}, bf16[768,128]{1,0:T(8,128)(2,1)S(1)}, bf16[768,128]{1,0:T(8,128)(2...) custom-call(bf16[832,128]{1,0:T(8,128)(2,1)S(1)} %get-tuple-element.110.refs_0_.refs_14_.refs_26_.refs_50_, ...), custom_call_target="tpu_custom_call" | custom-call | flops 3019898880 | bytes 6291456 | tf_op jit(solution)/shard_map/attention_1/pallas_call | solution.py:324
  87.9 2.3 %collective-permute-start.24 = (bf16[768,128]{1,0:T(8,128)(2,1)S(1)}, bf16[768,128]{1,0:T(8,128)(2,1)S(1)}, u32[]{:S(2)}, u32[]{:S(2)}) collective-permute-start(bf16[768,128]{1,0:T(8,128)(2,1)S(1)} %get-tuple-element.127), channel_id=1, source_target_pairs={{0,12},{4,8},{8,4},{12,0},{1,13},{5,9},{9,5},{13,1},{2,14},{6,10},... | collective-permute-start | bytes 589832 | tf_op jit(solution)/shard_map/returns_1/ppermute | solution.py:396
  90.1 2.1 %collective-permute-start.28 = (bf16[768,128]{1,0:T(8,128)(2,1)S(1)}, bf16[768,128]{1,0:T(8,128)(2,1)S(1)}, u32[]{:S(2)}, u32[]{:S(2)}) collective-permute-start(bf16[768,128]{1,0:T(8,128)(2,1)S(1)} %get-tuple-element.135), channel_id=1, source_target_pairs={{0,4},{4,0},{8,12},{12,8},{1,5},{5,1},{9,13},{13,9},{2,6},{6,2},{1... | collective-permute-start | bytes 589832 | tf_op jit(solution)/shard_map/returns_1/ppermute | solution.py:396
  92.3 3.8 %collective-permute-done.23.refs_3_ = bf16[1536,128]{1,0:T(8,128)(2,1)S(1)} collective-permute-done((bf16[1536,128]{1,0:T(8,128)(2,1)S(1)}, bf16[1536,128]{1,0:T(8,128)(2,1)S(1)}, u32[]{:S(2)}, u32[]{:S(2)}) %collective-permute-start.23) | collective-permute-done | bytes 393248 | tf_op jit(solution)/shard_map/halo_query_grads_1/ppermute | solution.py:545
  97.5 2.3 %collective-permute-start.25 = (bf16[576,128]{1,0:T(8,128)(2,1)S(1)}, bf16[576,128]{1,0:T(8,128)(2,1)S(1)}, u32[]{:S(2)}, u32[]{:S(2)}) collective-permute-start(bf16[576,128]{1,0:T(8,128)(2,1)S(1)} %get-tuple-element.128), channel_id=1, source_target_pairs={{0,12},{4,8},{8,4},{12,0},{1,13},{5,9},{9,5},{13,1},{2,14},{6,10},... | collective-permute-start | bytes 442376 | tf_op jit(solution)/shard_map/returns_last/ppermute | solution.py:396
  99.8 11.5 %collective-permute-done.26.refs_6_ = bf16[768,128]{1,0:T(8,128)(2,1)S(1)} collective-permute-done((bf16[768,128]{1,0:T(8,128)(2,1)S(1)}, bf16[768,128]{1,0:T(8,128)(2,1)S(1)}, u32[]{:S(2)}, u32[]{:S(2)}) %collective-permute-start.26) | collective-permute-done | bytes 196640 | tf_op jit(solution)/shard_map/returns_1/ppermute | solution.py:396
  111.3 3.4 %collective-permute-start.29 = (bf16[576,128]{1,0:T(8,128)(2,1)S(1)}, bf16[576,128]{1,0:T(8,128)(2,1)S(1)}, u32[]{:S(2)}, u32[]{:S(2)}) collective-permute-start(bf16[576,128]{1,0:T(8,128)(2,1)S(1)} %get-tuple-element.136), channel_id=1, source_target_pairs={{0,4},{4,0},{8,12},{12,8},{1,5},{5,1},{9,13},{13,9},{2,6},{6,2},{1... | collective-permute-start | bytes 442376 | tf_op jit(solution)/shard_map/returns_last/ppermute | solution.py:396
  116.6 2.4 %collective-permute-done.27.refs_2_ = bf16[576,128]{1,0:T(8,128)(2,1)S(1)} collective-permute-done((bf16[576,128]{1,0:T(8,128)(2,1)S(1)}, bf16[576,128]{1,0:T(8,128)(2,1)S(1)}, u32[]{:S(2)}, u32[]{:S(2)}) %collective-permute-start.27) | collective-permute-done | bytes 147488 | tf_op jit(solution)/shard_map/returns_last/ppermute | solution.py:396
  (67 shorter events, 20.9 us)
Async XLA Ops:
  3.8 13.3 %collective-permute-start.3 = (bf16[1152,128]{1,0:T(8,128)(2,1)}, bf16[1152,128]{1,0:T(8,128)(2,1)S(1)}, u32[]{:S(2)}, u32[]{:S(2)}) collective-permute-start(bf16[1152,128]{1,0:T(8,128)(2,1)} %get-tuple-element.76), channel_id=1, source_target_pairs={{0,12},{4,8},{8,4},{12,0},{1,13},{5,9},{9,5},{13,1},{2,14},{6,10},... | collective-permute-start | bytes 884744 | tf_op jit(solution)/shard_map/keys_queries/ppermute | solution.py:396
  8.9 25.3 %collective-permute-start.5 = (bf16[1152,128]{1,0:T(8,128)(2,1)S(1)}, bf16[1152,128]{1,0:T(8,128)(2,1)S(1)}, u32[]{:S(2)}, u32[]{:S(2)}) collective-permute-start(bf16[1152,128]{1,0:T(8,128)(2,1)S(1)} %get-tuple-element.79), channel_id=1, source_target_pairs={{0,8},{4,12},{8,0},{12,4},{1,9},{5,13},{9,1},{13,5},{2,10},{6,14},... | collective-permute-start | bytes 884744 | tf_op jit(solution)/shard_map/keys_queries/ppermute | solution.py:396
  8.9 25.3 %collective-permute-start.7 = (bf16[1152,128]{1,0:T(8,128)(2,1)S(1)}, bf16[1152,128]{1,0:T(8,128)(2,1)S(1)}, u32[]{:S(2)}, u32[]{:S(2)}) collective-permute-start(bf16[1152,128]{1,0:T(8,128)(2,1)S(1)} %get-tuple-element.82), channel_id=1, source_target_pairs={{0,4},{4,0},{8,12},{12,8},{1,5},{5,1},{9,13},{13,9},{2,6},{6,2},{1... | collective-permute-start | bytes 884744 | tf_op jit(solution)/shard_map/keys_queries/ppermute | solution.py:396
  9.6 8.2 %collective-permute-start.1 = (f32[12,128]{1,0:T(8,128)S(1)}, f32[12,128]{1,0:T(8,128)S(1)}, u32[]{:S(2)}, u32[]{:S(2)}) collective-permute-start(f32[12,128]{1,0:T(8,128)S(1)} %bitcast.20), channel_id=1, source_target_pairs={{0,2},{1,3},{2,0},{3,1},{4,6},{5,7},{6,4},{7,5},{8,10},{9,11},{10,... | collective-permute-start | bytes 18440 | tf_op jit(solution)/shard_map/gain/ppermute | solution.py:396
  11.4 8.2 %collective-permute-start.2 = (f32[12,128]{1,0:T(8,128)S(1)}, f32[12,128]{1,0:T(8,128)S(1)}, u32[]{:S(2)}, u32[]{:S(2)}) collective-permute-start(f32[12,128]{1,0:T(8,128)S(1)} %bitcast.21), channel_id=1, source_target_pairs={{0,3},{1,2},{2,1},{3,0},{4,7},{5,6},{6,5},{7,4},{8,11},{9,10},{10,... | collective-permute-start | bytes 18440 | tf_op jit(solution)/shard_map/gain/ppermute | solution.py:396
  19.6 14.6 %collective-permute-start.11 = (bf16[576,128]{1,0:T(8,128)(2,1)S(1)}, bf16[576,128]{1,0:T(8,128)(2,1)S(1)}, u32[]{:S(2)}, u32[]{:S(2)}) collective-permute-start(bf16[576,128]{1,0:T(8,128)(2,1)S(1)} %slice.16), channel_id=1, source_target_pairs={{0,16},{16,0},{1,17},{17,1},{2,18},{18,2},{3,19},{19,3},{4,20},{20... | collective-permute-start | bytes 442376 | tf_op jit(solution)/shard_map/halo_queries/ppermute | solution.py:463
  34.6 9.3 %collective-permute-start.12 = (bf16[1152,128]{1,0:T(8,128)(2,1)S(1)}, bf16[1152,128]{1,0:T(8,128)(2,1)S(1)}, u32[]{:S(2)}, u32[]{:S(2)}) collective-permute-start(bf16[1152,128]{1,0:T(8,128)(2,1)S(1)} %halo_queries.1), channel_id=1, source_target_pairs={{0,16},{16,0},{1,17},{17,1},{2,18},{18,2},{3,19},{19,3},{4,20},{20... | collective-permute-start | bytes 884744 | tf_op jit(solution)/shard_map/halo_queries/ppermute | solution.py:463
  36.2 11.3 %collective-permute-start.4 = (bf16[832,128]{1,0:T(8,128)(2,1)S(1)}, bf16[832,128]{1,0:T(8,128)(2,1)S(1)}, u32[]{:S(2)}, u32[]{:S(2)}) collective-permute-start(bf16[832,128]{1,0:T(8,128)(2,1)S(1)} %get-tuple-element.77), channel_id=1, source_target_pairs={{0,12},{4,8},{8,4},{12,0},{1,13},{5,9},{9,5},{13,1},{2,14},{6,10},... | collective-permute-start | bytes 638984 | tf_op jit(solution)/shard_map/grads/ppermute | solution.py:396
  38.6 19.0 %collective-permute-start.6 = (bf16[832,128]{1,0:T(8,128)(2,1)S(1)}, bf16[832,128]{1,0:T(8,128)(2,1)S(1)}, u32[]{:S(2)}, u32[]{:S(2)}) collective-permute-start(bf16[832,128]{1,0:T(8,128)(2,1)S(1)} %get-tuple-element.80), channel_id=1, source_target_pairs={{0,8},{4,12},{8,0},{12,4},{1,9},{5,13},{9,1},{13,5},{2,10},{6,14},... | collective-permute-start | bytes 638984 | tf_op jit(solution)/shard_map/grads/ppermute | solution.py:396
  43.0 14.7 %collective-permute-start.8 = (bf16[832,128]{1,0:T(8,128)(2,1)S(1)}, bf16[832,128]{1,0:T(8,128)(2,1)S(1)}, u32[]{:S(2)}, u32[]{:S(2)}) collective-permute-start(bf16[832,128]{1,0:T(8,128)(2,1)S(1)} %get-tuple-element.83), channel_id=1, source_target_pairs={{0,4},{4,0},{8,12},{12,8},{1,5},{5,1},{9,13},{13,9},{2,6},{6,2},{1... | collective-permute-start | bytes 638984 | tf_op jit(solution)/shard_map/grads/ppermute | solution.py:396
  43.3 15.1 %collective-permute-start.9 = (bf16[832,128]{1,0:T(8,128)(2,1)S(1)}, bf16[832,128]{1,0:T(8,128)(2,1)S(1)}, u32[]{:S(2)}, u32[]{:S(2)}) collective-permute-start(bf16[832,128]{1,0:T(8,128)(2,1)S(1)} %get-tuple-element.110.refs_0_.refs_14_.refs_26_.refs_50_), channel_id=1, source_target_pairs={{0,16},{16,0},{1,17},{17,1},{2,18},{18,2},{3,19},{19,3},{4,20},{20... | collective-permute-start | bytes 638984 | tf_op jit(solution)/shard_map/halo_own_grads/ppermute | solution.py:463
  60.4 8.1 %collective-permute-start.16 = (bf16[384,128]{1,0:T(8,128)(2,1)S(1)}, bf16[384,128]{1,0:T(8,128)(2,1)S(1)}, u32[]{:S(2)}, u32[]{:S(2)}) collective-permute-start(bf16[384,128]{1,0:T(8,128)(2,1)S(1)} %get-tuple-element.105), channel_id=1, source_target_pairs={{0,12},{4,8},{8,4},{12,0},{1,13},{5,9},{9,5},{13,1},{2,14},{6,10},... | collective-permute-start | bytes 294920 | tf_op jit(solution)/shard_map/rest_values/ppermute | solution.py:396
  70.8 10.0 %collective-permute-start.19 = (bf16[1152,128]{1,0:T(8,128)(2,1)S(1)}, bf16[1152,128]{1,0:T(8,128)(2,1)S(1)}, u32[]{:S(2)}, u32[]{:S(2)}) collective-permute-start(bf16[1152,128]{1,0:T(8,128)(2,1)S(1)} %halo_rest_grads.1), channel_id=1, source_target_pairs={{0,16},{16,0},{1,17},{17,1},{2,18},{18,2},{3,19},{19,3},{4,20},{20... | collective-permute-start | bytes 884744 | tf_op jit(solution)/shard_map/halo_rest_grads/ppermute | solution.py:463
  71.4 15.8 %collective-permute-start.15 = (bf16[768,128]{1,0:T(8,128)(2,1)S(1)}, bf16[768,128]{1,0:T(8,128)(2,1)S(1)}, u32[]{:S(2)}, u32[]{:S(2)}) collective-permute-start(bf16[768,128]{1,0:T(8,128)(2,1)S(1)} %get-tuple-element.95), channel_id=1, source_target_pairs={{0,16},{16,0},{1,17},{17,1},{2,18},{18,2},{3,19},{19,3},{4,20},{20... | collective-permute-start | bytes 589832 | tf_op jit(solution)/shard_map/halo_query_grads_0/ppermute | solution.py:545
  72.9 14.3 %collective-permute-start.20 = (bf16[384,128]{1,0:T(8,128)(2,1)S(1)}, bf16[384,128]{1,0:T(8,128)(2,1)S(1)}, u32[]{:S(2)}, u32[]{:S(2)}) collective-permute-start(bf16[384,128]{1,0:T(8,128)(2,1)S(1)} %get-tuple-element.117), channel_id=1, source_target_pairs={{0,12},{4,8},{8,4},{12,0},{1,13},{5,9},{9,5},{13,1},{2,14},{6,10},... | collective-permute-start | bytes 294920 | tf_op jit(solution)/shard_map/returns_0/ppermute | solution.py:396
  75.2 12.0 %collective-permute-start.21 = (bf16[384,128]{1,0:T(8,128)(2,1)S(1)}, bf16[384,128]{1,0:T(8,128)(2,1)S(1)}, u32[]{:S(2)}, u32[]{:S(2)}) collective-permute-start(bf16[384,128]{1,0:T(8,128)(2,1)S(1)} %get-tuple-element.119), channel_id=1, source_target_pairs={{0,8},{4,12},{8,0},{12,4},{1,9},{5,13},{9,1},{13,5},{2,10},{6,14},... | collective-permute-start | bytes 294920 | tf_op jit(solution)/shard_map/returns_0/ppermute | solution.py:396
  75.2 12.1 %collective-permute-start.22 = (bf16[384,128]{1,0:T(8,128)(2,1)S(1)}, bf16[384,128]{1,0:T(8,128)(2,1)S(1)}, u32[]{:S(2)}, u32[]{:S(2)}) collective-permute-start(bf16[384,128]{1,0:T(8,128)(2,1)S(1)} %get-tuple-element.121), channel_id=1, source_target_pairs={{0,4},{4,0},{8,12},{12,8},{1,5},{5,1},{9,13},{13,9},{2,6},{6,2},{1... | collective-permute-start | bytes 294920 | tf_op jit(solution)/shard_map/returns_0/ppermute | solution.py:396
  87.3 8.8 %collective-permute-start.23 = (bf16[1536,128]{1,0:T(8,128)(2,1)S(1)}, bf16[1536,128]{1,0:T(8,128)(2,1)S(1)}, u32[]{:S(2)}, u32[]{:S(2)}) collective-permute-start(bf16[1536,128]{1,0:T(8,128)(2,1)S(1)} %get-tuple-element.123), channel_id=1, source_target_pairs={{0,16},{16,0},{1,17},{17,1},{2,18},{18,2},{3,19},{19,3},{4,20},{20... | collective-permute-start | bytes 1179656 | tf_op jit(solution)/shard_map/halo_query_grads_1/ppermute | solution.py:545
  87.9 9.6 %collective-permute-start.24 = (bf16[768,128]{1,0:T(8,128)(2,1)S(1)}, bf16[768,128]{1,0:T(8,128)(2,1)S(1)}, u32[]{:S(2)}, u32[]{:S(2)}) collective-permute-start(bf16[768,128]{1,0:T(8,128)(2,1)S(1)} %get-tuple-element.127), channel_id=1, source_target_pairs={{0,12},{4,8},{8,4},{12,0},{1,13},{5,9},{9,5},{13,1},{2,14},{6,10},... | collective-permute-start | bytes 589832 | tf_op jit(solution)/shard_map/returns_1/ppermute | solution.py:396
  90.1 21.2 %collective-permute-start.26 = (bf16[768,128]{1,0:T(8,128)(2,1)S(1)}, bf16[768,128]{1,0:T(8,128)(2,1)S(1)}, u32[]{:S(2)}, u32[]{:S(2)}) collective-permute-start(bf16[768,128]{1,0:T(8,128)(2,1)S(1)} %get-tuple-element.131), channel_id=1, source_target_pairs={{0,8},{4,12},{8,0},{12,4},{1,9},{5,13},{9,1},{13,5},{2,10},{6,14},... | collective-permute-start | bytes 589832 | tf_op jit(solution)/shard_map/returns_1/ppermute | solution.py:396
  90.1 21.2 %collective-permute-start.28 = (bf16[768,128]{1,0:T(8,128)(2,1)S(1)}, bf16[768,128]{1,0:T(8,128)(2,1)S(1)}, u32[]{:S(2)}, u32[]{:S(2)}) collective-permute-start(bf16[768,128]{1,0:T(8,128)(2,1)S(1)} %get-tuple-element.135), channel_id=1, source_target_pairs={{0,4},{4,0},{8,12},{12,8},{1,5},{5,1},{9,13},{13,9},{2,6},{6,2},{1... | collective-permute-start | bytes 589832 | tf_op jit(solution)/shard_map/returns_1/ppermute | solution.py:396
  97.5 19.0 %collective-permute-start.25 = (bf16[576,128]{1,0:T(8,128)(2,1)S(1)}, bf16[576,128]{1,0:T(8,128)(2,1)S(1)}, u32[]{:S(2)}, u32[]{:S(2)}) collective-permute-start(bf16[576,128]{1,0:T(8,128)(2,1)S(1)} %get-tuple-element.128), channel_id=1, source_target_pairs={{0,12},{4,8},{8,4},{12,0},{1,13},{5,9},{9,5},{13,1},{2,14},{6,10},... | collective-permute-start | bytes 442376 | tf_op jit(solution)/shard_map/returns_last/ppermute | solution.py:396
  111.3 7.7 %collective-permute-start.27 = (bf16[576,128]{1,0:T(8,128)(2,1)S(1)}, bf16[576,128]{1,0:T(8,128)(2,1)S(1)}, u32[]{:S(2)}, u32[]{:S(2)}) collective-permute-start(bf16[576,128]{1,0:T(8,128)(2,1)S(1)} %get-tuple-element.132), channel_id=1, source_target_pairs={{0,8},{4,12},{8,0},{12,4},{1,9},{5,13},{9,1},{13,5},{2,10},{6,14},... | collective-permute-start | bytes 442376 | tf_op jit(solution)/shard_map/returns_last/ppermute | solution.py:396
  111.3 8.1 %collective-permute-start.29 = (bf16[576,128]{1,0:T(8,128)(2,1)S(1)}, bf16[576,128]{1,0:T(8,128)(2,1)S(1)}, u32[]{:S(2)}, u32[]{:S(2)}) collective-permute-start(bf16[576,128]{1,0:T(8,128)(2,1)S(1)} %get-tuple-element.136), channel_id=1, source_target_pairs={{0,4},{4,0},{8,12},{12,8},{1,5},{5,1},{9,13},{13,9},{2,6},{6,2},{1... | collective-permute-start | bytes 442376 | tf_op jit(solution)/shard_map/returns_last/ppermute | solution.py:396
  (11 other events, 64.0 us)

commit v12 on v10

--- a/solution.py
+++ b/solution.py
@@ -14,7 +14,6 @@
 KEY_BLOCK = 256
 QUERY_BLOCK = 256
 VMEM_LIMIT = 48 * 1024 * 1024
-VMEM_WHOLE = 62 * 1024 * 1024
 SCALE = 1.0 / math.sqrt(HD)
 SCALE_LOG2 = SCALE / math.log(2.0)
 COST = pl.CostEstimate(flops=1, bytes_accessed=1, transcendentals=0)
@@ -57,7 +56,7 @@
     run_copies(pairs, semaphores)
 
 
-def pack(sources, parts, chosen, limit=VMEM_LIMIT):
+def pack(sources, parts, chosen):
     rows = sources[0].shape[0]
     depth = len(sources) * len(chosen) * rows
     whole = pl.BlockSpec(memory_space=pl.ANY)
@@ -67,7 +66,7 @@
         out_specs=[whole] * parts,
         out_shape=[jax.ShapeDtypeStruct((depth, HD), sources[0].dtype)] * parts,
         scratch_shapes=[pltpu.SemaphoreType.DMA((len(sources) * len(chosen) * parts,))],
-        compiler_params=pltpu.CompilerParams(vmem_limit_bytes=limit),
+        compiler_params=params(),
         cost_estimate=COST,
     )(*sources)
 
@@ -464,8 +463,8 @@
         return [lax.ppermute(array, "tm", there) for there, _ in sides]
 
     with jax.named_scope("keys_queries"):
-        packed = pack([keys[0], queries[0]], parts, list(range(heads)), VMEM_WHOLE)
-        pairs = swap_pieces(packed)
+        packed = pack([keys[0], queries[0]], parts, list(range(heads)))
+        pairs = [packed[0]] + after(swap_pieces(packed)[:0:-1], [])[::-1]
     paired = span == 2
     with jax.named_scope("gain"):
         out_grad = after([out_grad], packed[0])[0]
@@ -532,7 +531,7 @@
         if number:
             with jax.named_scope("halo_rest_grads"):
                 ranges = [(part, (head + 1) * rows, rows) for head in rest for part in others]
-                rest_side = forward(gather_rows(after(lead, leaving[0], rest_values[1:]), ranges))
+                rest_side = forward(gather_rows(after(lead, lead_side), ranges))
         with jax.named_scope("attention_%d" % number):
             inputs = [inputs_of(head) for head in chosen]
             leaving, query_grads = attention(chosen, heads, rows, inputs, dot_places, totals)

time: 150 us -> 111 us (0.74)
  Pallas kernels: 55.6 us -> 19.6 us
  waiting for transfers between devices: 54.5 us -> 41.6 us
  starting transfers between devices: 39 us -> 46.3 us
  local copies, waits for them, and re-layouts: 0.04 us -> 2.16 us
    pallas_call x2, Pallas kernels: 37.2 us -> 1.25 us  [pack(): pl.pallas_call(functools.partial(pack_kernel, parts, chosen), in_specs=[w...]
    ppermute x5, waiting for transfers between devices: 13.5 us -> 0.6 us  [forward(): return [lax.ppermute(array, 'tm', there) for there, _ in sides]]
    ppermute x21, starting transfers between devices: 30.5 us -> 36.9 us  [swap(): lax.ppermute(value, axis, [(index, index ^ distance) for index in range(l...]
    unnamed x10 -> x12, local copies, waits for them, and re-layouts: 0.02 us -> 2.14 us
  transfers between devices with their start and end apart: 29 -> 29, of which waited for: 13 -> 11; matrix products, arithmetic and copies ran while one was open for 0% -> 0% of each run, Pallas kernels for 11% -> 15%
where the time goes in v12:
time: 111 us
  starting transfers between devices  46.3 us (42%)
  waiting for transfers between devices  41.6 us (37%)
  Pallas kernels  19.6 us (18%)
  local copies, waits for them, and re-layouts  2.16 us (2%)
    ppermute x21, waiting for transfers between devices, swap(): lax.ppermute(value, axis, [(index, index ^ distance) for index in range(l...  39.1 us
    ppermute x21, starting transfers between devices, swap(): lax.ppermute(value, axis, [(index, index ^ distance) for index in range(l...  36.9 us
    pallas_call x2, Pallas kernels, attention(): pl.pallas_call(functools.partial(attention_kernel, parts, sources, chosen...  9.8 us
    ppermute x5, starting transfers between devices, forward(): return [lax.ppermute(array, 'tm', there) for there, _ in sides]  6.69 us
    pallas_call x1, Pallas kernels, partial_totals(): pl.pallas_call(functools.partial(totals_kernel, parts, sources, heads), g...  3.61 us
  transfers between devices with their start and end apart: 29, of which 11 were waited for; matrix products, arithmetic and copies ran while one was open for 0% of the time, Pallas kernels for 15%

profile of v12, /device:TPU:0, one launch (start us, length us, event | category | flops | bytes accessed | tf_op | source)
XLA Modules:
  0.0 110.7 jit_solution(4424170593477496520)
XLA Ops:
  3.9 3.1 %collective-permute-start.3 = (bf16[1152,128]{1,0:T(8,128)(2,1)}, bf16[1152,128]{1,0:T(8,128)(2,1)S(1)}, u32[]{:S(2)}, u32[]{:S(2)}) collective-permute-start(bf16[1152,128]{1,0:T(8,128)(2,1)} %get-tuple-element.80), channel_id=1, source_target_pairs={{0,4},{4,0},{8,12},{12,8},{1,5},{5,1},{9,13},{13,9},{2,6},{6,2},{1... | collective-permute-start | bytes 884744 | tf_op jit(solution)/shard_map/keys_queries/ppermute | solution.py:396
  7.0 2.6 %collective-permute-start.4 = (bf16[1152,128]{1,0:T(8,128)(2,1)S(1)}, bf16[1152,128]{1,0:T(8,128)(2,1)S(1)}, u32[]{:S(2)}, u32[]{:S(2)}) collective-permute-start(bf16[1152,128]{1,0:T(8,128)(2,1)S(1)} %get-tuple-element.81), channel_id=1, source_target_pairs={{0,8},{4,12},{8,0},{12,4},{1,9},{5,13},{9,1},{13,5},{2,10},{6,14},... | collective-permute-start | bytes 884744 | tf_op jit(solution)/shard_map/keys_queries/ppermute | solution.py:396
  9.7 1.8 %collective-permute-start.1 = (f32[12,128]{1,0:T(8,128)S(1)}, f32[12,128]{1,0:T(8,128)S(1)}, u32[]{:S(2)}, u32[]{:S(2)}) collective-permute-start(f32[12,128]{1,0:T(8,128)S(1)} %bitcast.20), channel_id=1, source_target_pairs={{0,2},{1,3},{2,0},{3,1},{4,6},{5,7},{6,4},{7,5},{8,10},{9,11},{10,... | collective-permute-start | bytes 18440 | tf_op jit(solution)/shard_map/gain/ppermute | solution.py:396
  11.5 1.9 %collective-permute-done.1 = f32[12,128]{1,0:T(8,128)S(1)} collective-permute-done((f32[12,128]{1,0:T(8,128)S(1)}, f32[12,128]{1,0:T(8,128)S(1)}, u32[]{:S(2)}, u32[]{:S(2)}) %collective-permute-start.1) | collective-permute-done | bytes 6176 | tf_op jit(solution)/shard_map/gain/ppermute | solution.py:396
  16.6 3.3 %collective-permute-done.3.refs_2_.refs_3_.refs_7_.refs_11_.refs_15_.refs_19_.refs_23_.refs_13_.refs_21_.refs_37_.refs_45_ = bf16[1152,128]{1,0:T(8,128)(2,1)S(1)} collective-permute-done((bf16[1152,128]{1,0:T(8,128)(2,1)}, bf16[1152,128]{1,0:T(8,128)(2,1)S(1)}, u32[]{:S(2)}, u32[]{:S(2)}) %collective-permute-start.3) | collective-permute-done | bytes 294944 | tf_op jit(solution)/shard_map/keys_queries/ppermute | solution.py:396
  19.8 10.6 %collective-permute-done.4.refs_1_.refs_2_.refs_6_.refs_10_.refs_14_.refs_18_.refs_22_.refs_12_.refs_20_.refs_36_.refs_44_ = bf16[1152,128]{1,0:T(8,128)(2,1)S(1)} collective-permute-done((bf16[1152,128]{1,0:T(8,128)(2,1)S(1)}, bf16[1152,128]{1,0:T(8,128)(2,1)S(1)}, u32[]{:S(2)}, u32[]{:S(2)}) %collective-permute-start.4) | collective-permute-done | bytes 294944 | tf_op jit(solution)/shard_map/keys_queries/ppermute | solution.py:396
  33.1 2.5 %collective-permute-start.6 = (bf16[832,128]{1,0:T(8,128)(2,1)S(1)}, bf16[832,128]{1,0:T(8,128)(2,1)S(1)}, u32[]{:S(2)}, u32[]{:S(2)}) collective-permute-start(bf16[832,128]{1,0:T(8,128)(2,1)S(1)} %get-tuple-element.84), channel_id=1, source_target_pairs={{0,12},{4,8},{8,4},{12,0},{1,13},{5,9},{9,5},{13,1},{2,14},{6,10},... | collective-permute-start | bytes 638984 | tf_op jit(solution)/shard_map/grads/ppermute | solution.py:396
  35.6 6.7 %collective-permute-start.7 = (bf16[832,128]{1,0:T(8,128)(2,1)S(1)}, bf16[832,128]{1,0:T(8,128)(2,1)S(1)}, u32[]{:S(2)}, u32[]{:S(2)}) collective-permute-start(bf16[832,128]{1,0:T(8,128)(2,1)S(1)} %get-tuple-element.87), channel_id=1, source_target_pairs={{0,8},{4,12},{8,0},{12,4},{1,9},{5,13},{9,1},{13,5},{2,10},{6,14},... | collective-permute-start | bytes 638984 | tf_op jit(solution)/shard_map/grads/ppermute | solution.py:396
  43.0 3.6 %totals.1 = (f32[3,768]{1,0:T(4,128)S(1)}, f32[3,768]{1,0:T(4,128)S(1)}) custom-call(bf16[1152,128]{1,0:T(8,128)(2,1)S(1)} %get-tuple-element.76.refs_0_.refs_4_.refs_8_.refs_12_.refs_16_.refs_20_.refs_10_.refs_18_.refs_34_.refs_42_, ...), custom_call_target="tpu_custom_call" | custom-call | flops 905969664 | bytes 2359296 | tf_op jit(solution)/shard_map/totals/pallas_call | solution.py:239
  46.7 7.9 %collective-permute-done.7.refs_2_.refs_16_.refs_28_.refs_52_ = bf16[832,128]{1,0:T(8,128)(2,1)S(1)} collective-permute-done((bf16[832,128]{1,0:T(8,128)(2,1)S(1)}, bf16[832,128]{1,0:T(8,128)(2,1)S(1)}, u32[]{:S(2)}, u32[]{:S(2)}) %collective-permute-start.7) | collective-permute-done | bytes 213024 | tf_op jit(solution)/shard_map/grads/ppermute | solution.py:396
  57.2 2.7 %collective-permute-start.15 = (bf16[384,128]{1,0:T(8,128)(2,1)S(1)}, bf16[384,128]{1,0:T(8,128)(2,1)S(1)}, u32[]{:S(2)}, u32[]{:S(2)}) collective-permute-start(bf16[384,128]{1,0:T(8,128)(2,1)S(1)} %get-tuple-element.113), channel_id=1, source_target_pairs={{0,12},{4,8},{8,4},{12,0},{1,13},{5,9},{9,5},{13,1},{2,14},{6,10},... | collective-permute-start | bytes 294920 | tf_op jit(solution)/shard_map/rest_values/ppermute | solution.py:396
  59.9 1.7 %collective-permute-start.17 = (bf16[384,128]{1,0:T(8,128)(2,1)S(1)}, bf16[384,128]{1,0:T(8,128)(2,1)S(1)}, u32[]{:S(2)}, u32[]{:S(2)}) collective-permute-start(bf16[384,128]{1,0:T(8,128)(2,1)S(1)} %get-tuple-element.117), channel_id=1, source_target_pairs={{0,4},{4,0},{8,12},{12,8},{1,5},{5,1},{9,13},{13,9},{2,6},{6,2},{1... | collective-permute-start | bytes 294920 | tf_op jit(solution)/shard_map/rest_values/ppermute | solution.py:396
  63.9 3.4 %attention_0.1 = (bf16[384,128]{1,0:T(8,128)(2,1)S(1)}, bf16[384,128]{1,0:T(8,128)(2,1)S(1)}, bf16[384,128]{1,0:T(8,128)(2,1)S(1)}, bf16[384,128]{1,0:T(8,128)(2...) custom-call(bf16[832,128]{1,0:T(8,128)(2,1)S(1)} %get-tuple-element.118.refs_0_.refs_14_.refs_26_.refs_50_, ...), custom_call_target="tpu_custom_call" | custom-call | flops 1509949440 | bytes 3145728 | tf_op jit(solution)/shard_map/attention_0/pallas_call | solution.py:324
  67.8 2.6 %collective-permute-start.19 = (bf16[384,128]{1,0:T(8,128)(2,1)S(1)}, bf16[384,128]{1,0:T(8,128)(2,1)S(1)}, u32[]{:S(2)}, u32[]{:S(2)}) collective-permute-start(bf16[384,128]{1,0:T(8,128)(2,1)S(1)} %get-tuple-element.125), channel_id=1, source_target_pairs={{0,12},{4,8},{8,4},{12,0},{1,13},{5,9},{9,5},{13,1},{2,14},{6,10},... | collective-permute-start | bytes 294920 | tf_op jit(solution)/shard_map/returns_0/ppermute | solution.py:396
  70.5 1.7 %collective-permute-start.21 = (bf16[384,128]{1,0:T(8,128)(2,1)S(1)}, bf16[384,128]{1,0:T(8,128)(2,1)S(1)}, u32[]{:S(2)}, u32[]{:S(2)}) collective-permute-start(bf16[384,128]{1,0:T(8,128)(2,1)S(1)} %get-tuple-element.129), channel_id=1, source_target_pairs={{0,4},{4,0},{8,12},{12,8},{1,5},{5,1},{9,13},{13,9},{2,6},{6,2},{1... | collective-permute-start | bytes 294920 | tf_op jit(solution)/shard_map/returns_0/ppermute | solution.py:396
  72.2 6.4 %attention_1.1 = (bf16[768,128]{1,0:T(8,128)(2,1)S(1)}, bf16[768,128]{1,0:T(8,128)(2,1)S(1)}, bf16[768,128]{1,0:T(8,128)(2,1)S(1)}, bf16[768,128]{1,0:T(8,128)(2...) custom-call(bf16[832,128]{1,0:T(8,128)(2,1)S(1)} %get-tuple-element.118.refs_0_.refs_14_.refs_26_.refs_50_, ...), custom_call_target="tpu_custom_call" | custom-call | flops 3019898880 | bytes 6291456 | tf_op jit(solution)/shard_map/attention_1/pallas_call | solution.py:324
  80.3 2.6 %collective-permute-start.23 = (bf16[768,128]{1,0:T(8,128)(2,1)S(1)}, bf16[768,128]{1,0:T(8,128)(2,1)S(1)}, u32[]{:S(2)}, u32[]{:S(2)}) collective-permute-start(bf16[768,128]{1,0:T(8,128)(2,1)S(1)} %get-tuple-element.135), channel_id=1, source_target_pairs={{0,12},{4,8},{8,4},{12,0},{1,13},{5,9},{9,5},{13,1},{2,14},{6,10},... | collective-permute-start | bytes 589832 | tf_op jit(solution)/shard_map/returns_1/ppermute | solution.py:396
  82.9 1.7 %collective-permute-start.27 = (bf16[768,128]{1,0:T(8,128)(2,1)S(1)}, bf16[768,128]{1,0:T(8,128)(2,1)S(1)}, u32[]{:S(2)}, u32[]{:S(2)}) collective-permute-start(bf16[768,128]{1,0:T(8,128)(2,1)S(1)} %get-tuple-element.143), channel_id=1, source_target_pairs={{0,4},{4,0},{8,12},{12,8},{1,5},{5,1},{9,13},{13,9},{2,6},{6,2},{1... | collective-permute-start | bytes 589832 | tf_op jit(solution)/shard_map/returns_1/ppermute | solution.py:396
  84.7 1.9 %collective-permute-done.22.refs_3_ = bf16[1536,128]{1,0:T(8,128)(2,1)S(1)} collective-permute-done((bf16[1536,128]{1,0:T(8,128)(2,1)S(1)}, bf16[1536,128]{1,0:T(8,128)(2,1)S(1)}, u32[]{:S(2)}, u32[]{:S(2)}) %collective-permute-start.22) | collective-permute-done | bytes 393248 | tf_op jit(solution)/shard_map/halo_query_grads_1/ppermute | solution.py:542
  86.7 3.4 %collective-permute-done.23.refs_5_ = bf16[768,128]{1,0:T(8,128)(2,1)S(1)} collective-permute-done((bf16[768,128]{1,0:T(8,128)(2,1)S(1)}, bf16[768,128]{1,0:T(8,128)(2,1)S(1)}, u32[]{:S(2)}, u32[]{:S(2)}) %collective-permute-start.23) | collective-permute-done | bytes 196640 | tf_op jit(solution)/shard_map/returns_1/ppermute | solution.py:396
  90.0 2.7 %collective-permute-start.24 = (bf16[576,128]{1,0:T(8,128)(2,1)S(1)}, bf16[576,128]{1,0:T(8,128)(2,1)S(1)}, u32[]{:S(2)}, u32[]{:S(2)}) collective-permute-start(bf16[576,128]{1,0:T(8,128)(2,1)S(1)} %get-tuple-element.136), channel_id=1, source_target_pairs={{0,12},{4,8},{8,4},{12,0},{1,13},{5,9},{9,5},{13,1},{2,14},{6,10},... | collective-permute-start | bytes 442376 | tf_op jit(solution)/shard_map/returns_last/ppermute | solution.py:396
  92.7 8.9 %collective-permute-done.25.refs_6_ = bf16[768,128]{1,0:T(8,128)(2,1)S(1)} collective-permute-done((bf16[768,128]{1,0:T(8,128)(2,1)S(1)}, bf16[768,128]{1,0:T(8,128)(2,1)S(1)}, u32[]{:S(2)}, u32[]{:S(2)}) %collective-permute-start.25) | collective-permute-done | bytes 196640 | tf_op jit(solution)/shard_map/returns_1/ppermute | solution.py:396
  101.6 4.2 %collective-permute-start.28 = (bf16[576,128]{1,0:T(8,128)(2,1)S(1)}, bf16[576,128]{1,0:T(8,128)(2,1)S(1)}, u32[]{:S(2)}, u32[]{:S(2)}) collective-permute-start(bf16[576,128]{1,0:T(8,128)(2,1)S(1)} %get-tuple-element.144), channel_id=1, source_target_pairs={{0,4},{4,0},{8,12},{12,8},{1,5},{5,1},{9,13},{13,9},{2,6},{6,2},{1... | collective-permute-start | bytes 442376 | tf_op jit(solution)/shard_map/returns_last/ppermute | solution.py:396
  107.6 1.7 %collective-permute-done.26.refs_2_ = bf16[576,128]{1,0:T(8,128)(2,1)S(1)} collective-permute-done((bf16[576,128]{1,0:T(8,128)(2,1)S(1)}, bf16[576,128]{1,0:T(8,128)(2,1)S(1)}, u32[]{:S(2)}, u32[]{:S(2)}) %collective-permute-start.26) | collective-permute-done | bytes 147488 | tf_op jit(solution)/shard_map/returns_last/ppermute | solution.py:396
  (66 shorter events, 20.1 us)
Async XLA Ops:
  3.9 16.0 %collective-permute-start.3 = (bf16[1152,128]{1,0:T(8,128)(2,1)}, bf16[1152,128]{1,0:T(8,128)(2,1)S(1)}, u32[]{:S(2)}, u32[]{:S(2)}) collective-permute-start(bf16[1152,128]{1,0:T(8,128)(2,1)} %get-tuple-element.80), channel_id=1, source_target_pairs={{0,4},{4,0},{8,12},{12,8},{1,5},{5,1},{9,13},{13,9},{2,6},{6,2},{1... | collective-permute-start | bytes 884744 | tf_op jit(solution)/shard_map/keys_queries/ppermute | solution.py:396
  7.0 23.5 %collective-permute-start.4 = (bf16[1152,128]{1,0:T(8,128)(2,1)S(1)}, bf16[1152,128]{1,0:T(8,128)(2,1)S(1)}, u32[]{:S(2)}, u32[]{:S(2)}) collective-permute-start(bf16[1152,128]{1,0:T(8,128)(2,1)S(1)} %get-tuple-element.81), channel_id=1, source_target_pairs={{0,8},{4,12},{8,0},{12,4},{1,9},{5,13},{9,1},{13,5},{2,10},{6,14},... | collective-permute-start | bytes 884744 | tf_op jit(solution)/shard_map/keys_queries/ppermute | solution.py:396
  9.5 20.9 %collective-permute-start.5 = (bf16[1152,128]{1,0:T(8,128)(2,1)S(1)}, bf16[1152,128]{1,0:T(8,128)(2,1)S(1)}, u32[]{:S(2)}, u32[]{:S(2)}) collective-permute-start(bf16[1152,128]{1,0:T(8,128)(2,1)S(1)} %get-tuple-element.82), channel_id=1, source_target_pairs={{0,12},{4,8},{8,4},{12,0},{1,13},{5,9},{9,5},{13,1},{2,14},{6,10},... | collective-permute-start | bytes 884744 | tf_op jit(solution)/shard_map/keys_queries/ppermute | solution.py:396
  14.5 15.9 %collective-permute-start.10 = (bf16[576,128]{1,0:T(8,128)(2,1)S(1)}, bf16[576,128]{1,0:T(8,128)(2,1)S(1)}, u32[]{:S(2)}, u32[]{:S(2)}) collective-permute-start(bf16[576,128]{1,0:T(8,128)(2,1)S(1)} %slice.9), channel_id=1, source_target_pairs={{0,16},{16,0},{1,17},{17,1},{2,18},{18,2},{3,19},{19,3},{4,20},{20... | collective-permute-start | bytes 442376 | tf_op jit(solution)/shard_map/halo_queries/ppermute | solution.py:463
  31.0 12.0 %collective-permute-start.11 = (bf16[1728,128]{1,0:T(8,128)(2,1)S(1)}, bf16[1728,128]{1,0:T(8,128)(2,1)S(1)}, u32[]{:S(2)}, u32[]{:S(2)}) collective-permute-start(bf16[1728,128]{1,0:T(8,128)(2,1)S(1)} %halo_queries.1), channel_id=1, source_target_pairs={{0,16},{16,0},{1,17},{17,1},{2,18},{18,2},{3,19},{19,3},{4,20},{20... | collective-permute-start | bytes 1327112 | tf_op jit(solution)/shard_map/halo_queries/ppermute | solution.py:463
  32.6 14.0 %collective-permute-start.9 = (bf16[832,128]{1,0:T(8,128)(2,1)S(1)}, bf16[832,128]{1,0:T(8,128)(2,1)S(1)}, u32[]{:S(2)}, u32[]{:S(2)}) collective-permute-start(bf16[832,128]{1,0:T(8,128)(2,1)S(1)} %get-tuple-element.118.refs_0_.refs_14_.refs_26_.refs_50_), channel_id=1, source_target_pairs={{0,16},{16,0},{1,17},{17,1},{2,18},{18,2},{3,19},{19,3},{4,20},{20... | collective-permute-start | bytes 638984 | tf_op jit(solution)/shard_map/halo_own_grads/ppermute | solution.py:463
  33.1 13.5 %collective-permute-start.6 = (bf16[832,128]{1,0:T(8,128)(2,1)S(1)}, bf16[832,128]{1,0:T(8,128)(2,1)S(1)}, u32[]{:S(2)}, u32[]{:S(2)}) collective-permute-start(bf16[832,128]{1,0:T(8,128)(2,1)S(1)} %get-tuple-element.84), channel_id=1, source_target_pairs={{0,12},{4,8},{8,4},{12,0},{1,13},{5,9},{9,5},{13,1},{2,14},{6,10},... | collective-permute-start | bytes 638984 | tf_op jit(solution)/shard_map/grads/ppermute | solution.py:396
  35.6 18.9 %collective-permute-start.7 = (bf16[832,128]{1,0:T(8,128)(2,1)S(1)}, bf16[832,128]{1,0:T(8,128)(2,1)S(1)}, u32[]{:S(2)}, u32[]{:S(2)}) collective-permute-start(bf16[832,128]{1,0:T(8,128)(2,1)S(1)} %get-tuple-element.87), channel_id=1, source_target_pairs={{0,8},{4,12},{8,0},{12,4},{1,9},{5,13},{9,1},{13,5},{2,10},{6,14},... | collective-permute-start | bytes 638984 | tf_op jit(solution)/shard_map/grads/ppermute | solution.py:396
  42.3 12.2 %collective-permute-start.8 = (bf16[832,128]{1,0:T(8,128)(2,1)S(1)}, bf16[832,128]{1,0:T(8,128)(2,1)S(1)}, u32[]{:S(2)}, u32[]{:S(2)}) collective-permute-start(bf16[832,128]{1,0:T(8,128)(2,1)S(1)} %get-tuple-element.90), channel_id=1, source_target_pairs={{0,4},{4,0},{8,12},{12,8},{1,5},{5,1},{9,13},{13,9},{2,6},{6,2},{1... | collective-permute-start | bytes 638984 | tf_op jit(solution)/shard_map/grads/ppermute | solution.py:396
  57.2 10.6 %collective-permute-start.15 = (bf16[384,128]{1,0:T(8,128)(2,1)S(1)}, bf16[384,128]{1,0:T(8,128)(2,1)S(1)}, u32[]{:S(2)}, u32[]{:S(2)}) collective-permute-start(bf16[384,128]{1,0:T(8,128)(2,1)S(1)} %get-tuple-element.113), channel_id=1, source_target_pairs={{0,12},{4,8},{8,4},{12,0},{1,13},{5,9},{9,5},{13,1},{2,14},{6,10},... | collective-permute-start | bytes 294920 | tf_op jit(solution)/shard_map/rest_values/ppermute | solution.py:396
  59.9 10.6 %collective-permute-start.16 = (bf16[384,128]{1,0:T(8,128)(2,1)S(1)}, bf16[384,128]{1,0:T(8,128)(2,1)S(1)}, u32[]{:S(2)}, u32[]{:S(2)}) collective-permute-start(bf16[384,128]{1,0:T(8,128)(2,1)S(1)} %get-tuple-element.115), channel_id=1, source_target_pairs={{0,8},{4,12},{8,0},{12,4},{1,9},{5,13},{9,1},{13,5},{2,10},{6,14},... | collective-permute-start | bytes 294920 | tf_op jit(solution)/shard_map/rest_values/ppermute | solution.py:396
  59.9 10.6 %collective-permute-start.17 = (bf16[384,128]{1,0:T(8,128)(2,1)S(1)}, bf16[384,128]{1,0:T(8,128)(2,1)S(1)}, u32[]{:S(2)}, u32[]{:S(2)}) collective-permute-start(bf16[384,128]{1,0:T(8,128)(2,1)S(1)} %get-tuple-element.117), channel_id=1, source_target_pairs={{0,4},{4,0},{8,12},{12,8},{1,5},{5,1},{9,13},{13,9},{2,6},{6,2},{1... | collective-permute-start | bytes 294920 | tf_op jit(solution)/shard_map/rest_values/ppermute | solution.py:396
  62.3 10.0 %collective-permute-start.18 = (bf16[1152,128]{1,0:T(8,128)(2,1)S(1)}, bf16[1152,128]{1,0:T(8,128)(2,1)S(1)}, u32[]{:S(2)}, u32[]{:S(2)}) collective-permute-start(bf16[1152,128]{1,0:T(8,128)(2,1)S(1)} %halo_rest_grads.1), channel_id=1, source_target_pairs={{0,16},{16,0},{1,17},{17,1},{2,18},{18,2},{3,19},{19,3},{4,20},{20... | collective-permute-start | bytes 884744 | tf_op jit(solution)/shard_map/halo_rest_grads/ppermute | solution.py:463
  67.2 11.5 %collective-permute-start.14 = (bf16[768,128]{1,0:T(8,128)(2,1)S(1)}, bf16[768,128]{1,0:T(8,128)(2,1)S(1)}, u32[]{:S(2)}, u32[]{:S(2)}) collective-permute-start(bf16[768,128]{1,0:T(8,128)(2,1)S(1)} %get-tuple-element.103), channel_id=1, source_target_pairs={{0,16},{16,0},{1,17},{17,1},{2,18},{18,2},{3,19},{19,3},{4,20},{20... | collective-permute-start | bytes 589832 | tf_op jit(solution)/shard_map/halo_query_grads_0/ppermute | solution.py:542
  67.8 10.9 %collective-permute-start.19 = (bf16[384,128]{1,0:T(8,128)(2,1)S(1)}, bf16[384,128]{1,0:T(8,128)(2,1)S(1)}, u32[]{:S(2)}, u32[]{:S(2)}) collective-permute-start(bf16[384,128]{1,0:T(8,128)(2,1)S(1)} %get-tuple-element.125), channel_id=1, source_target_pairs={{0,12},{4,8},{8,4},{12,0},{1,13},{5,9},{9,5},{13,1},{2,14},{6,10},... | collective-permute-start | bytes 294920 | tf_op jit(solution)/shard_map/returns_0/ppermute | solution.py:396
  70.5 8.2 %collective-permute-start.20 = (bf16[384,128]{1,0:T(8,128)(2,1)S(1)}, bf16[384,128]{1,0:T(8,128)(2,1)S(1)}, u32[]{:S(2)}, u32[]{:S(2)}) collective-permute-start(bf16[384,128]{1,0:T(8,128)(2,1)S(1)} %get-tuple-element.127), channel_id=1, source_target_pairs={{0,8},{4,12},{8,0},{12,4},{1,9},{5,13},{9,1},{13,5},{2,10},{6,14},... | collective-permute-start | bytes 294920 | tf_op jit(solution)/shard_map/returns_0/ppermute | solution.py:396
  70.5 8.2 %collective-permute-start.21 = (bf16[384,128]{1,0:T(8,128)(2,1)S(1)}, bf16[384,128]{1,0:T(8,128)(2,1)S(1)}, u32[]{:S(2)}, u32[]{:S(2)}) collective-permute-start(bf16[384,128]{1,0:T(8,128)(2,1)S(1)} %get-tuple-element.129), channel_id=1, source_target_pairs={{0,4},{4,0},{8,12},{12,8},{1,5},{5,1},{9,13},{13,9},{2,6},{6,2},{1... | collective-permute-start | bytes 294920 | tf_op jit(solution)/shard_map/returns_0/ppermute | solution.py:396
  78.7 7.8 %collective-permute-start.22 = (bf16[1536,128]{1,0:T(8,128)(2,1)S(1)}, bf16[1536,128]{1,0:T(8,128)(2,1)S(1)}, u32[]{:S(2)}, u32[]{:S(2)}) collective-permute-start(bf16[1536,128]{1,0:T(8,128)(2,1)S(1)} %get-tuple-element.131), channel_id=1, source_target_pairs={{0,16},{16,0},{1,17},{17,1},{2,18},{18,2},{3,19},{19,3},{4,20},{20... | collective-permute-start | bytes 1179656 | tf_op jit(solution)/shard_map/halo_query_grads_1/ppermute | solution.py:542
  80.3 9.7 %collective-permute-start.23 = (bf16[768,128]{1,0:T(8,128)(2,1)S(1)}, bf16[768,128]{1,0:T(8,128)(2,1)S(1)}, u32[]{:S(2)}, u32[]{:S(2)}) collective-permute-start(bf16[768,128]{1,0:T(8,128)(2,1)S(1)} %get-tuple-element.135), channel_id=1, source_target_pairs={{0,12},{4,8},{8,4},{12,0},{1,13},{5,9},{9,5},{13,1},{2,14},{6,10},... | collective-permute-start | bytes 589832 | tf_op jit(solution)/shard_map/returns_1/ppermute | solution.py:396
  82.9 18.7 %collective-permute-start.25 = (bf16[768,128]{1,0:T(8,128)(2,1)S(1)}, bf16[768,128]{1,0:T(8,128)(2,1)S(1)}, u32[]{:S(2)}, u32[]{:S(2)}) collective-permute-start(bf16[768,128]{1,0:T(8,128)(2,1)S(1)} %get-tuple-element.139), channel_id=1, source_target_pairs={{0,8},{4,12},{8,0},{12,4},{1,9},{5,13},{9,1},{13,5},{2,10},{6,14},... | collective-permute-start | bytes 589832 | tf_op jit(solution)/shard_map/returns_1/ppermute | solution.py:396
  82.9 18.7 %collective-permute-start.27 = (bf16[768,128]{1,0:T(8,128)(2,1)S(1)}, bf16[768,128]{1,0:T(8,128)(2,1)S(1)}, u32[]{:S(2)}, u32[]{:S(2)}) collective-permute-start(bf16[768,128]{1,0:T(8,128)(2,1)S(1)} %get-tuple-element.143), channel_id=1, source_target_pairs={{0,4},{4,0},{8,12},{12,8},{1,5},{5,1},{9,13},{13,9},{2,6},{6,2},{1... | collective-permute-start | bytes 589832 | tf_op jit(solution)/shard_map/returns_1/ppermute | solution.py:396
  90.0 17.6 %collective-permute-start.24 = (bf16[576,128]{1,0:T(8,128)(2,1)S(1)}, bf16[576,128]{1,0:T(8,128)(2,1)S(1)}, u32[]{:S(2)}, u32[]{:S(2)}) collective-permute-start(bf16[576,128]{1,0:T(8,128)(2,1)S(1)} %get-tuple-element.136), channel_id=1, source_target_pairs={{0,12},{4,8},{8,4},{12,0},{1,13},{5,9},{9,5},{13,1},{2,14},{6,10},... | collective-permute-start | bytes 442376 | tf_op jit(solution)/shard_map/returns_last/ppermute | solution.py:396
  101.6 7.7 %collective-permute-start.26 = (bf16[576,128]{1,0:T(8,128)(2,1)S(1)}, bf16[576,128]{1,0:T(8,128)(2,1)S(1)}, u32[]{:S(2)}, u32[]{:S(2)}) collective-permute-start(bf16[576,128]{1,0:T(8,128)(2,1)S(1)} %get-tuple-element.140), channel_id=1, source_target_pairs={{0,8},{4,12},{8,0},{12,4},{1,9},{5,13},{9,1},{13,5},{2,10},{6,14},... | collective-permute-start | bytes 442376 | tf_op jit(solution)/shard_map/returns_last/ppermute | solution.py:396
  101.6 8.1 %collective-permute-start.28 = (bf16[576,128]{1,0:T(8,128)(2,1)S(1)}, bf16[576,128]{1,0:T(8,128)(2,1)S(1)}, u32[]{:S(2)}, u32[]{:S(2)}) collective-permute-start(bf16[576,128]{1,0:T(8,128)(2,1)S(1)} %get-tuple-element.144), channel_id=1, source_target_pairs={{0,4},{4,0},{8,12},{12,8},{1,5},{5,1},{9,13},{13,9},{2,6},{6,2},{1... | collective-permute-start | bytes 442376 | tf_op jit(solution)/shard_map/returns_last/ppermute | solution.py:396
  (11 other events, 49.6 us)

commit v13 on v10

--- a/solution.py
+++ b/solution.py
@@ -64,7 +64,7 @@
     return pl.pallas_call(
         functools.partial(pack_kernel, parts, chosen),
         in_specs=[whole] * len(sources),
-        out_specs=[whole] * parts,
+        out_specs=[pl.BlockSpec(memory_space=pltpu.VMEM)] * parts,
         out_shape=[jax.ShapeDtypeStruct((depth, HD), sources[0].dtype)] * parts,
         scratch_shapes=[pltpu.SemaphoreType.DMA((len(sources) * len(chosen) * parts,))],
         compiler_params=pltpu.CompilerParams(vmem_limit_bytes=limit),
@@ -465,7 +465,7 @@
 
     with jax.named_scope("keys_queries"):
         packed = pack([keys[0], queries[0]], parts, list(range(heads)), VMEM_WHOLE)
-        pairs = swap_pieces(packed)
+        pairs = [packed[0]] + after(swap_pieces(packed)[:0:-1], [])[::-1]
     paired = span == 2
     with jax.named_scope("gain"):
         out_grad = after([out_grad], packed[0])[0]
@@ -475,8 +475,6 @@
             gain = sum_over(gain, "tm")
     with jax.named_scope("grads"):
         sent_lead = pack_grads(out_grad[0], attn_out[0], values[0], out_gain, gain, parts)
-    with jax.named_scope("halo_own_grads"):
-        own_side = forward(sent_lead[0])
     with jax.named_scope("halo_queries"):
         width = heads * rows
         first_side = forward(pairs[0][width:])
@@ -487,6 +485,8 @@
         late_side = forward(gather_rows(late, [(number, width, width) for number in range(parts - 1)]))
     base = (heads + 1) * rows
     extra = gain_depth(channels)
+    with jax.named_scope("halo_own_grads"):
+        own_side = forward(after(sent_lead[:1], late_side)[0])
     with jax.named_scope("totals"):
         key_places = [[(piece, head) for piece in pairs] for head in range(heads)]
         query_places = [[[(piece, heads + head) for piece in pairs] for head in range(heads)]]
@@ -532,7 +532,7 @@
         if number:
             with jax.named_scope("halo_rest_grads"):
                 ranges = [(part, (head + 1) * rows, rows) for head in rest for part in others]
-                rest_side = forward(gather_rows(after(lead, leaving[0], rest_values[1:]), ranges))
+                rest_side = forward(gather_rows(after(lead, lead_side), ranges))
         with jax.named_scope("attention_%d" % number):
             inputs = [inputs_of(head) for head in chosen]
             leaving, query_grads = attention(chosen, heads, rows, inputs, dot_places, totals)

time: 150 us -> 112 us (0.75)
  Pallas kernels: 55.6 us -> 21.1 us
  waiting for transfers between devices: 54.5 us -> 37.5 us
  starting transfers between devices: 39 us -> 52 us
    pallas_call x2, Pallas kernels: 37.2 us -> 2.75 us  [pack(): pl.pallas_call(functools.partial(pack_kernel, parts, chosen), in_specs=[w...]
    ppermute x5, waiting for transfers between devices: 13.5 us -> 0.01 us  [forward(): return [lax.ppermute(array, 'tm', there) for there, _ in sides]]
    ppermute x21, starting transfers between devices: 30.5 us -> 41.1 us  [swap(): lax.ppermute(value, axis, [(index, index ^ distance) for index in range(l...]
    ppermute x21, waiting for transfers between devices: 38.2 us -> 36.1 us  [swap(): lax.ppermute(value, axis, [(index, index ^ distance) for index in range(l...]
    ppermute x2, starting transfers between devices: 2.09 us -> 3.87 us  [local(): lax.ppermute(other, 'tm', back)]
  transfers between devices with their start and end apart: 29 -> 29, of which waited for: 13 -> 11; matrix products, arithmetic and copies ran while one was open for 0% -> 0% of each run, Pallas kernels for 11% -> 15%
where the time goes in v13:
time: 112 us
  starting transfers between devices  52 us (46%)
  waiting for transfers between devices  37.5 us (33%)
  Pallas kernels  21.1 us (19%)
    ppermute x21, starting transfers between devices, swap(): lax.ppermute(value, axis, [(index, index ^ distance) for index in range(l...  41.1 us
    ppermute x21, waiting for transfers between devices, swap(): lax.ppermute(value, axis, [(index, index ^ distance) for index in range(l...  36.1 us
    pallas_call x2, Pallas kernels, attention(): pl.pallas_call(functools.partial(attention_kernel, parts, sources, chosen...  9.84 us
    ppermute x5, starting transfers between devices, forward(): return [lax.ppermute(array, 'tm', there) for there, _ in sides]  5.61 us
    ppermute x2, starting transfers between devices, local(): lax.ppermute(other, 'tm', back)  3.87 us
    pallas_call x1, Pallas kernels, partial_totals(): pl.pallas_call(functools.partial(totals_kernel, parts, sources, heads), g...  3.61 us
    pallas_call x2, Pallas kernels, pack(): pl.pallas_call(functools.partial(pack_kernel, parts, chosen), in_specs=[w...  2.75 us
  transfers between devices with their start and end apart: 29, of which 11 were waited for; matrix products, arithmetic and copies ran while one was open for 0% of the time, Pallas kernels for 15%

profile of v13, /device:TPU:0, one launch (start us, length us, event | category | flops | bytes accessed | tf_op | source)
XLA Modules:
  0.0 111.8 jit_solution(7673191849837325522)
XLA Ops:
  0.7 2.6 %keys_queries.1 = (bf16[1152,128]{1,0:T(8,128)(2,1)}, bf16[1152,128]{1,0:T(8,128)(2,1)}, bf16[1152,128]{1,0:T(8,128)(2,1)}, bf16[1152,128]{1,0:T(8,128)(2,1)}) custom-call(bf16[192,1536]{1,0:T(8,128)(2,1)} %bitcast.17, bf16[192,1536]{1,0:T(8,128)(2,1)} %bitcast.18), custom_call_target="tpu_custom_call" | custom-call | flops 1 | bytes 1 | tf_op jit(solution)/shard_map/keys_queries/pallas_call | solution.py:64
  3.2 3.1 %collective-permute-start.3 = (bf16[1152,128]{1,0:T(8,128)(2,1)}, bf16[1152,128]{1,0:T(8,128)(2,1)S(1)}, u32[]{:S(2)}, u32[]{:S(2)}) collective-permute-start(bf16[1152,128]{1,0:T(8,128)(2,1)} %get-tuple-element.81), channel_id=1, source_target_pairs={{0,4},{4,0},{8,12},{12,8},{1,5},{5,1},{9,13},{13,9},{2,6},{6,2},{1... | collective-permute-start | bytes 884744 | tf_op jit(solution)/shard_map/keys_queries/ppermute | solution.py:397
  6.3 2.6 %collective-permute-start.4 = (bf16[1152,128]{1,0:T(8,128)(2,1)}, bf16[1152,128]{1,0:T(8,128)(2,1)S(1)}, u32[]{:S(2)}, u32[]{:S(2)}) collective-permute-start(bf16[1152,128]{1,0:T(8,128)(2,1)} %get-tuple-element.82), channel_id=1, source_target_pairs={{0,8},{4,12},{8,0},{12,4},{1,9},{5,13},{9,1},{13,5},{2,10},{6,14},... | collective-permute-start | bytes 884744 | tf_op jit(solution)/shard_map/keys_queries/ppermute | solution.py:397
  9.1 1.8 %collective-permute-start.1 = (f32[12,128]{1,0:T(8,128)S(1)}, f32[12,128]{1,0:T(8,128)S(1)}, u32[]{:S(2)}, u32[]{:S(2)}) collective-permute-start(f32[12,128]{1,0:T(8,128)S(1)} %bitcast.20), channel_id=1, source_target_pairs={{0,2},{1,3},{2,0},{3,1},{4,6},{5,7},{6,4},{7,5},{8,10},{9,11},{10,... | collective-permute-start | bytes 18440 | tf_op jit(solution)/shard_map/gain/ppermute | solution.py:397
  10.9 1.9 %collective-permute-done.1 = f32[12,128]{1,0:T(8,128)S(1)} collective-permute-done((f32[12,128]{1,0:T(8,128)S(1)}, f32[12,128]{1,0:T(8,128)S(1)}, u32[]{:S(2)}, u32[]{:S(2)}) %collective-permute-start.1) | collective-permute-done | bytes 6176 | tf_op jit(solution)/shard_map/gain/ppermute | solution.py:397
  16.0 3.1 %collective-permute-done.3.refs_2_.refs_3_.refs_7_.refs_11_.refs_15_.refs_19_.refs_23_.refs_13_.refs_21_.refs_37_.refs_45_ = bf16[1152,128]{1,0:T(8,128)(2,1)S(1)} collective-permute-done((bf16[1152,128]{1,0:T(8,128)(2,1)}, bf16[1152,128]{1,0:T(8,128)(2,1)S(1)}, u32[]{:S(2)}, u32[]{:S(2)}) %collective-permute-start.3) | collective-permute-done | bytes 294944 | tf_op jit(solution)/shard_map/keys_queries/ppermute | solution.py:397
  19.1 10.9 %collective-permute-done.4.refs_1_.refs_2_.refs_6_.refs_10_.refs_14_.refs_18_.refs_22_.refs_12_.refs_20_.refs_36_.refs_44_ = bf16[1152,128]{1,0:T(8,128)(2,1)S(1)} collective-permute-done((bf16[1152,128]{1,0:T(8,128)(2,1)}, bf16[1152,128]{1,0:T(8,128)(2,1)S(1)}, u32[]{:S(2)}, u32[]{:S(2)}) %collective-permute-start.4) | collective-permute-done | bytes 294944 | tf_op jit(solution)/shard_map/keys_queries/ppermute | solution.py:397
  32.2 2.5 %collective-permute-start.6 = (bf16[832,128]{1,0:T(8,128)(2,1)S(1)}, bf16[832,128]{1,0:T(8,128)(2,1)S(1)}, u32[]{:S(2)}, u32[]{:S(2)}) collective-permute-start(bf16[832,128]{1,0:T(8,128)(2,1)S(1)} %get-tuple-element.85), channel_id=1, source_target_pairs={{0,12},{4,8},{8,4},{12,0},{1,13},{5,9},{9,5},{13,1},{2,14},{6,10},... | collective-permute-start | bytes 638984 | tf_op jit(solution)/shard_map/grads/ppermute | solution.py:397
  34.7 9.2 %collective-permute-start.7 = (bf16[832,128]{1,0:T(8,128)(2,1)S(1)}, bf16[832,128]{1,0:T(8,128)(2,1)S(1)}, u32[]{:S(2)}, u32[]{:S(2)}) collective-permute-start(bf16[832,128]{1,0:T(8,128)(2,1)S(1)} %get-tuple-element.88), channel_id=1, source_target_pairs={{0,8},{4,12},{8,0},{12,4},{1,9},{5,13},{9,1},{13,5},{2,10},{6,14},... | collective-permute-start | bytes 638984 | tf_op jit(solution)/shard_map/grads/ppermute | solution.py:397
  43.9 3.6 %totals.1 = (f32[3,768]{1,0:T(4,128)S(1)}, f32[3,768]{1,0:T(4,128)S(1)}) custom-call(bf16[1152,128]{1,0:T(8,128)(2,1)S(1)} %copy-done, bf16[1152,128]{1,0:T(8,128)(2,1)S(1)} %collective-permute-done.5.refs_0_.refs_1_.refs_5_.refs_9_.refs_13_.refs_17_.refs_21_.refs_11_.refs_19_.refs_35_.refs_43_, ...), custom_call_target="tpu_custom_call" | custom-call | flops 905969664 | bytes 2359296 | tf_op jit(solution)/shard_map/totals/pallas_call | solution.py:240
  47.6 6.5 %collective-permute-done.7.refs_2_.refs_16_.refs_28_.refs_52_ = bf16[832,128]{1,0:T(8,128)(2,1)S(1)} collective-permute-done((bf16[832,128]{1,0:T(8,128)(2,1)S(1)}, bf16[832,128]{1,0:T(8,128)(2,1)S(1)}, u32[]{:S(2)}, u32[]{:S(2)}) %collective-permute-start.7) | collective-permute-done | bytes 213024 | tf_op jit(solution)/shard_map/grads/ppermute | solution.py:397
  56.7 2.5 %collective-permute-start.15 = (bf16[384,128]{1,0:T(8,128)(2,1)S(1)}, bf16[384,128]{1,0:T(8,128)(2,1)S(1)}, u32[]{:S(2)}, u32[]{:S(2)}) collective-permute-start(bf16[384,128]{1,0:T(8,128)(2,1)S(1)} %get-tuple-element.115), channel_id=1, source_target_pairs={{0,12},{4,8},{8,4},{12,0},{1,13},{5,9},{9,5},{13,1},{2,14},{6,10},... | collective-permute-start | bytes 294920 | tf_op jit(solution)/shard_map/rest_values/ppermute | solution.py:397
  59.3 3.9 %collective-permute-start.16 = (bf16[384,128]{1,0:T(8,128)(2,1)S(1)}, bf16[384,128]{1,0:T(8,128)(2,1)S(1)}, u32[]{:S(2)}, u32[]{:S(2)}) collective-permute-start(bf16[384,128]{1,0:T(8,128)(2,1)S(1)} %get-tuple-element.117), channel_id=1, source_target_pairs={{0,8},{4,12},{8,0},{12,4},{1,9},{5,13},{9,1},{13,5},{2,10},{6,14},... | collective-permute-start | bytes 294920 | tf_op jit(solution)/shard_map/rest_values/ppermute | solution.py:397
  63.7 1.8 %collective-permute-start.18 = (bf16[1152,128]{1,0:T(8,128)(2,1)S(1)}, bf16[1152,128]{1,0:T(8,128)(2,1)S(1)}, u32[]{:S(2)}, u32[]{:S(2)}) collective-permute-start(bf16[1152,128]{1,0:T(8,128)(2,1)S(1)} %halo_rest_grads.1), channel_id=1, source_target_pairs={{0,16},{16,0},{1,17},{17,1},{2,18},{18,2},{3,19},{19,3},{4,20},{20... | collective-permute-start | bytes 884744 | tf_op jit(solution)/shard_map/halo_rest_grads/ppermute | solution.py:464
  65.6 3.4 %attention_0.1 = (bf16[384,128]{1,0:T(8,128)(2,1)S(1)}, bf16[384,128]{1,0:T(8,128)(2,1)S(1)}, bf16[384,128]{1,0:T(8,128)(2,1)S(1)}, bf16[384,128]{1,0:T(8,128)(2...) custom-call(bf16[832,128]{1,0:T(8,128)(2,1)S(1)} %get-tuple-element.120.refs_0_.refs_14_.refs_26_.refs_50_, ...), custom_call_target="tpu_custom_call" | custom-call | flops 1509949440 | bytes 3145728 | tf_op jit(solution)/shard_map/attention_0/pallas_call | solution.py:325
  69.3 2.1 %collective-permute-start.19 = (bf16[384,128]{1,0:T(8,128)(2,1)S(1)}, bf16[384,128]{1,0:T(8,128)(2,1)S(1)}, u32[]{:S(2)}, u32[]{:S(2)}) collective-permute-start(bf16[384,128]{1,0:T(8,128)(2,1)S(1)} %get-tuple-element.127), channel_id=1, source_target_pairs={{0,12},{4,8},{8,4},{12,0},{1,13},{5,9},{9,5},{13,1},{2,14},{6,10},... | collective-permute-start | bytes 294920 | tf_op jit(solution)/shard_map/returns_0/ppermute | solution.py:397
  71.4 3.4 %collective-permute-start.20 = (bf16[384,128]{1,0:T(8,128)(2,1)S(1)}, bf16[384,128]{1,0:T(8,128)(2,1)S(1)}, u32[]{:S(2)}, u32[]{:S(2)}) collective-permute-start(bf16[384,128]{1,0:T(8,128)(2,1)S(1)} %get-tuple-element.129), channel_id=1, source_target_pairs={{0,8},{4,12},{8,0},{12,4},{1,9},{5,13},{9,1},{13,5},{2,10},{6,14},... | collective-permute-start | bytes 294920 | tf_op jit(solution)/shard_map/returns_0/ppermute | solution.py:397
  74.8 6.5 %attention_1.1 = (bf16[768,128]{1,0:T(8,128)(2,1)S(1)}, bf16[768,128]{1,0:T(8,128)(2,1)S(1)}, bf16[768,128]{1,0:T(8,128)(2,1)S(1)}, bf16[768,128]{1,0:T(8,128)(2...) custom-call(bf16[832,128]{1,0:T(8,128)(2,1)S(1)} %get-tuple-element.120.refs_0_.refs_14_.refs_26_.refs_50_, ...), custom_call_target="tpu_custom_call" | custom-call | flops 3019898880 | bytes 6291456 | tf_op jit(solution)/shard_map/attention_1/pallas_call | solution.py:325
  81.2 4.3 %collective-permute-done.20.refs_2_ = bf16[384,128]{1,0:T(8,128)(2,1)S(1)} collective-permute-done((bf16[384,128]{1,0:T(8,128)(2,1)S(1)}, bf16[384,128]{1,0:T(8,128)(2,1)S(1)}, u32[]{:S(2)}, u32[]{:S(2)}) %collective-permute-start.20) | collective-permute-done | bytes 98336 | tf_op jit(solution)/shard_map/returns_0/ppermute | solution.py:397
  85.5 3.5 %collective-permute-start.22 = (bf16[1536,128]{1,0:T(8,128)(2,1)S(1)}, bf16[1536,128]{1,0:T(8,128)(2,1)S(1)}, u32[]{:S(2)}, u32[]{:S(2)}) collective-permute-start(bf16[1536,128]{1,0:T(8,128)(2,1)S(1)} %get-tuple-element.133), channel_id=1, source_target_pairs={{0,16},{16,0},{1,17},{17,1},{2,18},{18,2},{3,19},{19,3},{4,20},{20... | collective-permute-start | bytes 1179656 | tf_op jit(solution)/shard_map/halo_query_grads_1/ppermute | solution.py:543
  89.8 3.6 %collective-permute-start.27 = (bf16[768,128]{1,0:T(8,128)(2,1)S(1)}, bf16[768,128]{1,0:T(8,128)(2,1)S(1)}, u32[]{:S(2)}, u32[]{:S(2)}) collective-permute-start(bf16[768,128]{1,0:T(8,128)(2,1)S(1)} %get-tuple-element.145), channel_id=1, source_target_pairs={{0,4},{4,0},{8,12},{12,8},{1,5},{5,1},{9,13},{13,9},{2,6},{6,2},{1... | collective-permute-start | bytes 589832 | tf_op jit(solution)/shard_map/returns_1/ppermute | solution.py:397
  94.9 2.8 %collective-permute-done.23.refs_5_ = bf16[768,128]{1,0:T(8,128)(2,1)S(1)} collective-permute-done((bf16[768,128]{1,0:T(8,128)(2,1)S(1)}, bf16[768,128]{1,0:T(8,128)(2,1)S(1)}, u32[]{:S(2)}, u32[]{:S(2)}) %collective-permute-start.23) | collective-permute-done | bytes 196640 | tf_op jit(solution)/shard_map/returns_1/ppermute | solution.py:397
  99.2 3.4 %collective-permute-done.25.refs_6_ = bf16[768,128]{1,0:T(8,128)(2,1)S(1)} collective-permute-done((bf16[768,128]{1,0:T(8,128)(2,1)S(1)}, bf16[768,128]{1,0:T(8,128)(2,1)S(1)}, u32[]{:S(2)}, u32[]{:S(2)}) %collective-permute-start.25) | collective-permute-done | bytes 196640 | tf_op jit(solution)/shard_map/returns_1/ppermute | solution.py:397
  102.6 4.2 %collective-permute-start.28 = (bf16[576,128]{1,0:T(8,128)(2,1)S(1)}, bf16[576,128]{1,0:T(8,128)(2,1)S(1)}, u32[]{:S(2)}, u32[]{:S(2)}) collective-permute-start(bf16[576,128]{1,0:T(8,128)(2,1)S(1)} %get-tuple-element.146), channel_id=1, source_target_pairs={{0,4},{4,0},{8,12},{12,8},{1,5},{5,1},{9,13},{13,9},{2,6},{6,2},{1... | collective-permute-start | bytes 442376 | tf_op jit(solution)/shard_map/returns_last/ppermute | solution.py:397
  (64 shorter events, 17.7 us)
Async XLA Ops:
  3.2 15.9 %collective-permute-start.3 = (bf16[1152,128]{1,0:T(8,128)(2,1)}, bf16[1152,128]{1,0:T(8,128)(2,1)S(1)}, u32[]{:S(2)}, u32[]{:S(2)}) collective-permute-start(bf16[1152,128]{1,0:T(8,128)(2,1)} %get-tuple-element.81), channel_id=1, source_target_pairs={{0,4},{4,0},{8,12},{12,8},{1,5},{5,1},{9,13},{13,9},{2,6},{6,2},{1... | collective-permute-start | bytes 884744 | tf_op jit(solution)/shard_map/keys_queries/ppermute | solution.py:397
  6.3 23.7 %collective-permute-start.4 = (bf16[1152,128]{1,0:T(8,128)(2,1)}, bf16[1152,128]{1,0:T(8,128)(2,1)S(1)}, u32[]{:S(2)}, u32[]{:S(2)}) collective-permute-start(bf16[1152,128]{1,0:T(8,128)(2,1)} %get-tuple-element.82), channel_id=1, source_target_pairs={{0,8},{4,12},{8,0},{12,4},{1,9},{5,13},{9,1},{13,5},{2,10},{6,14},... | collective-permute-start | bytes 884744 | tf_op jit(solution)/shard_map/keys_queries/ppermute | solution.py:397
  8.9 21.1 %collective-permute-start.5 = (bf16[1152,128]{1,0:T(8,128)(2,1)}, bf16[1152,128]{1,0:T(8,128)(2,1)S(1)}, u32[]{:S(2)}, u32[]{:S(2)}) collective-permute-start(bf16[1152,128]{1,0:T(8,128)(2,1)} %get-tuple-element.83), channel_id=1, source_target_pairs={{0,12},{4,8},{8,4},{12,0},{1,13},{5,9},{9,5},{13,1},{2,14},{6,10},... | collective-permute-start | bytes 884744 | tf_op jit(solution)/shard_map/keys_queries/ppermute | solution.py:397
  13.9 16.1 %collective-permute-start.9 = (bf16[576,128]{1,0:T(8,128)(2,1)S(1)}, bf16[576,128]{1,0:T(8,128)(2,1)S(1)}, u32[]{:S(2)}, u32[]{:S(2)}) collective-permute-start(bf16[576,128]{1,0:T(8,128)(2,1)S(1)} %slice.9), channel_id=1, source_target_pairs={{0,16},{16,0},{1,17},{17,1},{2,18},{18,2},{3,19},{19,3},{4,20},{20... | collective-permute-start | bytes 442376 | tf_op jit(solution)/shard_map/halo_queries/ppermute | solution.py:464
  30.6 13.2 %collective-permute-start.10 = (bf16[1728,128]{1,0:T(8,128)(2,1)S(1)}, bf16[1728,128]{1,0:T(8,128)(2,1)S(1)}, u32[]{:S(2)}, u32[]{:S(2)}) collective-permute-start(bf16[1728,128]{1,0:T(8,128)(2,1)S(1)} %halo_queries.1), channel_id=1, source_target_pairs={{0,16},{16,0},{1,17},{17,1},{2,18},{18,2},{3,19},{19,3},{4,20},{20... | collective-permute-start | bytes 1327112 | tf_op jit(solution)/shard_map/halo_queries/ppermute | solution.py:464
  32.2 15.4 %collective-permute-start.6 = (bf16[832,128]{1,0:T(8,128)(2,1)S(1)}, bf16[832,128]{1,0:T(8,128)(2,1)S(1)}, u32[]{:S(2)}, u32[]{:S(2)}) collective-permute-start(bf16[832,128]{1,0:T(8,128)(2,1)S(1)} %get-tuple-element.85), channel_id=1, source_target_pairs={{0,12},{4,8},{8,4},{12,0},{1,13},{5,9},{9,5},{13,1},{2,14},{6,10},... | collective-permute-start | bytes 638984 | tf_op jit(solution)/shard_map/grads/ppermute | solution.py:397
  34.7 19.4 %collective-permute-start.7 = (bf16[832,128]{1,0:T(8,128)(2,1)S(1)}, bf16[832,128]{1,0:T(8,128)(2,1)S(1)}, u32[]{:S(2)}, u32[]{:S(2)}) collective-permute-start(bf16[832,128]{1,0:T(8,128)(2,1)S(1)} %get-tuple-element.88), channel_id=1, source_target_pairs={{0,8},{4,12},{8,0},{12,4},{1,9},{5,13},{9,1},{13,5},{2,10},{6,14},... | collective-permute-start | bytes 638984 | tf_op jit(solution)/shard_map/grads/ppermute | solution.py:397
  43.8 10.2 %collective-permute-start.8 = (bf16[832,128]{1,0:T(8,128)(2,1)S(1)}, bf16[832,128]{1,0:T(8,128)(2,1)S(1)}, u32[]{:S(2)}, u32[]{:S(2)}) collective-permute-start(bf16[832,128]{1,0:T(8,128)(2,1)S(1)} %get-tuple-element.91), channel_id=1, source_target_pairs={{0,4},{4,0},{8,12},{12,8},{1,5},{5,1},{9,13},{13,9},{2,6},{6,2},{1... | collective-permute-start | bytes 638984 | tf_op jit(solution)/shard_map/grads/ppermute | solution.py:397
  43.9 10.2 %collective-permute-start.11 = (bf16[832,128]{1,0:T(8,128)(2,1)S(1)}, bf16[832,128]{1,0:T(8,128)(2,1)S(1)}, u32[]{:S(2)}, u32[]{:S(2)}) collective-permute-start(bf16[832,128]{1,0:T(8,128)(2,1)S(1)} %get-tuple-element.120.refs_0_.refs_14_.refs_26_.refs_50_), channel_id=1, source_target_pairs={{0,16},{16,0},{1,17},{17,1},{2,18},{18,2},{3,19},{19,3},{4,20},{20... | collective-permute-start | bytes 638984 | tf_op jit(solution)/shard_map/halo_own_grads/ppermute | solution.py:464
  54.4 8.7 %collective-permute-start.12 = (bf16[768,128]{1,0:T(8,128)(2,1)S(1)}, bf16[768,128]{1,0:T(8,128)(2,1)S(1)}, u32[]{:S(2)}, u32[]{:S(2)}) collective-permute-start(bf16[768,128]{1,0:T(8,128)(2,1)S(1)} %halo_first_grads.1), channel_id=1, source_target_pairs={{0,16},{16,0},{1,17},{17,1},{2,18},{18,2},{3,19},{19,3},{4,20},{20... | collective-permute-start | bytes 589832 | tf_op jit(solution)/shard_map/halo_first_grads/ppermute | solution.py:464
  55.1 10.5 %collective-permute-start.13 = (f32[6,768]{1,0:T(8,128)S(1)}, f32[6,768]{1,0:T(8,128)S(1)}, u32[]{:S(2)}, u32[]{:S(2)}) collective-permute-start(f32[6,768]{1,0:T(8,128)S(1)} %pad_maximum_fusion), channel_id=1, source_target_pairs={{0,16},{16,0},{1,17},{17,1},{2,18},{18,2},{3,19},{19,3},{4,20},{20... | collective-permute-start | bytes 55304 | tf_op jit(solution)/shard_map/totals/ppermute | solution.py:441
  56.7 12.6 %collective-permute-start.15 = (bf16[384,128]{1,0:T(8,128)(2,1)S(1)}, bf16[384,128]{1,0:T(8,128)(2,1)S(1)}, u32[]{:S(2)}, u32[]{:S(2)}) collective-permute-start(bf16[384,128]{1,0:T(8,128)(2,1)S(1)} %get-tuple-element.115), channel_id=1, source_target_pairs={{0,12},{4,8},{8,4},{12,0},{1,13},{5,9},{9,5},{13,1},{2,14},{6,10},... | collective-permute-start | bytes 294920 | tf_op jit(solution)/shard_map/rest_values/ppermute | solution.py:397
  59.3 12.1 %collective-permute-start.16 = (bf16[384,128]{1,0:T(8,128)(2,1)S(1)}, bf16[384,128]{1,0:T(8,128)(2,1)S(1)}, u32[]{:S(2)}, u32[]{:S(2)}) collective-permute-start(bf16[384,128]{1,0:T(8,128)(2,1)S(1)} %get-tuple-element.117), channel_id=1, source_target_pairs={{0,8},{4,12},{8,0},{12,4},{1,9},{5,13},{9,1},{13,5},{2,10},{6,14},... | collective-permute-start | bytes 294920 | tf_op jit(solution)/shard_map/rest_values/ppermute | solution.py:397
  63.1 11.6 %collective-permute-start.17 = (bf16[384,128]{1,0:T(8,128)(2,1)S(1)}, bf16[384,128]{1,0:T(8,128)(2,1)S(1)}, u32[]{:S(2)}, u32[]{:S(2)}) collective-permute-start(bf16[384,128]{1,0:T(8,128)(2,1)S(1)} %get-tuple-element.119), channel_id=1, source_target_pairs={{0,4},{4,0},{8,12},{12,8},{1,5},{5,1},{9,13},{13,9},{2,6},{6,2},{1... | collective-permute-start | bytes 294920 | tf_op jit(solution)/shard_map/rest_values/ppermute | solution.py:397
  63.7 11.0 %collective-permute-start.18 = (bf16[1152,128]{1,0:T(8,128)(2,1)S(1)}, bf16[1152,128]{1,0:T(8,128)(2,1)S(1)}, u32[]{:S(2)}, u32[]{:S(2)}) collective-permute-start(bf16[1152,128]{1,0:T(8,128)(2,1)S(1)} %halo_rest_grads.1), channel_id=1, source_target_pairs={{0,16},{16,0},{1,17},{17,1},{2,18},{18,2},{3,19},{19,3},{4,20},{20... | collective-permute-start | bytes 884744 | tf_op jit(solution)/shard_map/halo_rest_grads/ppermute | solution.py:464
  68.9 16.6 %collective-permute-start.14 = (bf16[768,128]{1,0:T(8,128)(2,1)S(1)}, bf16[768,128]{1,0:T(8,128)(2,1)S(1)}, u32[]{:S(2)}, u32[]{:S(2)}) collective-permute-start(bf16[768,128]{1,0:T(8,128)(2,1)S(1)} %get-tuple-element.105), channel_id=1, source_target_pairs={{0,16},{16,0},{1,17},{17,1},{2,18},{18,2},{3,19},{19,3},{4,20},{20... | collective-permute-start | bytes 589832 | tf_op jit(solution)/shard_map/halo_query_grads_0/ppermute | solution.py:543
  69.3 11.9 %collective-permute-start.19 = (bf16[384,128]{1,0:T(8,128)(2,1)S(1)}, bf16[384,128]{1,0:T(8,128)(2,1)S(1)}, u32[]{:S(2)}, u32[]{:S(2)}) collective-permute-start(bf16[384,128]{1,0:T(8,128)(2,1)S(1)} %get-tuple-element.127), channel_id=1, source_target_pairs={{0,12},{4,8},{8,4},{12,0},{1,13},{5,9},{9,5},{13,1},{2,14},{6,10},... | collective-permute-start | bytes 294920 | tf_op jit(solution)/shard_map/returns_0/ppermute | solution.py:397
  71.4 14.1 %collective-permute-start.20 = (bf16[384,128]{1,0:T(8,128)(2,1)S(1)}, bf16[384,128]{1,0:T(8,128)(2,1)S(1)}, u32[]{:S(2)}, u32[]{:S(2)}) collective-permute-start(bf16[384,128]{1,0:T(8,128)(2,1)S(1)} %get-tuple-element.129), channel_id=1, source_target_pairs={{0,8},{4,12},{8,0},{12,4},{1,9},{5,13},{9,1},{13,5},{2,10},{6,14},... | collective-permute-start | bytes 294920 | tf_op jit(solution)/shard_map/returns_0/ppermute | solution.py:397
  74.7 10.8 %collective-permute-start.21 = (bf16[384,128]{1,0:T(8,128)(2,1)S(1)}, bf16[384,128]{1,0:T(8,128)(2,1)S(1)}, u32[]{:S(2)}, u32[]{:S(2)}) collective-permute-start(bf16[384,128]{1,0:T(8,128)(2,1)S(1)} %get-tuple-element.131), channel_id=1, source_target_pairs={{0,4},{4,0},{8,12},{12,8},{1,5},{5,1},{9,13},{13,9},{2,6},{6,2},{1... | collective-permute-start | bytes 294920 | tf_op jit(solution)/shard_map/returns_0/ppermute | solution.py:397
  85.5 9.3 %collective-permute-start.22 = (bf16[1536,128]{1,0:T(8,128)(2,1)S(1)}, bf16[1536,128]{1,0:T(8,128)(2,1)S(1)}, u32[]{:S(2)}, u32[]{:S(2)}) collective-permute-start(bf16[1536,128]{1,0:T(8,128)(2,1)S(1)} %get-tuple-element.133), channel_id=1, source_target_pairs={{0,16},{16,0},{1,17},{17,1},{2,18},{18,2},{3,19},{19,3},{4,20},{20... | collective-permute-start | bytes 1179656 | tf_op jit(solution)/shard_map/halo_query_grads_1/ppermute | solution.py:543
  89.0 8.7 %collective-permute-start.23 = (bf16[768,128]{1,0:T(8,128)(2,1)S(1)}, bf16[768,128]{1,0:T(8,128)(2,1)S(1)}, u32[]{:S(2)}, u32[]{:S(2)}) collective-permute-start(bf16[768,128]{1,0:T(8,128)(2,1)S(1)} %get-tuple-element.137), channel_id=1, source_target_pairs={{0,12},{4,8},{8,4},{12,0},{1,13},{5,9},{9,5},{13,1},{2,14},{6,10},... | collective-permute-start | bytes 589832 | tf_op jit(solution)/shard_map/returns_1/ppermute | solution.py:397
  89.8 12.8 %collective-permute-start.25 = (bf16[768,128]{1,0:T(8,128)(2,1)S(1)}, bf16[768,128]{1,0:T(8,128)(2,1)S(1)}, u32[]{:S(2)}, u32[]{:S(2)}) collective-permute-start(bf16[768,128]{1,0:T(8,128)(2,1)S(1)} %get-tuple-element.141), channel_id=1, source_target_pairs={{0,8},{4,12},{8,0},{12,4},{1,9},{5,13},{9,1},{13,5},{2,10},{6,14},... | collective-permute-start | bytes 589832 | tf_op jit(solution)/shard_map/returns_1/ppermute | solution.py:397
  89.8 12.8 %collective-permute-start.27 = (bf16[768,128]{1,0:T(8,128)(2,1)S(1)}, bf16[768,128]{1,0:T(8,128)(2,1)S(1)}, u32[]{:S(2)}, u32[]{:S(2)}) collective-permute-start(bf16[768,128]{1,0:T(8,128)(2,1)S(1)} %get-tuple-element.145), channel_id=1, source_target_pairs={{0,4},{4,0},{8,12},{12,8},{1,5},{5,1},{9,13},{13,9},{2,6},{6,2},{1... | collective-permute-start | bytes 589832 | tf_op jit(solution)/shard_map/returns_1/ppermute | solution.py:397
  97.7 11.0 %collective-permute-start.24 = (bf16[576,128]{1,0:T(8,128)(2,1)S(1)}, bf16[576,128]{1,0:T(8,128)(2,1)S(1)}, u32[]{:S(2)}, u32[]{:S(2)}) collective-permute-start(bf16[576,128]{1,0:T(8,128)(2,1)S(1)} %get-tuple-element.138), channel_id=1, source_target_pairs={{0,12},{4,8},{8,4},{12,0},{1,13},{5,9},{9,5},{13,1},{2,14},{6,10},... | collective-permute-start | bytes 442376 | tf_op jit(solution)/shard_map/returns_last/ppermute | solution.py:397
  (10 other events, 55.9 us)

commit v14 on v13

--- a/solution.py
+++ b/solution.py
@@ -11,7 +11,7 @@
 HD = 128
 LANES = 128
 TILE_ROWS = 16
-KEY_BLOCK = 256
+KEY_BLOCK = 768
 QUERY_BLOCK = 256
 VMEM_LIMIT = 48 * 1024 * 1024
 VMEM_WHOLE = 62 * 1024 * 1024
@@ -475,6 +475,8 @@
             gain = sum_over(gain, "tm")
     with jax.named_scope("grads"):
         sent_lead = pack_grads(out_grad[0], attn_out[0], values[0], out_gain, gain, parts)
+    with jax.named_scope("halo_own_grads"):
+        own_side = forward(sent_lead[0])
     with jax.named_scope("halo_queries"):
         width = heads * rows
         first_side = forward(pairs[0][width:])
@@ -485,8 +487,6 @@
         late_side = forward(gather_rows(late, [(number, width, width) for number in range(parts - 1)]))
     base = (heads + 1) * rows
     extra = gain_depth(channels)
-    with jax.named_scope("halo_own_grads"):
-        own_side = forward(after(sent_lead[:1], late_side)[0])
     with jax.named_scope("totals"):
         key_places = [[(piece, head) for piece in pairs] for head in range(heads)]
         query_places = [[[(piece, heads + head) for piece in pairs] for head in range(heads)]]

time: 112 us -> 110 us (0.982)
  starting transfers between devices: 52 us -> 46.3 us
  waiting for transfers between devices: 37.5 us -> 41.5 us
    ppermute x21, starting transfers between devices: 41.1 us -> 36.9 us  [swap(): lax.ppermute(value, axis, [(index, index ^ distance) for index in range(l...]
    ppermute x21, waiting for transfers between devices: 36.1 us -> 39.3 us  [swap(): lax.ppermute(value, axis, [(index, index ^ distance) for index in range(l...]
    ppermute x2, starting transfers between devices: 3.87 us -> 2.16 us  [local(): lax.ppermute(other, 'tm', back)]
where the time goes in v14:
time: 110 us
  starting transfers between devices  46.3 us (42%)
  waiting for transfers between devices  41.5 us (38%)
  Pallas kernels  21 us (19%)
    ppermute x21, waiting for transfers between devices, swap(): lax.ppermute(value, axis, [(index, index ^ distance) for index in range(l...  39.3 us
    ppermute x21, starting transfers between devices, swap(): lax.ppermute(value, axis, [(index, index ^ distance) for index in range(l...  36.9 us
    pallas_call x2, Pallas kernels, attention(): pl.pallas_call(functools.partial(attention_kernel, parts, sources, chosen...  9.54 us
    ppermute x5, starting transfers between devices, forward(): return [lax.ppermute(array, 'tm', there) for there, _ in sides]  6.69 us
    pallas_call x1, Pallas kernels, partial_totals(): pl.pallas_call(functools.partial(totals_kernel, parts, sources, heads), g...  3.85 us
    pallas_call x2, Pallas kernels, pack(): pl.pallas_call(functools.partial(pack_kernel, parts, chosen), in_specs=[w...  2.75 us
  transfers between devices with their start and end apart: 29, of which 11 were waited for; matrix products, arithmetic and copies ran while one was open for 0% of the time, Pallas kernels for 15%

profile of v14, /device:TPU:0, one launch (start us, length us, event | category | flops | bytes accessed | tf_op | source)
XLA Modules:
  0.0 110.1 jit_solution(13856660520380710618)
XLA Ops:
  0.7 2.6 %keys_queries.1 = (bf16[1152,128]{1,0:T(8,128)(2,1)}, bf16[1152,128]{1,0:T(8,128)(2,1)}, bf16[1152,128]{1,0:T(8,128)(2,1)}, bf16[1152,128]{1,0:T(8,128)(2,1)}) custom-call(bf16[192,1536]{1,0:T(8,128)(2,1)} %bitcast.17, bf16[192,1536]{1,0:T(8,128)(2,1)} %bitcast.18), custom_call_target="tpu_custom_call" | custom-call | flops 1 | bytes 1 | tf_op jit(solution)/shard_map/keys_queries/pallas_call | solution.py:64
  3.2 3.1 %collective-permute-start.3 = (bf16[1152,128]{1,0:T(8,128)(2,1)}, bf16[1152,128]{1,0:T(8,128)(2,1)S(1)}, u32[]{:S(2)}, u32[]{:S(2)}) collective-permute-start(bf16[1152,128]{1,0:T(8,128)(2,1)} %get-tuple-element.80), channel_id=1, source_target_pairs={{0,4},{4,0},{8,12},{12,8},{1,5},{5,1},{9,13},{13,9},{2,6},{6,2},{1... | collective-permute-start | bytes 884744 | tf_op jit(solution)/shard_map/keys_queries/ppermute | solution.py:397
  6.3 2.6 %collective-permute-start.4 = (bf16[1152,128]{1,0:T(8,128)(2,1)}, bf16[1152,128]{1,0:T(8,128)(2,1)S(1)}, u32[]{:S(2)}, u32[]{:S(2)}) collective-permute-start(bf16[1152,128]{1,0:T(8,128)(2,1)} %get-tuple-element.81), channel_id=1, source_target_pairs={{0,8},{4,12},{8,0},{12,4},{1,9},{5,13},{9,1},{13,5},{2,10},{6,14},... | collective-permute-start | bytes 884744 | tf_op jit(solution)/shard_map/keys_queries/ppermute | solution.py:397
  9.1 1.8 %collective-permute-start.1 = (f32[12,128]{1,0:T(8,128)S(1)}, f32[12,128]{1,0:T(8,128)S(1)}, u32[]{:S(2)}, u32[]{:S(2)}) collective-permute-start(f32[12,128]{1,0:T(8,128)S(1)} %bitcast.20), channel_id=1, source_target_pairs={{0,2},{1,3},{2,0},{3,1},{4,6},{5,7},{6,4},{7,5},{8,10},{9,11},{10,... | collective-permute-start | bytes 18440 | tf_op jit(solution)/shard_map/gain/ppermute | solution.py:397
  10.9 1.9 %collective-permute-done.1 = f32[12,128]{1,0:T(8,128)S(1)} collective-permute-done((f32[12,128]{1,0:T(8,128)S(1)}, f32[12,128]{1,0:T(8,128)S(1)}, u32[]{:S(2)}, u32[]{:S(2)}) %collective-permute-start.1) | collective-permute-done | bytes 6176 | tf_op jit(solution)/shard_map/gain/ppermute | solution.py:397
  16.0 3.1 %collective-permute-done.3.refs_2_.refs_3_.refs_7_.refs_11_.refs_15_.refs_19_.refs_23_.refs_13_.refs_21_.refs_37_.refs_45_ = bf16[1152,128]{1,0:T(8,128)(2,1)S(1)} collective-permute-done((bf16[1152,128]{1,0:T(8,128)(2,1)}, bf16[1152,128]{1,0:T(8,128)(2,1)S(1)}, u32[]{:S(2)}, u32[]{:S(2)}) %collective-permute-start.3) | collective-permute-done | bytes 294944 | tf_op jit(solution)/shard_map/keys_queries/ppermute | solution.py:397
  19.1 10.9 %collective-permute-done.4.refs_1_.refs_2_.refs_6_.refs_10_.refs_14_.refs_18_.refs_22_.refs_12_.refs_20_.refs_36_.refs_44_ = bf16[1152,128]{1,0:T(8,128)(2,1)S(1)} collective-permute-done((bf16[1152,128]{1,0:T(8,128)(2,1)}, bf16[1152,128]{1,0:T(8,128)(2,1)S(1)}, u32[]{:S(2)}, u32[]{:S(2)}) %collective-permute-start.4) | collective-permute-done | bytes 294944 | tf_op jit(solution)/shard_map/keys_queries/ppermute | solution.py:397
  32.7 2.5 %collective-permute-start.6 = (bf16[832,128]{1,0:T(8,128)(2,1)S(1)}, bf16[832,128]{1,0:T(8,128)(2,1)S(1)}, u32[]{:S(2)}, u32[]{:S(2)}) collective-permute-start(bf16[832,128]{1,0:T(8,128)(2,1)S(1)} %get-tuple-element.84), channel_id=1, source_target_pairs={{0,12},{4,8},{8,4},{12,0},{1,13},{5,9},{9,5},{13,1},{2,14},{6,10},... | collective-permute-start | bytes 638984 | tf_op jit(solution)/shard_map/grads/ppermute | solution.py:397
  35.2 6.7 %collective-permute-start.7 = (bf16[832,128]{1,0:T(8,128)(2,1)S(1)}, bf16[832,128]{1,0:T(8,128)(2,1)S(1)}, u32[]{:S(2)}, u32[]{:S(2)}) collective-permute-start(bf16[832,128]{1,0:T(8,128)(2,1)S(1)} %get-tuple-element.87), channel_id=1, source_target_pairs={{0,8},{4,12},{8,0},{12,4},{1,9},{5,13},{9,1},{13,5},{2,10},{6,14},... | collective-permute-start | bytes 638984 | tf_op jit(solution)/shard_map/grads/ppermute | solution.py:397
  42.4 3.8 %totals.1 = (f32[3,768]{1,0:T(4,128)S(1)}, f32[3,768]{1,0:T(4,128)S(1)}) custom-call(bf16[1152,128]{1,0:T(8,128)(2,1)S(1)} %copy-done, bf16[1152,128]{1,0:T(8,128)(2,1)S(1)} %collective-permute-done.5.refs_0_.refs_1_.refs_5_.refs_9_.refs_13_.refs_17_.refs_21_.refs_11_.refs_19_.refs_35_.refs_43_, ...), custom_call_target="tpu_custom_call" | custom-call | flops 905969664 | bytes 2359296 | tf_op jit(solution)/shard_map/totals/pallas_call | solution.py:240
  46.3 7.9 %collective-permute-done.7.refs_2_.refs_16_.refs_28_.refs_52_ = bf16[832,128]{1,0:T(8,128)(2,1)S(1)} collective-permute-done((bf16[832,128]{1,0:T(8,128)(2,1)S(1)}, bf16[832,128]{1,0:T(8,128)(2,1)S(1)}, u32[]{:S(2)}, u32[]{:S(2)}) %collective-permute-start.7) | collective-permute-done | bytes 213024 | tf_op jit(solution)/shard_map/grads/ppermute | solution.py:397
  56.8 2.7 %collective-permute-start.15 = (bf16[384,128]{1,0:T(8,128)(2,1)S(1)}, bf16[384,128]{1,0:T(8,128)(2,1)S(1)}, u32[]{:S(2)}, u32[]{:S(2)}) collective-permute-start(bf16[384,128]{1,0:T(8,128)(2,1)S(1)} %get-tuple-element.113), channel_id=1, source_target_pairs={{0,12},{4,8},{8,4},{12,0},{1,13},{5,9},{9,5},{13,1},{2,14},{6,10},... | collective-permute-start | bytes 294920 | tf_op jit(solution)/shard_map/rest_values/ppermute | solution.py:397
  59.5 1.7 %collective-permute-start.17 = (bf16[384,128]{1,0:T(8,128)(2,1)S(1)}, bf16[384,128]{1,0:T(8,128)(2,1)S(1)}, u32[]{:S(2)}, u32[]{:S(2)}) collective-permute-start(bf16[384,128]{1,0:T(8,128)(2,1)S(1)} %get-tuple-element.117), channel_id=1, source_target_pairs={{0,4},{4,0},{8,12},{12,8},{1,5},{5,1},{9,13},{13,9},{2,6},{6,2},{1... | collective-permute-start | bytes 294920 | tf_op jit(solution)/shard_map/rest_values/ppermute | solution.py:397
  63.5 3.3 %attention_0.1 = (bf16[384,128]{1,0:T(8,128)(2,1)S(1)}, bf16[384,128]{1,0:T(8,128)(2,1)S(1)}, bf16[384,128]{1,0:T(8,128)(2,1)S(1)}, bf16[384,128]{1,0:T(8,128)(2...) custom-call(bf16[832,128]{1,0:T(8,128)(2,1)S(1)} %get-tuple-element.118.refs_0_.refs_14_.refs_26_.refs_50_, ...), custom_call_target="tpu_custom_call" | custom-call | flops 1509949440 | bytes 3145728 | tf_op jit(solution)/shard_map/attention_0/pallas_call | solution.py:325
  67.3 2.6 %collective-permute-start.19 = (bf16[384,128]{1,0:T(8,128)(2,1)S(1)}, bf16[384,128]{1,0:T(8,128)(2,1)S(1)}, u32[]{:S(2)}, u32[]{:S(2)}) collective-permute-start(bf16[384,128]{1,0:T(8,128)(2,1)S(1)} %get-tuple-element.125), channel_id=1, source_target_pairs={{0,12},{4,8},{8,4},{12,0},{1,13},{5,9},{9,5},{13,1},{2,14},{6,10},... | collective-permute-start | bytes 294920 | tf_op jit(solution)/shard_map/returns_0/ppermute | solution.py:397
  70.0 1.7 %collective-permute-start.21 = (bf16[384,128]{1,0:T(8,128)(2,1)S(1)}, bf16[384,128]{1,0:T(8,128)(2,1)S(1)}, u32[]{:S(2)}, u32[]{:S(2)}) collective-permute-start(bf16[384,128]{1,0:T(8,128)(2,1)S(1)} %get-tuple-element.129), channel_id=1, source_target_pairs={{0,4},{4,0},{8,12},{12,8},{1,5},{5,1},{9,13},{13,9},{2,6},{6,2},{1... | collective-permute-start | bytes 294920 | tf_op jit(solution)/shard_map/returns_0/ppermute | solution.py:397
  71.7 6.3 %attention_1.1 = (bf16[768,128]{1,0:T(8,128)(2,1)S(1)}, bf16[768,128]{1,0:T(8,128)(2,1)S(1)}, bf16[768,128]{1,0:T(8,128)(2,1)S(1)}, bf16[768,128]{1,0:T(8,128)(2...) custom-call(bf16[832,128]{1,0:T(8,128)(2,1)S(1)} %get-tuple-element.118.refs_0_.refs_14_.refs_26_.refs_50_, ...), custom_call_target="tpu_custom_call" | custom-call | flops 3019898880 | bytes 6291456 | tf_op jit(solution)/shard_map/attention_1/pallas_call | solution.py:325
  79.6 2.6 %collective-permute-start.23 = (bf16[768,128]{1,0:T(8,128)(2,1)S(1)}, bf16[768,128]{1,0:T(8,128)(2,1)S(1)}, u32[]{:S(2)}, u32[]{:S(2)}) collective-permute-start(bf16[768,128]{1,0:T(8,128)(2,1)S(1)} %get-tuple-element.135), channel_id=1, source_target_pairs={{0,12},{4,8},{8,4},{12,0},{1,13},{5,9},{9,5},{13,1},{2,14},{6,10},... | collective-permute-start | bytes 589832 | tf_op jit(solution)/shard_map/returns_1/ppermute | solution.py:397
  82.3 1.7 %collective-permute-start.27 = (bf16[768,128]{1,0:T(8,128)(2,1)S(1)}, bf16[768,128]{1,0:T(8,128)(2,1)S(1)}, u32[]{:S(2)}, u32[]{:S(2)}) collective-permute-start(bf16[768,128]{1,0:T(8,128)(2,1)S(1)} %get-tuple-element.143), channel_id=1, source_target_pairs={{0,4},{4,0},{8,12},{12,8},{1,5},{5,1},{9,13},{13,9},{2,6},{6,2},{1... | collective-permute-start | bytes 589832 | tf_op jit(solution)/shard_map/returns_1/ppermute | solution.py:397
  84.0 1.9 %collective-permute-done.22.refs_3_ = bf16[1536,128]{1,0:T(8,128)(2,1)S(1)} collective-permute-done((bf16[1536,128]{1,0:T(8,128)(2,1)S(1)}, bf16[1536,128]{1,0:T(8,128)(2,1)S(1)}, u32[]{:S(2)}, u32[]{:S(2)}) %collective-permute-start.22) | collective-permute-done | bytes 393248 | tf_op jit(solution)/shard_map/halo_query_grads_1/ppermute | solution.py:543
  86.0 3.4 %collective-permute-done.23.refs_5_ = bf16[768,128]{1,0:T(8,128)(2,1)S(1)} collective-permute-done((bf16[768,128]{1,0:T(8,128)(2,1)S(1)}, bf16[768,128]{1,0:T(8,128)(2,1)S(1)}, u32[]{:S(2)}, u32[]{:S(2)}) %collective-permute-start.23) | collective-permute-done | bytes 196640 | tf_op jit(solution)/shard_map/returns_1/ppermute | solution.py:397
  89.4 2.7 %collective-permute-start.24 = (bf16[576,128]{1,0:T(8,128)(2,1)S(1)}, bf16[576,128]{1,0:T(8,128)(2,1)S(1)}, u32[]{:S(2)}, u32[]{:S(2)}) collective-permute-start(bf16[576,128]{1,0:T(8,128)(2,1)S(1)} %get-tuple-element.136), channel_id=1, source_target_pairs={{0,12},{4,8},{8,4},{12,0},{1,13},{5,9},{9,5},{13,1},{2,14},{6,10},... | collective-permute-start | bytes 442376 | tf_op jit(solution)/shard_map/returns_last/ppermute | solution.py:397
  92.0 8.9 %collective-permute-done.25.refs_6_ = bf16[768,128]{1,0:T(8,128)(2,1)S(1)} collective-permute-done((bf16[768,128]{1,0:T(8,128)(2,1)S(1)}, bf16[768,128]{1,0:T(8,128)(2,1)S(1)}, u32[]{:S(2)}, u32[]{:S(2)}) %collective-permute-start.25) | collective-permute-done | bytes 196640 | tf_op jit(solution)/shard_map/returns_1/ppermute | solution.py:397
  100.9 4.2 %collective-permute-start.28 = (bf16[576,128]{1,0:T(8,128)(2,1)S(1)}, bf16[576,128]{1,0:T(8,128)(2,1)S(1)}, u32[]{:S(2)}, u32[]{:S(2)}) collective-permute-start(bf16[576,128]{1,0:T(8,128)(2,1)S(1)} %get-tuple-element.144), channel_id=1, source_target_pairs={{0,4},{4,0},{8,12},{12,8},{1,5},{5,1},{9,13},{13,9},{2,6},{6,2},{1... | collective-permute-start | bytes 442376 | tf_op jit(solution)/shard_map/returns_last/ppermute | solution.py:397
  (64 shorter events, 18.4 us)
Async XLA Ops:
  3.2 15.9 %collective-permute-start.3 = (bf16[1152,128]{1,0:T(8,128)(2,1)}, bf16[1152,128]{1,0:T(8,128)(2,1)S(1)}, u32[]{:S(2)}, u32[]{:S(2)}) collective-permute-start(bf16[1152,128]{1,0:T(8,128)(2,1)} %get-tuple-element.80), channel_id=1, source_target_pairs={{0,4},{4,0},{8,12},{12,8},{1,5},{5,1},{9,13},{13,9},{2,6},{6,2},{1... | collective-permute-start | bytes 884744 | tf_op jit(solution)/shard_map/keys_queries/ppermute | solution.py:397
  6.3 23.7 %collective-permute-start.4 = (bf16[1152,128]{1,0:T(8,128)(2,1)}, bf16[1152,128]{1,0:T(8,128)(2,1)S(1)}, u32[]{:S(2)}, u32[]{:S(2)}) collective-permute-start(bf16[1152,128]{1,0:T(8,128)(2,1)} %get-tuple-element.81), channel_id=1, source_target_pairs={{0,8},{4,12},{8,0},{12,4},{1,9},{5,13},{9,1},{13,5},{2,10},{6,14},... | collective-permute-start | bytes 884744 | tf_op jit(solution)/shard_map/keys_queries/ppermute | solution.py:397
  8.9 21.1 %collective-permute-start.5 = (bf16[1152,128]{1,0:T(8,128)(2,1)}, bf16[1152,128]{1,0:T(8,128)(2,1)S(1)}, u32[]{:S(2)}, u32[]{:S(2)}) collective-permute-start(bf16[1152,128]{1,0:T(8,128)(2,1)} %get-tuple-element.82), channel_id=1, source_target_pairs={{0,12},{4,8},{8,4},{12,0},{1,13},{5,9},{9,5},{13,1},{2,14},{6,10},... | collective-permute-start | bytes 884744 | tf_op jit(solution)/shard_map/keys_queries/ppermute | solution.py:397
  13.9 16.1 %collective-permute-start.10 = (bf16[576,128]{1,0:T(8,128)(2,1)S(1)}, bf16[576,128]{1,0:T(8,128)(2,1)S(1)}, u32[]{:S(2)}, u32[]{:S(2)}) collective-permute-start(bf16[576,128]{1,0:T(8,128)(2,1)S(1)} %slice.9), channel_id=1, source_target_pairs={{0,16},{16,0},{1,17},{17,1},{2,18},{18,2},{3,19},{19,3},{4,20},{20... | collective-permute-start | bytes 442376 | tf_op jit(solution)/shard_map/halo_queries/ppermute | solution.py:464
  30.6 11.8 %collective-permute-start.11 = (bf16[1728,128]{1,0:T(8,128)(2,1)S(1)}, bf16[1728,128]{1,0:T(8,128)(2,1)S(1)}, u32[]{:S(2)}, u32[]{:S(2)}) collective-permute-start(bf16[1728,128]{1,0:T(8,128)(2,1)S(1)} %halo_queries.1), channel_id=1, source_target_pairs={{0,16},{16,0},{1,17},{17,1},{2,18},{18,2},{3,19},{19,3},{4,20},{20... | collective-permute-start | bytes 1327112 | tf_op jit(solution)/shard_map/halo_queries/ppermute | solution.py:464
  32.2 14.1 %collective-permute-start.9 = (bf16[832,128]{1,0:T(8,128)(2,1)S(1)}, bf16[832,128]{1,0:T(8,128)(2,1)S(1)}, u32[]{:S(2)}, u32[]{:S(2)}) collective-permute-start(bf16[832,128]{1,0:T(8,128)(2,1)S(1)} %get-tuple-element.118.refs_0_.refs_14_.refs_26_.refs_50_), channel_id=1, source_target_pairs={{0,16},{16,0},{1,17},{17,1},{2,18},{18,2},{3,19},{19,3},{4,20},{20... | collective-permute-start | bytes 638984 | tf_op jit(solution)/shard_map/halo_own_grads/ppermute | solution.py:464
  32.7 13.5 %collective-permute-start.6 = (bf16[832,128]{1,0:T(8,128)(2,1)S(1)}, bf16[832,128]{1,0:T(8,128)(2,1)S(1)}, u32[]{:S(2)}, u32[]{:S(2)}) collective-permute-start(bf16[832,128]{1,0:T(8,128)(2,1)S(1)} %get-tuple-element.84), channel_id=1, source_target_pairs={{0,12},{4,8},{8,4},{12,0},{1,13},{5,9},{9,5},{13,1},{2,14},{6,10},... | collective-permute-start | bytes 638984 | tf_op jit(solution)/shard_map/grads/ppermute | solution.py:397
  35.2 18.9 %collective-permute-start.7 = (bf16[832,128]{1,0:T(8,128)(2,1)S(1)}, bf16[832,128]{1,0:T(8,128)(2,1)S(1)}, u32[]{:S(2)}, u32[]{:S(2)}) collective-permute-start(bf16[832,128]{1,0:T(8,128)(2,1)S(1)} %get-tuple-element.87), channel_id=1, source_target_pairs={{0,8},{4,12},{8,0},{12,4},{1,9},{5,13},{9,1},{13,5},{2,10},{6,14},... | collective-permute-start | bytes 638984 | tf_op jit(solution)/shard_map/grads/ppermute | solution.py:397
  41.9 12.2 %collective-permute-start.8 = (bf16[832,128]{1,0:T(8,128)(2,1)S(1)}, bf16[832,128]{1,0:T(8,128)(2,1)S(1)}, u32[]{:S(2)}, u32[]{:S(2)}) collective-permute-start(bf16[832,128]{1,0:T(8,128)(2,1)S(1)} %get-tuple-element.90), channel_id=1, source_target_pairs={{0,4},{4,0},{8,12},{12,8},{1,5},{5,1},{9,13},{13,9},{2,6},{6,2},{1... | collective-permute-start | bytes 638984 | tf_op jit(solution)/shard_map/grads/ppermute | solution.py:397
  56.8 10.5 %collective-permute-start.15 = (bf16[384,128]{1,0:T(8,128)(2,1)S(1)}, bf16[384,128]{1,0:T(8,128)(2,1)S(1)}, u32[]{:S(2)}, u32[]{:S(2)}) collective-permute-start(bf16[384,128]{1,0:T(8,128)(2,1)S(1)} %get-tuple-element.113), channel_id=1, source_target_pairs={{0,12},{4,8},{8,4},{12,0},{1,13},{5,9},{9,5},{13,1},{2,14},{6,10},... | collective-permute-start | bytes 294920 | tf_op jit(solution)/shard_map/rest_values/ppermute | solution.py:397
  59.5 10.5 %collective-permute-start.16 = (bf16[384,128]{1,0:T(8,128)(2,1)S(1)}, bf16[384,128]{1,0:T(8,128)(2,1)S(1)}, u32[]{:S(2)}, u32[]{:S(2)}) collective-permute-start(bf16[384,128]{1,0:T(8,128)(2,1)S(1)} %get-tuple-element.115), channel_id=1, source_target_pairs={{0,8},{4,12},{8,0},{12,4},{1,9},{5,13},{9,1},{13,5},{2,10},{6,14},... | collective-permute-start | bytes 294920 | tf_op jit(solution)/shard_map/rest_values/ppermute | solution.py:397
  59.5 10.5 %collective-permute-start.17 = (bf16[384,128]{1,0:T(8,128)(2,1)S(1)}, bf16[384,128]{1,0:T(8,128)(2,1)S(1)}, u32[]{:S(2)}, u32[]{:S(2)}) collective-permute-start(bf16[384,128]{1,0:T(8,128)(2,1)S(1)} %get-tuple-element.117), channel_id=1, source_target_pairs={{0,4},{4,0},{8,12},{12,8},{1,5},{5,1},{9,13},{13,9},{2,6},{6,2},{1... | collective-permute-start | bytes 294920 | tf_op jit(solution)/shard_map/rest_values/ppermute | solution.py:397
  61.9 9.9 %collective-permute-start.18 = (bf16[1152,128]{1,0:T(8,128)(2,1)S(1)}, bf16[1152,128]{1,0:T(8,128)(2,1)S(1)}, u32[]{:S(2)}, u32[]{:S(2)}) collective-permute-start(bf16[1152,128]{1,0:T(8,128)(2,1)S(1)} %halo_rest_grads.1), channel_id=1, source_target_pairs={{0,16},{16,0},{1,17},{17,1},{2,18},{18,2},{3,19},{19,3},{4,20},{20... | collective-permute-start | bytes 884744 | tf_op jit(solution)/shard_map/halo_rest_grads/ppermute | solution.py:464
  66.7 11.3 %collective-permute-start.14 = (bf16[768,128]{1,0:T(8,128)(2,1)S(1)}, bf16[768,128]{1,0:T(8,128)(2,1)S(1)}, u32[]{:S(2)}, u32[]{:S(2)}) collective-permute-start(bf16[768,128]{1,0:T(8,128)(2,1)S(1)} %get-tuple-element.103), channel_id=1, source_target_pairs={{0,16},{16,0},{1,17},{17,1},{2,18},{18,2},{3,19},{19,3},{4,20},{20... | collective-permute-start | bytes 589832 | tf_op jit(solution)/shard_map/halo_query_grads_0/ppermute | solution.py:543
  67.3 10.7 %collective-permute-start.19 = (bf16[384,128]{1,0:T(8,128)(2,1)S(1)}, bf16[384,128]{1,0:T(8,128)(2,1)S(1)}, u32[]{:S(2)}, u32[]{:S(2)}) collective-permute-start(bf16[384,128]{1,0:T(8,128)(2,1)S(1)} %get-tuple-element.125), channel_id=1, source_target_pairs={{0,12},{4,8},{8,4},{12,0},{1,13},{5,9},{9,5},{13,1},{2,14},{6,10},... | collective-permute-start | bytes 294920 | tf_op jit(solution)/shard_map/returns_0/ppermute | solution.py:397
  70.0 8.1 %collective-permute-start.20 = (bf16[384,128]{1,0:T(8,128)(2,1)S(1)}, bf16[384,128]{1,0:T(8,128)(2,1)S(1)}, u32[]{:S(2)}, u32[]{:S(2)}) collective-permute-start(bf16[384,128]{1,0:T(8,128)(2,1)S(1)} %get-tuple-element.127), channel_id=1, source_target_pairs={{0,8},{4,12},{8,0},{12,4},{1,9},{5,13},{9,1},{13,5},{2,10},{6,14},... | collective-permute-start | bytes 294920 | tf_op jit(solution)/shard_map/returns_0/ppermute | solution.py:397
  70.0 8.1 %collective-permute-start.21 = (bf16[384,128]{1,0:T(8,128)(2,1)S(1)}, bf16[384,128]{1,0:T(8,128)(2,1)S(1)}, u32[]{:S(2)}, u32[]{:S(2)}) collective-permute-start(bf16[384,128]{1,0:T(8,128)(2,1)S(1)} %get-tuple-element.129), channel_id=1, source_target_pairs={{0,4},{4,0},{8,12},{12,8},{1,5},{5,1},{9,13},{13,9},{2,6},{6,2},{1... | collective-permute-start | bytes 294920 | tf_op jit(solution)/shard_map/returns_0/ppermute | solution.py:397
  78.1 7.8 %collective-permute-start.22 = (bf16[1536,128]{1,0:T(8,128)(2,1)S(1)}, bf16[1536,128]{1,0:T(8,128)(2,1)S(1)}, u32[]{:S(2)}, u32[]{:S(2)}) collective-permute-start(bf16[1536,128]{1,0:T(8,128)(2,1)S(1)} %get-tuple-element.131), channel_id=1, source_target_pairs={{0,16},{16,0},{1,17},{17,1},{2,18},{18,2},{3,19},{19,3},{4,20},{20... | collective-permute-start | bytes 1179656 | tf_op jit(solution)/shard_map/halo_query_grads_1/ppermute | solution.py:543
  79.6 9.7 %collective-permute-start.23 = (bf16[768,128]{1,0:T(8,128)(2,1)S(1)}, bf16[768,128]{1,0:T(8,128)(2,1)S(1)}, u32[]{:S(2)}, u32[]{:S(2)}) collective-permute-start(bf16[768,128]{1,0:T(8,128)(2,1)S(1)} %get-tuple-element.135), channel_id=1, source_target_pairs={{0,12},{4,8},{8,4},{12,0},{1,13},{5,9},{9,5},{13,1},{2,14},{6,10},... | collective-permute-start | bytes 589832 | tf_op jit(solution)/shard_map/returns_1/ppermute | solution.py:397
  82.3 18.6 %collective-permute-start.25 = (bf16[768,128]{1,0:T(8,128)(2,1)S(1)}, bf16[768,128]{1,0:T(8,128)(2,1)S(1)}, u32[]{:S(2)}, u32[]{:S(2)}) collective-permute-start(bf16[768,128]{1,0:T(8,128)(2,1)S(1)} %get-tuple-element.139), channel_id=1, source_target_pairs={{0,8},{4,12},{8,0},{12,4},{1,9},{5,13},{9,1},{13,5},{2,10},{6,14},... | collective-permute-start | bytes 589832 | tf_op jit(solution)/shard_map/returns_1/ppermute | solution.py:397
  82.3 18.7 %collective-permute-start.27 = (bf16[768,128]{1,0:T(8,128)(2,1)S(1)}, bf16[768,128]{1,0:T(8,128)(2,1)S(1)}, u32[]{:S(2)}, u32[]{:S(2)}) collective-permute-start(bf16[768,128]{1,0:T(8,128)(2,1)S(1)} %get-tuple-element.143), channel_id=1, source_target_pairs={{0,4},{4,0},{8,12},{12,8},{1,5},{5,1},{9,13},{13,9},{2,6},{6,2},{1... | collective-permute-start | bytes 589832 | tf_op jit(solution)/shard_map/returns_1/ppermute | solution.py:397
  89.4 17.5 %collective-permute-start.24 = (bf16[576,128]{1,0:T(8,128)(2,1)S(1)}, bf16[576,128]{1,0:T(8,128)(2,1)S(1)}, u32[]{:S(2)}, u32[]{:S(2)}) collective-permute-start(bf16[576,128]{1,0:T(8,128)(2,1)S(1)} %get-tuple-element.136), channel_id=1, source_target_pairs={{0,12},{4,8},{8,4},{12,0},{1,13},{5,9},{9,5},{13,1},{2,14},{6,10},... | collective-permute-start | bytes 442376 | tf_op jit(solution)/shard_map/returns_last/ppermute | solution.py:397
  100.9 7.7 %collective-permute-start.26 = (bf16[576,128]{1,0:T(8,128)(2,1)S(1)}, bf16[576,128]{1,0:T(8,128)(2,1)S(1)}, u32[]{:S(2)}, u32[]{:S(2)}) collective-permute-start(bf16[576,128]{1,0:T(8,128)(2,1)S(1)} %get-tuple-element.140), channel_id=1, source_target_pairs={{0,8},{4,12},{8,0},{12,4},{1,9},{5,13},{9,1},{13,5},{2,10},{6,14},... | collective-permute-start | bytes 442376 | tf_op jit(solution)/shard_map/returns_last/ppermute | solution.py:397
  100.9 8.1 %collective-permute-start.28 = (bf16[576,128]{1,0:T(8,128)(2,1)S(1)}, bf16[576,128]{1,0:T(8,128)(2,1)S(1)}, u32[]{:S(2)}, u32[]{:S(2)}) collective-permute-start(bf16[576,128]{1,0:T(8,128)(2,1)S(1)} %get-tuple-element.144), channel_id=1, source_target_pairs={{0,4},{4,0},{8,12},{12,8},{1,5},{5,1},{9,13},{13,9},{2,6},{6,2},{1... | collective-permute-start | bytes 442376 | tf_op jit(solution)/shard_map/returns_last/ppermute | solution.py:397
  (10 other events, 54.3 us)

commit v15 on v14

--- a/solution.py
+++ b/solution.py
@@ -548,7 +548,7 @@
         stages.append([(output, head) for head in chosen for output in (0, 1)])
     key_grad, value_grad = unpack(stages, pieces, rows, heads, 2)
     with jax.named_scope("returns_last"):
-        last = swap_pieces(close(open_grads, parts, rows), gate)
+        last = swap_pieces(close(open_grads, parts, rows), gate[:2] + gate[:1:-1])
     (query_grad,) = unpack([[(0, head) for head in range(heads)]], [last], rows, heads, 1)
     result = (query_grad, key_grad, value_grad)
     with jax.named_scope("gain"):

time: 110 us -> 111 us (level)
  starting transfers between devices: 46.3 us -> 50.4 us
  waiting for transfers between devices: 41.5 us -> 37.8 us
    ppermute x21, starting transfers between devices: 36.9 us -> 41 us  [swap(): lax.ppermute(value, axis, [(index, index ^ distance) for index in range(l...]
    ppermute x21, waiting for transfers between devices: 39.3 us -> 35.5 us  [swap(): lax.ppermute(value, axis, [(index, index ^ distance) for index in range(l...]
where the time goes in v15:
time: 111 us; the launch traced here: 110 us
  starting transfers between devices  50.4 us (45%)
  waiting for transfers between devices  37.8 us (34%)
  Pallas kernels  21 us (19%)
    ppermute x21, starting transfers between devices, swap(): lax.ppermute(value, axis, [(index, index ^ distance) for index in range(l...  41 us
    ppermute x21, waiting for transfers between devices, swap(): lax.ppermute(value, axis, [(index, index ^ distance) for index in range(l...  35.5 us
    pallas_call x2, Pallas kernels, attention(): pl.pallas_call(functools.partial(attention_kernel, parts, sources, chosen...  9.54 us
    ppermute x5, starting transfers between devices, forward(): return [lax.ppermute(array, 'tm', there) for there, _ in sides]  6.69 us
    pallas_call x1, Pallas kernels, partial_totals(): pl.pallas_call(functools.partial(totals_kernel, parts, sources, heads), g...  3.85 us
    pallas_call x2, Pallas kernels, pack(): pl.pallas_call(functools.partial(pack_kernel, parts, chosen), in_specs=[w...  2.75 us
  transfers between devices with their start and end apart: 29, of which 11 were waited for; matrix products, arithmetic and copies ran while one was open for 0% of the time, Pallas kernels for 15%

profile of v15, /device:TPU:0, one launch (start us, length us, event | category | flops | bytes accessed | tf_op | source)
XLA Modules:
  0.0 110.4 jit_solution(16665683495978916433)
XLA Ops:
  0.7 2.6 %keys_queries.1 = (bf16[1152,128]{1,0:T(8,128)(2,1)}, bf16[1152,128]{1,0:T(8,128)(2,1)}, bf16[1152,128]{1,0:T(8,128)(2,1)}, bf16[1152,128]{1,0:T(8,128)(2,1)}) custom-call(bf16[192,1536]{1,0:T(8,128)(2,1)} %bitcast.17, bf16[192,1536]{1,0:T(8,128)(2,1)} %bitcast.18), custom_call_target="tpu_custom_call" | custom-call | flops 1 | bytes 1 | tf_op jit(solution)/shard_map/keys_queries/pallas_call | solution.py:64
  3.2 3.1 %collective-permute-start.3 = (bf16[1152,128]{1,0:T(8,128)(2,1)}, bf16[1152,128]{1,0:T(8,128)(2,1)S(1)}, u32[]{:S(2)}, u32[]{:S(2)}) collective-permute-start(bf16[1152,128]{1,0:T(8,128)(2,1)} %get-tuple-element.80), channel_id=1, source_target_pairs={{0,4},{4,0},{8,12},{12,8},{1,5},{5,1},{9,13},{13,9},{2,6},{6,2},{1... | collective-permute-start | bytes 884744 | tf_op jit(solution)/shard_map/keys_queries/ppermute | solution.py:397
  6.3 2.6 %collective-permute-start.4 = (bf16[1152,128]{1,0:T(8,128)(2,1)}, bf16[1152,128]{1,0:T(8,128)(2,1)S(1)}, u32[]{:S(2)}, u32[]{:S(2)}) collective-permute-start(bf16[1152,128]{1,0:T(8,128)(2,1)} %get-tuple-element.81), channel_id=1, source_target_pairs={{0,8},{4,12},{8,0},{12,4},{1,9},{5,13},{9,1},{13,5},{2,10},{6,14},... | collective-permute-start | bytes 884744 | tf_op jit(solution)/shard_map/keys_queries/ppermute | solution.py:397
  9.1 1.8 %collective-permute-start.1 = (f32[12,128]{1,0:T(8,128)S(1)}, f32[12,128]{1,0:T(8,128)S(1)}, u32[]{:S(2)}, u32[]{:S(2)}) collective-permute-start(f32[12,128]{1,0:T(8,128)S(1)} %bitcast.20), channel_id=1, source_target_pairs={{0,2},{1,3},{2,0},{3,1},{4,6},{5,7},{6,4},{7,5},{8,10},{9,11},{10,... | collective-permute-start | bytes 18440 | tf_op jit(solution)/shard_map/gain/ppermute | solution.py:397
  10.9 1.9 %collective-permute-done.1 = f32[12,128]{1,0:T(8,128)S(1)} collective-permute-done((f32[12,128]{1,0:T(8,128)S(1)}, f32[12,128]{1,0:T(8,128)S(1)}, u32[]{:S(2)}, u32[]{:S(2)}) %collective-permute-start.1) | collective-permute-done | bytes 6176 | tf_op jit(solution)/shard_map/gain/ppermute | solution.py:397
  16.0 3.1 %collective-permute-done.3.refs_2_.refs_3_.refs_7_.refs_11_.refs_15_.refs_19_.refs_23_.refs_13_.refs_21_.refs_37_.refs_45_ = bf16[1152,128]{1,0:T(8,128)(2,1)S(1)} collective-permute-done((bf16[1152,128]{1,0:T(8,128)(2,1)}, bf16[1152,128]{1,0:T(8,128)(2,1)S(1)}, u32[]{:S(2)}, u32[]{:S(2)}) %collective-permute-start.3) | collective-permute-done | bytes 294944 | tf_op jit(solution)/shard_map/keys_queries/ppermute | solution.py:397
  19.1 10.9 %collective-permute-done.4.refs_1_.refs_2_.refs_6_.refs_10_.refs_14_.refs_18_.refs_22_.refs_12_.refs_20_.refs_36_.refs_44_ = bf16[1152,128]{1,0:T(8,128)(2,1)S(1)} collective-permute-done((bf16[1152,128]{1,0:T(8,128)(2,1)}, bf16[1152,128]{1,0:T(8,128)(2,1)S(1)}, u32[]{:S(2)}, u32[]{:S(2)}) %collective-permute-start.4) | collective-permute-done | bytes 294944 | tf_op jit(solution)/shard_map/keys_queries/ppermute | solution.py:397
  32.7 2.5 %collective-permute-start.6 = (bf16[832,128]{1,0:T(8,128)(2,1)S(1)}, bf16[832,128]{1,0:T(8,128)(2,1)S(1)}, u32[]{:S(2)}, u32[]{:S(2)}) collective-permute-start(bf16[832,128]{1,0:T(8,128)(2,1)S(1)} %get-tuple-element.84), channel_id=1, source_target_pairs={{0,12},{4,8},{8,4},{12,0},{1,13},{5,9},{9,5},{13,1},{2,14},{6,10},... | collective-permute-start | bytes 638984 | tf_op jit(solution)/shard_map/grads/ppermute | solution.py:397
  35.2 6.7 %collective-permute-start.7 = (bf16[832,128]{1,0:T(8,128)(2,1)S(1)}, bf16[832,128]{1,0:T(8,128)(2,1)S(1)}, u32[]{:S(2)}, u32[]{:S(2)}) collective-permute-start(bf16[832,128]{1,0:T(8,128)(2,1)S(1)} %get-tuple-element.87), channel_id=1, source_target_pairs={{0,8},{4,12},{8,0},{12,4},{1,9},{5,13},{9,1},{13,5},{2,10},{6,14},... | collective-permute-start | bytes 638984 | tf_op jit(solution)/shard_map/grads/ppermute | solution.py:397
  42.4 3.8 %totals.1 = (f32[3,768]{1,0:T(4,128)S(1)}, f32[3,768]{1,0:T(4,128)S(1)}) custom-call(bf16[1152,128]{1,0:T(8,128)(2,1)S(1)} %copy-done, bf16[1152,128]{1,0:T(8,128)(2,1)S(1)} %collective-permute-done.5.refs_0_.refs_1_.refs_5_.refs_9_.refs_13_.refs_17_.refs_21_.refs_11_.refs_19_.refs_35_.refs_43_, ...), custom_call_target="tpu_custom_call" | custom-call | flops 905969664 | bytes 2359296 | tf_op jit(solution)/shard_map/totals/pallas_call | solution.py:240
  46.3 7.9 %collective-permute-done.7.refs_2_.refs_16_.refs_28_.refs_52_ = bf16[832,128]{1,0:T(8,128)(2,1)S(1)} collective-permute-done((bf16[832,128]{1,0:T(8,128)(2,1)S(1)}, bf16[832,128]{1,0:T(8,128)(2,1)S(1)}, u32[]{:S(2)}, u32[]{:S(2)}) %collective-permute-start.7) | collective-permute-done | bytes 213024 | tf_op jit(solution)/shard_map/grads/ppermute | solution.py:397
  56.8 2.7 %collective-permute-start.15 = (bf16[384,128]{1,0:T(8,128)(2,1)S(1)}, bf16[384,128]{1,0:T(8,128)(2,1)S(1)}, u32[]{:S(2)}, u32[]{:S(2)}) collective-permute-start(bf16[384,128]{1,0:T(8,128)(2,1)S(1)} %get-tuple-element.113), channel_id=1, source_target_pairs={{0,12},{4,8},{8,4},{12,0},{1,13},{5,9},{9,5},{13,1},{2,14},{6,10},... | collective-permute-start | bytes 294920 | tf_op jit(solution)/shard_map/rest_values/ppermute | solution.py:397
  59.5 1.7 %collective-permute-start.17 = (bf16[384,128]{1,0:T(8,128)(2,1)S(1)}, bf16[384,128]{1,0:T(8,128)(2,1)S(1)}, u32[]{:S(2)}, u32[]{:S(2)}) collective-permute-start(bf16[384,128]{1,0:T(8,128)(2,1)S(1)} %get-tuple-element.117), channel_id=1, source_target_pairs={{0,4},{4,0},{8,12},{12,8},{1,5},{5,1},{9,13},{13,9},{2,6},{6,2},{1... | collective-permute-start | bytes 294920 | tf_op jit(solution)/shard_map/rest_values/ppermute | solution.py:397
  63.5 3.3 %attention_0.1 = (bf16[384,128]{1,0:T(8,128)(2,1)S(1)}, bf16[384,128]{1,0:T(8,128)(2,1)S(1)}, bf16[384,128]{1,0:T(8,128)(2,1)S(1)}, bf16[384,128]{1,0:T(8,128)(2...) custom-call(bf16[832,128]{1,0:T(8,128)(2,1)S(1)} %get-tuple-element.118.refs_0_.refs_14_.refs_26_.refs_50_, ...), custom_call_target="tpu_custom_call" | custom-call | flops 1509949440 | bytes 3145728 | tf_op jit(solution)/shard_map/attention_0/pallas_call | solution.py:325
  67.3 2.6 %collective-permute-start.19 = (bf16[384,128]{1,0:T(8,128)(2,1)S(1)}, bf16[384,128]{1,0:T(8,128)(2,1)S(1)}, u32[]{:S(2)}, u32[]{:S(2)}) collective-permute-start(bf16[384,128]{1,0:T(8,128)(2,1)S(1)} %get-tuple-element.125), channel_id=1, source_target_pairs={{0,12},{4,8},{8,4},{12,0},{1,13},{5,9},{9,5},{13,1},{2,14},{6,10},... | collective-permute-start | bytes 294920 | tf_op jit(solution)/shard_map/returns_0/ppermute | solution.py:397
  71.7 6.3 %attention_1.1 = (bf16[768,128]{1,0:T(8,128)(2,1)S(1)}, bf16[768,128]{1,0:T(8,128)(2,1)S(1)}, bf16[768,128]{1,0:T(8,128)(2,1)S(1)}, bf16[768,128]{1,0:T(8,128)(2...) custom-call(bf16[832,128]{1,0:T(8,128)(2,1)S(1)} %get-tuple-element.118.refs_0_.refs_14_.refs_26_.refs_50_, ...), custom_call_target="tpu_custom_call" | custom-call | flops 3019898880 | bytes 6291456 | tf_op jit(solution)/shard_map/attention_1/pallas_call | solution.py:325
  79.6 2.6 %collective-permute-start.23 = (bf16[768,128]{1,0:T(8,128)(2,1)S(1)}, bf16[768,128]{1,0:T(8,128)(2,1)S(1)}, u32[]{:S(2)}, u32[]{:S(2)}) collective-permute-start(bf16[768,128]{1,0:T(8,128)(2,1)S(1)} %get-tuple-element.135), channel_id=1, source_target_pairs={{0,12},{4,8},{8,4},{12,0},{1,13},{5,9},{9,5},{13,1},{2,14},{6,10},... | collective-permute-start | bytes 589832 | tf_op jit(solution)/shard_map/returns_1/ppermute | solution.py:397
  82.3 1.7 %collective-permute-start.27 = (bf16[768,128]{1,0:T(8,128)(2,1)S(1)}, bf16[768,128]{1,0:T(8,128)(2,1)S(1)}, u32[]{:S(2)}, u32[]{:S(2)}) collective-permute-start(bf16[768,128]{1,0:T(8,128)(2,1)S(1)} %get-tuple-element.143), channel_id=1, source_target_pairs={{0,8},{4,12},{8,0},{12,4},{1,9},{5,13},{9,1},{13,5},{2,10},{6,14},... | collective-permute-start | bytes 589832 | tf_op jit(solution)/shard_map/returns_1/ppermute | solution.py:397
  84.0 1.9 %collective-permute-done.22.refs_3_ = bf16[1536,128]{1,0:T(8,128)(2,1)S(1)} collective-permute-done((bf16[1536,128]{1,0:T(8,128)(2,1)S(1)}, bf16[1536,128]{1,0:T(8,128)(2,1)S(1)}, u32[]{:S(2)}, u32[]{:S(2)}) %collective-permute-start.22) | collective-permute-done | bytes 393248 | tf_op jit(solution)/shard_map/halo_query_grads_1/ppermute | solution.py:543
  86.0 3.4 %collective-permute-done.23.refs_5_ = bf16[768,128]{1,0:T(8,128)(2,1)S(1)} collective-permute-done((bf16[768,128]{1,0:T(8,128)(2,1)S(1)}, bf16[768,128]{1,0:T(8,128)(2,1)S(1)}, u32[]{:S(2)}, u32[]{:S(2)}) %collective-permute-start.23) | collective-permute-done | bytes 196640 | tf_op jit(solution)/shard_map/returns_1/ppermute | solution.py:397
  89.4 2.6 %collective-permute-start.24 = (bf16[576,128]{1,0:T(8,128)(2,1)S(1)}, bf16[576,128]{1,0:T(8,128)(2,1)S(1)}, u32[]{:S(2)}, u32[]{:S(2)}) collective-permute-start(bf16[576,128]{1,0:T(8,128)(2,1)S(1)} %get-tuple-element.136), channel_id=1, source_target_pairs={{0,12},{4,8},{8,4},{12,0},{1,13},{5,9},{9,5},{13,1},{2,14},{6,10},... | collective-permute-start | bytes 442376 | tf_op jit(solution)/shard_map/returns_last/ppermute | solution.py:397
  92.0 8.3 %collective-permute-start.26 = (bf16[576,128]{1,0:T(8,128)(2,1)S(1)}, bf16[576,128]{1,0:T(8,128)(2,1)S(1)}, u32[]{:S(2)}, u32[]{:S(2)}) collective-permute-start(bf16[576,128]{1,0:T(8,128)(2,1)S(1)} %get-tuple-element.140), channel_id=1, source_target_pairs={{0,8},{4,12},{8,0},{12,4},{1,9},{5,13},{9,1},{13,5},{2,10},{6,14},... | collective-permute-start | bytes 442376 | tf_op jit(solution)/shard_map/returns_last/ppermute | solution.py:397
  100.4 2.3 %collective-permute-done.27.refs_6_ = bf16[768,128]{1,0:T(8,128)(2,1)S(1)} collective-permute-done((bf16[768,128]{1,0:T(8,128)(2,1)S(1)}, bf16[768,128]{1,0:T(8,128)(2,1)S(1)}, u32[]{:S(2)}, u32[]{:S(2)}) %collective-permute-start.27) | collective-permute-done | bytes 196640 | tf_op jit(solution)/shard_map/returns_1/ppermute | solution.py:397
  104.5 3.4 %collective-permute-done.26.refs_2_ = bf16[576,128]{1,0:T(8,128)(2,1)S(1)} collective-permute-done((bf16[576,128]{1,0:T(8,128)(2,1)S(1)}, bf16[576,128]{1,0:T(8,128)(2,1)S(1)}, u32[]{:S(2)}, u32[]{:S(2)}) %collective-permute-start.26) | collective-permute-done | bytes 147488 | tf_op jit(solution)/shard_map/returns_last/ppermute | solution.py:397
  (64 shorter events, 19.5 us)
Async XLA Ops:
  3.2 15.9 %collective-permute-start.3 = (bf16[1152,128]{1,0:T(8,128)(2,1)}, bf16[1152,128]{1,0:T(8,128)(2,1)S(1)}, u32[]{:S(2)}, u32[]{:S(2)}) collective-permute-start(bf16[1152,128]{1,0:T(8,128)(2,1)} %get-tuple-element.80), channel_id=1, source_target_pairs={{0,4},{4,0},{8,12},{12,8},{1,5},{5,1},{9,13},{13,9},{2,6},{6,2},{1... | collective-permute-start | bytes 884744 | tf_op jit(solution)/shard_map/keys_queries/ppermute | solution.py:397
  6.3 23.7 %collective-permute-start.4 = (bf16[1152,128]{1,0:T(8,128)(2,1)}, bf16[1152,128]{1,0:T(8,128)(2,1)S(1)}, u32[]{:S(2)}, u32[]{:S(2)}) collective-permute-start(bf16[1152,128]{1,0:T(8,128)(2,1)} %get-tuple-element.81), channel_id=1, source_target_pairs={{0,8},{4,12},{8,0},{12,4},{1,9},{5,13},{9,1},{13,5},{2,10},{6,14},... | collective-permute-start | bytes 884744 | tf_op jit(solution)/shard_map/keys_queries/ppermute | solution.py:397
  8.9 21.1 %collective-permute-start.5 = (bf16[1152,128]{1,0:T(8,128)(2,1)}, bf16[1152,128]{1,0:T(8,128)(2,1)S(1)}, u32[]{:S(2)}, u32[]{:S(2)}) collective-permute-start(bf16[1152,128]{1,0:T(8,128)(2,1)} %get-tuple-element.82), channel_id=1, source_target_pairs={{0,12},{4,8},{8,4},{12,0},{1,13},{5,9},{9,5},{13,1},{2,14},{6,10},... | collective-permute-start | bytes 884744 | tf_op jit(solution)/shard_map/keys_queries/ppermute | solution.py:397
  13.9 16.1 %collective-permute-start.10 = (bf16[576,128]{1,0:T(8,128)(2,1)S(1)}, bf16[576,128]{1,0:T(8,128)(2,1)S(1)}, u32[]{:S(2)}, u32[]{:S(2)}) collective-permute-start(bf16[576,128]{1,0:T(8,128)(2,1)S(1)} %slice.9), channel_id=1, source_target_pairs={{0,16},{16,0},{1,17},{17,1},{2,18},{18,2},{3,19},{19,3},{4,20},{20... | collective-permute-start | bytes 442376 | tf_op jit(solution)/shard_map/halo_queries/ppermute | solution.py:464
  30.6 11.8 %collective-permute-start.11 = (bf16[1728,128]{1,0:T(8,128)(2,1)S(1)}, bf16[1728,128]{1,0:T(8,128)(2,1)S(1)}, u32[]{:S(2)}, u32[]{:S(2)}) collective-permute-start(bf16[1728,128]{1,0:T(8,128)(2,1)S(1)} %halo_queries.1), channel_id=1, source_target_pairs={{0,16},{16,0},{1,17},{17,1},{2,18},{18,2},{3,19},{19,3},{4,20},{20... | collective-permute-start | bytes 1327112 | tf_op jit(solution)/shard_map/halo_queries/ppermute | solution.py:464
  32.2 14.1 %collective-permute-start.9 = (bf16[832,128]{1,0:T(8,128)(2,1)S(1)}, bf16[832,128]{1,0:T(8,128)(2,1)S(1)}, u32[]{:S(2)}, u32[]{:S(2)}) collective-permute-start(bf16[832,128]{1,0:T(8,128)(2,1)S(1)} %get-tuple-element.118.refs_0_.refs_14_.refs_26_.refs_50_), channel_id=1, source_target_pairs={{0,16},{16,0},{1,17},{17,1},{2,18},{18,2},{3,19},{19,3},{4,20},{20... | collective-permute-start | bytes 638984 | tf_op jit(solution)/shard_map/halo_own_grads/ppermute | solution.py:464
  32.7 13.5 %collective-permute-start.6 = (bf16[832,128]{1,0:T(8,128)(2,1)S(1)}, bf16[832,128]{1,0:T(8,128)(2,1)S(1)}, u32[]{:S(2)}, u32[]{:S(2)}) collective-permute-start(bf16[832,128]{1,0:T(8,128)(2,1)S(1)} %get-tuple-element.84), channel_id=1, source_target_pairs={{0,12},{4,8},{8,4},{12,0},{1,13},{5,9},{9,5},{13,1},{2,14},{6,10},... | collective-permute-start | bytes 638984 | tf_op jit(solution)/shard_map/grads/ppermute | solution.py:397
  35.2 18.9 %collective-permute-start.7 = (bf16[832,128]{1,0:T(8,128)(2,1)S(1)}, bf16[832,128]{1,0:T(8,128)(2,1)S(1)}, u32[]{:S(2)}, u32[]{:S(2)}) collective-permute-start(bf16[832,128]{1,0:T(8,128)(2,1)S(1)} %get-tuple-element.87), channel_id=1, source_target_pairs={{0,8},{4,12},{8,0},{12,4},{1,9},{5,13},{9,1},{13,5},{2,10},{6,14},... | collective-permute-start | bytes 638984 | tf_op jit(solution)/shard_map/grads/ppermute | solution.py:397
  41.9 12.2 %collective-permute-start.8 = (bf16[832,128]{1,0:T(8,128)(2,1)S(1)}, bf16[832,128]{1,0:T(8,128)(2,1)S(1)}, u32[]{:S(2)}, u32[]{:S(2)}) collective-permute-start(bf16[832,128]{1,0:T(8,128)(2,1)S(1)} %get-tuple-element.90), channel_id=1, source_target_pairs={{0,4},{4,0},{8,12},{12,8},{1,5},{5,1},{9,13},{13,9},{2,6},{6,2},{1... | collective-permute-start | bytes 638984 | tf_op jit(solution)/shard_map/grads/ppermute | solution.py:397
  56.0 7.4 %collective-permute-start.13 = (f32[6,768]{1,0:T(8,128)S(1)}, f32[6,768]{1,0:T(8,128)S(1)}, u32[]{:S(2)}, u32[]{:S(2)}) collective-permute-start(f32[6,768]{1,0:T(8,128)S(1)} %pad_maximum_fusion), channel_id=1, source_target_pairs={{0,16},{16,0},{1,17},{17,1},{2,18},{18,2},{3,19},{19,3},{4,20},{20... | collective-permute-start | bytes 55304 | tf_op jit(solution)/shard_map/totals/ppermute | solution.py:441
  56.8 10.5 %collective-permute-start.15 = (bf16[384,128]{1,0:T(8,128)(2,1)S(1)}, bf16[384,128]{1,0:T(8,128)(2,1)S(1)}, u32[]{:S(2)}, u32[]{:S(2)}) collective-permute-start(bf16[384,128]{1,0:T(8,128)(2,1)S(1)} %get-tuple-element.113), channel_id=1, source_target_pairs={{0,12},{4,8},{8,4},{12,0},{1,13},{5,9},{9,5},{13,1},{2,14},{6,10},... | collective-permute-start | bytes 294920 | tf_op jit(solution)/shard_map/rest_values/ppermute | solution.py:397
  59.5 10.5 %collective-permute-start.16 = (bf16[384,128]{1,0:T(8,128)(2,1)S(1)}, bf16[384,128]{1,0:T(8,128)(2,1)S(1)}, u32[]{:S(2)}, u32[]{:S(2)}) collective-permute-start(bf16[384,128]{1,0:T(8,128)(2,1)S(1)} %get-tuple-element.115), channel_id=1, source_target_pairs={{0,8},{4,12},{8,0},{12,4},{1,9},{5,13},{9,1},{13,5},{2,10},{6,14},... | collective-permute-start | bytes 294920 | tf_op jit(solution)/shard_map/rest_values/ppermute | solution.py:397
  59.5 10.5 %collective-permute-start.17 = (bf16[384,128]{1,0:T(8,128)(2,1)S(1)}, bf16[384,128]{1,0:T(8,128)(2,1)S(1)}, u32[]{:S(2)}, u32[]{:S(2)}) collective-permute-start(bf16[384,128]{1,0:T(8,128)(2,1)S(1)} %get-tuple-element.117), channel_id=1, source_target_pairs={{0,4},{4,0},{8,12},{12,8},{1,5},{5,1},{9,13},{13,9},{2,6},{6,2},{1... | collective-permute-start | bytes 294920 | tf_op jit(solution)/shard_map/rest_values/ppermute | solution.py:397
  61.9 9.9 %collective-permute-start.18 = (bf16[1152,128]{1,0:T(8,128)(2,1)S(1)}, bf16[1152,128]{1,0:T(8,128)(2,1)S(1)}, u32[]{:S(2)}, u32[]{:S(2)}) collective-permute-start(bf16[1152,128]{1,0:T(8,128)(2,1)S(1)} %halo_rest_grads.1), channel_id=1, source_target_pairs={{0,16},{16,0},{1,17},{17,1},{2,18},{18,2},{3,19},{19,3},{4,20},{20... | collective-permute-start | bytes 884744 | tf_op jit(solution)/shard_map/halo_rest_grads/ppermute | solution.py:464
  66.7 11.3 %collective-permute-start.14 = (bf16[768,128]{1,0:T(8,128)(2,1)S(1)}, bf16[768,128]{1,0:T(8,128)(2,1)S(1)}, u32[]{:S(2)}, u32[]{:S(2)}) collective-permute-start(bf16[768,128]{1,0:T(8,128)(2,1)S(1)} %get-tuple-element.103), channel_id=1, source_target_pairs={{0,16},{16,0},{1,17},{17,1},{2,18},{18,2},{3,19},{19,3},{4,20},{20... | collective-permute-start | bytes 589832 | tf_op jit(solution)/shard_map/halo_query_grads_0/ppermute | solution.py:543
  67.3 10.7 %collective-permute-start.19 = (bf16[384,128]{1,0:T(8,128)(2,1)S(1)}, bf16[384,128]{1,0:T(8,128)(2,1)S(1)}, u32[]{:S(2)}, u32[]{:S(2)}) collective-permute-start(bf16[384,128]{1,0:T(8,128)(2,1)S(1)} %get-tuple-element.125), channel_id=1, source_target_pairs={{0,12},{4,8},{8,4},{12,0},{1,13},{5,9},{9,5},{13,1},{2,14},{6,10},... | collective-permute-start | bytes 294920 | tf_op jit(solution)/shard_map/returns_0/ppermute | solution.py:397
  70.0 8.1 %collective-permute-start.20 = (bf16[384,128]{1,0:T(8,128)(2,1)S(1)}, bf16[384,128]{1,0:T(8,128)(2,1)S(1)}, u32[]{:S(2)}, u32[]{:S(2)}) collective-permute-start(bf16[384,128]{1,0:T(8,128)(2,1)S(1)} %get-tuple-element.127), channel_id=1, source_target_pairs={{0,8},{4,12},{8,0},{12,4},{1,9},{5,13},{9,1},{13,5},{2,10},{6,14},... | collective-permute-start | bytes 294920 | tf_op jit(solution)/shard_map/returns_0/ppermute | solution.py:397
  70.0 8.1 %collective-permute-start.21 = (bf16[384,128]{1,0:T(8,128)(2,1)S(1)}, bf16[384,128]{1,0:T(8,128)(2,1)S(1)}, u32[]{:S(2)}, u32[]{:S(2)}) collective-permute-start(bf16[384,128]{1,0:T(8,128)(2,1)S(1)} %get-tuple-element.129), channel_id=1, source_target_pairs={{0,4},{4,0},{8,12},{12,8},{1,5},{5,1},{9,13},{13,9},{2,6},{6,2},{1... | collective-permute-start | bytes 294920 | tf_op jit(solution)/shard_map/returns_0/ppermute | solution.py:397
  78.1 7.8 %collective-permute-start.22 = (bf16[1536,128]{1,0:T(8,128)(2,1)S(1)}, bf16[1536,128]{1,0:T(8,128)(2,1)S(1)}, u32[]{:S(2)}, u32[]{:S(2)}) collective-permute-start(bf16[1536,128]{1,0:T(8,128)(2,1)S(1)} %get-tuple-element.131), channel_id=1, source_target_pairs={{0,16},{16,0},{1,17},{17,1},{2,18},{18,2},{3,19},{19,3},{4,20},{20... | collective-permute-start | bytes 1179656 | tf_op jit(solution)/shard_map/halo_query_grads_1/ppermute | solution.py:543
  79.6 9.8 %collective-permute-start.23 = (bf16[768,128]{1,0:T(8,128)(2,1)S(1)}, bf16[768,128]{1,0:T(8,128)(2,1)S(1)}, u32[]{:S(2)}, u32[]{:S(2)}) collective-permute-start(bf16[768,128]{1,0:T(8,128)(2,1)S(1)} %get-tuple-element.135), channel_id=1, source_target_pairs={{0,12},{4,8},{8,4},{12,0},{1,13},{5,9},{9,5},{13,1},{2,14},{6,10},... | collective-permute-start | bytes 589832 | tf_op jit(solution)/shard_map/returns_1/ppermute | solution.py:397
  82.3 9.8 %collective-permute-start.25 = (bf16[768,128]{1,0:T(8,128)(2,1)S(1)}, bf16[768,128]{1,0:T(8,128)(2,1)S(1)}, u32[]{:S(2)}, u32[]{:S(2)}) collective-permute-start(bf16[768,128]{1,0:T(8,128)(2,1)S(1)} %get-tuple-element.139), channel_id=1, source_target_pairs={{0,4},{4,0},{8,12},{12,8},{1,5},{5,1},{9,13},{13,9},{2,6},{6,2},{1... | collective-permute-start | bytes 589832 | tf_op jit(solution)/shard_map/returns_1/ppermute | solution.py:397
  82.3 20.4 %collective-permute-start.27 = (bf16[768,128]{1,0:T(8,128)(2,1)S(1)}, bf16[768,128]{1,0:T(8,128)(2,1)S(1)}, u32[]{:S(2)}, u32[]{:S(2)}) collective-permute-start(bf16[768,128]{1,0:T(8,128)(2,1)S(1)} %get-tuple-element.143), channel_id=1, source_target_pairs={{0,8},{4,12},{8,0},{12,4},{1,9},{5,13},{9,1},{13,5},{2,10},{6,14},... | collective-permute-start | bytes 589832 | tf_op jit(solution)/shard_map/returns_1/ppermute | solution.py:397
  89.4 15.1 %collective-permute-start.24 = (bf16[576,128]{1,0:T(8,128)(2,1)S(1)}, bf16[576,128]{1,0:T(8,128)(2,1)S(1)}, u32[]{:S(2)}, u32[]{:S(2)}) collective-permute-start(bf16[576,128]{1,0:T(8,128)(2,1)S(1)} %get-tuple-element.136), channel_id=1, source_target_pairs={{0,12},{4,8},{8,4},{12,0},{1,13},{5,9},{9,5},{13,1},{2,14},{6,10},... | collective-permute-start | bytes 442376 | tf_op jit(solution)/shard_map/returns_last/ppermute | solution.py:397
  92.0 15.9 %collective-permute-start.26 = (bf16[576,128]{1,0:T(8,128)(2,1)S(1)}, bf16[576,128]{1,0:T(8,128)(2,1)S(1)}, u32[]{:S(2)}, u32[]{:S(2)}) collective-permute-start(bf16[576,128]{1,0:T(8,128)(2,1)S(1)} %get-tuple-element.140), channel_id=1, source_target_pairs={{0,8},{4,12},{8,0},{12,4},{1,9},{5,13},{9,1},{13,5},{2,10},{6,14},... | collective-permute-start | bytes 442376 | tf_op jit(solution)/shard_map/returns_last/ppermute | solution.py:397
  (10 other events, 53.7 us)

commit v16 on v14

--- a/solution.py
+++ b/solution.py
@@ -12,6 +12,7 @@
 LANES = 128
 TILE_ROWS = 16
 KEY_BLOCK = 768
+TOTAL_BLOCK = 256
 QUERY_BLOCK = 256
 VMEM_LIMIT = 48 * 1024 * 1024
 VMEM_WHOLE = 62 * 1024 * 1024
@@ -215,15 +216,15 @@
             start = (source * heads + head) * parts
             flip = jnp.transpose(stacked(query_refs[start : start + parts]))
             top = None
-            for first in range(0, slab, KEY_BLOCK):
-                scores = jnp.dot(keys[first : first + KEY_BLOCK], flip, preferred_element_type=jnp.float32)
-                score_ref[first : first + KEY_BLOCK] = scores
+            for first in range(0, slab, TOTAL_BLOCK):
+                scores = jnp.dot(keys[first : first + TOTAL_BLOCK], flip, preferred_element_type=jnp.float32)
+                score_ref[first : first + TOTAL_BLOCK] = scores
                 part_top = jnp.max(scores.reshape(-1, 8, slab), axis=0)
                 top = part_top if top is None else jnp.maximum(top, part_top)
             top = jnp.max(top, axis=0, keepdims=True) * SCALE_LOG2
             total = None
-            for first in range(0, slab, KEY_BLOCK):
-                powers = jnp.exp2(score_ref[first : first + KEY_BLOCK] * SCALE_LOG2 - top)
+            for first in range(0, slab, TOTAL_BLOCK):
+                powers = jnp.exp2(score_ref[first : first + TOTAL_BLOCK] * SCALE_LOG2 - top)
                 part_total = jnp.sum(powers.reshape(-1, 8, slab), axis=0)
                 total = part_total if total is None else total + part_total
             total = jnp.sum(total, axis=0, keepdims=True)
@@ -302,14 +303,13 @@
                     local_rows = slice(low - first, high - first)
                     piece_refs[part][place : place + high - low] = key_grad[local_rows]
                     piece_refs[part][place + rows : place + rows + high - low] = value_grad[local_rows]
+        key_flip = jnp.transpose(keys)
         for source, ref in enumerate(query_grad_refs):
-            query_grad = lax.dot_general(
-                score_ref[:, source * slab : (source + 1) * slab],
-                keys,
-                (((0,), (0,)), ((), ())),
-                preferred_element_type=jnp.float32,
-            )
-            ref[number * slab : (number + 1) * slab] = (query_grad * SCALE).astype(ref.dtype)
+            for start in range(0, slab, QUERY_BLOCK):
+                span = slice(source * slab + start, source * slab + start + QUERY_BLOCK)
+                flat = jnp.dot(key_flip, score_ref[:, span], preferred_element_type=jnp.float32)
+                place = number * slab + start
+                ref[place : place + QUERY_BLOCK] = (jnp.transpose(flat) * SCALE).astype(ref.dtype)
 
 
 def attention(chosen, heads, rows, inputs, dots, totals):

time: 110 us -> 110 us (level)
  transfers between devices with their start and end apart: 29 -> 29, of which waited for: 11 -> 11; matrix products, arithmetic and copies ran while one was open for 0% -> 0% of each run, Pallas kernels for 15% -> 14%
where the time goes in v16:
time: 110 us; the launch traced here: 109 us
  starting transfers between devices  46.3 us (42%)
  waiting for transfers between devices  41.8 us (38%)
  Pallas kernels  20.1 us (18%)
    ppermute x21, waiting for transfers between devices, swap(): lax.ppermute(value, axis, [(index, index ^ distance) for index in range(l...  39.5 us
    ppermute x21, starting transfers between devices, swap(): lax.ppermute(value, axis, [(index, index ^ distance) for index in range(l...  36.9 us
    pallas_call x2, Pallas kernels, attention(): pl.pallas_call(functools.partial(attention_kernel, parts, sources, chosen...  8.84 us
    ppermute x5, starting transfers between devices, forward(): return [lax.ppermute(array, 'tm', there) for there, _ in sides]  6.69 us
    pallas_call x1, Pallas kernels, partial_totals(): pl.pallas_call(functools.partial(totals_kernel, parts, sources, heads), g...  3.61 us
    pallas_call x2, Pallas kernels, pack(): pl.pallas_call(functools.partial(pack_kernel, parts, chosen), in_specs=[w...  2.75 us
  transfers between devices with their start and end apart: 29, of which 11 were waited for; matrix products, arithmetic and copies ran while one was open for 0% of the time, Pallas kernels for 14%

profile of v16, /device:TPU:0, one launch (start us, length us, event | category | flops | bytes accessed | tf_op | source)
XLA Modules:
  0.0 109.4 jit_solution(18235268151060981614)
XLA Ops:
  0.7 2.6 %keys_queries.1 = (bf16[1152,128]{1,0:T(8,128)(2,1)}, bf16[1152,128]{1,0:T(8,128)(2,1)}, bf16[1152,128]{1,0:T(8,128)(2,1)}, bf16[1152,128]{1,0:T(8,128)(2,1)}) custom-call(bf16[192,1536]{1,0:T(8,128)(2,1)} %bitcast.17, bf16[192,1536]{1,0:T(8,128)(2,1)} %bitcast.18), custom_call_target="tpu_custom_call" | custom-call | flops 1 | bytes 1 | tf_op jit(solution)/shard_map/keys_queries/pallas_call | solution.py:65
  3.2 3.1 %collective-permute-start.3 = (bf16[1152,128]{1,0:T(8,128)(2,1)}, bf16[1152,128]{1,0:T(8,128)(2,1)S(1)}, u32[]{:S(2)}, u32[]{:S(2)}) collective-permute-start(bf16[1152,128]{1,0:T(8,128)(2,1)} %get-tuple-element.80), channel_id=1, source_target_pairs={{0,4},{4,0},{8,12},{12,8},{1,5},{5,1},{9,13},{13,9},{2,6},{6,2},{1... | collective-permute-start | bytes 884744 | tf_op jit(solution)/shard_map/keys_queries/ppermute | solution.py:397
  6.3 2.6 %collective-permute-start.4 = (bf16[1152,128]{1,0:T(8,128)(2,1)}, bf16[1152,128]{1,0:T(8,128)(2,1)S(1)}, u32[]{:S(2)}, u32[]{:S(2)}) collective-permute-start(bf16[1152,128]{1,0:T(8,128)(2,1)} %get-tuple-element.81), channel_id=1, source_target_pairs={{0,8},{4,12},{8,0},{12,4},{1,9},{5,13},{9,1},{13,5},{2,10},{6,14},... | collective-permute-start | bytes 884744 | tf_op jit(solution)/shard_map/keys_queries/ppermute | solution.py:397
  9.1 1.8 %collective-permute-start.1 = (f32[12,128]{1,0:T(8,128)S(1)}, f32[12,128]{1,0:T(8,128)S(1)}, u32[]{:S(2)}, u32[]{:S(2)}) collective-permute-start(f32[12,128]{1,0:T(8,128)S(1)} %bitcast.20), channel_id=1, source_target_pairs={{0,2},{1,3},{2,0},{3,1},{4,6},{5,7},{6,4},{7,5},{8,10},{9,11},{10,... | collective-permute-start | bytes 18440 | tf_op jit(solution)/shard_map/gain/ppermute | solution.py:397
  10.9 1.9 %collective-permute-done.1 = f32[12,128]{1,0:T(8,128)S(1)} collective-permute-done((f32[12,128]{1,0:T(8,128)S(1)}, f32[12,128]{1,0:T(8,128)S(1)}, u32[]{:S(2)}, u32[]{:S(2)}) %collective-permute-start.1) | collective-permute-done | bytes 6176 | tf_op jit(solution)/shard_map/gain/ppermute | solution.py:397
  16.0 3.1 %collective-permute-done.3.refs_2_.refs_3_.refs_7_.refs_11_.refs_15_.refs_19_.refs_23_.refs_13_.refs_21_.refs_37_.refs_45_ = bf16[1152,128]{1,0:T(8,128)(2,1)S(1)} collective-permute-done((bf16[1152,128]{1,0:T(8,128)(2,1)}, bf16[1152,128]{1,0:T(8,128)(2,1)S(1)}, u32[]{:S(2)}, u32[]{:S(2)}) %collective-permute-start.3) | collective-permute-done | bytes 294944 | tf_op jit(solution)/shard_map/keys_queries/ppermute | solution.py:397
  19.1 10.9 %collective-permute-done.4.refs_1_.refs_2_.refs_6_.refs_10_.refs_14_.refs_18_.refs_22_.refs_12_.refs_20_.refs_36_.refs_44_ = bf16[1152,128]{1,0:T(8,128)(2,1)S(1)} collective-permute-done((bf16[1152,128]{1,0:T(8,128)(2,1)}, bf16[1152,128]{1,0:T(8,128)(2,1)S(1)}, u32[]{:S(2)}, u32[]{:S(2)}) %collective-permute-start.4) | collective-permute-done | bytes 294944 | tf_op jit(solution)/shard_map/keys_queries/ppermute | solution.py:397
  32.7 2.5 %collective-permute-start.6 = (bf16[832,128]{1,0:T(8,128)(2,1)S(1)}, bf16[832,128]{1,0:T(8,128)(2,1)S(1)}, u32[]{:S(2)}, u32[]{:S(2)}) collective-permute-start(bf16[832,128]{1,0:T(8,128)(2,1)S(1)} %get-tuple-element.84), channel_id=1, source_target_pairs={{0,12},{4,8},{8,4},{12,0},{1,13},{5,9},{9,5},{13,1},{2,14},{6,10},... | collective-permute-start | bytes 638984 | tf_op jit(solution)/shard_map/grads/ppermute | solution.py:397
  35.2 6.7 %collective-permute-start.7 = (bf16[832,128]{1,0:T(8,128)(2,1)S(1)}, bf16[832,128]{1,0:T(8,128)(2,1)S(1)}, u32[]{:S(2)}, u32[]{:S(2)}) collective-permute-start(bf16[832,128]{1,0:T(8,128)(2,1)S(1)} %get-tuple-element.87), channel_id=1, source_target_pairs={{0,8},{4,12},{8,0},{12,4},{1,9},{5,13},{9,1},{13,5},{2,10},{6,14},... | collective-permute-start | bytes 638984 | tf_op jit(solution)/shard_map/grads/ppermute | solution.py:397
  42.4 3.6 %totals.1 = (f32[3,768]{1,0:T(4,128)S(1)}, f32[3,768]{1,0:T(4,128)S(1)}) custom-call(bf16[1152,128]{1,0:T(8,128)(2,1)S(1)} %copy-done, bf16[1152,128]{1,0:T(8,128)(2,1)S(1)} %collective-permute-done.5.refs_0_.refs_1_.refs_5_.refs_9_.refs_13_.refs_17_.refs_21_.refs_11_.refs_19_.refs_35_.refs_43_, ...), custom_call_target="tpu_custom_call" | custom-call | flops 905969664 | bytes 2359296 | tf_op jit(solution)/shard_map/totals/pallas_call | solution.py:241
  46.0 8.1 %collective-permute-done.7.refs_2_.refs_16_.refs_28_.refs_52_ = bf16[832,128]{1,0:T(8,128)(2,1)S(1)} collective-permute-done((bf16[832,128]{1,0:T(8,128)(2,1)S(1)}, bf16[832,128]{1,0:T(8,128)(2,1)S(1)}, u32[]{:S(2)}, u32[]{:S(2)}) %collective-permute-start.7) | collective-permute-done | bytes 213024 | tf_op jit(solution)/shard_map/grads/ppermute | solution.py:397
  56.8 2.7 %collective-permute-start.15 = (bf16[384,128]{1,0:T(8,128)(2,1)S(1)}, bf16[384,128]{1,0:T(8,128)(2,1)S(1)}, u32[]{:S(2)}, u32[]{:S(2)}) collective-permute-start(bf16[384,128]{1,0:T(8,128)(2,1)S(1)} %get-tuple-element.113), channel_id=1, source_target_pairs={{0,12},{4,8},{8,4},{12,0},{1,13},{5,9},{9,5},{13,1},{2,14},{6,10},... | collective-permute-start | bytes 294920 | tf_op jit(solution)/shard_map/rest_values/ppermute | solution.py:397
  59.5 1.7 %collective-permute-start.17 = (bf16[384,128]{1,0:T(8,128)(2,1)S(1)}, bf16[384,128]{1,0:T(8,128)(2,1)S(1)}, u32[]{:S(2)}, u32[]{:S(2)}) collective-permute-start(bf16[384,128]{1,0:T(8,128)(2,1)S(1)} %get-tuple-element.117), channel_id=1, source_target_pairs={{0,4},{4,0},{8,12},{12,8},{1,5},{5,1},{9,13},{13,9},{2,6},{6,2},{1... | collective-permute-start | bytes 294920 | tf_op jit(solution)/shard_map/rest_values/ppermute | solution.py:397
  63.5 3.0 %attention_0.1 = (bf16[384,128]{1,0:T(8,128)(2,1)S(1)}, bf16[384,128]{1,0:T(8,128)(2,1)S(1)}, bf16[384,128]{1,0:T(8,128)(2,1)S(1)}, bf16[384,128]{1,0:T(8,128)(2...) custom-call(bf16[832,128]{1,0:T(8,128)(2,1)S(1)} %get-tuple-element.118.refs_0_.refs_14_.refs_26_.refs_50_, ...), custom_call_target="tpu_custom_call" | custom-call | flops 1509949440 | bytes 3145728 | tf_op jit(solution)/shard_map/attention_0/pallas_call | solution.py:325
  67.1 2.6 %collective-permute-start.19 = (bf16[384,128]{1,0:T(8,128)(2,1)S(1)}, bf16[384,128]{1,0:T(8,128)(2,1)S(1)}, u32[]{:S(2)}, u32[]{:S(2)}) collective-permute-start(bf16[384,128]{1,0:T(8,128)(2,1)S(1)} %get-tuple-element.125), channel_id=1, source_target_pairs={{0,12},{4,8},{8,4},{12,0},{1,13},{5,9},{9,5},{13,1},{2,14},{6,10},... | collective-permute-start | bytes 294920 | tf_op jit(solution)/shard_map/returns_0/ppermute | solution.py:397
  69.8 1.7 %collective-permute-start.21 = (bf16[384,128]{1,0:T(8,128)(2,1)S(1)}, bf16[384,128]{1,0:T(8,128)(2,1)S(1)}, u32[]{:S(2)}, u32[]{:S(2)}) collective-permute-start(bf16[384,128]{1,0:T(8,128)(2,1)S(1)} %get-tuple-element.129), channel_id=1, source_target_pairs={{0,4},{4,0},{8,12},{12,8},{1,5},{5,1},{9,13},{13,9},{2,6},{6,2},{1... | collective-permute-start | bytes 294920 | tf_op jit(solution)/shard_map/returns_0/ppermute | solution.py:397
  71.5 5.8 %attention_1.1 = (bf16[768,128]{1,0:T(8,128)(2,1)S(1)}, bf16[768,128]{1,0:T(8,128)(2,1)S(1)}, bf16[768,128]{1,0:T(8,128)(2,1)S(1)}, bf16[768,128]{1,0:T(8,128)(2...) custom-call(bf16[832,128]{1,0:T(8,128)(2,1)S(1)} %get-tuple-element.118.refs_0_.refs_14_.refs_26_.refs_50_, ...), custom_call_target="tpu_custom_call" | custom-call | flops 3019898880 | bytes 6291456 | tf_op jit(solution)/shard_map/attention_1/pallas_call | solution.py:325
  78.9 2.6 %collective-permute-start.23 = (bf16[768,128]{1,0:T(8,128)(2,1)S(1)}, bf16[768,128]{1,0:T(8,128)(2,1)S(1)}, u32[]{:S(2)}, u32[]{:S(2)}) collective-permute-start(bf16[768,128]{1,0:T(8,128)(2,1)S(1)} %get-tuple-element.135), channel_id=1, source_target_pairs={{0,12},{4,8},{8,4},{12,0},{1,13},{5,9},{9,5},{13,1},{2,14},{6,10},... | collective-permute-start | bytes 589832 | tf_op jit(solution)/shard_map/returns_1/ppermute | solution.py:397
  81.6 1.7 %collective-permute-start.27 = (bf16[768,128]{1,0:T(8,128)(2,1)S(1)}, bf16[768,128]{1,0:T(8,128)(2,1)S(1)}, u32[]{:S(2)}, u32[]{:S(2)}) collective-permute-start(bf16[768,128]{1,0:T(8,128)(2,1)S(1)} %get-tuple-element.143), channel_id=1, source_target_pairs={{0,4},{4,0},{8,12},{12,8},{1,5},{5,1},{9,13},{13,9},{2,6},{6,2},{1... | collective-permute-start | bytes 589832 | tf_op jit(solution)/shard_map/returns_1/ppermute | solution.py:397
  83.3 1.9 %collective-permute-done.22.refs_3_ = bf16[1536,128]{1,0:T(8,128)(2,1)S(1)} collective-permute-done((bf16[1536,128]{1,0:T(8,128)(2,1)S(1)}, bf16[1536,128]{1,0:T(8,128)(2,1)S(1)}, u32[]{:S(2)}, u32[]{:S(2)}) %collective-permute-start.22) | collective-permute-done | bytes 393248 | tf_op jit(solution)/shard_map/halo_query_grads_1/ppermute | solution.py:543
  85.3 3.4 %collective-permute-done.23.refs_5_ = bf16[768,128]{1,0:T(8,128)(2,1)S(1)} collective-permute-done((bf16[768,128]{1,0:T(8,128)(2,1)S(1)}, bf16[768,128]{1,0:T(8,128)(2,1)S(1)}, u32[]{:S(2)}, u32[]{:S(2)}) %collective-permute-start.23) | collective-permute-done | bytes 196640 | tf_op jit(solution)/shard_map/returns_1/ppermute | solution.py:397
  88.7 2.7 %collective-permute-start.24 = (bf16[576,128]{1,0:T(8,128)(2,1)S(1)}, bf16[576,128]{1,0:T(8,128)(2,1)S(1)}, u32[]{:S(2)}, u32[]{:S(2)}) collective-permute-start(bf16[576,128]{1,0:T(8,128)(2,1)S(1)} %get-tuple-element.136), channel_id=1, source_target_pairs={{0,12},{4,8},{8,4},{12,0},{1,13},{5,9},{9,5},{13,1},{2,14},{6,10},... | collective-permute-start | bytes 442376 | tf_op jit(solution)/shard_map/returns_last/ppermute | solution.py:397
  91.4 8.9 %collective-permute-done.25.refs_6_ = bf16[768,128]{1,0:T(8,128)(2,1)S(1)} collective-permute-done((bf16[768,128]{1,0:T(8,128)(2,1)S(1)}, bf16[768,128]{1,0:T(8,128)(2,1)S(1)}, u32[]{:S(2)}, u32[]{:S(2)}) %collective-permute-start.25) | collective-permute-done | bytes 196640 | tf_op jit(solution)/shard_map/returns_1/ppermute | solution.py:397
  100.2 4.2 %collective-permute-start.28 = (bf16[576,128]{1,0:T(8,128)(2,1)S(1)}, bf16[576,128]{1,0:T(8,128)(2,1)S(1)}, u32[]{:S(2)}, u32[]{:S(2)}) collective-permute-start(bf16[576,128]{1,0:T(8,128)(2,1)S(1)} %get-tuple-element.144), channel_id=1, source_target_pairs={{0,4},{4,0},{8,12},{12,8},{1,5},{5,1},{9,13},{13,9},{2,6},{6,2},{1... | collective-permute-start | bytes 442376 | tf_op jit(solution)/shard_map/returns_last/ppermute | solution.py:397
  (64 shorter events, 18.4 us)
Async XLA Ops:
  3.2 15.9 %collective-permute-start.3 = (bf16[1152,128]{1,0:T(8,128)(2,1)}, bf16[1152,128]{1,0:T(8,128)(2,1)S(1)}, u32[]{:S(2)}, u32[]{:S(2)}) collective-permute-start(bf16[1152,128]{1,0:T(8,128)(2,1)} %get-tuple-element.80), channel_id=1, source_target_pairs={{0,4},{4,0},{8,12},{12,8},{1,5},{5,1},{9,13},{13,9},{2,6},{6,2},{1... | collective-permute-start | bytes 884744 | tf_op jit(solution)/shard_map/keys_queries/ppermute | solution.py:397
  6.3 23.7 %collective-permute-start.4 = (bf16[1152,128]{1,0:T(8,128)(2,1)}, bf16[1152,128]{1,0:T(8,128)(2,1)S(1)}, u32[]{:S(2)}, u32[]{:S(2)}) collective-permute-start(bf16[1152,128]{1,0:T(8,128)(2,1)} %get-tuple-element.81), channel_id=1, source_target_pairs={{0,8},{4,12},{8,0},{12,4},{1,9},{5,13},{9,1},{13,5},{2,10},{6,14},... | collective-permute-start | bytes 884744 | tf_op jit(solution)/shard_map/keys_queries/ppermute | solution.py:397
  8.9 21.1 %collective-permute-start.5 = (bf16[1152,128]{1,0:T(8,128)(2,1)}, bf16[1152,128]{1,0:T(8,128)(2,1)S(1)}, u32[]{:S(2)}, u32[]{:S(2)}) collective-permute-start(bf16[1152,128]{1,0:T(8,128)(2,1)} %get-tuple-element.82), channel_id=1, source_target_pairs={{0,12},{4,8},{8,4},{12,0},{1,13},{5,9},{9,5},{13,1},{2,14},{6,10},... | collective-permute-start | bytes 884744 | tf_op jit(solution)/shard_map/keys_queries/ppermute | solution.py:397
  13.9 16.1 %collective-permute-start.10 = (bf16[576,128]{1,0:T(8,128)(2,1)S(1)}, bf16[576,128]{1,0:T(8,128)(2,1)S(1)}, u32[]{:S(2)}, u32[]{:S(2)}) collective-permute-start(bf16[576,128]{1,0:T(8,128)(2,1)S(1)} %slice.9), channel_id=1, source_target_pairs={{0,16},{16,0},{1,17},{17,1},{2,18},{18,2},{3,19},{19,3},{4,20},{20... | collective-permute-start | bytes 442376 | tf_op jit(solution)/shard_map/halo_queries/ppermute | solution.py:464
  30.6 11.8 %collective-permute-start.11 = (bf16[1728,128]{1,0:T(8,128)(2,1)S(1)}, bf16[1728,128]{1,0:T(8,128)(2,1)S(1)}, u32[]{:S(2)}, u32[]{:S(2)}) collective-permute-start(bf16[1728,128]{1,0:T(8,128)(2,1)S(1)} %halo_queries.1), channel_id=1, source_target_pairs={{0,16},{16,0},{1,17},{17,1},{2,18},{18,2},{3,19},{19,3},{4,20},{20... | collective-permute-start | bytes 1327112 | tf_op jit(solution)/shard_map/halo_queries/ppermute | solution.py:464
  32.2 13.8 %collective-permute-start.9 = (bf16[832,128]{1,0:T(8,128)(2,1)S(1)}, bf16[832,128]{1,0:T(8,128)(2,1)S(1)}, u32[]{:S(2)}, u32[]{:S(2)}) collective-permute-start(bf16[832,128]{1,0:T(8,128)(2,1)S(1)} %get-tuple-element.118.refs_0_.refs_14_.refs_26_.refs_50_), channel_id=1, source_target_pairs={{0,16},{16,0},{1,17},{17,1},{2,18},{18,2},{3,19},{19,3},{4,20},{20... | collective-permute-start | bytes 638984 | tf_op jit(solution)/shard_map/halo_own_grads/ppermute | solution.py:464
  32.7 13.3 %collective-permute-start.6 = (bf16[832,128]{1,0:T(8,128)(2,1)S(1)}, bf16[832,128]{1,0:T(8,128)(2,1)S(1)}, u32[]{:S(2)}, u32[]{:S(2)}) collective-permute-start(bf16[832,128]{1,0:T(8,128)(2,1)S(1)} %get-tuple-element.84), channel_id=1, source_target_pairs={{0,12},{4,8},{8,4},{12,0},{1,13},{5,9},{9,5},{13,1},{2,14},{6,10},... | collective-permute-start | bytes 638984 | tf_op jit(solution)/shard_map/grads/ppermute | solution.py:397
  35.2 18.9 %collective-permute-start.7 = (bf16[832,128]{1,0:T(8,128)(2,1)S(1)}, bf16[832,128]{1,0:T(8,128)(2,1)S(1)}, u32[]{:S(2)}, u32[]{:S(2)}) collective-permute-start(bf16[832,128]{1,0:T(8,128)(2,1)S(1)} %get-tuple-element.87), channel_id=1, source_target_pairs={{0,8},{4,12},{8,0},{12,4},{1,9},{5,13},{9,1},{13,5},{2,10},{6,14},... | collective-permute-start | bytes 638984 | tf_op jit(solution)/shard_map/grads/ppermute | solution.py:397
  41.9 12.2 %collective-permute-start.8 = (bf16[832,128]{1,0:T(8,128)(2,1)S(1)}, bf16[832,128]{1,0:T(8,128)(2,1)S(1)}, u32[]{:S(2)}, u32[]{:S(2)}) collective-permute-start(bf16[832,128]{1,0:T(8,128)(2,1)S(1)} %get-tuple-element.90), channel_id=1, source_target_pairs={{0,4},{4,0},{8,12},{12,8},{1,5},{5,1},{9,13},{13,9},{2,6},{6,2},{1... | collective-permute-start | bytes 638984 | tf_op jit(solution)/shard_map/grads/ppermute | solution.py:397
  56.8 10.3 %collective-permute-start.15 = (bf16[384,128]{1,0:T(8,128)(2,1)S(1)}, bf16[384,128]{1,0:T(8,128)(2,1)S(1)}, u32[]{:S(2)}, u32[]{:S(2)}) collective-permute-start(bf16[384,128]{1,0:T(8,128)(2,1)S(1)} %get-tuple-element.113), channel_id=1, source_target_pairs={{0,12},{4,8},{8,4},{12,0},{1,13},{5,9},{9,5},{13,1},{2,14},{6,10},... | collective-permute-start | bytes 294920 | tf_op jit(solution)/shard_map/rest_values/ppermute | solution.py:397
  59.5 10.3 %collective-permute-start.16 = (bf16[384,128]{1,0:T(8,128)(2,1)S(1)}, bf16[384,128]{1,0:T(8,128)(2,1)S(1)}, u32[]{:S(2)}, u32[]{:S(2)}) collective-permute-start(bf16[384,128]{1,0:T(8,128)(2,1)S(1)} %get-tuple-element.115), channel_id=1, source_target_pairs={{0,8},{4,12},{8,0},{12,4},{1,9},{5,13},{9,1},{13,5},{2,10},{6,14},... | collective-permute-start | bytes 294920 | tf_op jit(solution)/shard_map/rest_values/ppermute | solution.py:397
  59.5 10.3 %collective-permute-start.17 = (bf16[384,128]{1,0:T(8,128)(2,1)S(1)}, bf16[384,128]{1,0:T(8,128)(2,1)S(1)}, u32[]{:S(2)}, u32[]{:S(2)}) collective-permute-start(bf16[384,128]{1,0:T(8,128)(2,1)S(1)} %get-tuple-element.117), channel_id=1, source_target_pairs={{0,4},{4,0},{8,12},{12,8},{1,5},{5,1},{9,13},{13,9},{2,6},{6,2},{1... | collective-permute-start | bytes 294920 | tf_op jit(solution)/shard_map/rest_values/ppermute | solution.py:397
  61.9 9.7 %collective-permute-start.18 = (bf16[1152,128]{1,0:T(8,128)(2,1)S(1)}, bf16[1152,128]{1,0:T(8,128)(2,1)S(1)}, u32[]{:S(2)}, u32[]{:S(2)}) collective-permute-start(bf16[1152,128]{1,0:T(8,128)(2,1)S(1)} %halo_rest_grads.1), channel_id=1, source_target_pairs={{0,16},{16,0},{1,17},{17,1},{2,18},{18,2},{3,19},{19,3},{4,20},{20... | collective-permute-start | bytes 884744 | tf_op jit(solution)/shard_map/halo_rest_grads/ppermute | solution.py:464
  66.5 10.8 %collective-permute-start.14 = (bf16[768,128]{1,0:T(8,128)(2,1)S(1)}, bf16[768,128]{1,0:T(8,128)(2,1)S(1)}, u32[]{:S(2)}, u32[]{:S(2)}) collective-permute-start(bf16[768,128]{1,0:T(8,128)(2,1)S(1)} %get-tuple-element.103), channel_id=1, source_target_pairs={{0,16},{16,0},{1,17},{17,1},{2,18},{18,2},{3,19},{19,3},{4,20},{20... | collective-permute-start | bytes 589832 | tf_op jit(solution)/shard_map/halo_query_grads_0/ppermute | solution.py:543
  67.1 10.2 %collective-permute-start.19 = (bf16[384,128]{1,0:T(8,128)(2,1)S(1)}, bf16[384,128]{1,0:T(8,128)(2,1)S(1)}, u32[]{:S(2)}, u32[]{:S(2)}) collective-permute-start(bf16[384,128]{1,0:T(8,128)(2,1)S(1)} %get-tuple-element.125), channel_id=1, source_target_pairs={{0,12},{4,8},{8,4},{12,0},{1,13},{5,9},{9,5},{13,1},{2,14},{6,10},... | collective-permute-start | bytes 294920 | tf_op jit(solution)/shard_map/returns_0/ppermute | solution.py:397
  69.8 7.6 %collective-permute-start.20 = (bf16[384,128]{1,0:T(8,128)(2,1)S(1)}, bf16[384,128]{1,0:T(8,128)(2,1)S(1)}, u32[]{:S(2)}, u32[]{:S(2)}) collective-permute-start(bf16[384,128]{1,0:T(8,128)(2,1)S(1)} %get-tuple-element.127), channel_id=1, source_target_pairs={{0,8},{4,12},{8,0},{12,4},{1,9},{5,13},{9,1},{13,5},{2,10},{6,14},... | collective-permute-start | bytes 294920 | tf_op jit(solution)/shard_map/returns_0/ppermute | solution.py:397
  69.8 7.6 %collective-permute-start.21 = (bf16[384,128]{1,0:T(8,128)(2,1)S(1)}, bf16[384,128]{1,0:T(8,128)(2,1)S(1)}, u32[]{:S(2)}, u32[]{:S(2)}) collective-permute-start(bf16[384,128]{1,0:T(8,128)(2,1)S(1)} %get-tuple-element.129), channel_id=1, source_target_pairs={{0,4},{4,0},{8,12},{12,8},{1,5},{5,1},{9,13},{13,9},{2,6},{6,2},{1... | collective-permute-start | bytes 294920 | tf_op jit(solution)/shard_map/returns_0/ppermute | solution.py:397
  77.4 7.8 %collective-permute-start.22 = (bf16[1536,128]{1,0:T(8,128)(2,1)S(1)}, bf16[1536,128]{1,0:T(8,128)(2,1)S(1)}, u32[]{:S(2)}, u32[]{:S(2)}) collective-permute-start(bf16[1536,128]{1,0:T(8,128)(2,1)S(1)} %get-tuple-element.131), channel_id=1, source_target_pairs={{0,16},{16,0},{1,17},{17,1},{2,18},{18,2},{3,19},{19,3},{4,20},{20... | collective-permute-start | bytes 1179656 | tf_op jit(solution)/shard_map/halo_query_grads_1/ppermute | solution.py:543
  78.9 9.7 %collective-permute-start.23 = (bf16[768,128]{1,0:T(8,128)(2,1)S(1)}, bf16[768,128]{1,0:T(8,128)(2,1)S(1)}, u32[]{:S(2)}, u32[]{:S(2)}) collective-permute-start(bf16[768,128]{1,0:T(8,128)(2,1)S(1)} %get-tuple-element.135), channel_id=1, source_target_pairs={{0,12},{4,8},{8,4},{12,0},{1,13},{5,9},{9,5},{13,1},{2,14},{6,10},... | collective-permute-start | bytes 589832 | tf_op jit(solution)/shard_map/returns_1/ppermute | solution.py:397
  81.6 18.6 %collective-permute-start.25 = (bf16[768,128]{1,0:T(8,128)(2,1)S(1)}, bf16[768,128]{1,0:T(8,128)(2,1)S(1)}, u32[]{:S(2)}, u32[]{:S(2)}) collective-permute-start(bf16[768,128]{1,0:T(8,128)(2,1)S(1)} %get-tuple-element.139), channel_id=1, source_target_pairs={{0,8},{4,12},{8,0},{12,4},{1,9},{5,13},{9,1},{13,5},{2,10},{6,14},... | collective-permute-start | bytes 589832 | tf_op jit(solution)/shard_map/returns_1/ppermute | solution.py:397
  81.6 18.6 %collective-permute-start.27 = (bf16[768,128]{1,0:T(8,128)(2,1)S(1)}, bf16[768,128]{1,0:T(8,128)(2,1)S(1)}, u32[]{:S(2)}, u32[]{:S(2)}) collective-permute-start(bf16[768,128]{1,0:T(8,128)(2,1)S(1)} %get-tuple-element.143), channel_id=1, source_target_pairs={{0,4},{4,0},{8,12},{12,8},{1,5},{5,1},{9,13},{13,9},{2,6},{6,2},{1... | collective-permute-start | bytes 589832 | tf_op jit(solution)/shard_map/returns_1/ppermute | solution.py:397
  88.7 17.5 %collective-permute-start.24 = (bf16[576,128]{1,0:T(8,128)(2,1)S(1)}, bf16[576,128]{1,0:T(8,128)(2,1)S(1)}, u32[]{:S(2)}, u32[]{:S(2)}) collective-permute-start(bf16[576,128]{1,0:T(8,128)(2,1)S(1)} %get-tuple-element.136), channel_id=1, source_target_pairs={{0,12},{4,8},{8,4},{12,0},{1,13},{5,9},{9,5},{13,1},{2,14},{6,10},... | collective-permute-start | bytes 442376 | tf_op jit(solution)/shard_map/returns_last/ppermute | solution.py:397
  100.2 7.7 %collective-permute-start.26 = (bf16[576,128]{1,0:T(8,128)(2,1)S(1)}, bf16[576,128]{1,0:T(8,128)(2,1)S(1)}, u32[]{:S(2)}, u32[]{:S(2)}) collective-permute-start(bf16[576,128]{1,0:T(8,128)(2,1)S(1)} %get-tuple-element.140), channel_id=1, source_target_pairs={{0,8},{4,12},{8,0},{12,4},{1,9},{5,13},{9,1},{13,5},{2,10},{6,14},... | collective-permute-start | bytes 442376 | tf_op jit(solution)/shard_map/returns_last/ppermute | solution.py:397
  100.2 8.1 %collective-permute-start.28 = (bf16[576,128]{1,0:T(8,128)(2,1)S(1)}, bf16[576,128]{1,0:T(8,128)(2,1)S(1)}, u32[]{:S(2)}, u32[]{:S(2)}) collective-permute-start(bf16[576,128]{1,0:T(8,128)(2,1)S(1)} %get-tuple-element.144), channel_id=1, source_target_pairs={{0,4},{4,0},{8,12},{12,8},{1,5},{5,1},{9,13},{13,9},{2,6},{6,2},{1... | collective-permute-start | bytes 442376 | tf_op jit(solution)/shard_map/returns_last/ppermute | solution.py:397
  (10 other events, 54.3 us)
